TPU v7x, 256 devices: a whole 4x4x8 slice. The times are simulated.
256 devices in a mesh: section: 2 (over core), expert: 16 (over x_lo, z), dp: 8 (over x_hi, y).
Axes of the slice: x: 4 (x_hi: 2, x_lo: 2; x = x_hi * 2 + x_lo), y: 4, z: 8, core: 2. Of those that a mesh axis runs over, the one named last changes fastest.
Arguments:
- section_input: bfloat16 [2, 16384, 4096], P('section', ('expert', 'dp')), may hold values from -6 to 6
- routing: int32 [2, 16384, 8], P('section', ('expert', 'dp')), may hold values from 0 to 127, as said below
- out_grad: bfloat16 [2, 16384, 4096], P('section', ('expert', 'dp')), may hold values from -6 to 6
- norm_gain: float32 [2, 4096], P('section'), may hold values from 0.1 to 1.9
- router: bfloat16 [2, 4096, 128], P('section'), may hold values from -0.09375 to 0.09375
- w_in: bfloat16 [2, 16, 4096, 1536], P('section', 'expert', 'dp'), may hold values from -0.09375 to 0.09375
- w_out: bfloat16 [2, 16, 768, 4096], P('section', 'expert', None, 'dp'), may hold values from -0.21875 to 0.21875
Outputs:
- handoff: bfloat16 [2, 16384, 4096], P('section', ('expert', 'dp'))
- handback: bfloat16 [2, 16384, 4096], P('section', ('expert', 'dp'))
- grad_in: bfloat16 [2, 16, 4096, 1536], P('section', 'expert', 'dp')
- grad_out: bfloat16 [2, 16, 768, 4096], P('section', 'expert', None, 'dp')
- grad_router: bfloat16 [2, 4096, 128], P('section')
- grad_gain: float32 [2, 4096], P('section')
Inputs may be any that keep to these rules, and one draw needn't show every extreme that they name: `routing`: each row names 8 different experts. In each aligned block of 128 rows (the rows of one device) no expert is named more than 10 times.
All inputs are finite; a program needn't handle non-finite values.
Results may differ from a plain program's by a relative error of at most 0.027.
Values may be sent and summed in bfloat16 or wider, within the bound.
No kernel may reach another device: no remote copies, remote signals or barrier semaphores. Data moves between devices by JAX's collectives and lax.ppermute only.
A program may use at most 128 MiB of HBM per device.

v0:
```python
import jax
import jax.numpy as jnp
from jax import lax
from jax.sharding import PartitionSpec as P

MOST = 10


def passed_along(block, axis, distance):
    devices = range(lax.axis_size(axis))
    route = [((i - distance) % len(devices), i) for i in devices]
    return lax.ppermute(block, axis, route)


def silu_parts(values):
    sigmoid = jax.nn.sigmoid(values)
    return (values * sigmoid, sigmoid * (1.0 + values * (1.0 - sigmoid)))


def send_rows(buffer):
    flattened = buffer.reshape((-1,) + buffer.shape[2:])
    return lax.all_to_all(
        flattened, ("expert", "dp"), split_axis=0, concat_axis=0, tiled=True
    ).reshape(buffer.shape)


def return_rows(buffer):
    flattened = buffer.reshape((-1,) + buffer.shape[2:])
    return lax.all_to_all(
        flattened, ("expert", "dp"), split_axis=0, concat_axis=0, tiled=True
    ).reshape(buffer.shape)


def contract_rows(left, right):
    return lax.dot_general(
        left, right, (((0,), (0,)), ((), ())), preferred_element_type=jnp.float32
    )


def contract_cols(left, right):
    return lax.dot_general(
        left, right, (((1,), (1,)), ((), ())), preferred_element_type=jnp.float32
    )


def shards(section_input, routing, out_grad, norm_gain, router, w_in, w_out):
    expert_count = lax.axis_size("expert")
    replica_count = lax.axis_size("dp")
    block_input = section_input[0]
    route_ids = routing[0]
    grad_top = out_grad[0]
    gain_vector = norm_gain[0]
    router_table = router[0]
    weight_first = w_in[0, 0]
    weight_second = w_out[0, 0]
    token_count, model_width = block_input.shape
    top_count = route_ids.shape[1]
    router_width = router_table.shape[1]
    part_width = model_width // replica_count
    hidden_width = weight_second.shape[0]
    slot_count = MOST
    highest = lax.Precision.HIGHEST
    x_wide = block_input.astype(jnp.float32)
    inv_rms = lax.rsqrt(jnp.mean(x_wide * x_wide, axis=1, keepdims=True) + 1e-06)
    normed = (x_wide * inv_rms * gain_vector[None, :]).astype(jnp.bfloat16)
    logits = jnp.dot(normed, router_table, preferred_element_type=jnp.float32)
    chosen = jnp.take_along_axis(logits, route_ids, axis=1)
    exp_terms = jnp.exp(chosen)
    gate_weights = exp_terms / jnp.sum(exp_terms, axis=1, keepdims=True)
    window = jnp.arange(expert_count, dtype=jnp.int32)
    matches = (
        (route_ids[:, :, None] == window)
        .astype(jnp.int32)
        .reshape(token_count * top_count, expert_count)
    )
    slot_rank = jnp.cumsum(matches, axis=0) - 1
    slot_ids = jnp.arange(slot_count, dtype=jnp.int32)
    slot_hits = matches[:, :, None] * (slot_rank[:, :, None] == slot_ids).astype(jnp.int32)
    slot_hits = slot_hits.reshape(token_count, top_count, expert_count, slot_count).astype(
        jnp.float32
    )
    dispatch = jnp.sum(slot_hits, axis=1)
    combine = jnp.sum(gate_weights[:, :, None, None] * slot_hits, axis=1)
    dispatch_half = dispatch.astype(jnp.bfloat16)
    normed_split = normed.reshape(token_count, replica_count, part_width)
    outgoing = jnp.einsum(
        "tes,tjd->ejsd", dispatch_half, normed_split, preferred_element_type=jnp.float32
    ).astype(jnp.bfloat16)
    expert_rows = send_rows(outgoing).reshape(-1, part_width)
    pre_act = lax.psum_scatter(
        jnp.dot(expert_rows, weight_first, preferred_element_type=jnp.float32).astype(jnp.bfloat16),
        "dp",
        scatter_dimension=0,
        tiled=True,
    ).astype(jnp.float32)
    activated, act_slope = silu_parts(pre_act[:, :hidden_width])
    up_part = pre_act[:, hidden_width:]
    hidden = lax.all_gather((activated * up_part).astype(jnp.bfloat16), "dp", axis=0, tiled=True)
    expert_out = jnp.dot(hidden, weight_second, preferred_element_type=jnp.float32).astype(
        jnp.bfloat16
    )
    returned = return_rows(expert_out.reshape(expert_count, replica_count, slot_count, part_width))
    mixed = jnp.einsum("tes,ejsd->tjd", combine, returned.astype(jnp.float32), precision=highest)
    layer_out = (x_wide + mixed.reshape(token_count, model_width)).astype(jnp.bfloat16)
    grad_split = grad_top.reshape(token_count, replica_count, part_width)
    intersection = jnp.einsum(
        "tjd,ejsd->tes", grad_split, returned, preferred_element_type=jnp.float32
    )
    gate_grad = jnp.sum(slot_hits * intersection[:, None, :, :], axis=(2, 3))
    sent_grad = jnp.einsum(
        "tes,tjd->ejsd", combine, grad_split.astype(jnp.float32), precision=highest
    ).astype(jnp.bfloat16)
    rows_grad = send_rows(sent_grad).reshape(-1, part_width)
    second_grad = contract_rows(hidden, rows_grad)
    hidden_grad = lax.psum_scatter(
        contract_cols(rows_grad, weight_second).astype(jnp.bfloat16),
        "dp",
        scatter_dimension=0,
        tiled=True,
    ).astype(jnp.float32)
    pre_grad = jnp.concatenate(
        [hidden_grad * up_part * act_slope, hidden_grad * activated], axis=1
    ).astype(jnp.bfloat16)
    incoming = lax.all_gather(pre_grad, "dp", axis=0, tiled=True)
    weight_total = contract_rows(expert_rows, incoming)
    back_total = contract_cols(incoming, weight_first)
    expert_back = back_total.astype(jnp.bfloat16)
    came_back = return_rows(
        expert_back.reshape(expert_count, replica_count, slot_count, part_width)
    )
    normed_back = jnp.einsum(
        "tes,ejsd->tjd", dispatch_half, came_back, preferred_element_type=jnp.float32
    )
    normed_back = normed_back.reshape(token_count, model_width)
    inner_sum = jnp.sum(gate_weights * gate_grad, axis=1, keepdims=True)
    chosen_grad = gate_weights * (gate_grad - inner_sum)
    columns = jnp.arange(router_width, dtype=jnp.int32)
    logit_grad = jnp.sum(
        chosen_grad[:, :, None] * (route_ids[:, :, None] == columns).astype(jnp.float32), axis=1
    )
    router_wide = router_table.astype(jnp.float32)
    normed_grad = normed_back + lax.dot_general(
        logit_grad, router_wide, (((1,), (1,)), ((), ())), precision=highest
    )
    local_router = lax.dot_general(
        normed.astype(jnp.float32), logit_grad, (((0,), (0,)), ((), ())), precision=highest
    )
    local_gain = jnp.sum(normed_grad * x_wide * inv_rms, axis=0)
    router_total, gain_total = lax.psum((local_router, local_gain), ("expert", "dp"))
    weighted = gain_vector[None, :] * normed_grad
    in_grad = (
        grad_top.astype(jnp.float32)
        + inv_rms * weighted
        - x_wide * inv_rms * inv_rms * inv_rms * jnp.mean(x_wide * weighted, axis=1, keepdims=True)
    ).astype(jnp.bfloat16)
    handoff = passed_along(layer_out, "section", 1)
    handback = passed_along(in_grad, "section", -1)
    return (
        handoff[None],
        handback[None],
        weight_total.astype(jnp.bfloat16)[None, None],
        second_grad.astype(jnp.bfloat16)[None, None],
        router_total.astype(jnp.bfloat16)[None],
        gain_total[None],
    )


def solution(mesh):
    return jax.shard_map(
        shards,
        mesh=mesh,
        in_specs=(
            P("section", ("expert", "dp"), None),
            P("section", ("expert", "dp"), None),
            P("section", ("expert", "dp"), None),
            P("section", None),
            P("section", None, None),
            P("section", "expert", "dp", None),
            P("section", "expert", None, "dp"),
        ),
        out_specs=(
            P("section", ("expert", "dp"), None),
            P("section", ("expert", "dp"), None),
            P("section", "expert", "dp", None),
            P("section", "expert", None, "dp"),
            P("section", None, None),
            P("section", None),
        ),
        check_vma=False,
    )
```

profile of v0, /device:TPU:128, one launch (start us, length us, event | category | flops | bytes accessed | tf_op | source)
XLA Modules:
  0.0 1355.9 jit_solution(11903097864201542375)
XLA Ops:
  12.4 4.5 reduce-window.6
  21.4 63.5 %all_to_all.20 = bf16[128,10,512]{2,1,0:T(8,128)(2,1)} all-to-all(bf16[128,10,512]{2,1,0:T(8,128)(2,1)S(1)} %copy.69), channel_id=1, replica_groups=mesh['section'=2,'expert'=16,'dp'=8] {'expert','dp'}, dimensions={0} | all-to-all | bytes 2621440 | tf_op jit(solution)/shard_map/all_to_all | solution.py:22
  85.0 3.6 reshape_reshape.12
  88.6 5.4 convolution_convert_fusion
  94.1 86.6 %reduce-scatter.3.cloned.1.call-done = bf16[160,1536]{1,0:T(8,128)(2,1)} async-done(((bf16[1280,1536]{1,0:T(8,128)(2,1)}), bf16[160,1536]{1,0:T(8,128)(2,1)}) %reduce-scatter.3.cloned.1.call-update) | async-done | bytes 491536 | tf_op jit(solution)/shard_map/reduce_scatter | solution.py:90
  183.6 57.2 %all-gather.3.cloned.1.call-done = bf16[1280,768]{1,0:T(8,128)(2,1)} async-done(((bf16[160,768]{1,0:T(8,128)(2,1)}), bf16[1280,768]{1,0:T(8,128)(2,1)}) %all-gather.3.cloned.1.call-update) | async-done | bytes 1966096 | tf_op jit(solution)/shard_map/all_gather | solution.py:98
  240.8 4.0 convolution_convert_fusion.3
  244.8 3.6 reshape_reshape.13
  248.4 10.8 all-to-all-start.1
  261.3 6.8 gather_fusion
  268.3 2.6 copy.85
  270.9 37.3 %all-to-all-done.1 = bf16[128,10,512]{2,1,0:T(8,128)(2,1)} async-done(((bf16[128,10,512]{2,1,0:T(8,128)(2,1)}), bf16[128,10,512]{2,1,0:T(8,128)(2,1)}, u32[]{:S(2)}, u32[]{:S(2)}) %all-to-all-start.1) | async-done | bytes 1310752 | tf_op jit(solution)/shard_map/all_to_all | solution.py:29
  308.3 3.4 fusion.25
  315.1 58.7 %all_to_all.21 = bf16[128,10,512]{2,1,0:T(8,128)(2,1)} all-to-all(bf16[128,10,512]{2,1,0:T(8,128)(2,1)S(1)} %copy.73), channel_id=1, replica_groups=mesh['section'=2,'expert'=16,'dp'=8] {'expert','dp'}, dimensions={0} | all-to-all | bytes 2621440 | tf_op jit(solution)/shard_map/all_to_all | solution.py:22
  373.7 3.6 reshape_reshape.14
  377.4 4.0 convolution_convert_fusion.1
  381.5 78.0 %reduce-scatter.5.cloned.1.call-done = bf16[160,768]{1,0:T(8,128)(2,1)} async-done(((bf16[1280,768]{1,0:T(8,128)(2,1)}), bf16[160,768]{1,0:T(8,128)(2,1)}) %reduce-scatter.5.cloned.1.call-update) | async-done | bytes 245776 | tf_op jit(solution)/shard_map/reduce_scatter | solution.py:115
  461.9 73.6 %all-gather.5.cloned.1.call-done = bf16[1280,1536]{1,0:T(8,128)(2,1)} async-done(((bf16[160,1536]{1,0:T(8,128)(2,1)}), bf16[1280,1536]{1,0:T(8,128)(2,1)}) %all-gather.5.cloned.1.call-update) | async-done | bytes 3932176 | tf_op jit(solution)/shard_map/all_gather | solution.py:124
  535.5 5.5 convolution_convert_fusion.4
  541.0 3.6 reshape_reshape.15
  544.6 10.6 all-to-all-start.3
  555.2 3.4 copy.112
  558.6 3.3 dot_general.57
  561.9 3.4 fusion.1
  565.9 2.7 fusion.33
  568.6 2.1 fusion.24
  571.4 3.4 fusion.2
  574.8 29.6 %all-to-all-done.3 = bf16[128,10,512]{2,1,0:T(8,128)(2,1)} async-done(((bf16[128,10,512]{2,1,0:T(8,128)(2,1)}), bf16[128,10,512]{2,1,0:T(8,128)(2,1)}, u32[]{:S(2)}, u32[]{:S(2)}) %all-to-all-start.3) | async-done | bytes 1310752 | tf_op jit(solution)/shard_map/all_to_all | solution.py:29
  604.4 3.4 copy.110
  607.7 3.3 dot_general.63
  616.4 729.4 %all-reduce.2 = (bf16[4096,128]{1,0:T(8,128)(2,1)}, f32[1,4096]{1,0:T(1,128)}) all-reduce(f32[4096,128]{1,0:T(8,128)} %fusion.33, f32[1,4096]{1,0:T(1,128)S(1)} %bitcast.172), channel_id=1, replica_groups=mesh['section'=2,'expert'=16,'dp'=8] {'expert','dp'}, use_global_device_ids=true, to_apply=%region_12.13 | all-reduce | flops 528384 | bytes 3178496 | tf_op jit(solution)/shard_map/psum | solution.py:149
  1345.7 2.3 copy.119
  (84 shorter events, 28.3 us)
Async XLA Ops:
  7.2 81.4 %copy-start = (bf16[1,1,512,1536]{3,2,1,0:T(8,128)(2,1)S(1)}, bf16[1,1,512,1536]{3,2,1,0:T(8,128)(2,1)}, u32[]{:S(2)}) copy-start(bf16[1,1,512,1536]{3,2,1,0:T(8,128)(2,1)} %param.12) | copy-start | bytes 4718596
  7.2 10.6 copy-start.1
  7.2 173.5 %reduce-scatter.3.cloned.1.call-start = ((), (), s32[]{:S(2)}) async-start(), calls=%async_computation.6 | async-start | bytes 4423680 | tf_op jit(solution)/shard_map/reduce_scatter | solution.py:90
  94.0 146.8 %all-gather.3.cloned.1.call-start = ((), (), s32[]{:S(2)}) async-start(), calls=%async_computation.7 | async-start | bytes 2211840 | tf_op jit(solution)/shard_map/all_gather | solution.py:98
  181.8 0.9 copy-start.2
  248.4 11.0 copy-start.9
  248.4 11.2 copy-start.8
  248.4 59.9 %all-to-all-start.1 = ((bf16[128,10,512]{2,1,0:T(8,128)(2,1)}), bf16[128,10,512]{2,1,0:T(8,128)(2,1)}, u32[]{:S(2)}, u32[]{:S(2)}) async-start(bf16[128,10,512]{2,1,0:T(8,128)(2,1)} %reshape_reshape.13), calls=%async_computation.2 | async-start | bytes 4194304 | tf_op jit(solution)/shard_map/all_to_all | solution.py:29
  259.1 200.3 %reduce-scatter.5.cloned.1.call-start = ((), (), s32[]{:S(2)}) async-start(), calls=%async_computation.8 | async-start | bytes 2211840 | tf_op jit(solution)/shard_map/reduce_scatter | solution.py:115
  308.3 3.6 copy-start.3
  381.4 154.1 %all-gather.5.cloned.1.call-start = ((), (), s32[]{:S(2)}) async-start(), calls=%async_computation.9 | async-start | bytes 4423680 | tf_op jit(solution)/shard_map/all_gather | solution.py:124
  544.6 59.8 %all-to-all-start.3 = ((bf16[128,10,512]{2,1,0:T(8,128)(2,1)}), bf16[128,10,512]{2,1,0:T(8,128)(2,1)}, u32[]{:S(2)}, u32[]{:S(2)}) async-start(bf16[128,10,512]{2,1,0:T(8,128)(2,1)} %reshape_reshape.15), calls=%async_computation.5 | async-start | bytes 4194304 | tf_op jit(solution)/shard_map/all_to_all | solution.py:29
  565.3 3.3 collective-permute-start
  565.5 3.1 copy-start.6
  565.5 3.1 copy-start.11
  568.6 2.1 copy-start.5
  568.6 2.8 copy-start.10
  611.0 1.9 copy-start.7
  612.9 1.7 copy-start.4
  616.4 729.4 %collective-permute-start.1 = (bf16[128,4096]{1,0:T(8,128)(2,1)}, bf16[128,4096]{1,0:T(8,128)(2,1)S(1)}, u32[]{:S(2)}, u32[]{:S(2)}) collective-permute-start(bf16[128,4096]{1,0:T(8,128)(2,1)} %fusion.4), channel_id=1, source_target_pairs={{128,0},{0,128},{129,1},{1,129},{130,2},{2,130},{131,3},{3,131},{1... | collective-permute-start | bytes 3145736 | tf_op jit(solution)/shard_map/ppermute | solution.py:12
Sparse Core Ops, SparseCore 0:
  94.1 86.4 reduce-scatter.2
  184.1 56.6 all-gather.2
  381.5 77.8 reduce-scatter.4
  462.5 72.9 all-gather.4
where the time goes:
time: 1370 us; the launch traced here: 1360 us
  blocking collectives  852 us (62%)
  waiting for transfers between devices  362 us (26%)
  local copies, waits for them, and re-layouts  48.4 us (4%)
  matrix products  42.2 us (3%)
  starting transfers between devices  21.7 us (2%)
  other arithmetic  15.2 us (1%)
  between operations  14.4 us (1%)
    psum x1, blocking collectives, shards(): lax.psum((local_router, local_gain), ('expert', 'dp'))  729 us
    all_to_all x2, blocking collectives, send_rows(): lax.all_to_all(flattened, ('expert', 'dp'), split_axis=0, concat_axis=0,...  122 us
    reduce_scatter x1, waiting for transfers between devices, shards(): lax.psum_scatter(jnp.dot(expert_rows, weight_first, preferred_element_typ...  86.6 us
    reduce_scatter x1, waiting for transfers between devices, shards(): lax.psum_scatter(contract_cols(rows_grad, weight_second).astype(jnp.bfloa...  78 us
    all_gather x1, waiting for transfers between devices, shards(): incoming = lax.all_gather(pre_grad, 'dp', axis=0, tiled=True)  73.6 us
    all_to_all x2, waiting for transfers between devices, return_rows(): lax.all_to_all(flattened, ('expert', 'dp'), split_axis=0, concat_axis=0,...  66.9 us
    all_gather x1, waiting for transfers between devices, shards(): lax.all_gather((activated * up_part).astype(jnp.bfloat16), 'dp', axis=0,...  57.2 us
  transfers between devices with their start and end apart: 8, of which 6 were waited for; matrix products, arithmetic and copies ran while one was open for 2% of the time, Pallas kernels for 0%

commit v1 on v0

v1 whole, which is shorter than its diff:
```python
import jax
import jax.numpy as jnp
from jax import lax
from jax.sharding import PartitionSpec as P

MOST = 10
LANES = 128
BF = jnp.bfloat16
F32 = jnp.float32
ALL = ("dp", "expert")


def exchange(blocks, axes):
    return lax.all_to_all(blocks, axes, split_axis=0, concat_axis=0, tiled=True)


def mm(left, right, contract):
    return lax.dot_general(left, right, (contract, ((), ())), preferred_element_type=F32)


def two_terms(values):
    high = values.astype(BF)
    return high, (values - high.astype(F32)).astype(BF)


def mm_wide_left(left, right, contract):
    high, low = two_terms(left)
    return mm(high, right, contract) + mm(low, right, contract)


def shards(section_input, routing, out_grad, norm_gain, router, w_in, w_out):
    experts = lax.axis_size("expert")
    replicas = lax.axis_size("dp")
    x = section_input[0]
    route_ids = routing[0]
    grad_top = out_grad[0]
    gain = norm_gain[0][None, :]
    table = router[0]
    first = w_in[0, 0]
    second = w_out[0, 0]
    tokens, width = x.shape
    part = width // replicas
    hidden_width = second.shape[0]
    slots = MOST
    rows = experts * slots
    router_width = table.shape[1]

    xw = x.astype(F32)
    inv_rms = lax.rsqrt(jnp.mean(xw * xw, axis=1, keepdims=True) + 1e-06)
    normed = (xw * inv_rms * gain).astype(BF)
    logits = jnp.dot(normed, table, preferred_element_type=F32)
    columns = jnp.arange(router_width, dtype=jnp.int32)
    named = jnp.any(route_ids[:, :, None] == columns, axis=1)
    powers = jnp.where(named, jnp.exp(logits), 0.0)
    gates = powers / jnp.sum(powers, axis=1, keepdims=True)
    window = named[:, :experts]
    earlier = jnp.tri(tokens, tokens, -1, dtype=BF)
    rank = jnp.dot(earlier, window.astype(BF), preferred_element_type=F32)
    slot_ids = jnp.arange(slots, dtype=F32)
    hits = (window[:, :, None] & (rank[:, :, None] == slot_ids)).reshape(tokens, rows)
    place = hits.astype(BF)
    combine = jnp.where(hits, jnp.repeat(gates[:, :experts], slots, axis=1), 0.0)
    slot_gate = jnp.sum(combine, axis=0)[:, None]

    def outbound(picked):
        return picked.astype(BF).reshape(experts, slots, replicas, part).transpose(2, 0, 1, 3)

    picked_normed = mm(place, normed, ((0,), (0,)))
    picked_grad = mm(place, grad_top, ((0,), (0,))) * slot_gate
    message = jnp.concatenate([outbound(picked_normed), outbound(picked_grad)], axis=2)
    message = message.reshape(replicas * experts, 2 * slots * part // LANES, LANES)
    arrived = exchange(message, ALL).reshape(replicas * experts, 2 * slots, part)
    expert_rows = arrived[:, :slots].reshape(-1, part)
    grad_rows = arrived[:, slots:].reshape(-1, part)

    partial = jnp.concatenate(
        [mm(expert_rows, first, ((1,), (0,))).astype(BF), mm(grad_rows, second, ((1,), (1,))).astype(BF)],
        axis=1,
    ).reshape(replicas, rows, 3 * hidden_width)
    total = jnp.sum(exchange(partial, "dp").astype(F32), axis=0)
    gate_pre = total[:, :hidden_width]
    up = total[:, hidden_width : 2 * hidden_width]
    hidden_grad = total[:, 2 * hidden_width :]
    sigmoid = jax.nn.sigmoid(gate_pre)
    silu = gate_pre * sigmoid
    slope = sigmoid * (1.0 + gate_pre * (1.0 - sigmoid))
    hidden = (silu * up).astype(BF)
    worth = jnp.sum(hidden_grad * hidden.astype(F32), axis=1)
    acts = jnp.concatenate(
        [(hidden_grad * up * slope).astype(BF), (hidden_grad * silu).astype(BF), hidden], axis=1
    )
    gathered = exchange(jnp.broadcast_to(acts[None], (replicas,) + acts.shape), "dp")
    gathered = gathered.reshape(-1, 3 * hidden_width)
    pre_grad = gathered[:, : 2 * hidden_width]
    hidden_all = gathered[:, 2 * hidden_width :]

    worth = jnp.pad(worth.reshape(experts, 1, slots), ((0, 0), (0, 0), (0, LANES - slots)))
    worth = exchange(worth, "expert")[:, 0, :slots].reshape(1, rows)
    gate_worth = jnp.sum(
        jnp.where(hits, worth, 0.0).reshape(tokens, experts, slots), axis=2
    )
    inner = jnp.sum(gate_worth, axis=1, keepdims=True)
    logit_grad = jnp.pad(gate_worth, ((0, 0), (0, router_width - experts))) - gates * inner
    logit_high, logit_low = two_terms(logit_grad)
    local_router = mm(normed, logit_high, ((0,), (0,))) + mm(normed, logit_low, ((0,), (0,)))
    router_part = exchange(local_router.astype(BF).reshape(replicas, part, router_width), "dp")
    router_part = jnp.sum(router_part.astype(F32), axis=0)

    out_rows = mm(hidden_all, second, ((1,), (0,))).astype(BF)
    back_rows = mm(pre_grad, first, ((1,), (1,))).astype(BF)
    message = jnp.concatenate(
        [out_rows.reshape(-1, slots, part), back_rows.reshape(-1, slots, part)], axis=1
    ).reshape(replicas * experts, 2 * slots * part // LANES, LANES)
    returned = exchange(message, ALL).reshape(replicas, experts, 2 * slots, part)

    first_grad = mm(expert_rows, pre_grad, ((0,), (0,)))
    second_grad = mm(hidden_all, grad_rows, ((0,), (0,)))
    gain_part = jnp.sum(first_grad * first.astype(F32), axis=1)

    piece = part // experts
    gain_rows = jnp.pad(gain_part.reshape(experts, 1, piece), ((0, 0), (0, 7), (0, LANES - piece)))
    owned = jnp.concatenate([router_part.reshape(experts, piece, router_width), gain_rows], axis=1)
    owned = jnp.sum(exchange(owned, "expert"), axis=0)
    router_own = owned[:piece]
    index = lax.axis_index("dp") * part + lax.axis_index("expert") * piece
    table_own = lax.dynamic_slice_in_dim(table, index, piece, axis=0).astype(F32)
    gain_here = lax.dynamic_slice_in_dim(gain[0], index, piece, axis=0)
    gain_own = (owned[piece, :piece] + jnp.sum(router_own * table_own, axis=1)) / gain_here
    gain_high = gain_own.astype(BF)
    gain_mid, gain_low = two_terms(gain_own - gain_high.astype(F32))
    gain_terms = jnp.stack([gain_high, gain_mid, gain_low])
    gain_terms = jnp.pad(gain_terms, ((0, 13), (0, LANES - piece)))
    block = jnp.concatenate([router_own.astype(BF), gain_terms], axis=0)
    joined = exchange(jnp.broadcast_to(block[None], (experts,) + block.shape), "expert")
    joined = exchange(jnp.broadcast_to(joined[None], (replicas,) + joined.shape), "dp")
    joined = joined.reshape(replicas * experts, piece + 16, LANES)
    router_total = joined[:, :piece].reshape(width, router_width)
    gain_total = jnp.sum(joined[:, piece : piece + 3, :piece].astype(F32), axis=1).reshape(width)

    def inbound(block):
        return block.transpose(1, 2, 0, 3).reshape(rows, width)

    mixed = mm_wide_left(combine, inbound(returned[:, :, :slots]), ((1,), (0,)))
    layer_out = (xw + mixed).astype(BF)
    normed_grad = mm(place, inbound(returned[:, :, slots:]), ((1,), (0,)))
    normed_grad = (
        normed_grad + mm(logit_high, table, ((1,), (1,))) + mm(logit_low, table, ((1,), (1,)))
    )
    weighted = gain * normed_grad
    in_grad = (
        grad_top.astype(F32)
        + inv_rms * weighted
        - xw * inv_rms * inv_rms * inv_rms * jnp.mean(xw * weighted, axis=1, keepdims=True)
    ).astype(BF)
    swap = [(0, 1), (1, 0)]
    handoff = lax.ppermute(layer_out, "section", swap)
    handback = lax.ppermute(in_grad, "section", swap)
    return (
        handoff[None],
        handback[None],
        first_grad.astype(BF)[None, None],
        second_grad.astype(BF)[None, None],
        router_total[None],
        gain_total[None],
    )


def solution(mesh):
    return jax.shard_map(
        shards,
        mesh=mesh,
        in_specs=(
            P("section", ("expert", "dp"), None),
            P("section", ("expert", "dp"), None),
            P("section", ("expert", "dp"), None),
            P("section", None),
            P("section", None, None),
            P("section", "expert", "dp", None),
            P("section", "expert", None, "dp"),
        ),
        out_specs=(
            P("section", ("expert", "dp"), None),
            P("section", ("expert", "dp"), None),
            P("section", "expert", "dp", None),
            P("section", "expert", None, "dp"),
            P("section", None, None),
            P("section", None),
        ),
        check_vma=False,
    )
```

time: 1370 us -> 474 us (0.35)
  the two profiles are of different devices: /device:TPU:128 before, /device:TPU:8 now
where the time goes in v1:
time: 474 us; the launch traced here: 471 us
  blocking collectives  162 us (34%)
  waiting for transfers between devices  139 us (29%)
  local copies, waits for them, and re-layouts  71.6 us (15%)
  starting transfers between devices  42.7 us (9%)
  matrix products  32.6 us (7%)
  other arithmetic  21.1 us (4%)
    all_to_all x3, blocking collectives, exchange(): return lax.all_to_all(blocks, axes, split_axis=0, concat_axis=0, tiled=True)  162 us
    all_to_all x6, waiting for transfers between devices, exchange(): return lax.all_to_all(blocks, axes, split_axis=0, concat_axis=0, tiled=True)  139 us
    all_to_all x6, starting transfers between devices, exchange(): return lax.all_to_all(blocks, axes, split_axis=0, concat_axis=0, tiled=True)  42.2 us
    dot_general x15, matrix products, mm(): lax.dot_general(left, right, (contract, ((), ())), preferred_element_type...  30.1 us
  transfers between devices with their start and end apart: 8, of which 4 were waited for; matrix products, arithmetic and copies ran while one was open for 11% of the time, Pallas kernels for 0%

profile of v1, /device:TPU:8, one launch (start us, length us, event | category | flops | bytes accessed | tf_op | source)
XLA Modules:
  0.0 470.6 jit_solution(18083001246850533698)
XLA Ops:
  10.3 2.8 pad_maximum_fusion.1
  13.2 5.5 %reshape.306 = bf16[128,80,128]{2,1,0:T(8,128)(2,1)} reshape(bf16[8,16,20,512]{3,2,1,0:T(8,128)(2,1)} %pad_maximum_fusion.1) | data formatting | bytes 5242880 | tf_op jit(solution)/shard_map/reshape | solution.py:71
  18.7 77.6 %all_to_all.45 = bf16[128,80,128]{2,1,0:T(8,128)(2,1)} all-to-all(bf16[128,80,128]{2,1,0:T(8,128)(2,1)} %reshape.306), channel_id=1, replica_groups=mesh['section'=2,'expert'=16,'dp'=8] {'dp','expert'}, dimensions={0} | all-to-all | bytes 5242880 | tf_op jit(solution)/shard_map/all_to_all | solution.py:14
  96.3 4.8 %copy.46 = bf16[128,80,128]{0,2,1:T(8,128)(2,1)} copy(bf16[128,80,128]{2,1,0:T(8,128)(2,1)} %all_to_all.45) | data formatting | bytes 5242880 | tf_op jit(solution)/shard_map/all_to_all | solution.py:14
  101.0 3.0 fusion.76
  104.0 4.4 copy.47
  108.4 3.6 reshape.308
  112.0 2.9 copy.48
  114.9 2.6 reshape.309
  125.2 72.6 %all_to_all.46 = bf16[8,160,2304]{2,1,0:T(8,128)(2,1)S(1)} all-to-all(bf16[8,160,2304]{2,1,0:T(8,128)(2,1)S(1)} %bitcast.126), channel_id=1, replica_groups=mesh['section'=2,'expert'=16,'dp'=8] {'dp'}, dimensions={0} | all-to-all | bytes 11796480 | tf_op jit(solution)/shard_map/all_to_all | solution.py:14
  199.7 12.0 %all_to_all.47 = f32[16,1,128]{2,1,0:T(1,128)S(1)} all-to-all(f32[16,1,128]{2,1,0:T(1,128)S(1)} %bitcast.150), channel_id=1, replica_groups=mesh['section'=2,'expert'=16,'dp'=8] {'expert'}, dimensions={0} | all-to-all | bytes 16384 | tf_op jit(solution)/shard_map/all_to_all | solution.py:14
  214.0 5.0 %all-to-all-start.5 = ((bf16[8,512,128]{2,1,0:T(8,128)(2,1)}), bf16[8,512,128]{2,1,0:T(8,128)(2,1)S(1)}, u32[]{:S(2)}, u32[]{:S(2)}) async-start(bf16[8,512,128]{2,1,0:T(8,128)(2,1)} %bitcast.22), calls=%async_computation.5 | async-start | bytes 2097152 | tf_op jit(solution)/shard_map/all_to_all | solution.py:14
  220.8 9.5 %all-to-all-done.5 = bf16[8,512,128]{2,1,0:T(8,128)(2,1)S(1)} async-done(((bf16[8,512,128]{2,1,0:T(8,128)(2,1)}), bf16[8,512,128]{2,1,0:T(8,128)(2,1)S(1)}, u32[]{:S(2)}, u32[]{:S(2)}) %all-to-all-start.5) | async-done | bytes 1048608 | tf_op jit(solution)/shard_map/all_to_all | solution.py:14
  230.4 4.1 broadcast_in_dim.65
  234.4 6.1 %all-to-all-start.2 = ((bf16[8,160,2304]{2,1,0:T(8,128)(2,1)}), bf16[8,160,2304]{2,1,0:T(8,128)(2,1)}, u32[]{:S(2)}, u32[]{:S(2)}) async-start(bf16[8,160,2304]{2,1,0:T(8,128)(2,1)} %broadcast_in_dim.65), calls=%async_computation.2 | async-start | bytes 11796480 | tf_op jit(solution)/shard_map/all_to_all | solution.py:14
  240.7 65.0 %all-to-all-done.2 = bf16[8,160,2304]{2,1,0:T(8,128)(2,1)} async-done(((bf16[8,160,2304]{2,1,0:T(8,128)(2,1)}), bf16[8,160,2304]{2,1,0:T(8,128)(2,1)}, u32[]{:S(2)}, u32[]{:S(2)}) %all-to-all-start.2) | async-done | bytes 5898272 | tf_op jit(solution)/shard_map/all_to_all | solution.py:14
  305.8 6.4 %multiply_reduce_fusion = (f32[512]{0:T(512)S(1)}, bf16[1,1,512,1536]{3,2,1,0:T(8,128)(2,1)}) fusion(bf16[1,1,512,1536]{3,2,1,0:T(8,128)(2,1)} %param.12, bf16[1280,512]{1,0:T(8,128)(2,1)} %reshape.308, bf16[1280,2304]{1,0:T(8,128)(2,1)} %bitcast.12), kind=kOutput, calls=%fused_computation.21 | convolution fusion | flops 2016411136 | bytes 8390656 | tf_op jit(solution)/shard_map/dot_general | solution.py:18
  313.0 4.4 all-to-all-start.6
  317.5 4.8 %fusion.9 = bf16[1280,512]{1,0:T(8,128)(2,1)S(1)} fusion(bf16[1280,2304]{1,0:T(8,128)(2,1)} %bitcast.12, bf16[1,1,512,1536]{3,2,1,0:T(8,128)(2,1)} %param.12), kind=kOutput, calls=%fused_computation.23 | convolution fusion | flops 2013921280 | bytes 6815744 | tf_op jit(solution)/shard_map/dot_general | solution.py:18
  322.3 4.8 %all-to-all-done.6 = f32[16,40,128]{2,1,0:T(8,128)} async-done(((f32[16,40,128]{2,1,0:T(8,128)}), f32[16,40,128]{2,1,0:T(8,128)}, u32[]{:S(2)}, u32[]{:S(2)}) %all-to-all-start.6) | async-done | bytes 327712 | tf_op jit(solution)/shard_map/all_to_all | solution.py:14
  329.8 4.0 all-to-all-start.7
  333.9 3.8 convolution_convert_fusion.3
  337.6 3.6 reshape.312
  342.8 5.1 %pad_maximum_fusion.2 = bf16[128,20,512]{2,1,0:T(8,128)(2,1)} fusion(bf16[128,10,512]{2,1,0:T(8,128)(2,1)} %reshape.313, bf16[128,10,512]{2,1,0:T(8,128)(2,1)} %reshape.312), kind=kLoop, calls=%fused_computation.20 | loop fusion | flops 5242880 | bytes 5242880 | tf_op jit(solution)/shard_map/concatenate | solution.py:111
  347.9 4.7 %copy.50 = bf16[128,20,512]{0,2,1:T(8,128)(2,1)} copy(bf16[128,20,512]{2,1,0:T(8,128)(2,1)} %pad_maximum_fusion.2) | data formatting | bytes 5242880 | tf_op jit(solution)/shard_map/concatenate | solution.py:111
  352.6 4.7 copy.51
  357.3 15.0 %all-to-all-start.3 = ((bf16[128,80,128]{2,1,0:T(8,128)(2,1)}), bf16[128,80,128]{2,1,0:T(8,128)(2,1)}, u32[]{:S(2)}, u32[]{:S(2)}) async-start(bf16[128,80,128]{2,1,0:T(8,128)(2,1)} %copy.51), calls=%async_computation.3 | async-start | bytes 5242880 | tf_op jit(solution)/shard_map/all_to_all | solution.py:14
  373.6 60.0 %all-to-all-done.3 = bf16[128,80,128]{2,1,0:T(8,128)(2,1)} async-done(((bf16[128,80,128]{2,1,0:T(8,128)(2,1)}), bf16[128,80,128]{2,1,0:T(8,128)(2,1)}, u32[]{:S(2)}, u32[]{:S(2)}) %all-to-all-start.3) | async-done | bytes 2621472 | tf_op jit(solution)/shard_map/all_to_all | solution.py:14
  435.0 7.6 %all-to-all-start.8 = ((bf16[8,16,48,128]{3,2,1,0:T(8,128)(2,1)}), bf16[8,16,48,128]{3,2,1,0:T(8,128)(2,1)S(1)}, u32[]{:S(2)}, u32[]{:S(2)}) async-start(bf16[8,16,48,128]{3,2,1,0:T(8,128)(2,1)} %broadcast_in_dim.73), calls=%async_computation.8 | async-start | bytes 3145728 | tf_op jit(solution)/shard_map/all_to_all | solution.py:14
  442.6 5.5 %reshape.315 = bf16[8,16,20,512]{3,2,1,0:T(8,128)(2,1)} reshape(bf16[128,80,128]{2,1,0:T(8,128)(2,1)} %all-to-all-done.3) | data formatting | bytes 5242880 | tf_op jit(solution)/shard_map/reshape | solution.py:114
  448.2 3.3 slice_bitcast_fusion
  461.8 3.6 fusion.34
  (95 shorter events, 46.6 us)
Async XLA Ops:
  0.6 117.9 %copy-start = (bf16[1,1,768,512]{3,2,1,0:T(8,128)(2,1)S(1)}, bf16[1,1,768,512]{3,2,1,0:T(8,128)(2,1)}, u32[]{:S(2)}) copy-start(bf16[1,1,768,512]{3,2,1,0:T(8,128)(2,1)} %param.13) | copy-start | bytes 2359300
  0.7 6.3 %copy-start.1 = (bf16[1,128,4096]{2,1,0:T(8,128)(2,1)S(1)}, bf16[1,128,4096]{2,1,0:T(8,128)(2,1)}, u32[]{:S(2)}) copy-start(bf16[1,128,4096]{2,1,0:T(8,128)(2,1)} %param.7) | copy-start | bytes 3145732
  0.7 6.3 %copy-start.8 = (f32[1,4096]{1,0:T(1,128)S(1)}, f32[1,4096]{1,0:T(1,128)}, u32[]{:S(2)}) copy-start(f32[1,4096]{1,0:T(1,128)} %param.10) | copy-start | bytes 49156
  3.9 3.7 copy-start.3
  117.5 1.1 copy-start.5
  118.6 2.5 copy-start.7
  118.6 2.5 copy-start.12
  214.0 16.4 %all-to-all-start.5 = ((bf16[8,512,128]{2,1,0:T(8,128)(2,1)}), bf16[8,512,128]{2,1,0:T(8,128)(2,1)S(1)}, u32[]{:S(2)}, u32[]{:S(2)}) async-start(bf16[8,512,128]{2,1,0:T(8,128)(2,1)} %bitcast.22), calls=%async_computation.5 | async-start | bytes 2097152 | tf_op jit(solution)/shard_map/all_to_all | solution.py:14
  234.4 71.3 %all-to-all-start.2 = ((bf16[8,160,2304]{2,1,0:T(8,128)(2,1)}), bf16[8,160,2304]{2,1,0:T(8,128)(2,1)}, u32[]{:S(2)}, u32[]{:S(2)}) async-start(bf16[8,160,2304]{2,1,0:T(8,128)(2,1)} %broadcast_in_dim.65), calls=%async_computation.2 | async-start | bytes 11796480 | tf_op jit(solution)/shard_map/all_to_all | solution.py:14
  313.0 14.1 %all-to-all-start.6 = ((f32[16,40,128]{2,1,0:T(8,128)}), f32[16,40,128]{2,1,0:T(8,128)}, u32[]{:S(2)}, u32[]{:S(2)}) async-start(f32[16,40,128]{2,1,0:T(8,128)} %select_maximum_fusion), calls=%async_computation.6 | async-start | bytes 655360 | tf_op jit(solution)/shard_map/all_to_all | solution.py:14
  329.8 27.5 %all-to-all-start.7 = ((bf16[16,48,128]{2,1,0:T(8,128)(2,1)}), bf16[16,48,128]{2,1,0:T(8,128)(2,1)S(1)}, u32[]{:S(2)}, u32[]{:S(2)}) async-start(bf16[16,48,128]{2,1,0:T(8,128)(2,1)} %broadcast_in_dim.72), calls=%async_computation.7 | async-start | bytes 393216 | tf_op jit(solution)/shard_map/all_to_all | solution.py:14
  357.3 15.7 %copy-start.9 = (bf16[128,16,10]{0,2,1:T(8,128)(2,1)S(1)}, bf16[128,16,10]{0,2,1:T(8,128)(2,1)}, u32[]{:S(2)}) copy-start(bf16[128,16,10]{0,2,1:T(8,128)(2,1)} %get-tuple-element.20) | copy-start | bytes 122884
  357.3 76.3 %all-to-all-start.3 = ((bf16[128,80,128]{2,1,0:T(8,128)(2,1)}), bf16[128,80,128]{2,1,0:T(8,128)(2,1)}, u32[]{:S(2)}, u32[]{:S(2)}) async-start(bf16[128,80,128]{2,1,0:T(8,128)(2,1)} %copy.51), calls=%async_computation.3 | async-start | bytes 5242880 | tf_op jit(solution)/shard_map/all_to_all | solution.py:14
  435.0 30.4 %all-to-all-start.8 = ((bf16[8,16,48,128]{3,2,1,0:T(8,128)(2,1)}), bf16[8,16,48,128]{3,2,1,0:T(8,128)(2,1)S(1)}, u32[]{:S(2)}, u32[]{:S(2)}) async-start(bf16[8,16,48,128]{3,2,1,0:T(8,128)(2,1)} %broadcast_in_dim.73), calls=%async_computation.8 | async-start | bytes 3145728 | tf_op jit(solution)/shard_map/all_to_all | solution.py:14
  452.9 1.2 copy-start.2
  454.6 1.2 copy-start.4
  457.6 9.8 %collective-permute-start.1 = (bf16[128,4096]{1,0:T(8,128)(2,1)}, bf16[128,4096]{1,0:T(8,128)(2,1)}, u32[]{:S(2)}, u32[]{:S(2)}) collective-permute-start(bf16[128,4096]{1,0:T(8,128)(2,1)} %fusion.20), channel_id=1, source_target_pairs={{0,128},{128,0},{1,129},{129,1},{2,130},{130,2},{3,131},{131,3},{4... | collective-permute-start | bytes 3145736 | tf_op jit(solution)/shard_map/ppermute | solution.py:157
  458.4 0.8 copy-start.11
  459.0 0.8 copy-start.10
  459.7 2.0 copy-start.6
  461.2 6.1 %collective-permute-start = (bf16[128,4096]{1,0:T(8,128)(2,1)}, bf16[128,4096]{1,0:T(8,128)(2,1)S(1)}, u32[]{:S(2)}, u32[]{:S(2)}) collective-permute-start(bf16[128,4096]{1,0:T(8,128)(2,1)} %fusion.3), channel_id=1, source_target_pairs={{0,128},{128,0},{1,129},{129,1},{2,130},{130,2},{3,131},{131,3},{4... | collective-permute-start | bytes 3145736 | tf_op jit(solution)/shard_map/ppermute | solution.py:156

commit v2 on v1

v2 whole, which is shorter than its diff:
```python
import functools

import jax
import jax.numpy as jnp
import numpy as np
from jax import lax
from jax.experimental import pallas as pl
from jax.experimental.pallas import tpu as pltpu
from jax.sharding import PartitionSpec as P

MOST = 10
LANES = 128
BF = jnp.bfloat16
F32 = jnp.float32
ALL = ("dp", "expert")
INTERPRET = False
HIDDEN_STEPS = 3


def exchange(blocks, axes):
    return lax.all_to_all(blocks, axes, split_axis=0, concat_axis=0, tiled=True)


def mm(left, right, contract=((1,), (0,))):
    return lax.dot_general(left, right, (contract, ((), ())), preferred_element_type=F32)


def two_terms(values):
    high = values.astype(BF)
    return high, (values - high.astype(F32)).astype(BF)


def three_terms(values):
    high = values.astype(BF)
    return (high,) + two_terms(values - high.astype(F32))


def kernel_call(body, outs, args, scratch=(), **grid):
    return pl.pallas_call(
        body,
        out_shape=outs,
        scratch_shapes=scratch,
        compiler_params=pltpu.CompilerParams(vmem_limit_bytes=52 * 2**20),
        interpret=INTERPRET,
        **grid,
    )(*args)


def iota(shape, dimension):
    return lax.broadcasted_iota(jnp.int32, shape, dimension)


def spread(values, owner):
    pick = (iota((values[0].shape[1], owner.shape[1]), 0) == owner).astype(BF)
    total = mm(values[0], pick)
    for term in values[1:]:
        total = total + mm(term, pick)
    return total


def send_kernel(experts, replicas, chunks, slots, x, ids, grad, gain, table, owner, chunk_of, slot_of,
                message, normed_out, gates_out, place_out, stack):
    tokens, width = x.shape
    part = width // replicas
    half = chunks * slots
    xw = x[...].astype(F32)
    inv_rms = lax.rsqrt(jnp.mean(xw * xw, axis=1, keepdims=True) + 1e-06)
    normed = (xw * inv_rms * gain[...]).astype(BF)
    normed_out[...] = normed
    logits = mm(normed, table[...])
    columns = iota(logits.shape, 1)
    named = columns == ids[:, 0:1]
    for k in range(1, ids.shape[1]):
        named = named | (columns == ids[:, k : k + 1])
    powers = jnp.where(named, jnp.exp(logits), 0.0)
    gates = powers / jnp.sum(powers, axis=1, keepdims=True)
    gates_out[...] = gates
    earlier = (iota((tokens, tokens), 1) < iota((tokens, tokens), 0)).astype(BF)
    rank = mm(earlier, named.astype(BF))
    place = jnp.where(named & (columns < experts), rank, -1.0)
    place_out[...] = place

    hits = spread((place.astype(BF),), owner[...]) == slot_of[...].astype(F32)
    weight = jnp.where(hits, spread(three_terms(gates), owner[...]), 0.0)
    slot_gate = jnp.sum(weight.T, axis=1, keepdims=True)
    hits_rows = jnp.where(hits, 1.0, 0.0).T
    pick = jnp.concatenate(
        [jnp.where(chunk_of[...] == c, hits_rows, 0.0).astype(BF) for c in range(chunks)], axis=1
    )

    def stacked(load):
        for c in range(chunks):
            for j in range(replicas):
                at = j * part + c * LANES
                stack[c * tokens : (c + 1) * tokens, j * LANES : (j + 1) * LANES] = load(at)
        return mm(pick, stack[...])

    sent = stacked(lambda at: normed_out[:, at : at + LANES])
    sent_grad = stacked(lambda at: grad[:, at : at + LANES]) * slot_gate
    for j in range(replicas):
        for e in range(experts):
            rows, lanes = slice(e * half, (e + 1) * half), slice(j * LANES, (j + 1) * LANES)
            message[j * experts + e] = jnp.concatenate(
                [sent[rows, lanes], sent_grad[rows, lanes]], axis=0
            ).astype(BF)


def products_kernel(group, chunks, slots, arrived, order, first, second, partial, rows_out, grads_out):
    step = pl.program_id(0)
    total, per_message, _ = arrived.shape
    size = group * per_message
    block = group * slots
    steps_first = 2 * HIDDEN_STEPS

    @pl.when(step == 0)
    def _():
        pick = (order[...] == iota((size, size), 1)).astype(BF)
        sets = total // group
        wide = 2 if sets % 2 == 0 else 1
        for pair in range(sets // wide):
            loaded = [
                arrived[(pair * wide + w) * group : (pair * wide + w + 1) * group].reshape(size, LANES)
                for w in range(wide)
            ]
            picked = mm(pick, jnp.concatenate(loaded, axis=1)).astype(BF)
            for w in range(wide):
                at = (pair * wide + w) * block
                for c in range(chunks):
                    lanes = slice(w * LANES, (w + 1) * LANES)
                    rows_out[at : at + block, c * LANES : (c + 1) * LANES] = picked[
                        c * block : (c + 1) * block, lanes
                    ]
                    grads_out[at : at + block, c * LANES : (c + 1) * LANES] = picked[
                        (chunks + c) * block : (chunks + c + 1) * block, lanes
                    ]

    @pl.when(step < steps_first)
    def _():
        partial[...] = mm(rows_out[...], first[...]).astype(BF)

    @pl.when(step >= steps_first)
    def _():
        partial[...] = mm(grads_out[...], second[...], ((1,), (1,))).astype(BF)


def act_kernel(slots, arrived, sender_of, slot_of, acts, worth):
    replicas, rows, width = arrived.shape
    hidden_width = width // 3
    total = arrived[0].astype(F32)
    for j in range(1, replicas):
        total = total + arrived[j].astype(F32)
    gate_pre = total[:, :hidden_width]
    up = total[:, hidden_width : 2 * hidden_width]
    hidden_grad = total[:, 2 * hidden_width :]
    sigmoid = 1.0 / (1.0 + jnp.exp(-gate_pre))
    silu = gate_pre * sigmoid
    slope = sigmoid * (1.0 + gate_pre * (1.0 - sigmoid))
    hidden = (silu * up).astype(BF)
    gate_grad = (hidden_grad * up * slope).astype(BF)
    up_grad = (hidden_grad * silu).astype(BF)
    for j in range(replicas):
        acts[j, :, :hidden_width] = gate_grad
        acts[j, :, hidden_width : 2 * hidden_width] = up_grad
        acts[j, :, 2 * hidden_width :] = hidden
    each = jnp.sum(hidden_grad * hidden.astype(F32), axis=1, keepdims=True)
    laid = jnp.where(slot_of[...] == iota((rows, LANES), 1), each, 0.0)
    pick = (sender_of[...] == iota((worth.shape[0], rows), 0)).astype(BF)
    terms = three_terms(laid)
    worth[...] = mm(pick, terms[0]) + mm(pick, terms[1]) + mm(pick, terms[2])


def back_kernel(group, chunks, slots, gathered, order, first, second, message):
    rows, width = gathered.shape
    hidden_width = width // 3
    block = group * slots
    size = 2 * chunks * block
    per_message = 2 * chunks * slots
    outs = mm(gathered[:, 2 * hidden_width :], second[...]).astype(BF)
    backs = mm(gathered[:, : 2 * hidden_width], first[...], ((1,), (1,))).astype(BF)
    pick = (order[...] == iota((size, size), 1)).astype(BF)
    sets = rows // block
    wide = 2 if sets % 2 == 0 else 1

    def column(at):
        return jnp.concatenate(
            [
                source[at : at + block, c * LANES : (c + 1) * LANES]
                for source in (outs, backs)
                for c in range(chunks)
            ],
            axis=0,
        )

    for pair in range(sets // wide):
        loaded = [column((pair * wide + w) * block) for w in range(wide)]
        picked = mm(pick, jnp.concatenate(loaded, axis=1)).astype(BF)
        for w in range(wide):
            at = (pair * wide + w) * group
            message[at : at + group] = picked[:, w * LANES : (w + 1) * LANES].reshape(
                group, per_message, LANES
            )


def combine_kernel(experts, replicas, chunks, slots, returned, x, grad, gain, table, gates, place, logit_grad,
                   owner, kind_of, chunk_of, slot_of, layer_out, in_grad, joined, normed_grad):
    tokens, width = x.shape
    part = width // replicas
    count, per_message, _ = returned.shape
    for j in range(replicas):
        block = returned[j * experts : (j + 1) * experts]
        joined[:, j * LANES : (j + 1) * LANES] = block.reshape(experts * per_message, LANES)
    hits = spread((place[...].astype(BF),), owner[...]) == slot_of[...].astype(F32)
    high, low = (
        jnp.where(hits, spread((term,), owner[...]), 0.0) for term in two_terms(gates[...])
    )
    ones = jnp.where(hits, 1.0, 0.0)
    kind = kind_of[...]
    chunk = chunk_of[...]

    def picks(values, which):
        return jnp.concatenate(
            [
                jnp.where((kind == which) & (chunk == c), values, 0.0).astype(BF)
                for c in range(chunks)
            ],
            axis=0,
        )

    source = joined[...]
    mixed = mm(picks(high, 0), source) + mm(picks(low, 0), source)
    back = mm(picks(ones, 1), source)
    logit_high, logit_low = two_terms(logit_grad[...])
    by_logits = mm(logit_high, table[...], ((1,), (1,))) + mm(logit_low, table[...], ((1,), (1,)))
    for c in range(chunks):
        rows = slice(c * tokens, (c + 1) * tokens)
        for j in range(replicas):
            lanes = slice(j * LANES, (j + 1) * LANES)
            at = slice(j * part + c * LANES, j * part + (c + 1) * LANES)
            layer_out[:, at] = (x[:, at].astype(F32) + mixed[rows, lanes]).astype(BF)
            normed_grad[:, at] = back[rows, lanes] + by_logits[:, at]
    xw = x[...].astype(F32)
    inv_rms = lax.rsqrt(jnp.mean(xw * xw, axis=1, keepdims=True) + 1e-06)
    weighted = gain[...] * normed_grad[...]
    mean = jnp.mean(xw * weighted, axis=1, keepdims=True)
    in_grad[...] = (
        grad[...].astype(F32) + inv_rms * weighted - xw * (inv_rms * inv_rms * inv_rms * mean)
    ).astype(BF)


def shards(section_input, routing, out_grad, norm_gain, router, w_in, w_out):
    experts = lax.axis_size("expert")
    replicas = lax.axis_size("dp")
    x = section_input[0]
    route_ids = routing[0]
    grad_top = out_grad[0]
    gain = norm_gain[0][None, :]
    table = router[0]
    first = w_in[0, 0]
    second = w_out[0, 0]
    tokens, width = x.shape
    part = width // replicas
    hidden_width = second.shape[0]
    slots = MOST
    rows = experts * slots
    router_width = table.shape[1]
    chunks = part // LANES
    half = chunks * slots
    peers = replicas * experts
    group = min(8, experts)
    message_shape = jax.ShapeDtypeStruct((peers, 2 * half, LANES), BF)

    at = np.arange(experts * half, dtype=np.int32)
    message, normed, gates, place = kernel_call(
        functools.partial(send_kernel, experts, replicas, chunks, slots),
        (
            message_shape,
            jax.ShapeDtypeStruct((tokens, width), BF),
            jax.ShapeDtypeStruct((tokens, router_width), F32),
            jax.ShapeDtypeStruct((tokens, router_width), F32),
        ),
        (x, route_ids, grad_top, gain, table, at[None] // half, (at % half // slots)[:, None], at[None] % slots),
        [pltpu.VMEM((chunks * tokens, replicas * LANES), BF)],
    )
    arrived = exchange(message, ALL)

    at = np.arange(group * 2 * half, dtype=np.int32)
    sender, inner_row, slot = at // (2 * half), at % (2 * half) // slots, at % slots
    into_rows = np.zeros_like(at)
    into_rows[(inner_row * group + sender) * slots + slot] = at
    into_messages = (inner_row * group + sender) * slots + slot
    step_width = hidden_width // HIDDEN_STEPS
    all_rows = peers * slots
    partial, expert_rows, grad_rows = kernel_call(
        functools.partial(products_kernel, group, chunks, slots),
        (
            jax.ShapeDtypeStruct((all_rows, 3 * hidden_width), BF),
            jax.ShapeDtypeStruct((all_rows, part), BF),
            jax.ShapeDtypeStruct((all_rows, part), BF),
        ),
        (arrived, into_rows[:, None], first, second),
        grid=(3 * HIDDEN_STEPS,),
        in_specs=[
            pl.BlockSpec(arrived.shape, lambda i: (0, 0, 0)),
            pl.BlockSpec((at.size, 1), lambda i: (0, 0)),
            pl.BlockSpec((part, step_width), lambda i: (0, jnp.minimum(i, 2 * HIDDEN_STEPS - 1))),
            pl.BlockSpec((step_width, part), lambda i: (jnp.maximum(i - 2 * HIDDEN_STEPS, 0), 0)),
        ],
        out_specs=[
            pl.BlockSpec((all_rows, step_width), lambda i: (0, i)),
            pl.BlockSpec((all_rows, part), lambda i: (0, 0)),
            pl.BlockSpec((all_rows, part), lambda i: (0, 0)),
        ],
    )
    summands = exchange(partial.reshape(replicas, rows, 3 * hidden_width), "dp")
    at = np.arange(rows, dtype=np.int32)
    acts, worth = kernel_call(
        functools.partial(act_kernel, slots),
        (
            jax.ShapeDtypeStruct(summands.shape, BF),
            jax.ShapeDtypeStruct((experts, LANES), F32),
        ),
        (summands, at[None] // slots, at[:, None] % slots),
    )
    gathered = exchange(acts, "dp").reshape(-1, 3 * hidden_width)
    pre_grad = gathered[:, : 2 * hidden_width]
    hidden_all = gathered[:, 2 * hidden_width :]

    worth = exchange(worth[:, None], "expert")[:, 0, :slots]
    slot_ids = jnp.arange(slots, dtype=F32)
    gate_worth = jnp.sum(
        jnp.where(place[:, :experts, None] == slot_ids, worth[None], 0.0), axis=2
    )
    inner = jnp.sum(gate_worth, axis=1, keepdims=True)
    logit_grad = jnp.pad(gate_worth, ((0, 0), (0, router_width - experts))) - gates * inner
    logit_high, logit_low = two_terms(logit_grad)
    local_router = mm(normed, logit_high, ((0,), (0,))) + mm(normed, logit_low, ((0,), (0,)))
    router_part = exchange(local_router.astype(BF).reshape(replicas, part, router_width), "dp")
    router_part = jnp.sum(router_part.astype(F32), axis=0)

    steps = 4 if replicas % 4 == 0 else 1
    message = kernel_call(
        functools.partial(back_kernel, group, chunks, slots),
        message_shape,
        (gathered, into_messages[:, None], first, second),
        grid=(steps,),
        in_specs=[
            pl.BlockSpec((all_rows // steps, 3 * hidden_width), lambda i: (i, 0)),
            pl.BlockSpec((into_messages.size, 1), lambda i: (0, 0)),
            pl.BlockSpec(first.shape, lambda i: (0, 0)),
            pl.BlockSpec(second.shape, lambda i: (0, 0)),
        ],
        out_specs=pl.BlockSpec((peers // steps, 2 * half, LANES), lambda i: (i, 0, 0)),
    )
    returned = exchange(message, ALL)

    first_grad = mm(expert_rows, pre_grad, ((0,), (0,)))
    second_grad = mm(hidden_all, grad_rows, ((0,), (0,)))
    gain_part = jnp.sum(first_grad * first.astype(F32), axis=1)

    piece = part // experts
    gain_rows = jnp.pad(gain_part.reshape(experts, 1, piece), ((0, 0), (0, 7), (0, LANES - piece)))
    owned = jnp.concatenate([router_part.reshape(experts, piece, router_width), gain_rows], axis=1)
    owned = jnp.sum(exchange(owned, "expert"), axis=0)
    router_own = owned[:piece]
    index = lax.axis_index("dp") * part + lax.axis_index("expert") * piece
    table_own = lax.dynamic_slice_in_dim(table, index, piece, axis=0).astype(F32)
    gain_here = lax.dynamic_slice_in_dim(gain[0], index, piece, axis=0)
    gain_own = (owned[piece, :piece] + jnp.sum(router_own * table_own, axis=1)) / gain_here
    gain_high = gain_own.astype(BF)
    gain_mid, gain_low = two_terms(gain_own - gain_high.astype(F32))
    gain_terms = jnp.stack([gain_high, gain_mid, gain_low])
    gain_terms = jnp.pad(gain_terms, ((0, 13), (0, LANES - piece)))
    block = jnp.concatenate([router_own.astype(BF), gain_terms], axis=0)
    joined = exchange(jnp.broadcast_to(block[None], (experts,) + block.shape), "expert")
    joined = exchange(jnp.broadcast_to(joined[None], (replicas,) + joined.shape), "dp")
    joined = joined.reshape(replicas * experts, piece + 16, LANES)
    router_total = joined[:, :piece].reshape(width, router_width)
    gain_total = jnp.sum(joined[:, piece : piece + 3, :piece].astype(F32), axis=1).reshape(width)

    at = np.arange(experts * 2 * half, dtype=np.int32)[None]
    layer_out, in_grad = kernel_call(
        functools.partial(combine_kernel, experts, replicas, chunks, slots),
        (
            jax.ShapeDtypeStruct((tokens, width), BF),
            jax.ShapeDtypeStruct((tokens, width), BF),
        ),
        (
            returned, x, grad_top, gain, table, gates, place, logit_grad,
            at // (2 * half), at % (2 * half) // half, at % half // slots, at % slots,
        ),
        [
            pltpu.VMEM((experts * 2 * half, replicas * LANES), BF),
            pltpu.VMEM((tokens, width), F32),
        ],
    )
    swap = [(0, 1), (1, 0)]
    handoff = lax.ppermute(layer_out, "section", swap)
    handback = lax.ppermute(in_grad, "section", swap)
    return (
        handoff[None],
        handback[None],
        first_grad.astype(BF)[None, None],
        second_grad.astype(BF)[None, None],
        router_total[None],
        gain_total[None],
    )


def solution(mesh):
    return jax.shard_map(
        shards,
        mesh=mesh,
        in_specs=(
            P("section", ("expert", "dp"), None),
            P("section", ("expert", "dp"), None),
            P("section", ("expert", "dp"), None),
            P("section", None),
            P("section", None, None),
            P("section", "expert", "dp", None),
            P("section", "expert", None, "dp"),
        ),
        out_specs=(
            P("section", ("expert", "dp"), None),
            P("section", ("expert", "dp"), None),
            P("section", "expert", "dp", None),
            P("section", "expert", None, "dp"),
            P("section", None, None),
            P("section", None),
        ),
        check_vma=False,
    )
```

time: 474 us -> 427 us (0.901)
  blocking collectives: 162 us -> 246 us
  local copies, waits for them, and re-layouts: 71.6 us -> 12.6 us
  waiting for transfers between devices: 139 us -> 81.9 us
  Pallas kernels: 0 us -> 43.9 us
  matrix products: 32.6 us -> 10.6 us
  other arithmetic: 21.1 us -> 3.44 us
  starting transfers between devices: 42.7 us -> 26.3 us
    all_to_all x3 -> x4, blocking collectives: 162 us -> 246 us  [exchange(): return lax.all_to_all(blocks, axes, split_axis=0, concat_axis=0, tiled=True)]
    all_to_all x6 -> x5, waiting for transfers between devices: 139 us -> 81.9 us  [exchange(): return lax.all_to_all(blocks, axes, split_axis=0, concat_axis=0, tiled=True)]
    pallas_call x0 -> x5, Pallas kernels: none -> 43.9 us  [kernel_call(): pl.pallas_call(body, out_shape=outs, scratch_shapes=scratch, compiler_par...]
    reshape x8 -> x0, local copies, waits for them, and re-layouts: 27.2 us -> none  [the longest x1 5.52 us: shards(): exchange(message, ALL).reshape(replicas, experts, 2 * slots, part)]
    dot_general x15 -> x4, matrix products: 30.1 us -> 10.6 us  [mm(): lax.dot_general(left, right, (contract, ((), ())), preferred_element_type...]
    all_to_all x6 -> x5, starting transfers between devices: 42.2 us -> 25.8 us  [exchange(): return lax.all_to_all(blocks, axes, split_axis=0, concat_axis=0, tiled=True)]
    concatenate x4 -> x0, other arithmetic: 11.7 us -> none  [the longest x1 5.07 us: shards(): jnp.concatenate([out_rows.reshape(-1, slots, part), back_rows.reshape(-1,...]
    slice x5 -> x1, local copies, waits for them, and re-layouts: 10.3 us -> 0.05 us  [shards(): place[:, :experts, None] == slot_ids]
  transfers between devices with their start and end apart: 8 -> 7, of which waited for: 4 -> 4; matrix products, arithmetic and copies ran while one was open for 11% -> 2% of each run, Pallas kernels for 0% -> 4%
where the time goes in v2:
time: 427 us; the launch traced here: 425 us
  blocking collectives  246 us (58%)
  waiting for transfers between devices  81.9 us (19%)
  Pallas kernels  43.9 us (10%)
  starting transfers between devices  26.3 us (6%)
  local copies, waits for them, and re-layouts  12.6 us (3%)
  matrix products  10.6 us (2%)
    all_to_all x4, blocking collectives, exchange(): return lax.all_to_all(blocks, axes, split_axis=0, concat_axis=0, tiled=True)  246 us
    all_to_all x5, waiting for transfers between devices, exchange(): return lax.all_to_all(blocks, axes, split_axis=0, concat_axis=0, tiled=True)  81.9 us
    pallas_call x5, Pallas kernels, kernel_call(): pl.pallas_call(body, out_shape=outs, scratch_shapes=scratch, compiler_par...  43.9 us
    all_to_all x5, starting transfers between devices, exchange(): return lax.all_to_all(blocks, axes, split_axis=0, concat_axis=0, tiled=True)  25.8 us
    dot_general x4, matrix products, mm(): lax.dot_general(left, right, (contract, ((), ())), preferred_element_type...  10.6 us
  transfers between devices with their start and end apart: 7, of which 4 were waited for; matrix products, arithmetic and copies ran while one was open for 2% of the time, Pallas kernels for 4%

profile of v2, /device:TPU:8, one launch (start us, length us, event | category | flops | bytes accessed | tf_op | source)
XLA Modules:
  0.0 425.4 jit_solution(12611578131181307835)
XLA Ops:
  0.6 0.8 copy.28
  1.4 1.0 copy-done.2
  2.4 0.7 copy-done.4
  4.5 6.1 %shard_map.217 = (bf16[128,80,128]{2,1,0:T(8,128)(2,1)}, bf16[128,4096]{1,0:T(8,128)(2,1)S(1)}, f32[128,128]{1,0:T(8,128)S(1)}, f32[128,128]{1,0:T(8,128)S(1)}) custom-call(bf16[128,4096]{1,0:T(8,128)(2,1)} %bitcast.46, s32[128,8]{1,0:T(8,128)S(1)} %bitcast.38, bf16[128,4096]{1,0:T(8,128)(2,1)} %bitcast.48, f32[1,4096]{1,0:T(1,128)S(1)} %copy-done.4, ...), custom_call_target="tpu_custom_call" | custom-call | tf_op jit(solution)/shard_map/pallas_call | solution.py:39
  10.6 77.7 %all_to_all.45.arrived = bf16[128,80,128]{2,1,0:T(8,128)(2,1)} all-to-all(bf16[128,80,128]{2,1,0:T(8,128)(2,1)} %get-tuple-element.17), channel_id=1, replica_groups=mesh['section'=2,'expert'=16,'dp'=8] {'dp','expert'}, dimensions={0} | all-to-all | bytes 5242880 | tf_op jit(solution)/shard_map/all_to_all | solution.py:21
  88.3 12.6 %shard_map.218 = (bf16[1280,2304]{1,0:T(8,128)(2,1)}, bf16[1280,512]{1,0:T(8,128)(2,1)}, bf16[1280,512]{1,0:T(8,128)(2,1)}) custom-call(bf16[128,80,128]{2,1,0:T(8,128)(2,1)} %all_to_all.45.arrived, s32[640,1]{1,0:T(8,128)S(1)} %copy-done.1, bf16[512,1536]{1,0:T(8,128)(2,1)} %bitcast.39, bf16[768,512]{1,0:T(8,128)(2,1)S(1)} %bitcast.35), custom_call_target="tpu_custom_call" | custom-call | tf_op jit(solution)/shard_map/pallas_call | solution.py:39
  100.9 75.4 %all_to_all.46.arrived = bf16[8,160,2304]{2,1,0:T(8,128)(2,1)} all-to-all(bf16[8,160,2304]{2,1,0:T(8,128)(2,1)} %bitcast.41), channel_id=1, replica_groups=mesh['section'=2,'expert'=16,'dp'=8] {'dp'}, dimensions={0} | all-to-all | bytes 11796480 | tf_op jit(solution)/shard_map/all_to_all | solution.py:21
  176.2 6.9 %shard_map.219 = (bf16[8,160,2304]{2,1,0:T(8,128)(2,1)}, f32[16,128]{1,0:T(8,128)}) custom-call(bf16[8,160,2304]{2,1,0:T(8,128)(2,1)} %all_to_all.46.arrived, s32[1,160]{1,0:T(1,128)S(1)} %copy-done.12, s32[160,1]{1,0:T(8,128)S(1)} %copy-done.3), custom_call_target="tpu_custom_call" | custom-call | tf_op jit(solution)/shard_map/pallas_call | solution.py:39
  183.1 3.5 all-to-all-start.4
  186.6 8.3 %all-to-all-done.4 = f32[16,1,128]{2,1,0:T(1,128)S(1)} async-done(((f32[16,1,128]{2,1,0:T(1,128)}), f32[16,1,128]{2,1,0:T(1,128)S(1)}, u32[]{:S(2)}, u32[]{:S(2)}) %all-to-all-start.4) | async-done | bytes 8224 | tf_op jit(solution)/shard_map/all_to_all | solution.py:21
  196.3 16.7 %all_to_all.47 = bf16[8,512,128]{2,1,0:T(8,128)(2,1)} all-to-all(bf16[8,512,128]{2,1,0:T(8,128)(2,1)S(1)} %bitcast.50), channel_id=1, replica_groups=mesh['section'=2,'expert'=16,'dp'=8] {'dp'}, dimensions={0} | all-to-all | bytes 2097152 | tf_op jit(solution)/shard_map/all_to_all | solution.py:21
  213.0 6.5 %all-to-all-start.2 = ((bf16[8,160,2304]{2,1,0:T(8,128)(2,1)}), bf16[8,160,2304]{2,1,0:T(8,128)(2,1)}, u32[]{:S(2)}, u32[]{:S(2)}) async-start(bf16[8,160,2304]{2,1,0:T(8,128)(2,1)} %get-tuple-element.19), calls=%async_computation.2 | async-start | bytes 11796480 | tf_op jit(solution)/shard_map/all_to_all | solution.py:21
  219.5 1.4 convert_reduce_fusion
  220.9 60.5 %all-to-all-done.2 = bf16[8,160,2304]{2,1,0:T(8,128)(2,1)} async-done(((bf16[8,160,2304]{2,1,0:T(8,128)(2,1)}), bf16[8,160,2304]{2,1,0:T(8,128)(2,1)}, u32[]{:S(2)}, u32[]{:S(2)}) %all-to-all-start.2) | async-done | bytes 5898272 | tf_op jit(solution)/shard_map/all_to_all | solution.py:21
  281.4 6.0 %multiply_reduce_fusion = (f32[512]{0:T(512)S(1)}, bf16[1,1,512,1536]{3,2,1,0:T(8,128)(2,1)}) fusion(bf16[1,1,512,1536]{3,2,1,0:T(8,128)(2,1)S(1)} %copy-done.13, bf16[1280,512]{1,0:T(8,128)(2,1)} %get-tuple-element.25, bf16[1280,2304]{1,0:T(8,128)(2,1)} %bitcast.7.gathered), kind=kOutput, calls=%fused_computation.4 | convolution fusion | flops 2016411136 | bytes 8390656 | tf_op jit(solution)/shard_map/dot_general | solution.py:25
  287.5 0.8 select_maximum_fusion
  288.2 3.5 all-to-all-start.6
  291.8 9.3 %all-to-all-done.6 = f32[16,40,128]{2,1,0:T(8,128)S(1)} async-done(((f32[16,40,128]{2,1,0:T(8,128)}), f32[16,40,128]{2,1,0:T(8,128)S(1)}, u32[]{:S(2)}, u32[]{:S(2)}) %all-to-all-start.6) | async-done | bytes 327712 | tf_op jit(solution)/shard_map/all_to_all | solution.py:21
  301.1 0.8 fusion.11
  302.1 0.7 broadcast_in_dim.52
  302.8 4.6 %all-to-all-start.7 = ((bf16[16,48,128]{2,1,0:T(8,128)(2,1)}), bf16[16,48,128]{2,1,0:T(8,128)(2,1)S(1)}, u32[]{:S(2)}, u32[]{:S(2)}) async-start(bf16[16,48,128]{2,1,0:T(8,128)(2,1)} %broadcast_in_dim.52), calls=%async_computation.7 | async-start | bytes 393216 | tf_op jit(solution)/shard_map/all_to_all | solution.py:21
  307.4 8.8 %shard_map.220 = bf16[128,80,128]{2,1,0:T(8,128)(2,1)} custom-call(bf16[1280,2304]{1,0:T(8,128)(2,1)} %bitcast.7.gathered, s32[640,1]{1,0:T(8,128)S(1)} %copy-done.1, bf16[512,1536]{1,0:T(8,128)(2,1)} %bitcast.40, bf16[768,512]{1,0:T(8,128)(2,1)S(1)} %bitcast.36), custom_call_target="tpu_custom_call" | custom-call | tf_op jit(solution)/shard_map/pallas_call | solution.py:39
  316.1 76.2 %all_to_all.48.returned = bf16[128,80,128]{2,1,0:T(8,128)(2,1)} all-to-all(bf16[128,80,128]{2,1,0:T(8,128)(2,1)} %shard_map.220), channel_id=1, replica_groups=mesh['section'=2,'expert'=16,'dp'=8] {'dp','expert'}, dimensions={0} | all-to-all | bytes 5242880 | tf_op jit(solution)/shard_map/all_to_all | solution.py:21
  392.3 1.4 broadcast_in_dim.53
  393.7 7.6 %all-to-all-start.8 = ((bf16[8,16,48,128]{3,2,1,0:T(8,128)(2,1)}), bf16[8,16,48,128]{3,2,1,0:T(8,128)(2,1)S(1)}, u32[]{:S(2)}, u32[]{:S(2)}) async-start(bf16[8,16,48,128]{3,2,1,0:T(8,128)(2,1)} %broadcast_in_dim.53), calls=%async_computation.8 | async-start | bytes 3145728 | tf_op jit(solution)/shard_map/all_to_all | solution.py:21
  401.4 9.6 %shard_map.221 = (bf16[128,4096]{1,0:T(8,128)(2,1)S(1)}, bf16[128,4096]{1,0:T(8,128)(2,1)}) custom-call(bf16[128,80,128]{2,1,0:T(8,128)(2,1)} %all_to_all.48.returned, bf16[128,4096]{1,0:T(8,128)(2,1)} %bitcast.47, bf16[128,4096]{1,0:T(8,128)(2,1)} %bitcast.49, f32[1,4096]{1,0:T(1,128)S(1)} %copy-done.5, bf16[4096,128]{1,0:T(8,128)(2,1)} %bitcast.45, ...), custom_call_target="tpu_custom_call" | custom-call | tf_op jit(solution)/shard_map/pallas_call | solution.py:39
  411.5 3.6 fusion.8
  415.1 3.8 all-to-all-done.8
  418.9 1.1 slice.37
  420.2 0.7 broadcast_in_dim_reshape.7
  420.9 2.3 copy.35
  423.1 2.3 copy.36
  (48 shorter events, 3.7 us)
Async XLA Ops:
  1.4 1.0 copy-start.2
  2.4 0.7 copy-start.4
  3.1 0.7 copy-start.10
  3.8 0.7 copy-start.11
  10.6 77.7 %copy-start = (bf16[1,1,768,512]{3,2,1,0:T(8,128)(2,1)S(1)}, bf16[1,1,768,512]{3,2,1,0:T(8,128)(2,1)}, u32[]{:S(2)}) copy-start(bf16[1,1,768,512]{3,2,1,0:T(8,128)(2,1)} %param.24) | copy-start | bytes 2359300
  10.6 77.7 %copy-start.1 = (s32[640,1]{1,0:T(8,128)S(1)}, s32[640,1]{1,0:T(8,128)}, u32[]{:S(2)}) copy-start(s32[640,1]{1,0:T(8,128)} %constant.47.clone.order) | copy-start | bytes 7684
  100.9 75.4 %copy-start.3 = (s32[160,1]{1,0:T(8,128)S(1)}, s32[160,1]{1,0:T(8,128)}, u32[]{:S(2)}) copy-start(s32[160,1]{1,0:T(8,128)} %constant.49.clone.slot_of) | copy-start | bytes 1924
  100.9 75.4 %copy-start.12 = (s32[1,160]{1,0:T(1,128)S(1)}, s32[1,160]{1,0:T(1,128)}, u32[]{:S(2)}) copy-start(s32[1,160]{1,0:T(1,128)} %constant.48.clone.sender_of) | copy-start | bytes 1924
  183.1 11.8 %all-to-all-start.4 = ((f32[16,1,128]{2,1,0:T(1,128)}), f32[16,1,128]{2,1,0:T(1,128)S(1)}, u32[]{:S(2)}, u32[]{:S(2)}) async-start(f32[16,1,128]{2,1,0:T(1,128)} %bitcast.9), calls=%async_computation.4 | async-start | bytes 16384 | tf_op jit(solution)/shard_map/all_to_all | solution.py:21
  213.0 68.5 %copy-start.13 = (bf16[1,1,512,1536]{3,2,1,0:T(8,128)(2,1)S(1)}, bf16[1,1,512,1536]{3,2,1,0:T(8,128)(2,1)}, u32[]{:S(2)}) copy-start(bf16[1,1,512,1536]{3,2,1,0:T(8,128)(2,1)} %param.23) | copy-start | bytes 4718596
  213.0 68.4 %all-to-all-start.2 = ((bf16[8,160,2304]{2,1,0:T(8,128)(2,1)}), bf16[8,160,2304]{2,1,0:T(8,128)(2,1)}, u32[]{:S(2)}, u32[]{:S(2)}) async-start(bf16[8,160,2304]{2,1,0:T(8,128)(2,1)} %get-tuple-element.19), calls=%async_computation.2 | async-start | bytes 11796480 | tf_op jit(solution)/shard_map/all_to_all | solution.py:21
  281.4 20.5 %copy-start.5 = (f32[1,4096]{1,0:T(1,128)S(1)}, f32[1,4096]{1,0:T(1,128)}, u32[]{:S(2)}) copy-start(f32[1,4096]{1,0:T(1,128)} %gain.3) | copy-start | bytes 49156
  288.2 12.8 %all-to-all-start.6 = ((f32[16,40,128]{2,1,0:T(8,128)}), f32[16,40,128]{2,1,0:T(8,128)S(1)}, u32[]{:S(2)}, u32[]{:S(2)}) async-start(f32[16,40,128]{2,1,0:T(8,128)} %select_maximum_fusion), calls=%async_computation.6 | async-start | bytes 655360 | tf_op jit(solution)/shard_map/all_to_all | solution.py:21
  302.8 13.4 %all-to-all-start.7 = ((bf16[16,48,128]{2,1,0:T(8,128)(2,1)}), bf16[16,48,128]{2,1,0:T(8,128)(2,1)S(1)}, u32[]{:S(2)}, u32[]{:S(2)}) async-start(bf16[16,48,128]{2,1,0:T(8,128)(2,1)} %broadcast_in_dim.52), calls=%async_computation.7 | async-start | bytes 393216 | tf_op jit(solution)/shard_map/all_to_all | solution.py:21
  392.3 9.0 %copy-start.6 = (s32[1,1280]{1,0:T(1,128)S(1)}, s32[1,1280]{1,0:T(1,128)}, u32[]{:S(2)}) copy-start(s32[1,1280]{1,0:T(1,128)} %constant.50.clone.owner) | copy-start | bytes 15364
  392.3 9.1 %copy-start.7 = (s32[1,1280]{1,0:T(1,128)S(1)}, s32[1,1280]{1,0:T(1,128)}, u32[]{:S(2)}) copy-start(s32[1,1280]{1,0:T(1,128)} %constant.51.clone.kind_of) | copy-start | bytes 15364
  392.3 9.1 %copy-start.8 = (s32[1,1280]{1,0:T(1,128)S(1)}, s32[1,1280]{1,0:T(1,128)}, u32[]{:S(2)}) copy-start(s32[1,1280]{1,0:T(1,128)} %constant.52.clone.chunk_of) | copy-start | bytes 15364
  392.3 9.1 %copy-start.9 = (s32[1,1280]{1,0:T(1,128)S(1)}, s32[1,1280]{1,0:T(1,128)}, u32[]{:S(2)}) copy-start(s32[1,1280]{1,0:T(1,128)} %constant.53.clone.slot_of) | copy-start | bytes 15364
  393.7 25.2 %all-to-all-start.8 = ((bf16[8,16,48,128]{3,2,1,0:T(8,128)(2,1)}), bf16[8,16,48,128]{3,2,1,0:T(8,128)(2,1)S(1)}, u32[]{:S(2)}, u32[]{:S(2)}) async-start(bf16[8,16,48,128]{3,2,1,0:T(8,128)(2,1)} %broadcast_in_dim.53), calls=%async_computation.8 | async-start | bytes 3145728 | tf_op jit(solution)/shard_map/all_to_all | solution.py:21
  401.4 10.1 %copy-start.14 = (bf16[1280,512]{1,0:T(8,128)(2,1)S(1)}, bf16[1280,512]{1,0:T(8,128)(2,1)}, u32[]{:S(2)}) copy-start(bf16[1280,512]{1,0:T(8,128)(2,1)} %get-tuple-element.26) | copy-start | bytes 3932164
  411.0 9.9 %collective-permute-start = (bf16[128,4096]{1,0:T(8,128)(2,1)S(1)}, bf16[128,4096]{1,0:T(8,128)(2,1)}, u32[]{:S(2)}, u32[]{:S(2)}) collective-permute-start(bf16[128,4096]{1,0:T(8,128)(2,1)S(1)} %get-tuple-element.23), channel_id=1, source_target_pairs={{0,128},{128,0},{1,129},{129,1},{2,130},{130,2},{3,131},{131,3},{4... | collective-permute-start | bytes 3145736 | tf_op jit(solution)/shard_map/ppermute | solution.py:397
  411.0 9.9 %collective-permute-start.1 = (bf16[128,4096]{1,0:T(8,128)(2,1)}, bf16[128,4096]{1,0:T(8,128)(2,1)}, u32[]{:S(2)}, u32[]{:S(2)}) collective-permute-start(bf16[128,4096]{1,0:T(8,128)(2,1)} %get-tuple-element.24), channel_id=1, source_target_pairs={{0,128},{128,0},{1,129},{129,1},{2,130},{130,2},{3,131},{131,3},{4... | collective-permute-start | bytes 3145736 | tf_op jit(solution)/shard_map/ppermute | solution.py:398

commit v3 on v2

v3 whole, which is shorter than its diff:
```python
import functools

import jax
import jax.numpy as jnp
import numpy as np
from jax import lax
from jax.experimental import pallas as pl
from jax.experimental.pallas import tpu as pltpu
from jax.sharding import Mesh
from jax.sharding import PartitionSpec as P

MOST = 10
LANES = 128
BF = jnp.bfloat16
F32 = jnp.float32
SHARE = ("dp", "expert")
OWNERS = ("half", "expert")
INTERPRET = False
HIDDEN_STEPS = 3


def exchange(blocks, axes):
    return lax.all_to_all(blocks, axes, split_axis=0, concat_axis=0, tiled=True)


def mm(left, right, contract=((1,), (0,))):
    return lax.dot_general(left, right, (contract, ((), ())), preferred_element_type=F32)


def two_terms(values):
    high = values.astype(BF)
    return high, (values - high.astype(F32)).astype(BF)


def three_terms(values):
    high = values.astype(BF)
    return (high,) + two_terms(values - high.astype(F32))


def kernel_call(body, outs, args, scratch=(), **grid):
    return pl.pallas_call(
        body,
        out_shape=outs,
        scratch_shapes=scratch,
        compiler_params=pltpu.CompilerParams(vmem_limit_bytes=52 * 2**20),
        interpret=INTERPRET,
        **grid,
    )(*args)


def iota(shape, dimension):
    return lax.broadcasted_iota(jnp.int32, shape, dimension)


def spread(values, owner):
    pick = (iota((values[0].shape[1], owner.shape[1]), 0) == owner).astype(BF)
    total = mm(values[0], pick)
    for term in values[1:]:
        total = total + mm(term, pick)
    return total


def feature(replicas, width, c, j):
    part = width // (2 * replicas)
    block, inner = divmod(c * LANES, part)
    return (block * replicas + j) * part + inner


def send_kernel(experts, replicas, chunks, slots, x, ids, grad, gain, table, owner, chunk_of, slot_of,
                message, normed_out, gates_out, place_out, stack):
    tokens, width = x.shape
    half = chunks * slots
    xw = x[...].astype(F32)
    inv_rms = lax.rsqrt(jnp.mean(xw * xw, axis=1, keepdims=True) + 1e-06)
    normed = (xw * inv_rms * gain[...]).astype(BF)
    normed_out[...] = normed
    logits = mm(normed, table[...])
    columns = iota(logits.shape, 1)
    named = columns == ids[:, 0:1]
    for k in range(1, ids.shape[1]):
        named = named | (columns == ids[:, k : k + 1])
    powers = jnp.where(named, jnp.exp(logits), 0.0)
    gates = powers / jnp.sum(powers, axis=1, keepdims=True)
    gates_out[...] = gates
    earlier = (iota((tokens, tokens), 1) < iota((tokens, tokens), 0)).astype(BF)
    rank = mm(earlier, named.astype(BF))
    place = jnp.where(named & (columns < experts), rank, -1.0)
    place_out[...] = place

    hits = spread((place.astype(BF),), owner[...]) == slot_of[...].astype(F32)
    weight = jnp.where(hits, spread(three_terms(gates), owner[...]), 0.0)
    slot_gate = jnp.sum(weight.T, axis=1, keepdims=True)
    hits_rows = jnp.where(hits, 1.0, 0.0).T
    pick = jnp.concatenate(
        [jnp.where(chunk_of[...] == c, hits_rows, 0.0).astype(BF) for c in range(chunks)], axis=1
    )

    def stacked(source):
        for c in range(chunks):
            for j in range(replicas):
                at = feature(replicas, width, c, j)
                stack[c * tokens : (c + 1) * tokens, j * LANES : (j + 1) * LANES] = source[
                    :, at : at + LANES
                ]
        return mm(pick, stack[...])

    for kind, sent in enumerate((stacked(normed_out), stacked(grad) * slot_gate)):
        sent = sent.astype(BF)
        for j in range(replicas):
            for e in range(experts):
                message[j * experts + e, kind * half : (kind + 1) * half] = sent[
                    e * half : (e + 1) * half, j * LANES : (j + 1) * LANES
                ]


def products_kernel(group, chunks, slots, index, arrived, order, first, first_other, second, second_other,
                    partial, rows_out, grads_out):
    step = pl.program_id(0)
    half = chunks * slots
    size = group * half
    block = group * slots
    own_chunks = chunks // 2
    part = own_chunks * LANES

    @pl.when(step == 0)
    def _():
        lower = index[0] == 0
        pick = (order[...] == iota((size, size), 1)).astype(BF)
        for at in range(arrived.shape[0] // group):
            lanes = [
                arrived[at * group : (at + 1) * group, kind * half : (kind + 1) * half].reshape(size, LANES)
                for kind in range(2)
            ]
            picked = mm(pick, jnp.concatenate(lanes, axis=1)).astype(BF)
            rows = slice(at * block, (at + 1) * block)
            for c in range(own_chunks):
                low = picked[c * block : (c + 1) * block]
                high = picked[(own_chunks + c) * block : (own_chunks + c + 1) * block]
                own = jnp.where(lower, low, high)
                other = jnp.where(lower, high, low)
                here = slice(c * LANES, (c + 1) * LANES)
                there = slice(part + c * LANES, part + (c + 1) * LANES)
                rows_out[rows, here] = own[:, :LANES]
                rows_out[rows, there] = other[:, :LANES]
                grads_out[rows, here] = own[:, LANES:]
                grads_out[rows, there] = other[:, LANES:]

    @pl.when(step < 2 * HIDDEN_STEPS)
    def _():
        partial[...] = (
            mm(rows_out[:, :part], first[...]) + mm(rows_out[:, part:], first_other[...])
        ).astype(BF)

    @pl.when(step >= 2 * HIDDEN_STEPS)
    def _():
        partial[...] = (
            mm(grads_out[:, :part], second[...], ((1,), (1,)))
            + mm(grads_out[:, part:], second_other[...], ((1,), (1,)))
        ).astype(BF)


def act_kernel(slots, arrived, sender_of, slot_of, acts, worth):
    replicas, rows, width = arrived.shape
    hidden_width = width // 3
    total = arrived[0].astype(F32)
    for j in range(1, replicas):
        total = total + arrived[j].astype(F32)
    gate_pre = total[:, :hidden_width]
    up = total[:, hidden_width : 2 * hidden_width]
    hidden_grad = total[:, 2 * hidden_width :]
    sigmoid = 1.0 / (1.0 + jnp.exp(-gate_pre))
    silu = gate_pre * sigmoid
    slope = sigmoid * (1.0 + gate_pre * (1.0 - sigmoid))
    hidden = (silu * up).astype(BF)
    gate_grad = (hidden_grad * up * slope).astype(BF)
    up_grad = (hidden_grad * silu).astype(BF)
    for j in range(replicas):
        acts[j, :, :hidden_width] = gate_grad
        acts[j, :, hidden_width : 2 * hidden_width] = up_grad
        acts[j, :, 2 * hidden_width :] = hidden
    each = jnp.sum(hidden_grad * hidden.astype(F32), axis=1, keepdims=True)
    laid = jnp.where(slot_of[...] == iota((rows, LANES), 1), each, 0.0)
    pick = (sender_of[...] == iota((worth.shape[0], rows), 0)).astype(BF)
    terms = three_terms(laid)
    worth[...] = mm(pick, terms[0]) + mm(pick, terms[1]) + mm(pick, terms[2])


def back_kernel(group, chunks, slots, index, gathered, order, first, first_other, second, second_other, message):
    rows, width = gathered.shape
    hidden_width = width // 3
    block = group * slots
    half = chunks * slots
    size = group * half
    own_chunks = chunks // 2
    hidden = gathered[:, 2 * hidden_width :]
    pre_grad = gathered[:, : 2 * hidden_width]
    lower = index[0] == 0

    def ordered(own, other):
        own, other = own.astype(BF), other.astype(BF)
        return jnp.where(lower, own, other), jnp.where(lower, other, own)

    outs = ordered(mm(hidden, second[...]), mm(hidden, second_other[...]))
    backs = ordered(mm(pre_grad, first[...], ((1,), (1,))), mm(pre_grad, first_other[...], ((1,), (1,))))
    pick = (order[...] == iota((size, size), 1)).astype(BF)

    def column(source, at):
        return jnp.concatenate(
            [
                side[at : at + block, c * LANES : (c + 1) * LANES]
                for side in source
                for c in range(own_chunks)
            ],
            axis=0,
        )

    for at in range(rows // block):
        lanes = [column(source, at * block) for source in (outs, backs)]
        picked = mm(pick, jnp.concatenate(lanes, axis=1)).astype(BF)
        for kind in range(2):
            message[at * group : (at + 1) * group, kind * half : (kind + 1) * half] = picked[
                :, kind * LANES : (kind + 1) * LANES
            ].reshape(group, half, LANES)


def combine_kernel(experts, replicas, chunks, slots, returned, x, grad, gain, table, gates, place, logit_grad,
                   owner, chunk_of, slot_of, layer_out, in_grad, joined, normed_grad):
    tokens, width = x.shape
    half = chunks * slots

    def join(kind):
        for j in range(replicas):
            block = returned[j * experts : (j + 1) * experts, kind * half : (kind + 1) * half]
            joined[:, j * LANES : (j + 1) * LANES] = block.reshape(experts * half, LANES)
        return joined[...]

    hits = spread((place[...].astype(BF),), owner[...]) == slot_of[...].astype(F32)
    high, low = (
        jnp.where(hits, spread((term,), owner[...]), 0.0) for term in two_terms(gates[...])
    )
    ones = jnp.where(hits, 1.0, 0.0)
    chunk = chunk_of[...]

    def picks(values):
        return jnp.concatenate(
            [jnp.where(chunk == c, values, 0.0).astype(BF) for c in range(chunks)], axis=0
        )

    source = join(0)
    mixed = mm(picks(high), source) + mm(picks(low), source)
    back = mm(picks(ones), join(1))
    logit_high, logit_low = two_terms(logit_grad[...])
    by_logits = mm(logit_high, table[...], ((1,), (1,))) + mm(logit_low, table[...], ((1,), (1,)))
    for c in range(chunks):
        rows = slice(c * tokens, (c + 1) * tokens)
        for j in range(replicas):
            lanes = slice(j * LANES, (j + 1) * LANES)
            at = feature(replicas, width, c, j)
            at = slice(at, at + LANES)
            layer_out[:, at] = (x[:, at].astype(F32) + mixed[rows, lanes]).astype(BF)
            normed_grad[:, at] = back[rows, lanes] + by_logits[:, at]
    xw = x[...].astype(F32)
    inv_rms = lax.rsqrt(jnp.mean(xw * xw, axis=1, keepdims=True) + 1e-06)
    weighted = gain[...] * normed_grad[...]
    mean = jnp.mean(xw * weighted, axis=1, keepdims=True)
    in_grad[...] = (
        grad[...].astype(F32) + inv_rms * weighted - xw * (inv_rms * inv_rms * inv_rms * mean)
    ).astype(BF)


def swapped(block, axis):
    return lax.ppermute(block, axis, [(0, 1), (1, 0)])


def shards(section_input, routing, out_grad, norm_gain, router, w_in, w_out):
    experts = lax.axis_size("expert")
    replicas = lax.axis_size("dp")
    x = section_input[0]
    route_ids = routing[0]
    grad_top = out_grad[0]
    gain = norm_gain[0][None, :]
    table = router[0]
    first = w_in[0, 0]
    second = w_out[0, 0]
    tokens, width = x.shape
    part = first.shape[0]
    hidden_width = second.shape[0]
    slots = MOST
    rows = experts * slots
    router_width = table.shape[1]
    chunks = 2 * part // LANES
    half = chunks * slots
    peers = replicas * experts
    group = min(8, experts)
    message_shape = jax.ShapeDtypeStruct((peers, 2 * half, LANES), BF)
    side = lax.axis_index("half")
    index = side.astype(jnp.int32)[None]
    first_other = swapped(first, "half")
    second_other = swapped(second, "half")

    at = np.arange(experts * half, dtype=np.int32)
    owner, chunk_of, slot_of = at // half, at % half // slots, at % slots
    message, normed, gates, place = kernel_call(
        functools.partial(send_kernel, experts, replicas, chunks, slots),
        (
            message_shape,
            jax.ShapeDtypeStruct((tokens, width), BF),
            jax.ShapeDtypeStruct((tokens, router_width), F32),
            jax.ShapeDtypeStruct((tokens, router_width), F32),
        ),
        (x, route_ids, grad_top, gain, table, owner[None], chunk_of[:, None], slot_of[None]),
        [pltpu.VMEM((chunks * tokens, replicas * LANES), BF)],
    )
    arrived = exchange(message, SHARE)

    at = np.arange(group * half, dtype=np.int32)
    into_messages = (at % half // slots * group + at // half) * slots + at % slots
    into_rows = np.zeros_like(at)
    into_rows[into_messages] = at
    step_width = hidden_width // HIDDEN_STEPS
    all_rows = peers * slots
    whole = lambda shape: pl.BlockSpec(shape, lambda i: (0,) * len(shape))
    scalar = pl.BlockSpec(memory_space=pltpu.SMEM)
    by_column = pl.BlockSpec((part, step_width), lambda i: (0, jnp.minimum(i, 2 * HIDDEN_STEPS - 1)))
    by_row = pl.BlockSpec((step_width, part), lambda i: (jnp.maximum(i - 2 * HIDDEN_STEPS, 0), 0))
    partial, expert_rows, grad_rows = kernel_call(
        functools.partial(products_kernel, group, chunks, slots),
        (
            jax.ShapeDtypeStruct((all_rows, 3 * hidden_width), BF),
            jax.ShapeDtypeStruct((all_rows, 2 * part), BF),
            jax.ShapeDtypeStruct((all_rows, 2 * part), BF),
        ),
        (index, arrived, into_rows[:, None], first, first_other, second, second_other),
        grid=(3 * HIDDEN_STEPS,),
        in_specs=[scalar, whole(arrived.shape), whole((at.size, 1)), by_column, by_column, by_row, by_row],
        out_specs=[
            pl.BlockSpec((all_rows, step_width), lambda i: (0, i)),
            whole((all_rows, 2 * part)),
            whole((all_rows, 2 * part)),
        ],
    )
    summands = exchange(partial.reshape(replicas, rows, 3 * hidden_width), "dp")
    at = np.arange(rows, dtype=np.int32)
    acts, worth = kernel_call(
        functools.partial(act_kernel, slots),
        (
            jax.ShapeDtypeStruct(summands.shape, BF),
            jax.ShapeDtypeStruct((experts, LANES), F32),
        ),
        (summands, at[None] // slots, at[:, None] % slots),
    )
    gathered = exchange(acts, "dp").reshape(-1, 3 * hidden_width)
    pre_grad = gathered[:, : 2 * hidden_width]
    hidden_all = gathered[:, 2 * hidden_width :]

    worth = exchange(worth[:, None], "expert")[:, 0, :slots]
    slot_ids = jnp.arange(slots, dtype=F32)
    gate_worth = jnp.sum(
        jnp.where(place[:, :experts, None] == slot_ids, worth[None], 0.0), axis=2
    )
    inner = jnp.sum(gate_worth, axis=1, keepdims=True)
    logit_grad = jnp.pad(gate_worth, ((0, 0), (0, router_width - experts))) - gates * inner
    logit_high, logit_low = two_terms(logit_grad)
    local_router = mm(normed, logit_high, ((0,), (0,))) + mm(normed, logit_low, ((0,), (0,)))
    local_router = local_router.astype(BF).reshape(2, replicas, part, router_width).transpose(1, 0, 2, 3)
    router_part = exchange(local_router.reshape(replicas, 2 * part, router_width), "dp")
    router_part = jnp.sum(router_part.astype(F32), axis=0)

    steps = 2 if replicas % 2 == 0 else 1
    message = kernel_call(
        functools.partial(back_kernel, group, chunks, slots),
        message_shape,
        (index, gathered, into_messages[:, None], first, first_other, second, second_other),
        grid=(steps,),
        in_specs=[
            scalar,
            pl.BlockSpec((all_rows // steps, 3 * hidden_width), lambda i: (i, 0)),
            whole((into_messages.size, 1)),
            whole(first.shape),
            whole(first.shape),
            whole(second.shape),
            whole(second.shape),
        ],
        out_specs=pl.BlockSpec((peers // steps, 2 * half, LANES), lambda i: (i, 0, 0)),
    )
    returned = exchange(message, SHARE)

    rows_own, rows_other = expert_rows[:, :part], expert_rows[:, part:]
    first_other_grad = mm(rows_other, pre_grad, ((0,), (0,)))
    second_other_grad = mm(hidden_all, grad_rows[:, part:], ((0,), (0,)))
    first_sent = swapped(first_other_grad.astype(BF), "half")
    second_sent = swapped(second_other_grad.astype(BF), "half")
    first_own_grad = mm(rows_own, pre_grad, ((0,), (0,)))
    second_own_grad = mm(hidden_all, grad_rows[:, :part], ((0,), (0,)))
    first_grad = (first_own_grad + first_sent.astype(F32)).astype(BF)
    second_grad = (second_own_grad + second_sent.astype(F32)).astype(BF)
    gain_own = jnp.sum(first_own_grad * first.astype(F32), axis=1)
    gain_other = jnp.sum(first_other_grad * first_other.astype(F32), axis=1)
    gain_part = jnp.where(
        side == 0, jnp.stack([gain_own, gain_other]), jnp.stack([gain_other, gain_own])
    )

    owners = 2 * experts
    piece = 2 * part // owners
    gain_rows = jnp.pad(gain_part.reshape(owners, 1, piece), ((0, 0), (0, 7), (0, LANES - piece)))
    owned = jnp.concatenate([router_part.reshape(owners, piece, router_width), gain_rows], axis=1)
    owned = jnp.sum(exchange(owned, OWNERS), axis=0)
    router_own = owned[:piece]
    at = (side * replicas + lax.axis_index("dp")) * part + lax.axis_index("expert") * piece
    table_own = lax.dynamic_slice_in_dim(table, at, piece, axis=0).astype(F32)
    gain_here = lax.dynamic_slice_in_dim(gain[0], at, piece, axis=0)
    gain_sum = (owned[piece, :piece] + jnp.sum(router_own * table_own, axis=1)) / gain_here
    gain_terms = jnp.pad(jnp.stack(three_terms(gain_sum)), ((0, 13), (0, LANES - piece)))
    block = jnp.concatenate([router_own.astype(BF), gain_terms], axis=0)
    joined = exchange(jnp.broadcast_to(block[None], (owners,) + block.shape), OWNERS)
    joined = exchange(jnp.broadcast_to(joined[None], (replicas,) + joined.shape), "dp")
    joined = joined.reshape(replicas, 2, experts, piece + 16, LANES).transpose(1, 0, 2, 3, 4)
    router_total = joined[:, :, :, :piece].reshape(width, router_width)
    gain_total = jnp.sum(joined[:, :, :, piece : piece + 3, :piece].astype(F32), axis=3).reshape(width)

    layer_out, in_grad = kernel_call(
        functools.partial(combine_kernel, experts, replicas, chunks, slots),
        (
            jax.ShapeDtypeStruct((tokens, width), BF),
            jax.ShapeDtypeStruct((tokens, width), BF),
        ),
        (
            returned, x, grad_top, gain, table, gates, place, logit_grad,
            owner[None], chunk_of[None], slot_of[None],
        ),
        [
            pltpu.VMEM((experts * half, replicas * LANES), BF),
            pltpu.VMEM((tokens, width), F32),
        ],
    )
    handoff = swapped(layer_out, "section")
    handback = swapped(in_grad, "section")
    return (
        handoff[None],
        handback[None],
        first_grad[None, None],
        second_grad[None, None],
        router_total[None],
        gain_total[None],
    )


def solution(mesh):
    sizes = mesh.shape
    halves = (sizes["section"], sizes["expert"], 2, sizes["dp"] // 2)
    split = Mesh(mesh.devices.reshape(halves), ("section", "expert", "half", "dp"))
    blocks = ("half", "dp")
    tokens = ("expert",) + blocks
    return jax.shard_map(
        shards,
        mesh=split,
        in_specs=(
            P("section", tokens, None),
            P("section", tokens, None),
            P("section", tokens, None),
            P("section", None),
            P("section", None, None),
            P("section", "expert", blocks, None),
            P("section", "expert", None, blocks),
        ),
        out_specs=(
            P("section", tokens, None),
            P("section", tokens, None),
            P("section", "expert", blocks, None),
            P("section", "expert", None, blocks),
            P("section", None, None),
            P("section", None),
        ),
        check_vma=False,
    )
```

time: 427 us -> 398 us (0.932)
  blocking collectives: 246 us -> 120 us
  waiting for transfers between devices: 81.9 us -> 151 us
  starting transfers between devices: 26.3 us -> 48.5 us
  matrix products: 10.6 us -> 16.1 us
    all_to_all x4 -> x3, blocking collectives: 246 us -> 120 us  [exchange(): return lax.all_to_all(blocks, axes, split_axis=0, concat_axis=0, tiled=True)]
    ppermute x2 -> x6, waiting for transfers between devices: 0.01 us -> 92.7 us  [swapped(): return lax.ppermute(block, axis, [(0, 1), (1, 0)])]
    all_to_all x5 -> x6, waiting for transfers between devices: 81.9 us -> 58.6 us  [exchange(): return lax.all_to_all(blocks, axes, split_axis=0, concat_axis=0, tiled=True)]
    all_to_all x5 -> x6, starting transfers between devices: 25.8 us -> 39.3 us  [exchange(): return lax.all_to_all(blocks, axes, split_axis=0, concat_axis=0, tiled=True)]
    ppermute x2 -> x6, starting transfers between devices: 0.51 us -> 9.16 us  [swapped(): return lax.ppermute(block, axis, [(0, 1), (1, 0)])]
    dot_general x4 -> x6, matrix products: 10.6 us -> 16.1 us  [mm(): lax.dot_general(left, right, (contract, ((), ())), preferred_element_type...]
  transfers between devices with their start and end apart: 7 -> 12, of which waited for: 4 -> 7; matrix products, arithmetic and copies ran while one was open for 2% -> 3% of each run, Pallas kernels for 4% -> 5%
where the time goes in v3:
time: 398 us; the launch traced here: 397 us
  waiting for transfers between devices  151 us (38%)
  blocking collectives  120 us (30%)
  starting transfers between devices  48.5 us (12%)
  Pallas kernels  43.5 us (11%)
  matrix products  16.1 us (4%)
  local copies, waits for them, and re-layouts  12.6 us (3%)
  other arithmetic  4.15 us (1%)
    all_to_all x3, blocking collectives, exchange(): return lax.all_to_all(blocks, axes, split_axis=0, concat_axis=0, tiled=True)  120 us
    ppermute x6, waiting for transfers between devices, swapped(): return lax.ppermute(block, axis, [(0, 1), (1, 0)])  92.7 us
    all_to_all x6, waiting for transfers between devices, exchange(): return lax.all_to_all(blocks, axes, split_axis=0, concat_axis=0, tiled=True)  58.6 us
    pallas_call x5, Pallas kernels, kernel_call(): pl.pallas_call(body, out_shape=outs, scratch_shapes=scratch, compiler_par...  43.5 us
    all_to_all x6, starting transfers between devices, exchange(): return lax.all_to_all(blocks, axes, split_axis=0, concat_axis=0, tiled=True)  39.3 us
    dot_general x6, matrix products, mm(): lax.dot_general(left, right, (contract, ((), ())), preferred_element_type...  16.1 us
    ppermute x6, starting transfers between devices, swapped(): return lax.ppermute(block, axis, [(0, 1), (1, 0)])  9.16 us
  transfers between devices with their start and end apart: 12, of which 7 were waited for; matrix products, arithmetic and copies ran while one was open for 3% of the time, Pallas kernels for 5%

profile of v3, /device:TPU:8, one launch (start us, length us, event | category | flops | bytes accessed | tf_op | source)
XLA Modules:
  0.0 396.6 jit_solution(8706881216993514123)
XLA Ops:
  1.4 1.1 copy-done.2
  4.6 8.0 %shard_map.208 = (bf16[64,160,128]{2,1,0:T(8,128)(2,1)}, bf16[128,4096]{1,0:T(8,128)(2,1)S(1)}, f32[128,128]{1,0:T(8,128)S(1)}, f32[128,128]{1,0:T(8,128)S(1)}) custom-call(bf16[128,4096]{1,0:T(8,128)(2,1)} %bitcast.54, s32[128,8]{1,0:T(8,128)S(1)} %bitcast.47, bf16[128,4096]{1,0:T(8,128)(2,1)} %bitcast.56, f32[1,4096]{1,0:T(1,128)S(1)} %copy-done.4, ...), custom_call_target="tpu_custom_call" | custom-call | tf_op jit(solution)/shard_map/pallas_call | solution.py:41
  12.7 13.3 %all-to-all-start = ((bf16[64,160,128]{2,1,0:T(8,128)(2,1)}), bf16[64,160,128]{2,1,0:T(8,128)(2,1)}, u32[]{:S(2)}, u32[]{:S(2)}) async-start(bf16[64,160,128]{2,1,0:T(8,128)(2,1)} %get-tuple-element.17), calls=%async_computation | async-start | bytes 5242880 | tf_op jit(solution)/shard_map/all_to_all | solution.py:23
  26.0 2.8 collective-permute-start
  29.6 77.6 %collective-permute-done.1.second_other = bf16[768,512]{1,0:T(8,128)(2,1)S(1)} collective-permute-done((bf16[768,512]{1,0:T(8,128)(2,1)S(1)}, bf16[768,512]{1,0:T(8,128)(2,1)S(1)}, u32[]{:S(2)}, u32[]{:S(2)}) %collective-permute-start.1) | collective-permute-done | bytes 786464 | tf_op jit(solution)/shard_map/ppermute | solution.py:272
  107.2 12.6 %shard_map.209 = (bf16[640,2304]{1,0:T(8,128)(2,1)}, bf16[640,1024]{1,0:T(8,128)(2,1)}, bf16[640,1024]{1,0:T(8,128)(2,1)}) custom-call(s32[1]{0:T(128)} %bitcast.index, bf16[64,160,128]{2,1,0:T(8,128)(2,1)} %all-to-all-done.arrived, s32[640,1]{1,0:T(8,128)S(1)} %copy-done.1, bf16[512,1536]{1,0:T(8,128)(2,1)} %bitcast.50, ...), custom_call_target="tpu_custom_call" | custom-call | tf_op jit(solution)/shard_map/pallas_call | solution.py:41
  119.8 39.6 %all_to_all.45.arrived = bf16[4,160,2304]{2,1,0:T(8,128)(2,1)} all-to-all(bf16[4,160,2304]{2,1,0:T(8,128)(2,1)} %bitcast.60), channel_id=1, replica_groups=mesh['section'=2,'expert'=16,'half'=2,'dp'=4] {'dp'}, dimensions={0} | all-to-all | bytes 5898240 | tf_op jit(solution)/shard_map/all_to_all | solution.py:23
  159.4 4.2 %shard_map.210 = (bf16[4,160,2304]{2,1,0:T(8,128)(2,1)}, f32[16,128]{1,0:T(8,128)S(1)}) custom-call(bf16[4,160,2304]{2,1,0:T(8,128)(2,1)} %all_to_all.45.arrived, s32[1,160]{1,0:T(1,128)S(1)} %copy-done.11, s32[160,1]{1,0:T(8,128)S(1)} %copy-done.3), custom_call_target="tpu_custom_call" | custom-call | tf_op jit(solution)/shard_map/pallas_call | solution.py:41
  163.5 15.1 %all_to_all.46 = f32[16,1,128]{2,1,0:T(1,128)S(1)} all-to-all(f32[16,1,128]{2,1,0:T(1,128)S(1)} %bitcast.48), channel_id=1, replica_groups=mesh['section'=2,'expert'=16,'half'=2,'dp'=4] {'expert'}, dimensions={0} | all-to-all | bytes 16384 | tf_op jit(solution)/shard_map/all_to_all | solution.py:23
  178.6 6.0 %all-to-all-start.2 = ((bf16[4,160,2304]{2,1,0:T(8,128)(2,1)}), bf16[4,160,2304]{2,1,0:T(8,128)(2,1)}, u32[]{:S(2)}, u32[]{:S(2)}) async-start(bf16[4,160,2304]{2,1,0:T(8,128)(2,1)} %get-tuple-element.19), calls=%async_computation.2 | async-start | bytes 5898240 | tf_op jit(solution)/shard_map/all_to_all | solution.py:23
  185.1 30.9 %all-to-all-done.2 = bf16[4,160,2304]{2,1,0:T(8,128)(2,1)} async-done(((bf16[4,160,2304]{2,1,0:T(8,128)(2,1)}), bf16[4,160,2304]{2,1,0:T(8,128)(2,1)}, u32[]{:S(2)}, u32[]{:S(2)}) %all-to-all-start.2) | async-done | bytes 2949152 | tf_op jit(solution)/shard_map/all_to_all | solution.py:23
  215.9 4.8 %multiply_reduce_fusion = (f32[512]{0:T(512)S(1)}, bf16[512,1536]{1,0:T(8,128)(2,1)}) fusion(bf16[512,1536]{1,0:T(8,128)(2,1)} %collective-permute-done.first_other, bf16[640,2304]{1,0:T(8,128)(2,1)} %bitcast.8.gathered, bf16[640,1024]{1,0:T(8,128)(2,1)} %get-tuple-element.25), kind=kOutput, calls=%fused_computation.2 | convolution fusion | flops 1009778176 | bytes 5769216 | tf_op jit(solution)/shard_map/dot_general | solution.py:27
  220.7 2.0 collective-permute-start.4
  224.7 4.9 %all-to-all-start.5 = ((bf16[4,1024,128]{2,1,0:T(8,128)(2,1)}), bf16[4,1024,128]{2,1,0:T(8,128)(2,1)S(1)}, u32[]{:S(2)}, u32[]{:S(2)}) async-start(bf16[4,1024,128]{2,1,0:T(8,128)(2,1)} %bitcast.58), calls=%async_computation.5 | async-start | bytes 2097152 | tf_op jit(solution)/shard_map/all_to_all | solution.py:23
  229.7 9.6 %all-to-all-done.5 = bf16[4,1024,128]{2,1,0:T(8,128)(2,1)S(1)} async-done(((bf16[4,1024,128]{2,1,0:T(8,128)(2,1)}), bf16[4,1024,128]{2,1,0:T(8,128)(2,1)S(1)}, u32[]{:S(2)}, u32[]{:S(2)}) %all-to-all-start.5) | async-done | bytes 1048608 | tf_op jit(solution)/shard_map/all_to_all | solution.py:23
  240.3 14.5 %collective-permute-done.4 = bf16[512,1536]{1,0:T(8,128)(2,1)} collective-permute-done((bf16[512,1536]{1,0:T(8,128)(2,1)}, bf16[512,1536]{1,0:T(8,128)(2,1)}, u32[]{:S(2)}, u32[]{:S(2)}) %collective-permute-start.4) | collective-permute-done | bytes 1572896 | tf_op jit(solution)/shard_map/ppermute | solution.py:272
  254.7 5.5 %multiply_reduce_fusion.1 = (f32[512]{0:T(512)S(1)}, bf16[1,1,512,1536]{3,2,1,0:T(8,128)(2,1)}) fusion(bf16[1,1,512,1536]{3,2,1,0:T(8,128)(2,1)} %param.22, bf16[512,1536]{1,0:T(8,128)(2,1)} %collective-permute-done.4, bf16[640,2304]{1,0:T(8,128)(2,1)} %bitcast.8.gathered, bf16[640,1024]{1,0:T(8,128)(2,1)} %get-tuple-element.25), kind=kOutput, calls=%fused_computation.3 | convolution fusion | flops 1011351040 | bytes 7342080 | tf_op jit(solution)/shard_map/dot_general | solution.py:27
  261.2 3.9 all-to-all-start.6
  265.1 15.7 %all-to-all-done.6 = f32[32,40,128]{2,1,0:T(8,128)S(1)} async-done(((f32[32,40,128]{2,1,0:T(8,128)}), f32[32,40,128]{2,1,0:T(8,128)S(1)}, u32[]{:S(2)}, u32[]{:S(2)}) %all-to-all-start.6) | async-done | bytes 655392 | tf_op jit(solution)/shard_map/all_to_all | solution.py:23
  282.6 4.9 %all-to-all-start.7 = ((bf16[32,48,128]{2,1,0:T(8,128)(2,1)}), bf16[32,48,128]{2,1,0:T(8,128)(2,1)S(1)}, u32[]{:S(2)}, u32[]{:S(2)}) async-start(bf16[32,48,128]{2,1,0:T(8,128)(2,1)} %broadcast_in_dim.56), calls=%async_computation.7 | async-start | bytes 786432 | tf_op jit(solution)/shard_map/all_to_all | solution.py:23
  287.6 9.1 %shard_map.211 = bf16[64,160,128]{2,1,0:T(8,128)(2,1)} custom-call(s32[1]{0:T(128)} %bitcast.index, bf16[640,2304]{1,0:T(8,128)(2,1)} %bitcast.8.gathered, s32[640,1]{1,0:T(8,128)S(1)} %copy-done.1, bf16[512,1536]{1,0:T(8,128)(2,1)} %bitcast.51, bf16[512,1536]{1,0:T(8,128)(2,1)} %collective-permute-done.first_other, bf16[768,512]{1,0:T(8,128)(2,1)S(1)} %bitcast.45, ...), custom_call_target="tpu_custom_call" | custom-call | tf_op jit(solution)/shard_map/pallas_call | solution.py:41
  296.6 2.4 all-to-all-done.7
  299.0 65.0 %all_to_all.47.returned = bf16[64,160,128]{2,1,0:T(8,128)(2,1)} all-to-all(bf16[64,160,128]{2,1,0:T(8,128)(2,1)} %shard_map.211), channel_id=1, replica_groups=mesh['section'=2,'expert'=16,'half'=2,'dp'=4] {'dp','expert'}, dimensions={0} | all-to-all | bytes 5242880 | tf_op jit(solution)/shard_map/all_to_all | solution.py:23
  364.0 1.4 broadcast_in_dim.57
  365.4 6.2 %all-to-all-start.8 = ((bf16[4,32,48,128]{3,2,1,0:T(8,128)(2,1)}), bf16[4,32,48,128]{3,2,1,0:T(8,128)(2,1)}, u32[]{:S(2)}, u32[]{:S(2)}) async-start(bf16[4,32,48,128]{3,2,1,0:T(8,128)(2,1)} %broadcast_in_dim.57), calls=%async_computation.8 | async-start | bytes 3145728 | tf_op jit(solution)/shard_map/all_to_all | solution.py:23
  371.6 2.0 convolution_convert_fusion
  373.7 3.0 collective-permute-start.5
  376.7 9.6 %shard_map.212 = (bf16[128,4096]{1,0:T(8,128)(2,1)S(1)}, bf16[128,4096]{1,0:T(8,128)(2,1)}) custom-call(bf16[64,160,128]{2,1,0:T(8,128)(2,1)} %all_to_all.47.returned, bf16[128,4096]{1,0:T(8,128)(2,1)} %bitcast.55, bf16[128,4096]{1,0:T(8,128)(2,1)} %bitcast.57, f32[1,4096]{1,0:T(1,128)S(1)} %copy-done.5, bf16[4096,128]{1,0:T(8,128)(2,1)} %bitcast.53, ...), custom_call_target="tpu_custom_call" | custom-call | tf_op jit(solution)/shard_map/pallas_call | solution.py:41
  387.5 2.9 fusion.6
  390.4 1.3 slice.53
  391.7 1.1 copy.44
  392.8 1.1 convert_reduce_fusion.1
  (63 shorter events, 13.7 us)
Async XLA Ops:
  1.4 1.1 copy-start.2
  2.5 0.7 copy-start.4
  3.2 0.7 copy-start.6
  3.9 0.7 copy-start.8
  12.6 16.2 %copy-start = (bf16[1,1,768,512]{3,2,1,0:T(8,128)(2,1)S(1)}, bf16[1,1,768,512]{3,2,1,0:T(8,128)(2,1)}, u32[]{:S(2)}) copy-start(bf16[1,1,768,512]{3,2,1,0:T(8,128)(2,1)} %param.23) | copy-start | bytes 2359300
  12.6 94.5 %copy-start.1 = (s32[640,1]{1,0:T(8,128)S(1)}, s32[640,1]{1,0:T(8,128)}, u32[]{:S(2)}) copy-start(s32[640,1]{1,0:T(8,128)} %constant.48.clone.order) | copy-start | bytes 7684
  12.7 94.5 %all-to-all-start = ((bf16[64,160,128]{2,1,0:T(8,128)(2,1)}), bf16[64,160,128]{2,1,0:T(8,128)(2,1)}, u32[]{:S(2)}, u32[]{:S(2)}) async-start(bf16[64,160,128]{2,1,0:T(8,128)(2,1)} %get-tuple-element.17), calls=%async_computation | async-start | bytes 5242880 | tf_op jit(solution)/shard_map/all_to_all | solution.py:23
  26.0 81.2 %collective-permute-start = (bf16[512,1536]{1,0:T(8,128)(2,1)}, bf16[512,1536]{1,0:T(8,128)(2,1)}, u32[]{:S(2)}, u32[]{:S(2)}) collective-permute-start(bf16[512,1536]{1,0:T(8,128)(2,1)} %bitcast.49), channel_id=1, source_target_pairs={{0,4},{4,0},{1,5},{5,1},{2,6},{6,2},{3,7},{7,3},{8,12},{12,8},{9,1... | collective-permute-start | bytes 4718600 | tf_op jit(solution)/shard_map/ppermute | solution.py:272
  28.8 78.4 %collective-permute-start.1 = (bf16[768,512]{1,0:T(8,128)(2,1)S(1)}, bf16[768,512]{1,0:T(8,128)(2,1)S(1)}, u32[]{:S(2)}, u32[]{:S(2)}) collective-permute-start(bf16[768,512]{1,0:T(8,128)(2,1)S(1)} %bitcast.43), channel_id=1, source_target_pairs={{0,4},{4,0},{1,5},{5,1},{2,6},{6,2},{3,7},{7,3},{8,12},{12,8},{9,1... | collective-permute-start | bytes 2359304 | tf_op jit(solution)/shard_map/ppermute | solution.py:272
  119.8 39.6 %copy-start.3 = (s32[160,1]{1,0:T(8,128)S(1)}, s32[160,1]{1,0:T(8,128)}, u32[]{:S(2)}) copy-start(s32[160,1]{1,0:T(8,128)} %constant.50.clone.slot_of) | copy-start | bytes 1924
  119.8 39.6 %copy-start.11 = (s32[1,160]{1,0:T(1,128)S(1)}, s32[1,160]{1,0:T(1,128)}, u32[]{:S(2)}) copy-start(s32[1,160]{1,0:T(1,128)} %constant.49.clone.sender_of) | copy-start | bytes 1924
  178.6 37.3 %all-to-all-start.2 = ((bf16[4,160,2304]{2,1,0:T(8,128)(2,1)}), bf16[4,160,2304]{2,1,0:T(8,128)(2,1)}, u32[]{:S(2)}, u32[]{:S(2)}) async-start(bf16[4,160,2304]{2,1,0:T(8,128)(2,1)} %get-tuple-element.19), calls=%async_computation.2 | async-start | bytes 5898240 | tf_op jit(solution)/shard_map/all_to_all | solution.py:23
  220.7 34.0 %collective-permute-start.4 = (bf16[512,1536]{1,0:T(8,128)(2,1)}, bf16[512,1536]{1,0:T(8,128)(2,1)}, u32[]{:S(2)}, u32[]{:S(2)}) collective-permute-start(bf16[512,1536]{1,0:T(8,128)(2,1)} %get-tuple-element.35), channel_id=1, source_target_pairs={{0,4},{4,0},{1,5},{5,1},{2,6},{6,2},{3,7},{7,3},{8,12},{12,8},{9,1... | collective-permute-start | bytes 4718600 | tf_op jit(solution)/shard_map/ppermute | solution.py:272
  224.7 14.6 %all-to-all-start.5 = ((bf16[4,1024,128]{2,1,0:T(8,128)(2,1)}), bf16[4,1024,128]{2,1,0:T(8,128)(2,1)S(1)}, u32[]{:S(2)}, u32[]{:S(2)}) async-start(bf16[4,1024,128]{2,1,0:T(8,128)(2,1)} %bitcast.58), calls=%async_computation.5 | async-start | bytes 2097152 | tf_op jit(solution)/shard_map/all_to_all | solution.py:23
  240.2 20.0 %copy-start.12 = (f32[1024,128]{1,0:T(8,128)S(1)}, f32[1024,128]{1,0:T(8,128)}, u32[]{:S(2)}) copy-start(f32[1024,128]{1,0:T(8,128)} %convert_reduce_fusion) | copy-start | bytes 1572868
  260.2 21.5 %copy-start.5 = (f32[1,4096]{1,0:T(1,128)S(1)}, f32[1,4096]{1,0:T(1,128)}, u32[]{:S(2)}) copy-start(f32[1,4096]{1,0:T(1,128)} %gain.3) | copy-start | bytes 49156
  261.2 19.7 %all-to-all-start.6 = ((f32[32,40,128]{2,1,0:T(8,128)}), f32[32,40,128]{2,1,0:T(8,128)S(1)}, u32[]{:S(2)}, u32[]{:S(2)}) async-start(f32[32,40,128]{2,1,0:T(8,128)} %select_maximum_fusion), calls=%async_computation.6 | async-start | bytes 1310720 | tf_op jit(solution)/shard_map/all_to_all | solution.py:23
  282.6 16.4 %all-to-all-start.7 = ((bf16[32,48,128]{2,1,0:T(8,128)(2,1)}), bf16[32,48,128]{2,1,0:T(8,128)(2,1)S(1)}, u32[]{:S(2)}, u32[]{:S(2)}) async-start(bf16[32,48,128]{2,1,0:T(8,128)(2,1)} %broadcast_in_dim.56), calls=%async_computation.7 | async-start | bytes 786432 | tf_op jit(solution)/shard_map/all_to_all | solution.py:23
  365.4 6.2 %copy-start.13 = (bf16[640,1024]{1,0:T(8,128)(2,1)S(1)}, bf16[640,1024]{1,0:T(8,128)(2,1)}, u32[]{:S(2)}) copy-start(bf16[640,1024]{1,0:T(8,128)(2,1)} %get-tuple-element.26) | copy-start | bytes 3932164
  365.4 25.0 %all-to-all-start.8 = ((bf16[4,32,48,128]{3,2,1,0:T(8,128)(2,1)}), bf16[4,32,48,128]{3,2,1,0:T(8,128)(2,1)}, u32[]{:S(2)}, u32[]{:S(2)}) async-start(bf16[4,32,48,128]{3,2,1,0:T(8,128)(2,1)} %broadcast_in_dim.57), calls=%async_computation.8 | async-start | bytes 3145728 | tf_op jit(solution)/shard_map/all_to_all | solution.py:23
  371.6 5.1 %copy-start.7 = (s32[1,1280]{1,0:T(1,128)S(1)}, s32[1,1280]{1,0:T(1,128)}, u32[]{:S(2)}) copy-start(s32[1,1280]{1,0:T(1,128)} %constant.45.clone.owner) | copy-start | bytes 15364
  371.6 5.1 %copy-start.9 = (s32[1,1280]{1,0:T(1,128)S(1)}, s32[1,1280]{1,0:T(1,128)}, u32[]{:S(2)}) copy-start(s32[1,1280]{1,0:T(1,128)} %constant.47.clone.slot_of) | copy-start | bytes 15364
  371.6 5.1 %copy-start.10 = (s32[1,1280]{1,0:T(1,128)S(1)}, s32[1,1280]{1,0:T(1,128)}, u32[]{:S(2)}) copy-start(s32[1,1280]{1,0:T(1,128)} %constant.51.clone.chunk_of) | copy-start | bytes 15364
  373.6 13.8 %copy-start.14 = (bf16[640,1024]{1,0:T(8,128)(2,1)S(1)}, bf16[640,1024]{1,0:T(8,128)(2,1)}, u32[]{:S(2)}) copy-start(bf16[640,1024]{1,0:T(8,128)(2,1)} %get-tuple-element.26) | copy-start | bytes 3932164
  373.7 13.8 %collective-permute-start.5 = (bf16[768,512]{1,0:T(8,128)(2,1)S(1)}, bf16[768,512]{1,0:T(8,128)(2,1)S(1)}, u32[]{:S(2)}, u32[]{:S(2)}) collective-permute-start(bf16[768,512]{1,0:T(8,128)(2,1)S(1)} %convolution_convert_fusion), channel_id=1, source_target_pairs={{0,4},{4,0},{1,5},{5,1},{2,6},{6,2},{3,7},{7,3},{8,12},{12,8},{9,1... | collective-permute-start | bytes 2359304 | tf_op jit(solution)/shard_map/ppermute | solution.py:272
  386.3 8.3 %collective-permute-start.2 = (bf16[128,4096]{1,0:T(8,128)(2,1)S(1)}, bf16[128,4096]{1,0:T(8,128)(2,1)S(1)}, u32[]{:S(2)}, u32[]{:S(2)}) collective-permute-start(bf16[128,4096]{1,0:T(8,128)(2,1)S(1)} %get-tuple-element.23), channel_id=1, source_target_pairs={{0,128},{128,0},{1,129},{129,1},{2,130},{130,2},{3,131},{131,3},{4... | collective-permute-start | bytes 3145736 | tf_op jit(solution)/shard_map/ppermute | solution.py:272
  386.3 8.3 %collective-permute-start.3 = (bf16[128,4096]{1,0:T(8,128)(2,1)}, bf16[128,4096]{1,0:T(8,128)(2,1)S(1)}, u32[]{:S(2)}, u32[]{:S(2)}) collective-permute-start(bf16[128,4096]{1,0:T(8,128)(2,1)} %get-tuple-element.24), channel_id=1, source_target_pairs={{0,128},{128,0},{1,129},{129,1},{2,130},{130,2},{3,131},{131,3},{4... | collective-permute-start | bytes 3145736 | tf_op jit(solution)/shard_map/ppermute | solution.py:272

commit v4 on v3

v4 whole, which is shorter than its diff:
```python
import functools

import jax
import jax.numpy as jnp
import numpy as np
from jax import lax
from jax.experimental import pallas as pl
from jax.experimental.pallas import tpu as pltpu
from jax.sharding import Mesh
from jax.sharding import PartitionSpec as P

MOST = 10
LANES = 128
BF = jnp.bfloat16
F32 = jnp.float32
SHARE = ("dp", "expert")
OWNERS = ("half", "expert")
INTERPRET = False
HIDDEN_STEPS = 3


def exchange(blocks, axes):
    return lax.all_to_all(blocks, axes, split_axis=0, concat_axis=0, tiled=True)


def mm(left, right, contract=((1,), (0,))):
    return lax.dot_general(left, right, (contract, ((), ())), preferred_element_type=F32)


def two_terms(values):
    high = values.astype(BF)
    return high, (values - high.astype(F32)).astype(BF)


def three_terms(values):
    high = values.astype(BF)
    return (high,) + two_terms(values - high.astype(F32))


def kernel_call(body, outs, args, scratch=(), **grid):
    return pl.pallas_call(
        body,
        out_shape=outs,
        scratch_shapes=scratch,
        compiler_params=pltpu.CompilerParams(vmem_limit_bytes=52 * 2**20),
        interpret=INTERPRET,
        **grid,
    )(*args)


def iota(shape, dimension):
    return lax.broadcasted_iota(jnp.int32, shape, dimension)


def spread(values, owner):
    pick = (iota((values[0].shape[1], owner.shape[1]), 0) == owner).astype(BF)
    total = mm(values[0], pick)
    for term in values[1:]:
        total = total + mm(term, pick)
    return total


def feature(replicas, width, c, j):
    part = width // (2 * replicas)
    block, inner = divmod(c * LANES, part)
    return (block * replicas + j) * part + inner


def picks_of(chunks, hits, chunk_of):
    rows = jnp.where(hits, 1.0, 0.0).T
    return jnp.concatenate(
        [jnp.where(chunk_of == c, rows, 0.0).astype(BF) for c in range(chunks)], axis=1
    )


def stacked(chunks, replicas, source, stack):
    tokens, width = source.shape
    for c in range(chunks):
        for j in range(replicas):
            at = feature(replicas, width, c, j)
            stack[c * tokens : (c + 1) * tokens, j * LANES : (j + 1) * LANES] = source[:, at : at + LANES]
    return stack[...]


def write_messages(experts, replicas, half, sent, message):
    for j in range(replicas):
        for e in range(experts):
            message[j * experts + e] = sent[e * half : (e + 1) * half, j * LANES : (j + 1) * LANES]


def slot_hits(place, owner, slot_of):
    return spread((place[...].astype(BF),), owner[...]) == slot_of[...].astype(F32)


def named_by(ids, shape):
    columns = iota(shape, 1)
    named = columns == ids[:, 0:1]
    for k in range(1, ids.shape[1]):
        named = named | (columns == ids[:, k : k + 1])
    return named


def send_kernel(experts, replicas, chunks, slots, x, ids, gain, owner, chunk_of, slot_of,
                message, normed, place, stack):
    tokens, width = x.shape
    xw = x[...].astype(F32)
    inv_rms = lax.rsqrt(jnp.mean(xw * xw, axis=1, keepdims=True) + 1e-06)
    normed[...] = (xw * inv_rms * gain[...]).astype(BF)
    named = named_by(ids, place.shape)
    earlier = (iota((tokens, tokens), 1) < iota((tokens, tokens), 0)).astype(BF)
    rank = mm(earlier, named.astype(BF))
    place[...] = jnp.where(named & (iota(place.shape, 1) < experts), rank, -1.0)
    pick = picks_of(chunks, slot_hits(place, owner, slot_of), chunk_of[...])
    sent = mm(pick, stacked(chunks, replicas, normed, stack)).astype(BF)
    write_messages(experts, replicas, chunks * slots, sent, message)


def send_grad_kernel(experts, replicas, chunks, slots, normed, ids, grad, table, place, owner, chunk_of, slot_of,
                     message, gates_out, stack):
    logits = mm(normed[...], table[...])
    powers = jnp.where(named_by(ids, logits.shape), jnp.exp(logits), 0.0)
    gates = powers / jnp.sum(powers, axis=1, keepdims=True)
    gates_out[...] = gates
    hits = slot_hits(place, owner, slot_of)
    weight = jnp.where(hits, spread(three_terms(gates), owner[...]), 0.0)
    slot_gate = jnp.sum(weight.T, axis=1, keepdims=True)
    pick = picks_of(chunks, hits, chunk_of[...])
    sent = (mm(pick, stacked(chunks, replicas, grad, stack)) * slot_gate).astype(BF)
    write_messages(experts, replicas, chunks * slots, sent, message)


def products_kernel(group, chunks, slots, contract, index, arrived, order, weight, weight_other, partial, rows_out):
    half = chunks * slots
    size = group * half
    block = group * slots
    own_chunks = chunks // 2
    part = own_chunks * LANES

    @pl.when(pl.program_id(0) == 0)
    def _():
        lower = index[0] == 0
        pick = (order[...] == iota((size, size), 1)).astype(BF)
        for pair in range(arrived.shape[0] // group // 2):
            lanes = [
                arrived[(2 * pair + w) * group : (2 * pair + w + 1) * group].reshape(size, LANES)
                for w in range(2)
            ]
            picked = mm(pick, jnp.concatenate(lanes, axis=1)).astype(BF)
            for c in range(own_chunks):
                low = picked[c * block : (c + 1) * block]
                high = picked[(own_chunks + c) * block : (own_chunks + c + 1) * block]
                own = jnp.where(lower, low, high)
                other = jnp.where(lower, high, low)
                for w in range(2):
                    rows = slice((2 * pair + w) * block, (2 * pair + w + 1) * block)
                    lanes = slice(w * LANES, (w + 1) * LANES)
                    rows_out[rows, c * LANES : (c + 1) * LANES] = own[:, lanes]
                    rows_out[rows, part + c * LANES : part + (c + 1) * LANES] = other[:, lanes]

    partial[...] = (
        mm(rows_out[:, :part], weight[...], contract) + mm(rows_out[:, part:], weight_other[...], contract)
    ).astype(BF)


def act_kernel(slots, arrived, pre_act, hidden, sender_of, slot_of, pre_grad, worth):
    replicas, rows, hidden_width = arrived.shape
    hidden_grad = arrived[0].astype(F32)
    for j in range(1, replicas):
        hidden_grad = hidden_grad + arrived[j].astype(F32)
    gate_pre = pre_act[:, :hidden_width].astype(F32)
    up = pre_act[:, hidden_width:].astype(F32)
    sigmoid = 1.0 / (1.0 + jnp.exp(-gate_pre))
    silu = gate_pre * sigmoid
    slope = sigmoid * (1.0 + gate_pre * (1.0 - sigmoid))
    pre_grad[:, :hidden_width] = (hidden_grad * up * slope).astype(BF)
    pre_grad[:, hidden_width:] = (hidden_grad * silu).astype(BF)
    each = jnp.sum(hidden_grad * hidden[...].astype(F32), axis=1, keepdims=True)
    laid = jnp.where(slot_of[...] == iota((rows, LANES), 1), each, 0.0)
    pick = (sender_of[...] == iota((worth.shape[0], rows), 0)).astype(BF)
    terms = three_terms(laid)
    worth[...] = mm(pick, terms[0]) + mm(pick, terms[1]) + mm(pick, terms[2])


def return_rows(group, chunks, slots, lower, order, own, other, message):
    block = group * slots
    half = chunks * slots
    size = group * half
    own_chunks = chunks // 2
    own, other = own.astype(BF), other.astype(BF)
    sides = jnp.where(lower, own, other), jnp.where(lower, other, own)
    pick = (order[...] == iota((size, size), 1)).astype(BF)

    def column(at):
        return jnp.concatenate(
            [
                side[at : at + block, c * LANES : (c + 1) * LANES]
                for side in sides
                for c in range(own_chunks)
            ],
            axis=0,
        )

    for pair in range(own.shape[0] // block // 2):
        lanes = [column((2 * pair + w) * block) for w in range(2)]
        picked = mm(pick, jnp.concatenate(lanes, axis=1)).astype(BF)
        for w in range(2):
            message[(2 * pair + w) * group : (2 * pair + w + 1) * group] = picked[
                :, w * LANES : (w + 1) * LANES
            ].reshape(group, half, LANES)


def out_kernel(group, chunks, slots, index, hidden, order, second, second_other, message):
    own = mm(hidden[...], second[...])
    other = mm(hidden[...], second_other[...])
    return_rows(group, chunks, slots, index[0] == 0, order, own, other, message)


def back_kernel(group, chunks, slots, index, pre_grad, order, first, first_other, rows, message, gain):
    own = mm(pre_grad[...], first[...], ((1,), (1,)))
    other = mm(pre_grad[...], first_other[...], ((1,), (1,)))
    return_rows(group, chunks, slots, index[0] == 0, order, own, other, message)

    @pl.when(pl.program_id(0) == 0)
    def _():
        gain[...] = jnp.zeros_like(gain)

    part = own.shape[1]
    gain[:, :part] += jnp.sum(own * rows[:, :part].astype(F32), axis=0, keepdims=True)
    gain[:, part:] += jnp.sum(other * rows[:, part:].astype(F32), axis=0, keepdims=True)


def join(experts, replicas, returned, joined):
    half = returned.shape[1]
    for j in range(replicas):
        block = returned[j * experts : (j + 1) * experts]
        joined[:, j * LANES : (j + 1) * LANES] = block.reshape(experts * half, LANES)
    return joined[...]


def to_tokens(chunks, values, chunk_of):
    return jnp.concatenate(
        [jnp.where(chunk_of == c, values, 0.0).astype(BF) for c in range(chunks)], axis=0
    )


def layer_kernel(experts, replicas, chunks, returned, x, gates, place, owner, chunk_of, slot_of, layer_out, joined):
    tokens, width = x.shape
    hits = slot_hits(place, owner, slot_of)
    source = join(experts, replicas, returned, joined)
    mixed = 0.0
    for term in two_terms(gates[...]):
        weight = jnp.where(hits, spread((term,), owner[...]), 0.0)
        mixed = mixed + mm(to_tokens(chunks, weight, chunk_of[...]), source)
    for c in range(chunks):
        for j in range(replicas):
            at = feature(replicas, width, c, j)
            at = slice(at, at + LANES)
            here = mixed[c * tokens : (c + 1) * tokens, j * LANES : (j + 1) * LANES]
            layer_out[:, at] = (x[:, at].astype(F32) + here).astype(BF)


def in_grad_kernel(experts, replicas, chunks, returned, x, grad, gain, table, place, logit_grad,
                   owner, chunk_of, slot_of, in_grad, joined, normed_grad):
    tokens, width = x.shape
    ones = jnp.where(slot_hits(place, owner, slot_of), 1.0, 0.0)
    back = mm(to_tokens(chunks, ones, chunk_of[...]), join(experts, replicas, returned, joined))
    high, low = two_terms(logit_grad[...])
    by_logits = mm(high, table[...], ((1,), (1,))) + mm(low, table[...], ((1,), (1,)))
    for c in range(chunks):
        for j in range(replicas):
            at = feature(replicas, width, c, j)
            at = slice(at, at + LANES)
            here = back[c * tokens : (c + 1) * tokens, j * LANES : (j + 1) * LANES]
            normed_grad[:, at] = here + by_logits[:, at]
    xw = x[...].astype(F32)
    inv_rms = lax.rsqrt(jnp.mean(xw * xw, axis=1, keepdims=True) + 1e-06)
    weighted = gain[...] * normed_grad[...]
    mean = jnp.mean(xw * weighted, axis=1, keepdims=True)
    in_grad[...] = (
        grad[...].astype(F32) + inv_rms * weighted - xw * (inv_rms * inv_rms * inv_rms * mean)
    ).astype(BF)


def after(value, *earlier):
    return lax.optimization_barrier((value,) + earlier)[0]


def swapped(block, axis):
    return lax.ppermute(block, axis, [(0, 1), (1, 0)])


def shards(section_input, routing, out_grad, norm_gain, router, w_in, w_out):
    experts = lax.axis_size("expert")
    replicas = lax.axis_size("dp")
    x = section_input[0]
    route_ids = routing[0]
    grad_top = out_grad[0]
    gain = norm_gain[0][None, :]
    table = router[0]
    first = w_in[0, 0]
    second = w_out[0, 0]
    tokens, width = x.shape
    part = first.shape[0]
    hidden_width = second.shape[0]
    slots = MOST
    rows = experts * slots
    router_width = table.shape[1]
    chunks = 2 * part // LANES
    half = chunks * slots
    peers = replicas * experts
    group = min(8, experts)
    message_shape = jax.ShapeDtypeStruct((peers, half, LANES), BF)
    side = lax.axis_index("half")
    index = side.astype(jnp.int32)[None]
    first_other = swapped(first, "half")
    second_other = swapped(second, "half")

    at = np.arange(experts * half, dtype=np.int32)
    owner, chunk_of, slot_of = (at // half)[None], at % half // slots, (at % slots)[None]
    sizes = (experts, replicas, chunks, slots)
    token_scratch = [pltpu.VMEM((chunks * tokens, replicas * LANES), BF)]
    message, normed, place = kernel_call(
        functools.partial(send_kernel, *sizes),
        (
            message_shape,
            jax.ShapeDtypeStruct((tokens, width), BF),
            jax.ShapeDtypeStruct((tokens, router_width), F32),
        ),
        (x, route_ids, gain, owner, chunk_of[:, None], slot_of),
        token_scratch,
    )
    arrived = exchange(message, SHARE)

    message, gates = kernel_call(
        functools.partial(send_grad_kernel, *sizes),
        (message_shape, jax.ShapeDtypeStruct((tokens, router_width), F32)),
        (normed, route_ids, grad_top, table, place, owner, chunk_of[:, None], slot_of),
        token_scratch,
    )
    message, arrived = lax.optimization_barrier((message, arrived))
    arrived_grad = exchange(message, SHARE)

    at = np.arange(group * half, dtype=np.int32)
    into_messages = (at % half // slots * group + at // half) * slots + at % slots
    into_rows = np.zeros_like(at)
    into_rows[into_messages] = at
    step_width = hidden_width // HIDDEN_STEPS
    all_rows = peers * slots
    whole = lambda shape: pl.BlockSpec(shape, lambda i: (0,) * len(shape))
    scalar = pl.BlockSpec(memory_space=pltpu.SMEM)

    def products(arrived, weights, contract, steps, weight_spec):
        return kernel_call(
            functools.partial(products_kernel, group, chunks, slots, contract),
            (
                jax.ShapeDtypeStruct((all_rows, steps * step_width), BF),
                jax.ShapeDtypeStruct((all_rows, 2 * part), BF),
            ),
            (index, arrived, into_rows[:, None]) + weights,
            grid=(steps,),
            in_specs=[scalar, whole(arrived.shape), whole((at.size, 1)), weight_spec, weight_spec],
            out_specs=[pl.BlockSpec((all_rows, step_width), lambda i: (0, i)), whole((all_rows, 2 * part))],
        )

    partial, expert_rows = products(
        arrived,
        (first, first_other),
        ((1,), (0,)),
        2 * HIDDEN_STEPS,
        pl.BlockSpec((part, step_width), lambda i: (0, i)),
    )
    pre_act = lax.psum_scatter(partial, "dp", scatter_dimension=0, tiled=True)
    gate_pre = pre_act[:, :hidden_width].astype(F32)
    up = pre_act[:, hidden_width:].astype(F32)
    hidden = (gate_pre / (1.0 + jnp.exp(-gate_pre)) * up).astype(BF)
    hidden_all = lax.all_gather(hidden, "dp", axis=0, tiled=True)

    partial, grad_rows = products(
        arrived_grad,
        (second, second_other),
        ((1,), (1,)),
        HIDDEN_STEPS,
        pl.BlockSpec((step_width, part), lambda i: (i, 0)),
    )
    summands = exchange(partial.reshape(replicas, rows, hidden_width), "dp")
    at = np.arange(rows, dtype=np.int32)
    pre_grad, worth = kernel_call(
        functools.partial(act_kernel, slots),
        (
            jax.ShapeDtypeStruct((rows, 2 * hidden_width), BF),
            jax.ShapeDtypeStruct((experts, LANES), F32),
        ),
        (summands, pre_act, hidden, at[None] // slots, at[:, None] % slots),
    )
    pre_grad_all = lax.all_gather(pre_grad, "dp", axis=0, tiled=True)

    worth = exchange(worth[:, None], "expert")[:, 0, :slots]
    slot_ids = jnp.arange(slots, dtype=F32)
    gate_worth = jnp.sum(
        jnp.where(place[:, :experts, None] == slot_ids, worth[None], 0.0), axis=2
    )
    inner = jnp.sum(gate_worth, axis=1, keepdims=True)
    logit_grad = jnp.pad(gate_worth, ((0, 0), (0, router_width - experts))) - gates * inner
    logit_high, logit_low = two_terms(logit_grad)
    local_router = mm(normed, logit_high, ((0,), (0,))) + mm(normed, logit_low, ((0,), (0,)))
    local_router = local_router.astype(BF).reshape(2, replicas, part, router_width).transpose(1, 0, 2, 3)
    router_part = lax.psum_scatter(
        local_router.reshape(-1, router_width), "dp", scatter_dimension=0, tiled=True
    ).astype(F32)

    steps = 2 if all_rows // 2 % (2 * group * slots) == 0 else 1

    def by_rows(width):
        return pl.BlockSpec((all_rows // steps, width), lambda i: (i, 0))

    messages = pl.BlockSpec((peers // steps, half, LANES), lambda i: (i, 0, 0))
    order = into_messages[:, None]
    message = kernel_call(
        functools.partial(out_kernel, group, chunks, slots),
        message_shape,
        (index, hidden_all, order, second, second_other),
        grid=(steps,),
        in_specs=[scalar, by_rows(hidden_width), whole(order.shape), whole(second.shape), whole(second.shape)],
        out_specs=messages,
    )
    returned = exchange(after(message, worth), SHARE)
    second_other_grad = mm(hidden_all, grad_rows[:, part:], ((0,), (0,)))
    second_own_grad = mm(hidden_all, grad_rows[:, :part], ((0,), (0,)))
    second_sent = swapped(second_other_grad.astype(BF), "half")
    second_grad = (second_own_grad + second_sent.astype(F32)).astype(BF)

    message, gain_part = kernel_call(
        functools.partial(back_kernel, group, chunks, slots),
        (message_shape, jax.ShapeDtypeStruct((1, 2 * part), F32)),
        (index, pre_grad_all, order, first, first_other, expert_rows),
        grid=(steps,),
        in_specs=[
            scalar,
            by_rows(2 * hidden_width),
            whole(order.shape),
            whole(first.shape),
            whole(first.shape),
            by_rows(2 * part),
        ],
        out_specs=[messages, whole((1, 2 * part))],
    )
    gain_part = gain_part.reshape(2, part)
    gain_part = jnp.where(side == 0, gain_part, gain_part[::-1])

    owners = 2 * experts
    piece = 2 * part // owners
    gain_rows = jnp.pad(gain_part.reshape(owners, 1, piece), ((0, 0), (0, 7), (0, LANES - piece)))
    owned = jnp.concatenate([router_part.reshape(owners, piece, router_width), gain_rows], axis=1)
    owned = jnp.sum(exchange(after(owned, returned), OWNERS), axis=0)
    router_own = owned[:piece]
    at = (side * replicas + lax.axis_index("dp")) * part + lax.axis_index("expert") * piece
    table_own = lax.dynamic_slice_in_dim(table, at, piece, axis=0).astype(F32)
    gain_here = lax.dynamic_slice_in_dim(gain[0], at, piece, axis=0)
    gain_sum = (owned[piece, :piece] + jnp.sum(router_own * table_own, axis=1)) / gain_here
    gain_terms = jnp.pad(jnp.stack(three_terms(gain_sum)), ((0, 13), (0, LANES - piece)))
    block = jnp.concatenate([router_own.astype(BF), gain_terms], axis=0)
    joined = exchange(jnp.broadcast_to(block[None], (owners,) + block.shape), OWNERS)
    returned_back = exchange(after(message, joined), SHARE)
    joined = lax.all_gather(joined.reshape(-1, LANES), "dp", axis=0, tiled=True)
    joined = joined.reshape(replicas, 2, experts, piece + 16, LANES).transpose(1, 0, 2, 3, 4)
    router_total = joined[:, :, :, :piece].reshape(width, router_width)
    gain_total = jnp.sum(joined[:, :, :, piece : piece + 3, :piece].astype(F32), axis=3).reshape(width)

    first_other_grad = mm(expert_rows[:, part:], pre_grad_all, ((0,), (0,)))
    first_own_grad = mm(expert_rows[:, :part], pre_grad_all, ((0,), (0,)))
    first_sent = swapped(first_other_grad.astype(BF), "half")
    first_grad = (first_own_grad + first_sent.astype(F32)).astype(BF)

    token_shape = jax.ShapeDtypeStruct((tokens, width), BF)
    joined_scratch = pltpu.VMEM((experts * half, replicas * LANES), BF)
    layer_out = kernel_call(
        functools.partial(layer_kernel, experts, replicas, chunks),
        token_shape,
        (returned, x, gates, place, owner, chunk_of[None], slot_of),
        [joined_scratch],
    )
    in_grad = kernel_call(
        functools.partial(in_grad_kernel, experts, replicas, chunks),
        token_shape,
        (returned_back, x, grad_top, gain, table, place, logit_grad, owner, chunk_of[None], slot_of),
        [joined_scratch, pltpu.VMEM((tokens, width), F32)],
    )
    handoff = swapped(layer_out, "section")
    handback = swapped(in_grad, "section")
    return (
        handoff[None],
        handback[None],
        first_grad[None, None],
        second_grad[None, None],
        router_total[None],
        gain_total[None],
    )


def solution(mesh):
    sizes = mesh.shape
    halves = (sizes["section"], sizes["expert"], 2, sizes["dp"] // 2)
    split = Mesh(mesh.devices.reshape(halves), ("section", "expert", "half", "dp"))
    blocks = ("half", "dp")
    tokens = ("expert",) + blocks
    return jax.shard_map(
        shards,
        mesh=split,
        in_specs=(
            P("section", tokens, None),
            P("section", tokens, None),
            P("section", tokens, None),
            P("section", None),
            P("section", None, None),
            P("section", "expert", blocks, None),
            P("section", "expert", None, blocks),
        ),
        out_specs=(
            P("section", tokens, None),
            P("section", tokens, None),
            P("section", "expert", blocks, None),
            P("section", "expert", None, blocks),
            P("section", None, None),
            P("section", None),
        ),
        check_vma=False,
    )
```

time: 398 us -> 397 us (level)
  blocking collectives: 120 us -> 37 us
  waiting for transfers between devices: 151 us -> 192 us
  starting transfers between devices: 48.5 us -> 66.7 us
  between operations: 0.82 us -> 14.1 us
  Pallas kernels: 43.5 us -> 49.3 us
    all_to_all x3 -> x1, blocking collectives: 120 us -> 19.3 us  [exchange(): return lax.all_to_all(blocks, axes, split_axis=0, concat_axis=0, tiled=True)]
    all_gather x0 -> x2, waiting for transfers between devices: none -> 32.2 us  [the longest x1 32.2 us: shards(): pre_grad_all = lax.all_gather(pre_grad, 'dp', axis=0, tiled=True)]
    all_to_all x6 -> x7, waiting for transfers between devices: 58.6 us -> 80.8 us  [exchange(): return lax.all_to_all(blocks, axes, split_axis=0, concat_axis=0, tiled=True)]
    all_to_all x6 -> x7, starting transfers between devices: 39.3 us -> 58 us  [exchange(): return lax.all_to_all(blocks, axes, split_axis=0, concat_axis=0, tiled=True)]
    all_gather x0 -> x1, blocking collectives: none -> 17.7 us  [shards(): hidden_all = lax.all_gather(hidden, 'dp', axis=0, tiled=True)]
    ppermute x6, waiting for transfers between devices: 92.7 us -> 77.7 us  [swapped(): return lax.ppermute(block, axis, [(0, 1), (1, 0)])]
    pallas_call x5 -> x9, Pallas kernels: 43.5 us -> 49.3 us  [kernel_call(): pl.pallas_call(body, out_shape=outs, scratch_shapes=scratch, compiler_par...]
    unnamed x33 -> x45, local copies, waits for them, and re-layouts: 5.95 us -> 10.7 us
  transfers between devices with their start and end apart: 12 -> 17, of which waited for: 7 -> 10; matrix products, arithmetic and copies ran while one was open for 3% -> 6% of each run, Pallas kernels for 5% -> 9%
where the time goes in v4:
time: 397 us; the launch traced here: 395 us
  waiting for transfers between devices  192 us (48%)
  starting transfers between devices  66.7 us (17%)
  Pallas kernels  49.3 us (12%)
  blocking collectives  37 us (9%)
  local copies, waits for them, and re-layouts  15.9 us (4%)
  between operations  14.1 us (4%)
  matrix products  14 us (4%)
  other arithmetic  6.06 us (2%)
    all_to_all x7, waiting for transfers between devices, exchange(): return lax.all_to_all(blocks, axes, split_axis=0, concat_axis=0, tiled=True)  80.8 us
    ppermute x6, waiting for transfers between devices, swapped(): return lax.ppermute(block, axis, [(0, 1), (1, 0)])  77.7 us
    all_to_all x7, starting transfers between devices, exchange(): return lax.all_to_all(blocks, axes, split_axis=0, concat_axis=0, tiled=True)  58 us
    pallas_call x9, Pallas kernels, kernel_call(): pl.pallas_call(body, out_shape=outs, scratch_shapes=scratch, compiler_par...  49.3 us
    all_gather x1, waiting for transfers between devices, shards(): pre_grad_all = lax.all_gather(pre_grad, 'dp', axis=0, tiled=True)  32.2 us
    all_to_all x1, blocking collectives, exchange(): return lax.all_to_all(blocks, axes, split_axis=0, concat_axis=0, tiled=True)  19.3 us
    all_gather x1, blocking collectives, shards(): hidden_all = lax.all_gather(hidden, 'dp', axis=0, tiled=True)  17.7 us
    dot_general x6, matrix products, mm(): lax.dot_general(left, right, (contract, ((), ())), preferred_element_type...  14 us
  transfers between devices with their start and end apart: 17, of which 10 were waited for; matrix products, arithmetic and copies ran while one was open for 6% of the time, Pallas kernels for 9%

profile of v4, /device:TPU:8, one launch (start us, length us, event | category | flops | bytes accessed | tf_op | source)
XLA Modules:
  0.0 394.9 jit_solution(7638020318573020668)
XLA Ops:
  11.1 4.9 %shard_map.217 = (bf16[64,80,128]{2,1,0:T(8,128)(2,1)}, bf16[128,4096]{1,0:T(8,128)(2,1)S(1)}, f32[128,128]{1,0:T(8,128)S(1)}) custom-call(bf16[128,4096]{1,0:T(8,128)(2,1)} %bitcast.52, s32[128,8]{1,0:T(8,128)S(1)} %bitcast.50, f32[1,4096]{1,0:T(1,128)S(1)} %copy-done.12, s32[1,1280]{1,0:T(1,128)S(1)} %copy-done.9, s32[1280,1]{1,0:T(8,128)S(1)} %copy-done.2, ...), custom_call_target="tpu_custom_call" | custom-call | tf_op jit(solution)/shard_map/pallas_call | solution.py:41
  16.1 13.2 %all-to-all-start = ((bf16[64,80,128]{2,1,0:T(8,128)(2,1)}), bf16[64,80,128]{2,1,0:T(8,128)(2,1)S(1)}, u32[]{:S(2)}, u32[]{:S(2)}) async-start(bf16[64,80,128]{2,1,0:T(8,128)(2,1)} %get-tuple-element.26), calls=%async_computation | async-start | bytes 2621440 | tf_op jit(solution)/shard_map/all_to_all | solution.py:23
  29.3 2.8 collective-permute-start
  32.1 5.8 %shard_map.218 = (bf16[64,80,128]{2,1,0:T(8,128)(2,1)}, f32[128,128]{1,0:T(8,128)S(1)}) custom-call(bf16[128,4096]{1,0:T(8,128)(2,1)S(1)} %get-tuple-element.23.normed, s32[128,8]{1,0:T(8,128)S(1)} %bitcast.51, bf16[128,4096]{1,0:T(8,128)(2,1)} %bitcast.60, bf16[4096,128]{1,0:T(8,128)(2,1)} %bitcast.58, f32[128,128]{1,0:T(8,128)S(1)} %get-tuple-element.24.place, ...), custom_call_target="tpu_custom_call" | custom-call | tf_op jit(solution)/shard_map/pallas_call | solution.py:41
  37.9 25.3 %all-to-all-done.arrived = bf16[64,80,128]{2,1,0:T(8,128)(2,1)S(1)} async-done(((bf16[64,80,128]{2,1,0:T(8,128)(2,1)}), bf16[64,80,128]{2,1,0:T(8,128)(2,1)S(1)}, u32[]{:S(2)}, u32[]{:S(2)}) %all-to-all-start) | async-done | bytes 1310752 | tf_op jit(solution)/shard_map/all_to_all | solution.py:23
  63.2 16.7 %collective-permute-done.weight_other.first_other = bf16[512,1536]{1,0:T(8,128)(2,1)} collective-permute-done((bf16[512,1536]{1,0:T(8,128)(2,1)}, bf16[512,1536]{1,0:T(8,128)(2,1)}, u32[]{:S(2)}, u32[]{:S(2)}) %collective-permute-start) | collective-permute-done | bytes 1572896 | tf_op jit(solution)/shard_map/ppermute | solution.py:289
  79.8 8.2 %shard_map.219 = (bf16[640,1536]{1,0:T(8,128)(2,1)}, bf16[640,1024]{1,0:T(8,128)(2,1)S(1)}) custom-call(s32[1]{0:T(128)} %bitcast.index, bf16[64,80,128]{2,1,0:T(8,128)(2,1)} %copy-done.16, s32[640,1]{1,0:T(8,128)S(1)} %copy-done, bf16[512,1536]{1,0:T(8,128)(2,1)} %bitcast.56, bf16[512,1536]{1,0:T(8,128)(2,1)} %collective-permute-done.weight_other.first_other), custom_call_target="tpu_custom_call" | custom-call | tf_op jit(solution)/shard_map/pallas_call | solution.py:41
  89.2 10.9 %all-to-all-start.2 = ((bf16[64,80,128]{2,1,0:T(8,128)(2,1)}), bf16[64,80,128]{2,1,0:T(8,128)(2,1)}, u32[]{:S(2)}, u32[]{:S(2)}) async-start(bf16[64,80,128]{2,1,0:T(8,128)(2,1)} %get-tuple-element.30), calls=%async_computation.3 | async-start | bytes 2621440 | tf_op jit(solution)/shard_map/all_to_all | solution.py:23
  102.2 30.6 %collective-permute-done.1.second_other.weight_other = bf16[768,512]{1,0:T(8,128)(2,1)S(1)} collective-permute-done((bf16[768,512]{1,0:T(8,128)(2,1)S(1)}, bf16[768,512]{1,0:T(8,128)(2,1)S(1)}, u32[]{:S(2)}, u32[]{:S(2)}) %collective-permute-start.1) | collective-permute-done | bytes 786464 | tf_op jit(solution)/shard_map/ppermute | solution.py:289
  133.2 5.2 %shard_map.222 = (bf16[640,768]{1,0:T(8,128)(2,1)}, bf16[640,1024]{1,0:T(8,128)(2,1)}) custom-call(s32[1]{0:T(128)} %bitcast.index, bf16[64,80,128]{2,1,0:T(8,128)(2,1)} %all-to-all-done.2.arrived, s32[640,1]{1,0:T(8,128)S(1)} %copy-done, bf16[768,512]{1,0:T(8,128)(2,1)S(1)} %bitcast.47, bf16[768,512]{1,0:T(8,128)(2,1)S(1)} %collective-permute-done.1.second_other.weight_other), custom_call_target="tpu_custom_call" | custom-call | tf_op jit(solution)/shard_map/pallas_call | solution.py:41
  138.4 5.5 %all-to-all-start.3 = ((bf16[4,160,768]{2,1,0:T(8,128)(2,1)}), bf16[4,160,768]{2,1,0:T(8,128)(2,1)}, u32[]{:S(2)}, u32[]{:S(2)}) async-start(bf16[4,160,768]{2,1,0:T(8,128)(2,1)} %bitcast.66), calls=%async_computation.4 | async-start | bytes 1966080 | tf_op jit(solution)/shard_map/all_to_all | solution.py:23
  145.1 10.6 %all-to-all-done.3.arrived = bf16[4,160,768]{2,1,0:T(8,128)(2,1)} async-done(((bf16[4,160,768]{2,1,0:T(8,128)(2,1)}), bf16[4,160,768]{2,1,0:T(8,128)(2,1)}, u32[]{:S(2)}, u32[]{:S(2)}) %all-to-all-start.3) | async-done | bytes 983072 | tf_op jit(solution)/shard_map/all_to_all | solution.py:23
  156.7 2.4 shard_map.223
  159.1 7.3 %all-to-all-start.4 = ((f32[16,1,128]{2,1,0:T(1,128)}), f32[16,1,128]{2,1,0:T(1,128)S(1)}, u32[]{:S(2)}, u32[]{:S(2)}) async-start(f32[16,1,128]{2,1,0:T(1,128)} %bitcast.10), calls=%async_computation.5 | async-start | bytes 16384 | tf_op jit(solution)/shard_map/all_to_all | solution.py:23
  166.6 8.3 %all-to-all-done.4 = f32[16,1,128]{2,1,0:T(1,128)S(1)} async-done(((f32[16,1,128]{2,1,0:T(1,128)}), f32[16,1,128]{2,1,0:T(1,128)S(1)}, u32[]{:S(2)}, u32[]{:S(2)}) %all-to-all-start.4) | async-done | bytes 8224 | tf_op jit(solution)/shard_map/all_to_all | solution.py:23
  178.0 17.7 %all_gather.9.hidden = bf16[640,768]{1,0:T(8,128)(2,1)} all-gather(bf16[160,768]{1,0:T(8,128)(2,1)S(1)} %fusion.11.hidden), channel_id=1, replica_groups=mesh['section'=2,'expert'=16,'half'=2,'dp'=4] {'dp'}, dimensions={0}, use_global_device_ids=true | all-gather | bytes 1228800 | tf_op jit(solution)/shard_map/all_gather | solution.py:376
  195.7 4.5 %shard_map.220 = bf16[64,80,128]{2,1,0:T(8,128)(2,1)} custom-call(s32[1]{0:T(128)} %bitcast.index, bf16[640,768]{1,0:T(8,128)(2,1)} %all_gather.9.hidden, s32[640,1]{1,0:T(8,128)S(1)} %copy-done, bf16[768,512]{1,0:T(8,128)(2,1)S(1)} %bitcast.48, bf16[768,512]{1,0:T(8,128)(2,1)S(1)} %collective-permute-done.1.second_other.weight_other), custom_call_target="tpu_custom_call" | custom-call | tf_op jit(solution)/shard_map/pallas_call | solution.py:41
  200.3 6.3 %all-to-all-start.1 = ((bf16[64,80,128]{2,1,0:T(8,128)(2,1)}), bf16[64,80,128]{2,1,0:T(8,128)(2,1)S(1)}, u32[]{:S(2)}, u32[]{:S(2)}) async-start(bf16[64,80,128]{2,1,0:T(8,128)(2,1)} %shard_map.220), calls=%async_computation.2 | async-start | bytes 2621440 | tf_op jit(solution)/shard_map/all_to_all | solution.py:23
  207.7 32.2 %all-gather.3.cloned.1.call-done.pre_grad = bf16[640,1536]{1,0:T(8,128)(2,1)} async-done(((bf16[160,1536]{1,0:T(8,128)(2,1)}), bf16[640,1536]{1,0:T(8,128)(2,1)}) %all-gather.3.cloned.1.call-update) | async-done | bytes 1966096 | tf_op jit(solution)/shard_map/all_gather | solution.py:395
  239.8 7.2 %shard_map.224 = (bf16[64,80,128]{2,1,0:T(8,128)(2,1)}, f32[1,1024]{1,0:T(1,128)S(1)}) custom-call(s32[1]{0:T(128)} %bitcast.index, bf16[640,1536]{1,0:T(8,128)(2,1)} %all-gather.3.cloned.1.call-done.pre_grad, s32[640,1]{1,0:T(8,128)S(1)} %copy-done, bf16[512,1536]{1,0:T(8,128)(2,1)} %bitcast.57, ...), custom_call_target="tpu_custom_call" | custom-call | tf_op jit(solution)/shard_map/pallas_call | solution.py:41
  249.3 7.5 %all-to-all-start.5 = ((f32[32,40,128]{2,1,0:T(8,128)}), f32[32,40,128]{2,1,0:T(8,128)S(1)}, u32[]{:S(2)}, u32[]{:S(2)}) async-start(f32[32,40,128]{2,1,0:T(8,128)} %select_maximum_fusion), calls=%async_computation.7 | async-start | bytes 1310720 | tf_op jit(solution)/shard_map/all_to_all | solution.py:23
  256.9 20.3 %all-to-all-done.5 = f32[32,40,128]{2,1,0:T(8,128)S(1)} async-done(((f32[32,40,128]{2,1,0:T(8,128)}), f32[32,40,128]{2,1,0:T(8,128)S(1)}, u32[]{:S(2)}, u32[]{:S(2)}) %all-to-all-start.5) | async-done | bytes 655392 | tf_op jit(solution)/shard_map/all_to_all | solution.py:23
  278.3 19.3 %all_to_all.40 = bf16[32,48,128]{2,1,0:T(8,128)(2,1)} all-to-all(bf16[32,48,128]{2,1,0:T(8,128)(2,1)S(1)} %broadcast_in_dim.47), channel_id=1, replica_groups=mesh['section'=2,'expert'=16,'half'=2,'dp'=4] {'half','expert'}, dimensions={0} | all-to-all | bytes 786432 | tf_op jit(solution)/shard_map/all_to_all | solution.py:23
  297.6 7.2 %all-to-all-start.7 = ((bf16[64,80,128]{2,1,0:T(8,128)(2,1)}), bf16[64,80,128]{2,1,0:T(8,128)(2,1)}, u32[]{:S(2)}, u32[]{:S(2)}) async-start(bf16[64,80,128]{2,1,0:T(8,128)(2,1)} %get-tuple-element.38), calls=%async_computation.9 | async-start | bytes 2621440 | tf_op jit(solution)/shard_map/all_to_all | solution.py:23
  305.4 4.3 %convolution_convert_fusion = bf16[512,1536]{1,0:T(8,128)(2,1)} fusion(bf16[640,1536]{1,0:T(8,128)(2,1)} %all-gather.3.cloned.1.call-done.pre_grad, bf16[640,1024]{1,0:T(8,128)(2,1)S(1)} %copy-done.6), kind=kOutput, calls=%fused_computation.3 | convolution fusion | flops 1007419392 | bytes 4194304 | tf_op jit(solution)/shard_map/dot_general | solution.py:27
  314.9 5.9 %shard_map.221 = bf16[128,4096]{1,0:T(8,128)(2,1)} custom-call(bf16[64,80,128]{2,1,0:T(8,128)(2,1)} %copy-done.17, bf16[128,4096]{1,0:T(8,128)(2,1)} %bitcast.53, f32[128,128]{1,0:T(8,128)S(1)} %get-tuple-element.29.gates, f32[128,128]{1,0:T(8,128)S(1)} %get-tuple-element.24.place, s32[1,1280]{1,0:T(1,128)S(1)} %copy-done.10, s32[1,1280]{1,0:T(1,128)S(1)} %copy-done.14, ...), custom_call_target="tpu_custom_call" | custom-call | tf_op jit(solution)/shard_map/pallas_call | solution.py:41
  320.8 16.0 %all-to-all-done.7.returned = bf16[64,80,128]{2,1,0:T(8,128)(2,1)} async-done(((bf16[64,80,128]{2,1,0:T(8,128)(2,1)}), bf16[64,80,128]{2,1,0:T(8,128)(2,1)}, u32[]{:S(2)}, u32[]{:S(2)}) %all-to-all-start.7) | async-done | bytes 1310752 | tf_op jit(solution)/shard_map/all_to_all | solution.py:23
  336.8 5.1 %shard_map.225 = bf16[128,4096]{1,0:T(8,128)(2,1)S(1)} custom-call(bf16[64,80,128]{2,1,0:T(8,128)(2,1)} %all-to-all-done.7.returned, bf16[128,4096]{1,0:T(8,128)(2,1)} %bitcast.54, bf16[128,4096]{1,0:T(8,128)(2,1)} %bitcast.61, f32[1,4096]{1,0:T(1,128)S(1)} %copy-done.13, bf16[4096,128]{1,0:T(8,128)(2,1)} %bitcast.59, ...), custom_call_target="tpu_custom_call" | custom-call | tf_op jit(solution)/shard_map/pallas_call | solution.py:41
  342.0 30.5 %collective-permute-done.5 = bf16[768,512]{1,0:T(8,128)(2,1)S(1)} collective-permute-done((bf16[768,512]{1,0:T(8,128)(2,1)}, bf16[768,512]{1,0:T(8,128)(2,1)S(1)}, u32[]{:S(2)}, u32[]{:S(2)}) %collective-permute-start.5) | collective-permute-done | bytes 786464 | tf_op jit(solution)/shard_map/ppermute | solution.py:289
  372.5 3.1 fusion.3
  375.5 4.0 %fusion.2 = bf16[1,1,512,1536]{3,2,1,0:T(8,128)(2,1)} fusion(bf16[512,1536]{1,0:T(8,128)(2,1)} %collective-permute-done.4, bf16[640,1536]{1,0:T(8,128)(2,1)S(1)} %copy-done.19, bf16[640,1024]{1,0:T(8,128)(2,1)S(1)} %copy-done.6), kind=kOutput, calls=%fused_computation.5 | convolution fusion | flops 1008992256 | bytes 5767168 | tf_op jit(solution)/shard_map/dot_general | solution.py:27
  383.8 2.3 copy.55
  (96 shorter events, 29.9 us)
Async XLA Ops:
  16.1 16.0 %copy-start.3 = (s32[1280,1]{1,0:T(8,128)S(1)}, s32[1280,1]{1,0:T(8,128)}, u32[]{:S(2)}) copy-start(s32[1280,1]{1,0:T(8,128)} %constant.48.clone.chunk_of) | copy-start | bytes 15364
  16.1 16.0 %copy-start.8 = (s32[1,1280]{1,0:T(1,128)S(1)}, s32[1,1280]{1,0:T(1,128)}, u32[]{:S(2)}) copy-start(s32[1,1280]{1,0:T(1,128)} %constant.49.clone.slot_of) | copy-start | bytes 15364
  16.1 16.0 %copy-start.10 = (s32[1,1280]{1,0:T(1,128)S(1)}, s32[1,1280]{1,0:T(1,128)}, u32[]{:S(2)}) copy-start(s32[1,1280]{1,0:T(1,128)} %constant.47.clone.owner) | copy-start | bytes 15364
  16.1 47.1 %all-to-all-start = ((bf16[64,80,128]{2,1,0:T(8,128)(2,1)}), bf16[64,80,128]{2,1,0:T(8,128)(2,1)S(1)}, u32[]{:S(2)}, u32[]{:S(2)}) async-start(bf16[64,80,128]{2,1,0:T(8,128)(2,1)} %get-tuple-element.26), calls=%async_computation | async-start | bytes 2621440 | tf_op jit(solution)/shard_map/all_to_all | solution.py:23
  29.3 114.6 %reduce-scatter.3.cloned.1.call-start = ((), (), s32[]{:S(2)}) async-start(), calls=%async_computation.10 | async-start | bytes 2457600 | tf_op jit(solution)/shard_map/reduce_scatter | solution.py:372
  29.3 50.5 %collective-permute-start = (bf16[512,1536]{1,0:T(8,128)(2,1)}, bf16[512,1536]{1,0:T(8,128)(2,1)}, u32[]{:S(2)}, u32[]{:S(2)}) collective-permute-start(bf16[512,1536]{1,0:T(8,128)(2,1)} %bitcast.55), channel_id=1, source_target_pairs={{0,4},{4,0},{1,5},{5,1},{2,6},{6,2},{3,7},{7,3},{8,12},{12,8},{9,1... | collective-permute-start | bytes 4718600 | tf_op jit(solution)/shard_map/ppermute | solution.py:289
  32.1 47.7 %copy-start = (s32[640,1]{1,0:T(8,128)S(1)}, s32[640,1]{1,0:T(8,128)}, u32[]{:S(2)}) copy-start(s32[640,1]{1,0:T(8,128)} %constant.50.clone.order) | copy-start | bytes 7684
  63.2 16.7 %copy-start.16 = (bf16[64,80,128]{2,1,0:T(8,128)(2,1)}, bf16[64,80,128]{2,1,0:T(8,128)(2,1)S(1)}, u32[]{:S(2)}) copy-start(bf16[64,80,128]{2,1,0:T(8,128)(2,1)S(1)} %all-to-all-done.arrived) | copy-start | bytes 3932164
  89.1 11.0 %copy-start.1 = (bf16[1,1,768,512]{3,2,1,0:T(8,128)(2,1)S(1)}, bf16[1,1,768,512]{3,2,1,0:T(8,128)(2,1)}, u32[]{:S(2)}) copy-start(bf16[1,1,768,512]{3,2,1,0:T(8,128)(2,1)} %param.24) | copy-start | bytes 2359300
  89.2 44.0 %all-to-all-start.2 = ((bf16[64,80,128]{2,1,0:T(8,128)(2,1)}), bf16[64,80,128]{2,1,0:T(8,128)(2,1)}, u32[]{:S(2)}, u32[]{:S(2)}) async-start(bf16[64,80,128]{2,1,0:T(8,128)(2,1)} %get-tuple-element.30), calls=%async_computation.3 | async-start | bytes 2621440 | tf_op jit(solution)/shard_map/all_to_all | solution.py:23
  100.1 32.7 %collective-permute-start.1 = (bf16[768,512]{1,0:T(8,128)(2,1)S(1)}, bf16[768,512]{1,0:T(8,128)(2,1)S(1)}, u32[]{:S(2)}, u32[]{:S(2)}) collective-permute-start(bf16[768,512]{1,0:T(8,128)(2,1)S(1)} %bitcast.46), channel_id=1, source_target_pairs={{0,4},{4,0},{1,5},{5,1},{2,6},{6,2},{3,7},{7,3},{8,12},{12,8},{9,1... | collective-permute-start | bytes 2359304 | tf_op jit(solution)/shard_map/ppermute | solution.py:289
  138.4 17.3 %copy-start.11 = (s32[160,1]{1,0:T(8,128)S(1)}, s32[160,1]{1,0:T(8,128)}, u32[]{:S(2)}) copy-start(s32[160,1]{1,0:T(8,128)} %constant.52.clone.slot_of) | copy-start | bytes 1924
  138.4 17.3 %copy-start.15 = (s32[1,160]{1,0:T(1,128)S(1)}, s32[1,160]{1,0:T(1,128)}, u32[]{:S(2)}) copy-start(s32[1,160]{1,0:T(1,128)} %constant.51.clone.sender_of) | copy-start | bytes 1924
  138.4 17.3 %all-to-all-start.3 = ((bf16[4,160,768]{2,1,0:T(8,128)(2,1)}), bf16[4,160,768]{2,1,0:T(8,128)(2,1)}, u32[]{:S(2)}, u32[]{:S(2)}) async-start(bf16[4,160,768]{2,1,0:T(8,128)(2,1)} %bitcast.66), calls=%async_computation.4 | async-start | bytes 1966080 | tf_op jit(solution)/shard_map/all_to_all | solution.py:23
  159.1 15.7 %all-to-all-start.4 = ((f32[16,1,128]{2,1,0:T(1,128)}), f32[16,1,128]{2,1,0:T(1,128)S(1)}, u32[]{:S(2)}, u32[]{:S(2)}) async-start(f32[16,1,128]{2,1,0:T(1,128)} %bitcast.10), calls=%async_computation.5 | async-start | bytes 16384 | tf_op jit(solution)/shard_map/all_to_all | solution.py:23
  166.5 40.2 %reduce-scatter.5.cloned.1.call-start = ((), (), s32[]{:S(2)}) async-start(), calls=%async_computation.12 | async-start | bytes 1310720 | tf_op jit(solution)/shard_map/reduce_scatter | solution.py:407
  177.3 62.5 %all-gather.3.cloned.1.call-start = ((), (), s32[]{:S(2)}) async-start(), calls=%async_computation.11 | async-start | bytes 2457600 | tf_op jit(solution)/shard_map/all_gather | solution.py:395
  200.3 49.0 %all-to-all-start.1 = ((bf16[64,80,128]{2,1,0:T(8,128)(2,1)}), bf16[64,80,128]{2,1,0:T(8,128)(2,1)S(1)}, u32[]{:S(2)}, u32[]{:S(2)}) async-start(bf16[64,80,128]{2,1,0:T(8,128)(2,1)} %shard_map.220), calls=%async_computation.2 | async-start | bytes 2621440 | tf_op jit(solution)/shard_map/all_to_all | solution.py:23
  248.5 29.7 %copy-start.13 = (f32[1,4096]{1,0:T(1,128)S(1)}, f32[1,4096]{1,0:T(1,128)}, u32[]{:S(2)}) copy-start(f32[1,4096]{1,0:T(1,128)} %gain.3) | copy-start | bytes 49156
  249.3 29.0 %copy-start.17 = (bf16[64,80,128]{2,1,0:T(8,128)(2,1)}, bf16[64,80,128]{2,1,0:T(8,128)(2,1)S(1)}, u32[]{:S(2)}) copy-start(bf16[64,80,128]{2,1,0:T(8,128)(2,1)S(1)} %all-to-all-done.1.returned) | copy-start | bytes 3932164
  249.3 27.9 %all-to-all-start.5 = ((f32[32,40,128]{2,1,0:T(8,128)}), f32[32,40,128]{2,1,0:T(8,128)S(1)}, u32[]{:S(2)}, u32[]{:S(2)}) async-start(f32[32,40,128]{2,1,0:T(8,128)} %select_maximum_fusion), calls=%async_computation.7 | async-start | bytes 1310720 | tf_op jit(solution)/shard_map/all_to_all | solution.py:23
  297.6 7.8 %copy-start.6 = (bf16[640,1024]{1,0:T(8,128)(2,1)S(1)}, bf16[640,1024]{1,0:T(8,128)(2,1)}, u32[]{:S(2)}) copy-start(bf16[640,1024]{1,0:T(8,128)(2,1)} %copy-done.5) | copy-start | bytes 3932164
  297.6 39.2 %all-to-all-start.7 = ((bf16[64,80,128]{2,1,0:T(8,128)(2,1)}), bf16[64,80,128]{2,1,0:T(8,128)(2,1)}, u32[]{:S(2)}, u32[]{:S(2)}) async-start(bf16[64,80,128]{2,1,0:T(8,128)(2,1)} %get-tuple-element.38), calls=%async_computation.9 | async-start | bytes 2621440 | tf_op jit(solution)/shard_map/all_to_all | solution.py:23
  304.8 74.7 %all-gather.5.cloned.1.call-start = ((), (), s32[]{:S(2)}) async-start(), calls=%async_computation.13 | async-start | bytes 1966080 | tf_op jit(solution)/shard_map/all_gather | solution.py:464
  305.4 6.2 %copy-start.18 = (bf16[640,768]{1,0:T(8,128)(2,1)S(1)}, bf16[640,768]{1,0:T(8,128)(2,1)}, u32[]{:S(2)}) copy-start(bf16[640,768]{1,0:T(8,128)(2,1)} %all_gather.9.hidden) | copy-start | bytes 2949124
  305.4 6.2 %copy-start.20 = (bf16[640,1024]{1,0:T(8,128)(2,1)S(1)}, bf16[640,1024]{1,0:T(8,128)(2,1)}, u32[]{:S(2)}) copy-start(bf16[640,1024]{1,0:T(8,128)(2,1)} %get-tuple-element.39) | copy-start | bytes 3932164
  309.7 65.9 %collective-permute-start.4 = (bf16[512,1536]{1,0:T(8,128)(2,1)}, bf16[512,1536]{1,0:T(8,128)(2,1)}, u32[]{:S(2)}, u32[]{:S(2)}) collective-permute-start(bf16[512,1536]{1,0:T(8,128)(2,1)} %convolution_convert_fusion), channel_id=1, source_target_pairs={{0,4},{4,0},{1,5},{5,1},{2,6},{6,2},{3,7},{7,3},{8,12},{12,8},{9,1... | collective-permute-start | bytes 4718600 | tf_op jit(solution)/shard_map/ppermute | solution.py:289
  311.6 3.3 copy-start.14
  313.3 59.1 %collective-permute-start.5 = (bf16[768,512]{1,0:T(8,128)(2,1)}, bf16[768,512]{1,0:T(8,128)(2,1)S(1)}, u32[]{:S(2)}, u32[]{:S(2)}) collective-permute-start(bf16[768,512]{1,0:T(8,128)(2,1)} %convolution_convert_fusion.1), channel_id=1, source_target_pairs={{0,4},{4,0},{1,5},{5,1},{2,6},{6,2},{3,7},{7,3},{8,12},{12,8},{9,1... | collective-permute-start | bytes 2359304 | tf_op jit(solution)/shard_map/ppermute | solution.py:289
  320.8 54.8 %collective-permute-start.2 = (bf16[128,4096]{1,0:T(8,128)(2,1)}, bf16[128,4096]{1,0:T(8,128)(2,1)}, u32[]{:S(2)}, u32[]{:S(2)}) collective-permute-start(bf16[128,4096]{1,0:T(8,128)(2,1)} %shard_map.221), channel_id=1, source_target_pairs={{0,128},{128,0},{1,129},{129,1},{2,130},{130,2},{3,131},{131,3},{4... | collective-permute-start | bytes 3145736 | tf_op jit(solution)/shard_map/ppermute | solution.py:289
  341.9 33.7 %copy-start.19 = (bf16[640,1536]{1,0:T(8,128)(2,1)S(1)}, bf16[640,1536]{1,0:T(8,128)(2,1)}, u32[]{:S(2)}) copy-start(bf16[640,1536]{1,0:T(8,128)(2,1)} %all-gather.3.cloned.1.call-done.pre_grad) | copy-start | bytes 5898244
  341.9 41.9 %collective-permute-start.3 = (bf16[128,4096]{1,0:T(8,128)(2,1)S(1)}, bf16[128,4096]{1,0:T(8,128)(2,1)}, u32[]{:S(2)}, u32[]{:S(2)}) collective-permute-start(bf16[128,4096]{1,0:T(8,128)(2,1)S(1)} %shard_map.225), channel_id=1, source_target_pairs={{0,128},{128,0},{1,129},{129,1},{2,130},{130,2},{3,131},{131,3},{4... | collective-permute-start | bytes 3145736 | tf_op jit(solution)/shard_map/ppermute | solution.py:289
  (6 other events, 5.3 us)
Sparse Core Ops, SparseCore 0:
  89.3 42.5 reduce-scatter.2
  177.4 21.3 reduce-scatter.4
  201.4 38.3 all-gather.2
  307.3 34.5 all-gather.4

commit v5 on v4

--- a/solution.py
+++ b/solution.py
@@ -129,7 +129,8 @@
     write_messages(experts, replicas, chunks * slots, sent, message)
 
 
-def products_kernel(group, chunks, slots, contract, index, arrived, order, weight, weight_other, partial, rows_out):
+def products_kernel(group, chunks, slots, side, index, arrived, order, *refs):
+    weights, partial, rows_out = refs[:-2], refs[-2], refs[-1]
     half = chunks * slots
     size = group * half
     block = group * slots
@@ -157,9 +158,12 @@
                     rows_out[rows, c * LANES : (c + 1) * LANES] = own[:, lanes]
                     rows_out[rows, part + c * LANES : part + (c + 1) * LANES] = other[:, lanes]
 
-    partial[...] = (
-        mm(rows_out[:, :part], weight[...], contract) + mm(rows_out[:, part:], weight_other[...], contract)
-    ).astype(BF)
+    total, at = 0.0, 0
+    for weight in weights:
+        end = at + weight.shape[side]
+        total = total + mm(rows_out[:, at:end], weight[...], ((1,), (side,)))
+        at = end
+    partial[...] = total.astype(BF)
 
 
 def act_kernel(slots, arrived, pre_act, hidden, sender_of, slot_of, pre_grad, worth):
@@ -181,7 +185,7 @@
     worth[...] = mm(pick, terms[0]) + mm(pick, terms[1]) + mm(pick, terms[2])
 
 
-def return_rows(group, chunks, slots, lower, order, own, other, message):
+def return_rows(group, chunks, slots, lower, order, own, other, message, first_row=0):
     block = group * slots
     half = chunks * slots
     size = group * half
@@ -204,9 +208,10 @@
         lanes = [column((2 * pair + w) * block) for w in range(2)]
         picked = mm(pick, jnp.concatenate(lanes, axis=1)).astype(BF)
         for w in range(2):
-            message[(2 * pair + w) * group : (2 * pair + w + 1) * group] = picked[
-                :, w * LANES : (w + 1) * LANES
-            ].reshape(group, half, LANES)
+            to = slice((2 * pair + w) * group, (2 * pair + w + 1) * group)
+            message[to, first_row : first_row + half] = picked[:, w * LANES : (w + 1) * LANES].reshape(
+                group, half, LANES
+            )
 
 
 def out_kernel(group, chunks, slots, index, hidden, order, second, second_other, message):
@@ -215,10 +220,15 @@
     return_rows(group, chunks, slots, index[0] == 0, order, own, other, message)
 
 
-def back_kernel(group, chunks, slots, index, pre_grad, order, first, first_other, rows, message, gain):
+def back_kernel(group, chunks, slots, index, pre_grad, order, first, first_early, first_late, rows, outs,
+                message, gain):
     own = mm(pre_grad[...], first[...], ((1,), (1,)))
-    other = mm(pre_grad[...], first_other[...], ((1,), (1,)))
-    return_rows(group, chunks, slots, index[0] == 0, order, own, other, message)
+    other = jnp.concatenate(
+        [mm(pre_grad[...], weight[...], ((1,), (1,))) for weight in (first_early, first_late)], axis=1
+    )
+    half = chunks * slots
+    message[:, :half] = outs[...]
+    return_rows(group, chunks, slots, index[0] == 0, order, own, other, message, half)
 
     @pl.when(pl.program_id(0) == 0)
     def _():
@@ -229,10 +239,10 @@
     gain[:, part:] += jnp.sum(other * rows[:, part:].astype(F32), axis=0, keepdims=True)
 
 
-def join(experts, replicas, returned, joined):
-    half = returned.shape[1]
+def join(experts, replicas, kind, returned, joined):
+    half = returned.shape[1] // 2
     for j in range(replicas):
-        block = returned[j * experts : (j + 1) * experts]
+        block = returned[j * experts : (j + 1) * experts, kind * half : (kind + 1) * half]
         joined[:, j * LANES : (j + 1) * LANES] = block.reshape(experts * half, LANES)
     return joined[...]
 
@@ -246,7 +256,7 @@
 def layer_kernel(experts, replicas, chunks, returned, x, gates, place, owner, chunk_of, slot_of, layer_out, joined):
     tokens, width = x.shape
     hits = slot_hits(place, owner, slot_of)
-    source = join(experts, replicas, returned, joined)
+    source = join(experts, replicas, 0, returned, joined)
     mixed = 0.0
     for term in two_terms(gates[...]):
         weight = jnp.where(hits, spread((term,), owner[...]), 0.0)
@@ -263,7 +273,7 @@
                    owner, chunk_of, slot_of, in_grad, joined, normed_grad):
     tokens, width = x.shape
     ones = jnp.where(slot_hits(place, owner, slot_of), 1.0, 0.0)
-    back = mm(to_tokens(chunks, ones, chunk_of[...]), join(experts, replicas, returned, joined))
+    back = mm(to_tokens(chunks, ones, chunk_of[...]), join(experts, replicas, 1, returned, joined))
     high, low = two_terms(logit_grad[...])
     by_logits = mm(high, table[...], ((1,), (1,))) + mm(low, table[...], ((1,), (1,)))
     for c in range(chunks):
@@ -312,7 +322,9 @@
     message_shape = jax.ShapeDtypeStruct((peers, half, LANES), BF)
     side = lax.axis_index("half")
     index = side.astype(jnp.int32)[None]
-    first_other = swapped(first, "half")
+    early = part // 4
+    first_early = swapped(first[:early], "half")
+    first_late = swapped(first[early:], "half")
     second_other = swapped(second, "half")
 
     at = np.arange(experts * half, dtype=np.int32)
@@ -329,7 +341,7 @@
         (x, route_ids, gain, owner, chunk_of[:, None], slot_of),
         token_scratch,
     )
-    arrived = exchange(message, SHARE)
+    arrived = exchange(after(message, first_early), SHARE)
 
     message, gates = kernel_call(
         functools.partial(send_grad_kernel, *sizes),
@@ -349,40 +361,40 @@
     whole = lambda shape: pl.BlockSpec(shape, lambda i: (0,) * len(shape))
     scalar = pl.BlockSpec(memory_space=pltpu.SMEM)
 
-    def products(arrived, weights, contract, steps, weight_spec):
+    def products(arrived, weights, side, steps, weight_specs):
         return kernel_call(
-            functools.partial(products_kernel, group, chunks, slots, contract),
+            functools.partial(products_kernel, group, chunks, slots, side),
             (
                 jax.ShapeDtypeStruct((all_rows, steps * step_width), BF),
                 jax.ShapeDtypeStruct((all_rows, 2 * part), BF),
             ),
             (index, arrived, into_rows[:, None]) + weights,
             grid=(steps,),
-            in_specs=[scalar, whole(arrived.shape), whole((at.size, 1)), weight_spec, weight_spec],
+            in_specs=[scalar, whole(arrived.shape), whole((at.size, 1))] + weight_specs,
             out_specs=[pl.BlockSpec((all_rows, step_width), lambda i: (0, i)), whole((all_rows, 2 * part))],
         )
 
     partial, expert_rows = products(
         arrived,
-        (first, first_other),
-        ((1,), (0,)),
+        (first, first_early, first_late),
+        0,
         2 * HIDDEN_STEPS,
-        pl.BlockSpec((part, step_width), lambda i: (0, i)),
+        [pl.BlockSpec((size, step_width), lambda i: (0, i)) for size in (part, early, part - early)],
     )
     pre_act = lax.psum_scatter(partial, "dp", scatter_dimension=0, tiled=True)
+    partial, grad_rows = products(
+        arrived_grad,
+        (second, second_other),
+        1,
+        HIDDEN_STEPS,
+        [pl.BlockSpec((step_width, part), lambda i: (i, 0))] * 2,
+    )
+    partial, pre_act = lax.optimization_barrier((partial, pre_act))
+    summands = exchange(partial.reshape(replicas, rows, hidden_width), "dp")
     gate_pre = pre_act[:, :hidden_width].astype(F32)
     up = pre_act[:, hidden_width:].astype(F32)
     hidden = (gate_pre / (1.0 + jnp.exp(-gate_pre)) * up).astype(BF)
     hidden_all = lax.all_gather(hidden, "dp", axis=0, tiled=True)
-
-    partial, grad_rows = products(
-        arrived_grad,
-        (second, second_other),
-        ((1,), (1,)),
-        HIDDEN_STEPS,
-        pl.BlockSpec((step_width, part), lambda i: (i, 0)),
-    )
-    summands = exchange(partial.reshape(replicas, rows, hidden_width), "dp")
     at = np.arange(rows, dtype=np.int32)
     pre_grad, worth = kernel_call(
         functools.partial(act_kernel, slots),
@@ -390,7 +402,7 @@
             jax.ShapeDtypeStruct((rows, 2 * hidden_width), BF),
             jax.ShapeDtypeStruct((experts, LANES), F32),
         ),
-        (summands, pre_act, hidden, at[None] // slots, at[:, None] % slots),
+        (summands, pre_act, after(hidden, hidden_all), at[None] // slots, at[:, None] % slots),
     )
     pre_grad_all = lax.all_gather(pre_grad, "dp", axis=0, tiled=True)
 
@@ -404,9 +416,11 @@
     logit_high, logit_low = two_terms(logit_grad)
     local_router = mm(normed, logit_high, ((0,), (0,))) + mm(normed, logit_low, ((0,), (0,)))
     local_router = local_router.astype(BF).reshape(2, replicas, part, router_width).transpose(1, 0, 2, 3)
-    router_part = lax.psum_scatter(
-        local_router.reshape(-1, router_width), "dp", scatter_dimension=0, tiled=True
-    ).astype(F32)
+    second_other_grad = mm(hidden_all, grad_rows[:, part:], ((0,), (0,))).astype(BF)
+    second_sent = swapped(second_other_grad, "half")
+    local_router = after(local_router, second_other_grad)
+    router_part = exchange(local_router.reshape(replicas, 2 * part, router_width), "dp")
+    router_part = jnp.sum(router_part.astype(F32), axis=0)
 
     steps = 2 if all_rows // 2 % (2 * group * slots) == 0 else 1
 
@@ -415,7 +429,7 @@
 
     messages = pl.BlockSpec((peers // steps, half, LANES), lambda i: (i, 0, 0))
     order = into_messages[:, None]
-    message = kernel_call(
+    out_message = kernel_call(
         functools.partial(out_kernel, group, chunks, slots),
         message_shape,
         (index, hidden_all, order, second, second_other),
@@ -423,26 +437,25 @@
         in_specs=[scalar, by_rows(hidden_width), whole(order.shape), whole(second.shape), whole(second.shape)],
         out_specs=messages,
     )
-    returned = exchange(after(message, worth), SHARE)
-    second_other_grad = mm(hidden_all, grad_rows[:, part:], ((0,), (0,)))
-    second_own_grad = mm(hidden_all, grad_rows[:, :part], ((0,), (0,)))
-    second_sent = swapped(second_other_grad.astype(BF), "half")
-    second_grad = (second_own_grad + second_sent.astype(F32)).astype(BF)
-
     message, gain_part = kernel_call(
         functools.partial(back_kernel, group, chunks, slots),
-        (message_shape, jax.ShapeDtypeStruct((1, 2 * part), F32)),
-        (index, pre_grad_all, order, first, first_other, expert_rows),
+        (jax.ShapeDtypeStruct((peers, 2 * half, LANES), BF), jax.ShapeDtypeStruct((1, 2 * part), F32)),
+        (index, pre_grad_all, order, first, first_early, first_late, expert_rows, after(out_message, second_sent)),
         grid=(steps,),
         in_specs=[
             scalar,
             by_rows(2 * hidden_width),
             whole(order.shape),
             whole(first.shape),
-            whole(first.shape),
+            whole(first_early.shape),
+            whole(first_late.shape),
             by_rows(2 * part),
+            messages,
         ],
-        out_specs=[messages, whole((1, 2 * part))],
+        out_specs=[
+            pl.BlockSpec((peers // steps, 2 * half, LANES), lambda i: (i, 0, 0)),
+            whole((1, 2 * part)),
+        ],
     )
     gain_part = gain_part.reshape(2, part)
     gain_part = jnp.where(side == 0, gain_part, gain_part[::-1])
@@ -451,7 +464,11 @@
     piece = 2 * part // owners
     gain_rows = jnp.pad(gain_part.reshape(owners, 1, piece), ((0, 0), (0, 7), (0, LANES - piece)))
     owned = jnp.concatenate([router_part.reshape(owners, piece, router_width), gain_rows], axis=1)
-    owned = jnp.sum(exchange(after(owned, returned), OWNERS), axis=0)
+    owned = jnp.sum(exchange(owned, OWNERS), axis=0)
+    first_other_grad = mm(expert_rows[:, part:], pre_grad_all, ((0,), (0,))).astype(BF)
+    first_sent = swapped(first_other_grad, "half")
+    message, owned = lax.optimization_barrier((message, owned, first_other_grad))[:2]
+    returned = exchange(message, SHARE)
     router_own = owned[:piece]
     at = (side * replicas + lax.axis_index("dp")) * part + lax.axis_index("expert") * piece
     table_own = lax.dynamic_slice_in_dim(table, at, piece, axis=0).astype(F32)
@@ -459,16 +476,17 @@
     gain_sum = (owned[piece, :piece] + jnp.sum(router_own * table_own, axis=1)) / gain_here
     gain_terms = jnp.pad(jnp.stack(three_terms(gain_sum)), ((0, 13), (0, LANES - piece)))
     block = jnp.concatenate([router_own.astype(BF), gain_terms], axis=0)
-    joined = exchange(jnp.broadcast_to(block[None], (owners,) + block.shape), OWNERS)
-    returned_back = exchange(after(message, joined), SHARE)
+    block_other = swapped(block, "half")
+    joined = jnp.where(side == 0, jnp.stack([block, block_other]), jnp.stack([block_other, block]))
+    joined = lax.all_gather(joined, "expert", axis=0)
     joined = lax.all_gather(joined.reshape(-1, LANES), "dp", axis=0, tiled=True)
-    joined = joined.reshape(replicas, 2, experts, piece + 16, LANES).transpose(1, 0, 2, 3, 4)
+    joined = joined.reshape(replicas, experts, 2, piece + 16, LANES).transpose(2, 0, 1, 3, 4)
     router_total = joined[:, :, :, :piece].reshape(width, router_width)
     gain_total = jnp.sum(joined[:, :, :, piece : piece + 3, :piece].astype(F32), axis=3).reshape(width)
 
-    first_other_grad = mm(expert_rows[:, part:], pre_grad_all, ((0,), (0,)))
+    second_own_grad = mm(hidden_all, grad_rows[:, :part], ((0,), (0,)))
+    second_grad = (second_own_grad + second_sent.astype(F32)).astype(BF)
     first_own_grad = mm(expert_rows[:, :part], pre_grad_all, ((0,), (0,)))
-    first_sent = swapped(first_other_grad.astype(BF), "half")
     first_grad = (first_own_grad + first_sent.astype(F32)).astype(BF)
 
     token_shape = jax.ShapeDtypeStruct((tokens, width), BF)
@@ -476,13 +494,13 @@
     layer_out = kernel_call(
         functools.partial(layer_kernel, experts, replicas, chunks),
         token_shape,
-        (returned, x, gates, place, owner, chunk_of[None], slot_of),
+        (returned, after(x, first_grad, second_grad), gates, place, owner, chunk_of[None], slot_of),
         [joined_scratch],
     )
     in_grad = kernel_call(
         functools.partial(in_grad_kernel, experts, replicas, chunks),
         token_shape,
-        (returned_back, x, grad_top, gain, table, place, logit_grad, owner, chunk_of[None], slot_of),
+        (returned, x, grad_top, gain, table, place, logit_grad, owner, chunk_of[None], slot_of),
         [joined_scratch, pltpu.VMEM((tokens, width), F32)],
     )
     handoff = swapped(layer_out, "section")

time: 397 us -> 398 us (level)
  waiting for transfers between devices: 192 us -> 151 us
  blocking collectives: 37 us -> 59 us
  local copies, waits for them, and re-layouts: 15.9 us -> 24 us
  starting transfers between devices: 66.7 us -> 73.3 us
    all_gather x0 -> x1, blocking collectives: none -> 37.3 us  [shards(): joined = lax.all_gather(joined, 'expert', axis=0)]
    all_gather x1, waiting for transfers between devices: 32.2 us -> 0.02 us  [shards(): pre_grad_all = lax.all_gather(pre_grad, 'dp', axis=0, tiled=True)]
    all_to_all x7, waiting for transfers between devices: 80.8 us -> 49.9 us  [exchange(): return lax.all_to_all(blocks, axes, split_axis=0, concat_axis=0, tiled=True)]
    all_to_all x1 -> x0, blocking collectives: 19.3 us -> none  [exchange(): return lax.all_to_all(blocks, axes, split_axis=0, concat_axis=0, tiled=True)]
    ppermute x6 -> x8, waiting for transfers between devices: 77.7 us -> 95.8 us  [swapped(): return lax.ppermute(block, axis, [(0, 1), (1, 0)])]
    ppermute x6 -> x8, starting transfers between devices: 8.54 us -> 14.5 us  [swapped(): return lax.ppermute(block, axis, [(0, 1), (1, 0)])]
    all_gather x1, waiting for transfers between devices: 0.01 us -> 5.04 us  [shards(): joined = lax.all_gather(joined.reshape(-1, LANES), 'dp', axis=0, tiled=True)]
    all_gather x1, blocking collectives: 17.7 us -> 21.7 us  [shards(): hidden_all = lax.all_gather(hidden, 'dp', axis=0, tiled=True)]
  transfers between devices with their start and end apart: 17 -> 18, of which waited for: 10 -> 9; matrix products, arithmetic and copies ran while one was open for 6% -> 7% of each run, Pallas kernels for 9% -> 8%
where the time goes in v5:
time: 398 us; the launch traced here: 394 us
  waiting for transfers between devices  151 us (38%)
  starting transfers between devices  73.3 us (18%)
  blocking collectives  59 us (15%)
  Pallas kernels  50.4 us (13%)
  local copies, waits for them, and re-layouts  24 us (6%)
  matrix products  15.5 us (4%)
  between operations  14.1 us (4%)
  other arithmetic  6.87 us (2%)
    ppermute x8, waiting for transfers between devices, swapped(): return lax.ppermute(block, axis, [(0, 1), (1, 0)])  95.8 us
    all_to_all x7, starting transfers between devices, exchange(): return lax.all_to_all(blocks, axes, split_axis=0, concat_axis=0, tiled=True)  58.8 us
    pallas_call x9, Pallas kernels, kernel_call(): pl.pallas_call(body, out_shape=outs, scratch_shapes=scratch, compiler_par...  50.4 us
    all_to_all x7, waiting for transfers between devices, exchange(): return lax.all_to_all(blocks, axes, split_axis=0, concat_axis=0, tiled=True)  49.9 us
    all_gather x1, blocking collectives, shards(): joined = lax.all_gather(joined, 'expert', axis=0)  37.3 us
    all_gather x1, blocking collectives, shards(): hidden_all = lax.all_gather(hidden, 'dp', axis=0, tiled=True)  21.7 us
    dot_general x6, matrix products, mm(): lax.dot_general(left, right, (contract, ((), ())), preferred_element_type...  15.5 us
    unnamed x55, local copies, waits for them, and re-layouts  14.6 us
  transfers between devices with their start and end apart: 18, of which 9 were waited for; matrix products, arithmetic and copies ran while one was open for 7% of the time, Pallas kernels for 8%

profile of v5, /device:TPU:8, one launch (start us, length us, event | category | flops | bytes accessed | tf_op | source)
XLA Modules:
  0.0 394.1 jit_solution(8377857010952436242)
XLA Ops:
  8.2 3.1 collective-permute-start
  15.3 4.9 %shard_map.217 = (bf16[64,80,128]{2,1,0:T(8,128)(2,1)}, bf16[128,4096]{1,0:T(8,128)(2,1)S(1)}, f32[128,128]{1,0:T(8,128)S(1)}) custom-call(bf16[128,4096]{1,0:T(8,128)(2,1)} %bitcast.61, s32[128,8]{1,0:T(8,128)S(1)} %bitcast.57, f32[1,4096]{1,0:T(1,128)S(1)} %copy-done.19, s32[1,1280]{1,0:T(1,128)S(1)} %copy-done.16, s32[1280,1]{1,0:T(8,128)S(1)} %copy-done.5, ...), custom_call_target="tpu_custom_call" | custom-call | tf_op jit(solution)/shard_map/pallas_call | solution.py:41
  20.6 13.2 %all-to-all-start = ((bf16[64,80,128]{2,1,0:T(8,128)(2,1)}), bf16[64,80,128]{2,1,0:T(8,128)(2,1)}, u32[]{:S(2)}, u32[]{:S(2)}) async-start(bf16[64,80,128]{2,1,0:T(8,128)(2,1)} %get-tuple-element.34), calls=%async_computation | async-start | bytes 2621440 | tf_op jit(solution)/shard_map/all_to_all | solution.py:23
  36.4 2.7 collective-permute-start.2
  39.1 5.7 %shard_map.218 = (bf16[64,80,128]{2,1,0:T(8,128)(2,1)}, f32[128,128]{1,0:T(8,128)S(1)}) custom-call(bf16[128,4096]{1,0:T(8,128)(2,1)S(1)} %get-tuple-element.30.normed, s32[128,8]{1,0:T(8,128)S(1)} %bitcast.58, bf16[128,4096]{1,0:T(8,128)(2,1)} %bitcast.68, bf16[4096,128]{1,0:T(8,128)(2,1)} %bitcast.66, f32[128,128]{1,0:T(8,128)S(1)} %get-tuple-element.31.place, ...), custom_call_target="tpu_custom_call" | custom-call | tf_op jit(solution)/shard_map/pallas_call | solution.py:41
  44.9 21.7 %all-to-all-done.arrived = bf16[64,80,128]{2,1,0:T(8,128)(2,1)} async-done(((bf16[64,80,128]{2,1,0:T(8,128)(2,1)}), bf16[64,80,128]{2,1,0:T(8,128)(2,1)}, u32[]{:S(2)}, u32[]{:S(2)}) %all-to-all-start) | async-done | bytes 1310752 | tf_op jit(solution)/shard_map/all_to_all | solution.py:23
  66.6 9.5 %collective-permute-done.2.refs_2_.first_late = bf16[384,1536]{1,0:T(8,128)(2,1)S(1)} collective-permute-done((bf16[384,1536]{1,0:T(8,128)(2,1)}, bf16[384,1536]{1,0:T(8,128)(2,1)S(1)}, u32[]{:S(2)}, u32[]{:S(2)}) %collective-permute-start.2) | collective-permute-done | bytes 1179680 | tf_op jit(solution)/shard_map/ppermute | solution.py:299
  77.1 8.1 %shard_map.220 = (bf16[640,1536]{1,0:T(8,128)(2,1)}, bf16[640,1024]{1,0:T(8,128)(2,1)}) custom-call(s32[1]{0:T(128)} %bitcast.index, bf16[64,80,128]{2,1,0:T(8,128)(2,1)} %all-to-all-done.arrived, s32[640,1]{1,0:T(8,128)S(1)} %copy-done, bf16[512,1536]{1,0:T(8,128)(2,1)} %bitcast.59, bf16[128,1536]{1,0:T(8,128)(2,1)S(1)} %copy-done.11, ...), custom_call_target="tpu_custom_call" | custom-call | tf_op jit(solution)/shard_map/pallas_call | solution.py:41
  85.2 10.4 %all-to-all-start.1 = ((bf16[64,80,128]{2,1,0:T(8,128)(2,1)}), bf16[64,80,128]{2,1,0:T(8,128)(2,1)}, u32[]{:S(2)}, u32[]{:S(2)}) async-start(bf16[64,80,128]{2,1,0:T(8,128)(2,1)} %get-tuple-element.35), calls=%async_computation.1 | async-start | bytes 2621440 | tf_op jit(solution)/shard_map/all_to_all | solution.py:23
  97.9 30.0 %collective-permute-done.1.refs_1_.second_other = bf16[768,512]{1,0:T(8,128)(2,1)S(1)} collective-permute-done((bf16[768,512]{1,0:T(8,128)(2,1)S(1)}, bf16[768,512]{1,0:T(8,128)(2,1)S(1)}, u32[]{:S(2)}, u32[]{:S(2)}) %collective-permute-start.1) | collective-permute-done | bytes 786464 | tf_op jit(solution)/shard_map/ppermute | solution.py:299
  130.0 5.2 %shard_map.219 = (bf16[640,768]{1,0:T(8,128)(2,1)}, bf16[640,1024]{1,0:T(8,128)(2,1)}) custom-call(s32[1]{0:T(128)} %bitcast.index, bf16[64,80,128]{2,1,0:T(8,128)(2,1)} %all-to-all-done.1.arrived, s32[640,1]{1,0:T(8,128)S(1)} %copy-done, bf16[768,512]{1,0:T(8,128)(2,1)S(1)} %bitcast.54, bf16[768,512]{1,0:T(8,128)(2,1)S(1)} %copy-done.3), custom_call_target="tpu_custom_call" | custom-call | tf_op jit(solution)/shard_map/pallas_call | solution.py:41
  135.1 5.0 %all-to-all-start.2 = ((bf16[4,160,768]{2,1,0:T(8,128)(2,1)}), bf16[4,160,768]{2,1,0:T(8,128)(2,1)}, u32[]{:S(2)}, u32[]{:S(2)}) async-start(bf16[4,160,768]{2,1,0:T(8,128)(2,1)} %bitcast.77), calls=%async_computation.3 | async-start | bytes 1966080 | tf_op jit(solution)/shard_map/all_to_all | solution.py:23
  141.4 21.7 %all_gather.13.hidden = bf16[640,768]{1,0:T(8,128)(2,1)} all-gather(bf16[160,768]{1,0:T(8,128)(2,1)S(1)} %fusion.9.hidden), channel_id=1, replica_groups=mesh['section'=2,'expert'=16,'half'=2,'dp'=4] {'dp'}, dimensions={0}, use_global_device_ids=true | all-gather | bytes 1228800 | tf_op jit(solution)/shard_map/all_gather | solution.py:397
  166.7 2.4 shard_map.221
  170.0 6.7 %all-to-all-start.3 = ((f32[16,1,128]{2,1,0:T(1,128)}), f32[16,1,128]{2,1,0:T(1,128)S(1)}, u32[]{:S(2)}, u32[]{:S(2)}) async-start(f32[16,1,128]{2,1,0:T(1,128)} %bitcast.11), calls=%async_computation.4 | async-start | bytes 16384 | tf_op jit(solution)/shard_map/all_to_all | solution.py:23
  176.7 3.1 convolution_convert_fusion.1
  181.7 3.4 all-to-all-done.3
  189.4 6.6 %all-to-all-start.4 = ((bf16[4,1024,128]{2,1,0:T(8,128)(2,1)}), bf16[4,1024,128]{2,1,0:T(8,128)(2,1)}, u32[]{:S(2)}, u32[]{:S(2)}) async-start(bf16[4,1024,128]{2,1,0:T(8,128)(2,1)} %bitcast.70), calls=%async_computation.5 | async-start | bytes 2097152 | tf_op jit(solution)/shard_map/all_to_all | solution.py:23
  196.1 4.5 %shard_map.222.outs = bf16[64,80,128]{2,1,0:T(8,128)(2,1)} custom-call(s32[1]{0:T(128)} %bitcast.index, bf16[640,768]{1,0:T(8,128)(2,1)} %all_gather.13.hidden, s32[640,1]{1,0:T(8,128)S(1)} %copy-done, bf16[768,512]{1,0:T(8,128)(2,1)S(1)} %bitcast.55, bf16[768,512]{1,0:T(8,128)(2,1)S(1)} %copy-done.4), custom_call_target="tpu_custom_call" | custom-call | tf_op jit(solution)/shard_map/pallas_call | solution.py:41
  200.6 11.5 %all-to-all-done.4 = bf16[4,1024,128]{2,1,0:T(8,128)(2,1)} async-done(((bf16[4,1024,128]{2,1,0:T(8,128)(2,1)}), bf16[4,1024,128]{2,1,0:T(8,128)(2,1)}, u32[]{:S(2)}, u32[]{:S(2)}) %all-to-all-start.4) | async-done | bytes 1048608 | tf_op jit(solution)/shard_map/all_to_all | solution.py:23
  213.5 8.5 %shard_map.223 = (bf16[64,160,128]{2,1,0:T(8,128)(2,1)}, f32[1,1024]{1,0:T(1,128)S(1)}) custom-call(s32[1]{0:T(128)} %bitcast.index, bf16[640,1536]{1,0:T(8,128)(2,1)} %all-gather.3.cloned.1.call-done.pre_grad, s32[640,1]{1,0:T(8,128)S(1)} %copy-done, bf16[512,1536]{1,0:T(8,128)(2,1)} %bitcast.60, bf16[128,1536]{1,0:T(8,128)(2,1)S(1)} %copy-done.12, ...), custom_call_target="tpu_custom_call" | custom-call | tf_op jit(solution)/shard_map/pallas_call | solution.py:41
  224.4 9.8 %all-to-all-start.5 = ((f32[32,40,128]{2,1,0:T(8,128)}), f32[32,40,128]{2,1,0:T(8,128)S(1)}, u32[]{:S(2)}, u32[]{:S(2)}) async-start(f32[32,40,128]{2,1,0:T(8,128)} %select_maximum_fusion), calls=%async_computation.6 | async-start | bytes 1310720 | tf_op jit(solution)/shard_map/all_to_all | solution.py:23
  234.2 4.3 %convolution_convert_fusion = bf16[512,1536]{1,0:T(8,128)(2,1)} fusion(bf16[640,1536]{1,0:T(8,128)(2,1)} %all-gather.3.cloned.1.call-done.pre_grad, bf16[640,1024]{1,0:T(8,128)(2,1)} %get-tuple-element.43.rows), kind=kOutput, calls=%fused_computation.3 | convolution fusion | flops 1007419392 | bytes 4194304 | tf_op jit(solution)/shard_map/dot_general | solution.py:27
  238.5 13.4 %all-to-all-done.5 = f32[32,40,128]{2,1,0:T(8,128)S(1)} async-done(((f32[32,40,128]{2,1,0:T(8,128)}), f32[32,40,128]{2,1,0:T(8,128)S(1)}, u32[]{:S(2)}, u32[]{:S(2)}) %all-to-all-start.5) | async-done | bytes 655392 | tf_op jit(solution)/shard_map/all_to_all | solution.py:23
  252.0 7.1 %all-to-all-start.6 = ((bf16[64,160,128]{2,1,0:T(8,128)(2,1)}), bf16[64,160,128]{2,1,0:T(8,128)(2,1)}, u32[]{:S(2)}, u32[]{:S(2)}) async-start(bf16[64,160,128]{2,1,0:T(8,128)(2,1)} %get-tuple-element.51), calls=%async_computation.7 | async-start | bytes 5242880 | tf_op jit(solution)/shard_map/all_to_all | solution.py:23
  263.7 55.9 %collective-permute-done.7 = bf16[48,128]{1,0:T(8,128)(2,1)S(1)} collective-permute-done((bf16[48,128]{1,0:T(8,128)(2,1)S(1)}, bf16[48,128]{1,0:T(8,128)(2,1)S(1)}, u32[]{:S(2)}, u32[]{:S(2)}) %collective-permute-start.7) | collective-permute-done | bytes 12320 | tf_op jit(solution)/shard_map/ppermute | solution.py:299
  319.6 37.3 %all_gather.15 = bf16[16,2,48,128]{3,2,1,0:T(8,128)(2,1)} all-gather(bf16[1,2,48,128]{3,2,1,0:T(8,128)(2,1)S(1)} %maximum_select_fusion), channel_id=1, replica_groups=mesh['section'=2,'expert'=16,'half'=2,'dp'=4] {'expert'}, dimensions={0}, use_global_device_ids=true | all-gather | bytes 417792 | tf_op jit(solution)/shard_map/all_gather | solution.py:481
  356.9 3.2 add_convert_fusion
  360.1 4.0 %fusion.1 = bf16[512,1536]{1,0:T(8,128)(2,1)} fusion(bf16[512,1536]{1,0:T(8,128)(2,1)} %collective-permute-done.4, bf16[640,1536]{1,0:T(8,128)(2,1)S(1)} %copy-done.24, bf16[640,1024]{1,0:T(8,128)(2,1)S(1)} %copy-done.25), kind=kOutput, calls=%fused_computation.4 | convolution fusion | flops 1008992256 | bytes 5767168 | tf_op jit(solution)/shard_map/dot_general | solution.py:27
  364.1 5.4 %shard_map.224 = bf16[128,4096]{1,0:T(8,128)(2,1)S(1)} custom-call(bf16[64,160,128]{2,1,0:T(8,128)(2,1)} %all-to-all-done.6.returned, bf16[128,4096]{1,0:T(8,128)(2,1)} %bitcast.62, f32[128,128]{1,0:T(8,128)S(1)} %get-tuple-element.48.gates, f32[128,128]{1,0:T(8,128)S(1)} %get-tuple-element.31.place, s32[1,1280]{1,0:T(1,128)S(1)} %copy-done.17, ...), custom_call_target="tpu_custom_call" | custom-call | tf_op jit(solution)/shard_map/pallas_call | solution.py:41
  369.7 5.5 %shard_map.225 = bf16[128,4096]{1,0:T(8,128)(2,1)S(1)} custom-call(bf16[64,160,128]{2,1,0:T(8,128)(2,1)} %all-to-all-done.6.returned, bf16[128,4096]{1,0:T(8,128)(2,1)} %bitcast.63, bf16[128,4096]{1,0:T(8,128)(2,1)} %bitcast.69, f32[1,4096]{1,0:T(1,128)S(1)} %copy-done.20, bf16[4096,128]{1,0:T(8,128)(2,1)} %bitcast.67, ...), custom_call_target="tpu_custom_call" | custom-call | tf_op jit(solution)/shard_map/pallas_call | solution.py:41
  375.8 5.0 %all-gather.5.cloned.1.call-done = bf16[6144,128]{1,0:T(8,128)(2,1)} async-done(((bf16[1536,128]{1,0:T(8,128)(2,1)}), bf16[6144,128]{1,0:T(8,128)(2,1)}) %all-gather.5.cloned.1.call-update) | async-done | bytes 1572880 | tf_op jit(solution)/shard_map/all_gather | solution.py:482
  (108 shorter events, 41.1 us)
Async XLA Ops:
  8.2 12.4 %collective-permute-start = (bf16[128,1536]{1,0:T(8,128)(2,1)S(1)}, bf16[128,1536]{1,0:T(8,128)(2,1)S(1)}, u32[]{:S(2)}, u32[]{:S(2)}) collective-permute-start(bf16[128,1536]{1,0:T(8,128)(2,1)S(1)} %slice_bitcast_fusion.1), channel_id=1, source_target_pairs={{0,4},{4,0},{1,5},{5,1},{2,6},{6,2},{3,7},{7,3},{8,12},{12,8},{9,1... | collective-permute-start | bytes 1179656 | tf_op jit(solution)/shard_map/ppermute | solution.py:299
  20.6 13.3 %copy-start.10 = (bf16[128,1536]{1,0:T(8,128)(2,1)}, bf16[128,1536]{1,0:T(8,128)(2,1)S(1)}, u32[]{:S(2)}) copy-start(bf16[128,1536]{1,0:T(8,128)(2,1)S(1)} %collective-permute-done.refs_1_.first_early) | copy-start | bytes 1179652
  20.6 45.9 %all-to-all-start = ((bf16[64,80,128]{2,1,0:T(8,128)(2,1)}), bf16[64,80,128]{2,1,0:T(8,128)(2,1)}, u32[]{:S(2)}, u32[]{:S(2)}) async-start(bf16[64,80,128]{2,1,0:T(8,128)(2,1)} %get-tuple-element.34), calls=%async_computation | async-start | bytes 2621440 | tf_op jit(solution)/shard_map/all_to_all | solution.py:23
  33.9 5.3 %copy-start.6 = (s32[1280,1]{1,0:T(8,128)S(1)}, s32[1280,1]{1,0:T(8,128)}, u32[]{:S(2)}) copy-start(s32[1280,1]{1,0:T(8,128)} %constant.48.clone.chunk_of) | copy-start | bytes 15364
  33.9 5.2 %copy-start.15 = (s32[1,1280]{1,0:T(1,128)S(1)}, s32[1,1280]{1,0:T(1,128)}, u32[]{:S(2)}) copy-start(s32[1,1280]{1,0:T(1,128)} %constant.49.clone.slot_of) | copy-start | bytes 15364
  33.9 5.2 %copy-start.17 = (s32[1,1280]{1,0:T(1,128)S(1)}, s32[1,1280]{1,0:T(1,128)}, u32[]{:S(2)}) copy-start(s32[1,1280]{1,0:T(1,128)} %constant.47.clone.owner) | copy-start | bytes 15364
  33.9 101.2 %reduce-scatter.2.cloned.1.call-start = ((), (), s32[]{:S(2)}) async-start(), calls=%async_computation.8 | async-start | bytes 2457600 | tf_op jit(solution)/shard_map/reduce_scatter | solution.py:384
  36.4 39.7 %collective-permute-start.2 = (bf16[384,1536]{1,0:T(8,128)(2,1)}, bf16[384,1536]{1,0:T(8,128)(2,1)S(1)}, u32[]{:S(2)}, u32[]{:S(2)}) collective-permute-start(bf16[384,1536]{1,0:T(8,128)(2,1)} %slice_bitcast_fusion), channel_id=1, source_target_pairs={{0,4},{4,0},{1,5},{5,1},{2,6},{6,2},{3,7},{7,3},{8,12},{12,8},{9,1... | collective-permute-start | bytes 3538952 | tf_op jit(solution)/shard_map/ppermute | solution.py:299
  39.1 37.0 %copy-start = (s32[640,1]{1,0:T(8,128)S(1)}, s32[640,1]{1,0:T(8,128)}, u32[]{:S(2)}) copy-start(s32[640,1]{1,0:T(8,128)} %constant.50.clone.order) | copy-start | bytes 7684
  85.2 10.4 %copy-start.1 = (bf16[1,1,768,512]{3,2,1,0:T(8,128)(2,1)S(1)}, bf16[1,1,768,512]{3,2,1,0:T(8,128)(2,1)}, u32[]{:S(2)}) copy-start(bf16[1,1,768,512]{3,2,1,0:T(8,128)(2,1)} %param.24) | copy-start | bytes 2359300
  85.2 43.6 %all-to-all-start.1 = ((bf16[64,80,128]{2,1,0:T(8,128)(2,1)}), bf16[64,80,128]{2,1,0:T(8,128)(2,1)}, u32[]{:S(2)}, u32[]{:S(2)}) async-start(bf16[64,80,128]{2,1,0:T(8,128)(2,1)} %get-tuple-element.35), calls=%async_computation.1 | async-start | bytes 2621440 | tf_op jit(solution)/shard_map/all_to_all | solution.py:23
  95.6 32.4 %collective-permute-start.1 = (bf16[768,512]{1,0:T(8,128)(2,1)S(1)}, bf16[768,512]{1,0:T(8,128)(2,1)S(1)}, u32[]{:S(2)}, u32[]{:S(2)}) collective-permute-start(bf16[768,512]{1,0:T(8,128)(2,1)S(1)} %bitcast.53), channel_id=1, source_target_pairs={{0,4},{4,0},{1,5},{5,1},{2,6},{6,2},{3,7},{7,3},{8,12},{12,8},{9,1... | collective-permute-start | bytes 2359304 | tf_op jit(solution)/shard_map/ppermute | solution.py:299
  135.1 28.7 %copy-start.22 = (s32[1,160]{1,0:T(1,128)S(1)}, s32[1,160]{1,0:T(1,128)}, u32[]{:S(2)}) copy-start(s32[1,160]{1,0:T(1,128)} %constant.51.clone.sender_of) | copy-start | bytes 1924
  135.1 28.7 %all-to-all-start.2 = ((bf16[4,160,768]{2,1,0:T(8,128)(2,1)}), bf16[4,160,768]{2,1,0:T(8,128)(2,1)}, u32[]{:S(2)}, u32[]{:S(2)}) async-start(bf16[4,160,768]{2,1,0:T(8,128)(2,1)} %bitcast.77), calls=%async_computation.3 | async-start | bytes 1966080 | tf_op jit(solution)/shard_map/all_to_all | solution.py:23
  140.1 73.4 %all-gather.3.cloned.1.call-start = ((), (), s32[]{:S(2)}) async-start(), calls=%async_computation.9 | async-start | bytes 2457600 | tf_op jit(solution)/shard_map/all_gather | solution.py:407
  170.0 15.1 %all-to-all-start.3 = ((f32[16,1,128]{2,1,0:T(1,128)}), f32[16,1,128]{2,1,0:T(1,128)S(1)}, u32[]{:S(2)}, u32[]{:S(2)}) async-start(f32[16,1,128]{2,1,0:T(1,128)} %bitcast.11), calls=%async_computation.4 | async-start | bytes 16384 | tf_op jit(solution)/shard_map/all_to_all | solution.py:23
  179.7 20.9 %collective-permute-start.3 = (bf16[768,512]{1,0:T(8,128)(2,1)}, bf16[768,512]{1,0:T(8,128)(2,1)}, u32[]{:S(2)}, u32[]{:S(2)}) collective-permute-start(bf16[768,512]{1,0:T(8,128)(2,1)} %convolution_convert_fusion.1), channel_id=1, source_target_pairs={{0,4},{4,0},{1,5},{5,1},{2,6},{6,2},{3,7},{7,3},{8,12},{12,8},{9,1... | collective-permute-start | bytes 2359304 | tf_op jit(solution)/shard_map/ppermute | solution.py:299
  189.4 6.6 %copy-start.4 = (bf16[768,512]{1,0:T(8,128)(2,1)S(1)}, bf16[768,512]{1,0:T(8,128)(2,1)}, u32[]{:S(2)}) copy-start(bf16[768,512]{1,0:T(8,128)(2,1)} %copy-done.2) | copy-start | bytes 2359300
  189.4 22.6 %all-to-all-start.4 = ((bf16[4,1024,128]{2,1,0:T(8,128)(2,1)}), bf16[4,1024,128]{2,1,0:T(8,128)(2,1)}, u32[]{:S(2)}, u32[]{:S(2)}) async-start(bf16[4,1024,128]{2,1,0:T(8,128)(2,1)} %bitcast.70), calls=%async_computation.5 | async-start | bytes 2097152 | tf_op jit(solution)/shard_map/all_to_all | solution.py:23
  200.6 12.9 %copy-start.12 = (bf16[128,1536]{1,0:T(8,128)(2,1)S(1)}, bf16[128,1536]{1,0:T(8,128)(2,1)}, u32[]{:S(2)}) copy-start(bf16[128,1536]{1,0:T(8,128)(2,1)} %copy-done.10) | copy-start | bytes 1179652
  224.4 27.5 %all-to-all-start.5 = ((f32[32,40,128]{2,1,0:T(8,128)}), f32[32,40,128]{2,1,0:T(8,128)S(1)}, u32[]{:S(2)}, u32[]{:S(2)}) async-start(f32[32,40,128]{2,1,0:T(8,128)} %select_maximum_fusion), calls=%async_computation.6 | async-start | bytes 1310720 | tf_op jit(solution)/shard_map/all_to_all | solution.py:23
  251.9 10.0 %copy-start.20 = (f32[1,4096]{1,0:T(1,128)S(1)}, f32[1,4096]{1,0:T(1,128)}, u32[]{:S(2)}) copy-start(f32[1,4096]{1,0:T(1,128)} %gain.3) | copy-start | bytes 49156
  251.9 105.0 %copy-start.23 = (bf16[640,768]{1,0:T(8,128)(2,1)S(1)}, bf16[640,768]{1,0:T(8,128)(2,1)}, u32[]{:S(2)}) copy-start(bf16[640,768]{1,0:T(8,128)(2,1)} %all_gather.13.hidden) | copy-start | bytes 2949124
  252.0 112.2 %all-to-all-start.6 = ((bf16[64,160,128]{2,1,0:T(8,128)(2,1)}), bf16[64,160,128]{2,1,0:T(8,128)(2,1)}, u32[]{:S(2)}, u32[]{:S(2)}) async-start(bf16[64,160,128]{2,1,0:T(8,128)(2,1)} %get-tuple-element.51), calls=%async_computation.7 | async-start | bytes 5242880 | tf_op jit(solution)/shard_map/all_to_all | solution.py:23
  259.0 121.8 %all-gather.5.cloned.1.call-start = ((), (), s32[]{:S(2)}) async-start(), calls=%async_computation.10 | async-start | bytes 1966080 | tf_op jit(solution)/shard_map/all_gather | solution.py:482
  259.1 101.0 %collective-permute-start.4 = (bf16[512,1536]{1,0:T(8,128)(2,1)}, bf16[512,1536]{1,0:T(8,128)(2,1)}, u32[]{:S(2)}, u32[]{:S(2)}) collective-permute-start(bf16[512,1536]{1,0:T(8,128)(2,1)} %convolution_convert_fusion), channel_id=1, source_target_pairs={{0,4},{4,0},{1,5},{5,1},{2,6},{6,2},{3,7},{7,3},{8,12},{12,8},{9,1... | collective-permute-start | bytes 4718600 | tf_op jit(solution)/shard_map/ppermute | solution.py:299
  262.1 57.5 %collective-permute-start.7 = (bf16[48,128]{1,0:T(8,128)(2,1)S(1)}, bf16[48,128]{1,0:T(8,128)(2,1)S(1)}, u32[]{:S(2)}, u32[]{:S(2)}) collective-permute-start(bf16[48,128]{1,0:T(8,128)(2,1)S(1)} %get-tuple-element.59), channel_id=1, source_target_pairs={{0,4},{4,0},{1,5},{5,1},{2,6},{6,2},{3,7},{7,3},{8,12},{12,8},{9,1... | collective-permute-start | bytes 36872 | tf_op jit(solution)/shard_map/ppermute | solution.py:299
  356.9 3.2 copy-start.24
  356.9 3.2 copy-start.25
  360.1 4.0 %copy-start.21 = (s32[1,1280]{1,0:T(1,128)S(1)}, s32[1,1280]{1,0:T(1,128)}, u32[]{:S(2)}) copy-start(s32[1,1280]{1,0:T(1,128)} %constant.53.clone.chunk_of) | copy-start | bytes 15364
  369.6 14.7 %collective-permute-start.5 = (bf16[128,4096]{1,0:T(8,128)(2,1)S(1)}, bf16[128,4096]{1,0:T(8,128)(2,1)S(1)}, u32[]{:S(2)}, u32[]{:S(2)}) collective-permute-start(bf16[128,4096]{1,0:T(8,128)(2,1)S(1)} %shard_map.224), channel_id=1, source_target_pairs={{0,128},{128,0},{1,129},{129,1},{2,130},{130,2},{3,131},{131,3},{4... | collective-permute-start | bytes 3145736 | tf_op jit(solution)/shard_map/ppermute | solution.py:299
  375.2 9.1 %collective-permute-start.6 = (bf16[128,4096]{1,0:T(8,128)(2,1)S(1)}, bf16[128,4096]{1,0:T(8,128)(2,1)}, u32[]{:S(2)}, u32[]{:S(2)}) collective-permute-start(bf16[128,4096]{1,0:T(8,128)(2,1)S(1)} %shard_map.225), channel_id=1, source_target_pairs={{0,128},{128,0},{1,129},{129,1},{2,130},{130,2},{3,131},{131,3},{4... | collective-permute-start | bytes 3145736 | tf_op jit(solution)/shard_map/ppermute | solution.py:299
  (12 other events, 10.5 us)
Sparse Core Ops, SparseCore 0:
  85.3 41.7 reduce-scatter.1
  170.0 35.9 all-gather.2
  357.0 23.7 all-gather.4

commit v6 on v5

--- a/solution.py
+++ b/solution.py
@@ -158,12 +158,8 @@
                     rows_out[rows, c * LANES : (c + 1) * LANES] = own[:, lanes]
                     rows_out[rows, part + c * LANES : part + (c + 1) * LANES] = other[:, lanes]
 
-    total, at = 0.0, 0
-    for weight in weights:
-        end = at + weight.shape[side]
-        total = total + mm(rows_out[:, at:end], weight[...], ((1,), (side,)))
-        at = end
-    partial[...] = total.astype(BF)
+    weight = jnp.concatenate([piece[...] for piece in weights], axis=side)
+    partial[...] = mm(rows_out[...], weight, ((1,), (side,))).astype(BF)
 
 
 def act_kernel(slots, arrived, pre_act, hidden, sender_of, slot_of, pre_grad, worth):
@@ -171,8 +167,7 @@
     hidden_grad = arrived[0].astype(F32)
     for j in range(1, replicas):
         hidden_grad = hidden_grad + arrived[j].astype(F32)
-    gate_pre = pre_act[:, :hidden_width].astype(F32)
-    up = pre_act[:, hidden_width:].astype(F32)
+    gate_pre, up = pre_act[:, :hidden_width], pre_act[:, hidden_width:]
     sigmoid = 1.0 / (1.0 + jnp.exp(-gate_pre))
     silu = gate_pre * sigmoid
     slope = sigmoid * (1.0 + gate_pre * (1.0 - sigmoid))
@@ -220,12 +215,10 @@
     return_rows(group, chunks, slots, index[0] == 0, order, own, other, message)
 
 
-def back_kernel(group, chunks, slots, index, pre_grad, order, first, first_early, first_late, rows, outs,
-                message, gain):
+def back_kernel(group, chunks, slots, index, pre_grad, order, first, rows, outs, *refs):
+    message, gain = refs[-2:]
     own = mm(pre_grad[...], first[...], ((1,), (1,)))
-    other = jnp.concatenate(
-        [mm(pre_grad[...], weight[...], ((1,), (1,))) for weight in (first_early, first_late)], axis=1
-    )
+    other = mm(pre_grad[...], jnp.concatenate([piece[...] for piece in refs[:-2]], axis=0), ((1,), (1,)))
     half = chunks * slots
     message[:, :half] = outs[...]
     return_rows(group, chunks, slots, index[0] == 0, order, own, other, message, half)
@@ -322,9 +315,8 @@
     message_shape = jax.ShapeDtypeStruct((peers, half, LANES), BF)
     side = lax.axis_index("half")
     index = side.astype(jnp.int32)[None]
-    early = part // 4
-    first_early = swapped(first[:early], "half")
-    first_late = swapped(first[early:], "half")
+    cuts = (0, part // 4, 7 * part // 8, part)
+    first_other = tuple(swapped(first[a:b], "half") for a, b in zip(cuts, cuts[1:]))
     second_other = swapped(second, "half")
 
     at = np.arange(experts * half, dtype=np.int32)
@@ -341,7 +333,7 @@
         (x, route_ids, gain, owner, chunk_of[:, None], slot_of),
         token_scratch,
     )
-    arrived = exchange(after(message, first_early), SHARE)
+    arrived = exchange(after(message, first_other[0]), SHARE)
 
     message, gates = kernel_call(
         functools.partial(send_grad_kernel, *sizes),
@@ -349,7 +341,7 @@
         (normed, route_ids, grad_top, table, place, owner, chunk_of[:, None], slot_of),
         token_scratch,
     )
-    message, arrived = lax.optimization_barrier((message, arrived))
+    message, arrived = lax.optimization_barrier((message, arrived, first_other[1]))[:2]
     arrived_grad = exchange(message, SHARE)
 
     at = np.arange(group * half, dtype=np.int32)
@@ -360,6 +352,8 @@
     all_rows = peers * slots
     whole = lambda shape: pl.BlockSpec(shape, lambda i: (0,) * len(shape))
     scalar = pl.BlockSpec(memory_space=pltpu.SMEM)
+
+    sizes_other = tuple(piece.shape[0] for piece in first_other)
 
     def products(arrived, weights, side, steps, weight_specs):
         return kernel_call(
@@ -376,12 +370,18 @@
 
     partial, expert_rows = products(
         arrived,
-        (first, first_early, first_late),
+        (first,) + first_other,
         0,
         2 * HIDDEN_STEPS,
-        [pl.BlockSpec((size, step_width), lambda i: (0, i)) for size in (part, early, part - early)],
-    )
-    pre_act = lax.psum_scatter(partial, "dp", scatter_dimension=0, tiled=True)
+        [pl.BlockSpec((size, step_width), lambda i: (0, i)) for size in (part,) + sizes_other],
+    )
+    partial = partial.reshape(replicas, rows, 2 * hidden_width)
+    place_in_dp = lax.axis_index("dp")
+    pre_act = lax.dynamic_index_in_dim(partial, place_in_dp, 0, False).astype(F32)
+    for step in range(1, replicas):
+        shift = [(j, (j + step) % replicas) for j in range(replicas)]
+        block = lax.dynamic_index_in_dim(partial, (place_in_dp + step) % replicas, 0, False)
+        pre_act = pre_act + lax.ppermute(block, "dp", shift).astype(F32)
     partial, grad_rows = products(
         arrived_grad,
         (second, second_other),
@@ -389,12 +389,15 @@
         HIDDEN_STEPS,
         [pl.BlockSpec((step_width, part), lambda i: (i, 0))] * 2,
     )
-    partial, pre_act = lax.optimization_barrier((partial, pre_act))
     summands = exchange(partial.reshape(replicas, rows, hidden_width), "dp")
-    gate_pre = pre_act[:, :hidden_width].astype(F32)
-    up = pre_act[:, hidden_width:].astype(F32)
+    gate_pre, up = pre_act[:, :hidden_width], pre_act[:, hidden_width:]
     hidden = (gate_pre / (1.0 + jnp.exp(-gate_pre)) * up).astype(BF)
-    hidden_all = lax.all_gather(hidden, "dp", axis=0, tiled=True)
+    hidden_all = jnp.zeros((all_rows, hidden_width), BF)
+    for step in range(replicas):
+        shift = [(j, (j + step) % replicas) for j in range(replicas)]
+        block = lax.ppermute(hidden, "dp", shift) if step else hidden
+        at_row = (place_in_dp + replicas - step) % replicas * rows
+        hidden_all = lax.dynamic_update_slice(hidden_all, block, (at_row, 0))
     at = np.arange(rows, dtype=np.int32)
     pre_grad, worth = kernel_call(
         functools.partial(act_kernel, slots),
@@ -402,7 +405,7 @@
             jax.ShapeDtypeStruct((rows, 2 * hidden_width), BF),
             jax.ShapeDtypeStruct((experts, LANES), F32),
         ),
-        (summands, pre_act, after(hidden, hidden_all), at[None] // slots, at[:, None] % slots),
+        (summands, pre_act, hidden, at[None] // slots, at[:, None] % slots),
     )
     pre_grad_all = lax.all_gather(pre_grad, "dp", axis=0, tiled=True)
 
@@ -415,12 +418,17 @@
     logit_grad = jnp.pad(gate_worth, ((0, 0), (0, router_width - experts))) - gates * inner
     logit_high, logit_low = two_terms(logit_grad)
     local_router = mm(normed, logit_high, ((0,), (0,))) + mm(normed, logit_low, ((0,), (0,)))
-    local_router = local_router.astype(BF).reshape(2, replicas, part, router_width).transpose(1, 0, 2, 3)
+    local_router = local_router.astype(BF).reshape(experts, -1, router_width)
     second_other_grad = mm(hidden_all, grad_rows[:, part:], ((0,), (0,))).astype(BF)
     second_sent = swapped(second_other_grad, "half")
     local_router = after(local_router, second_other_grad)
-    router_part = exchange(local_router.reshape(replicas, 2 * part, router_width), "dp")
-    router_part = jnp.sum(router_part.astype(F32), axis=0)
+    router_part = jnp.sum(exchange(local_router, "expert").astype(F32), axis=0)
+    piece = router_part.shape[0] // (2 * replicas)
+    router_part = router_part.reshape(2 * replicas, piece, router_width)
+    router_own = jnp.sum(exchange(router_part, ("half", "dp")), axis=0)
+    at = lax.axis_index("expert") * 2 * replicas + side * replicas + place_in_dp
+    table_own = lax.dynamic_slice_in_dim(table, at * piece, piece, axis=0).astype(F32)
+    gain_own = jnp.sum(router_own * table_own, axis=1)
 
     steps = 2 if all_rows // 2 % (2 * group * slots) == 0 else 1
 
@@ -440,17 +448,16 @@
     message, gain_part = kernel_call(
         functools.partial(back_kernel, group, chunks, slots),
         (jax.ShapeDtypeStruct((peers, 2 * half, LANES), BF), jax.ShapeDtypeStruct((1, 2 * part), F32)),
-        (index, pre_grad_all, order, first, first_early, first_late, expert_rows, after(out_message, second_sent)),
+        (index, pre_grad_all, order, first, expert_rows, after(out_message, second_sent)) + first_other,
         grid=(steps,),
         in_specs=[
             scalar,
             by_rows(2 * hidden_width),
             whole(order.shape),
             whole(first.shape),
-            whole(first_early.shape),
-            whole(first_late.shape),
             by_rows(2 * part),
             messages,
+            *(whole(piece.shape) for piece in first_other),
         ],
         out_specs=[
             pl.BlockSpec((peers // steps, 2 * half, LANES), lambda i: (i, 0, 0)),
@@ -460,29 +467,33 @@
     gain_part = gain_part.reshape(2, part)
     gain_part = jnp.where(side == 0, gain_part, gain_part[::-1])
 
+    lines = 2 * part // LANES
+    terms = three_terms(gain_part.reshape(lines, LANES))
+    lone = [jnp.pad(term[None], ((0, 0), (0, LANES - piece))) for term in three_terms(gain_own)]
+    block = jnp.concatenate([router_own.astype(BF), *terms, *lone], axis=0)
+    block = jnp.pad(block, ((0, -block.shape[0] % 16), (0, 0)))
     owners = 2 * experts
-    piece = 2 * part // owners
-    gain_rows = jnp.pad(gain_part.reshape(owners, 1, piece), ((0, 0), (0, 7), (0, LANES - piece)))
-    owned = jnp.concatenate([router_part.reshape(owners, piece, router_width), gain_rows], axis=1)
-    owned = jnp.sum(exchange(owned, OWNERS), axis=0)
+    joined = exchange(jnp.broadcast_to(block[None], (owners,) + block.shape), OWNERS)
     first_other_grad = mm(expert_rows[:, part:], pre_grad_all, ((0,), (0,))).astype(BF)
     first_sent = swapped(first_other_grad, "half")
-    message, owned = lax.optimization_barrier((message, owned, first_other_grad))[:2]
+    message, joined = lax.optimization_barrier((message, joined, first_other_grad))[:2]
     returned = exchange(message, SHARE)
-    router_own = owned[:piece]
-    at = (side * replicas + lax.axis_index("dp")) * part + lax.axis_index("expert") * piece
-    table_own = lax.dynamic_slice_in_dim(table, at, piece, axis=0).astype(F32)
-    gain_here = lax.dynamic_slice_in_dim(gain[0], at, piece, axis=0)
-    gain_sum = (owned[piece, :piece] + jnp.sum(router_own * table_own, axis=1)) / gain_here
-    gain_terms = jnp.pad(jnp.stack(three_terms(gain_sum)), ((0, 13), (0, LANES - piece)))
-    block = jnp.concatenate([router_own.astype(BF), gain_terms], axis=0)
-    block_other = swapped(block, "half")
-    joined = jnp.where(side == 0, jnp.stack([block, block_other]), jnp.stack([block_other, block]))
-    joined = lax.all_gather(joined, "expert", axis=0)
-    joined = lax.all_gather(joined.reshape(-1, LANES), "dp", axis=0, tiled=True)
-    joined = joined.reshape(replicas, experts, 2, piece + 16, LANES).transpose(2, 0, 1, 3, 4)
-    router_total = joined[:, :, :, :piece].reshape(width, router_width)
-    gain_total = jnp.sum(joined[:, :, :, piece : piece + 3, :piece].astype(F32), axis=3).reshape(width)
+    end = piece + 3 * lines
+    gain_rows = jnp.sum(joined[:, piece:end].astype(F32).reshape(owners, 3, lines, LANES), axis=(0, 1))
+    lone = jnp.sum(joined[:, end : end + 3, :piece].astype(F32), axis=1).reshape(-1, LANES)
+    sums = jnp.concatenate([*three_terms(gain_rows), *three_terms(lone)], axis=0)
+    sums = jnp.pad(sums, ((0, -sums.shape[0] % 16), (0, 0)))
+    packed = jnp.concatenate([joined[:, :piece].reshape(-1, LANES), sums], axis=0)
+    packed = lax.all_gather(packed, "dp", axis=0)
+    router_rows = owners * piece
+    router_total = packed[:, :router_rows].reshape(replicas, 2, experts, piece, router_width)
+    router_total = router_total.transpose(2, 1, 0, 3, 4).reshape(width, router_width)
+    gain_rows = packed[:, router_rows : router_rows + 3 * lines].astype(F32)
+    gain_rows = jnp.sum(gain_rows.reshape(replicas, 3, 2, part), axis=1)
+    lone = packed[:, router_rows + 3 * lines : router_rows + 6 * lines].astype(F32)
+    lone = jnp.sum(lone.reshape(replicas, 3, 2, experts, piece), axis=1)
+    gain_total = gain_rows.transpose(1, 0, 2).reshape(width) + lone.transpose(2, 1, 0, 3).reshape(width)
+    gain_total = gain_total / gain[0]
 
     second_own_grad = mm(hidden_all, grad_rows[:, :part], ((0,), (0,)))
     second_grad = (second_own_grad + second_sent.astype(F32)).astype(BF)

time: 398 us -> 370 us (0.930)
  blocking collectives: 59 us -> 0 us
  waiting for transfers between devices: 151 us -> 168 us
  starting transfers between devices: 73.3 us -> 81.3 us
    all_gather x2 -> x0, blocking collectives: 59 us -> none  [the longest x1 37.3 us: shards(): joined = lax.all_gather(joined, 'expert', axis=0)]
    ppermute x0 -> x6, waiting for transfers between devices: none -> 33.5 us  [the longest x3 22 us: shards(): pre_act = pre_act + lax.ppermute(block, 'dp', shift).astype(F32)]
    ppermute x0 -> x6, starting transfers between devices: none -> 8.99 us  [the longest x3 4.7 us: shards(): block = lax.ppermute(hidden, 'dp', shift) if step else hidden]
    all_to_all x7 -> x8, waiting for transfers between devices: 49.9 us -> 41.8 us  [exchange(): return lax.all_to_all(blocks, axes, split_axis=0, concat_axis=0, tiled=True)]
    all_gather x1, waiting for transfers between devices: 5.04 us -> 0.01 us  [shards(): packed = lax.all_gather(packed, 'dp', axis=0)]
    dynamic_update_slice x0 -> x3, local copies, waits for them, and re-layouts: none -> 4.96 us  [shards(): hidden_all = lax.dynamic_update_slice(hidden_all, block, (at_row, 0))]
    unnamed x55 -> x52, local copies, waits for them, and re-layouts: 14.6 us -> 11.6 us
    all_to_all x7 -> x8, starting transfers between devices: 58.8 us -> 58.4 us  [exchange(): return lax.all_to_all(blocks, axes, split_axis=0, concat_axis=0, tiled=True)]
  transfers between devices with their start and end apart: 18 -> 24, of which waited for: 9 -> 15; matrix products, arithmetic and copies ran while one was open for 7% -> 10% of each run, Pallas kernels for 8% -> 8%
where the time goes in v6:
time: 370 us; the launch traced here: 366 us
  waiting for transfers between devices  168 us (45%)
  starting transfers between devices  81.3 us (22%)
  Pallas kernels  49.7 us (13%)
  local copies, waits for them, and re-layouts  27.2 us (7%)
  matrix products  16.5 us (4%)
  between operations  14.5 us (4%)
  other arithmetic  8.82 us (2%)
    ppermute x8, waiting for transfers between devices, swapped(): return lax.ppermute(block, axis, [(0, 1), (1, 0)])  92.9 us
    all_to_all x8, starting transfers between devices, exchange(): return lax.all_to_all(blocks, axes, split_axis=0, concat_axis=0, tiled=True)  58.4 us
    pallas_call x9, Pallas kernels, kernel_call(): pl.pallas_call(body, out_shape=outs, scratch_shapes=scratch, compiler_par...  49.7 us
    all_to_all x8, waiting for transfers between devices, exchange(): return lax.all_to_all(blocks, axes, split_axis=0, concat_axis=0, tiled=True)  41.8 us
    ppermute x3, waiting for transfers between devices, shards(): pre_act = pre_act + lax.ppermute(block, 'dp', shift).astype(F32)  22 us
    dot_general x6, matrix products, mm(): lax.dot_general(left, right, (contract, ((), ())), preferred_element_type...  16.5 us
    ppermute x8, starting transfers between devices, swapped(): return lax.ppermute(block, axis, [(0, 1), (1, 0)])  13.9 us
    unnamed x52, local copies, waits for them, and re-layouts  11.6 us
  transfers between devices with their start and end apart: 24, of which 15 were waited for; matrix products, arithmetic and copies ran while one was open for 10% of the time, Pallas kernels for 8%

profile of v6, /device:TPU:8, one launch (start us, length us, event | category | flops | bytes accessed | tf_op | source)
XLA Modules:
  0.0 366.3 jit_solution(8435148428892469190)
XLA Ops:
  8.2 3.1 collective-permute-start
  15.3 4.9 %shard_map.217 = (bf16[64,80,128]{2,1,0:T(8,128)(2,1)}, bf16[128,4096]{1,0:T(8,128)(2,1)S(1)}, f32[128,128]{1,0:T(8,128)S(1)}) custom-call(bf16[128,4096]{1,0:T(8,128)(2,1)} %bitcast.76, s32[128,8]{1,0:T(8,128)S(1)} %bitcast.72, f32[1,4096]{1,0:T(1,128)S(1)} %copy-done.9, s32[1,1280]{1,0:T(1,128)S(1)} %copy-done.13, s32[1280,1]{1,0:T(8,128)S(1)} %copy-done.3, ...), custom_call_target="tpu_custom_call" | custom-call | tf_op jit(solution)/shard_map/pallas_call | solution.py:41
  20.6 13.2 %all-to-all-start = ((bf16[64,80,128]{2,1,0:T(8,128)(2,1)}), bf16[64,80,128]{2,1,0:T(8,128)(2,1)}, u32[]{:S(2)}, u32[]{:S(2)}) async-start(bf16[64,80,128]{2,1,0:T(8,128)(2,1)} %get-tuple-element.31), calls=%async_computation | async-start | bytes 2621440 | tf_op jit(solution)/shard_map/all_to_all | solution.py:23
  35.2 2.8 collective-permute-start.1
  38.0 5.7 %shard_map.218 = (bf16[64,80,128]{2,1,0:T(8,128)(2,1)}, f32[128,128]{1,0:T(8,128)S(1)}) custom-call(bf16[128,4096]{1,0:T(8,128)(2,1)S(1)} %get-tuple-element.27.normed, s32[128,8]{1,0:T(8,128)S(1)} %bitcast.73, bf16[128,4096]{1,0:T(8,128)(2,1)} %bitcast.81, bf16[4096,128]{1,0:T(8,128)(2,1)} %bitcast.79, f32[128,128]{1,0:T(8,128)S(1)} %get-tuple-element.28.place, ...), custom_call_target="tpu_custom_call" | custom-call | tf_op jit(solution)/shard_map/pallas_call | solution.py:41
  43.7 28.1 %collective-permute-done.1.refs_2_.refs_1_ = bf16[320,1536]{1,0:T(8,128)(2,1)S(1)} collective-permute-done((bf16[320,1536]{1,0:T(8,128)(2,1)S(1)}, bf16[320,1536]{1,0:T(8,128)(2,1)S(1)}, u32[]{:S(2)}, u32[]{:S(2)}) %collective-permute-start.1) | collective-permute-done | bytes 983072 | tf_op jit(solution)/shard_map/ppermute | solution.py:292
  71.8 10.3 %all-to-all-start.1 = ((bf16[64,80,128]{2,1,0:T(8,128)(2,1)}), bf16[64,80,128]{2,1,0:T(8,128)(2,1)}, u32[]{:S(2)}, u32[]{:S(2)}) async-start(bf16[64,80,128]{2,1,0:T(8,128)(2,1)} %get-tuple-element.32), calls=%async_computation.1 | async-start | bytes 2621440 | tf_op jit(solution)/shard_map/all_to_all | solution.py:23
  85.1 9.0 %collective-permute-done.3.refs_3_.refs_2_ = bf16[64,1536]{1,0:T(8,128)(2,1)S(1)} collective-permute-done((bf16[64,1536]{1,0:T(8,128)(2,1)S(1)}, bf16[64,1536]{1,0:T(8,128)(2,1)S(1)}, u32[]{:S(2)}, u32[]{:S(2)}) %collective-permute-start.3) | collective-permute-done | bytes 196640 | tf_op jit(solution)/shard_map/ppermute | solution.py:292
  94.1 7.9 %shard_map.220 = (bf16[640,1536]{1,0:T(8,128)(2,1)}, bf16[640,1024]{1,0:T(8,128)(2,1)}) custom-call(s32[1]{0:T(128)} %bitcast.index, bf16[64,80,128]{2,1,0:T(8,128)(2,1)} %all-to-all-done.arrived, s32[640,1]{1,0:T(8,128)S(1)} %copy-done, bf16[512,1536]{1,0:T(8,128)(2,1)} %bitcast.74, bf16[128,1536]{1,0:T(8,128)(2,1)S(1)} %collective-permute-done.refs_1_.refs_0_, ...), custom_call_target="tpu_custom_call" | custom-call | tf_op jit(solution)/shard_map/pallas_call | solution.py:41
  110.6 10.8 %collective-permute-done.4 = bf16[160,1536]{1,0:T(8,128)(2,1)} collective-permute-done((bf16[160,1536]{1,0:T(8,128)(2,1)}, bf16[160,1536]{1,0:T(8,128)(2,1)}, u32[]{:S(2)}, u32[]{:S(2)}) %collective-permute-start.4) | collective-permute-done | bytes 491552 | tf_op jit(solution)/shard_map/ppermute | solution.py:384
  122.3 10.3 %collective-permute-done.5 = bf16[160,1536]{1,0:T(8,128)(2,1)} collective-permute-done((bf16[160,1536]{1,0:T(8,128)(2,1)}, bf16[160,1536]{1,0:T(8,128)(2,1)}, u32[]{:S(2)}, u32[]{:S(2)}) %collective-permute-start.5) | collective-permute-done | bytes 491552 | tf_op jit(solution)/shard_map/ppermute | solution.py:384
  132.6 2.6 fusion.3.pre_act
  135.3 5.6 %shard_map.219 = (bf16[640,768]{1,0:T(8,128)(2,1)}, bf16[640,1024]{1,0:T(8,128)(2,1)}) custom-call(s32[1]{0:T(128)} %bitcast.index, bf16[64,80,128]{2,1,0:T(8,128)(2,1)} %all-to-all-done.1.arrived, s32[640,1]{1,0:T(8,128)S(1)} %copy-done, bf16[768,512]{1,0:T(8,128)(2,1)S(1)} %bitcast.69, bf16[768,512]{1,0:T(8,128)(2,1)} %collective-permute-done.2.refs_1_.second_other), custom_call_target="tpu_custom_call" | custom-call | tf_op jit(solution)/shard_map/pallas_call | solution.py:41
  140.9 4.8 %all-to-all-start.2 = ((bf16[4,160,768]{2,1,0:T(8,128)(2,1)}), bf16[4,160,768]{2,1,0:T(8,128)(2,1)S(1)}, u32[]{:S(2)}, u32[]{:S(2)}) async-start(bf16[4,160,768]{2,1,0:T(8,128)(2,1)} %bitcast.92), calls=%async_computation.2 | async-start | bytes 1966080 | tf_op jit(solution)/shard_map/all_to_all | solution.py:23
  153.5 10.0 %collective-permute-done.7 = bf16[160,768]{1,0:T(8,128)(2,1)} collective-permute-done((bf16[160,768]{1,0:T(8,128)(2,1)}, bf16[160,768]{1,0:T(8,128)(2,1)}, u32[]{:S(2)}, u32[]{:S(2)}) %collective-permute-start.7) | collective-permute-done | bytes 245792 | tf_op jit(solution)/shard_map/ppermute | solution.py:398
  173.3 6.7 %all-to-all-start.3 = ((f32[16,1,128]{2,1,0:T(1,128)}), f32[16,1,128]{2,1,0:T(1,128)S(1)}, u32[]{:S(2)}, u32[]{:S(2)}) async-start(f32[16,1,128]{2,1,0:T(1,128)} %bitcast.17), calls=%async_computation.3 | async-start | bytes 16384 | tf_op jit(solution)/shard_map/all_to_all | solution.py:23
  180.1 3.1 convolution_convert_fusion.1
  183.2 5.2 %all-to-all-done.3 = f32[16,1,128]{2,1,0:T(1,128)S(1)} async-done(((f32[16,1,128]{2,1,0:T(1,128)}), f32[16,1,128]{2,1,0:T(1,128)S(1)}, u32[]{:S(2)}, u32[]{:S(2)}) %all-to-all-start.3) | async-done | bytes 8224 | tf_op jit(solution)/shard_map/all_to_all | solution.py:23
  190.7 4.5 %all-to-all-start.4 = ((bf16[16,256,128]{2,1,0:T(8,128)(2,1)}), bf16[16,256,128]{2,1,0:T(8,128)(2,1)}, u32[]{:S(2)}, u32[]{:S(2)}) async-start(bf16[16,256,128]{2,1,0:T(8,128)(2,1)} %bitcast.84), calls=%async_computation.4 | async-start | bytes 2097152 | tf_op jit(solution)/shard_map/all_to_all | solution.py:23
  197.3 23.7 %all-to-all-done.4 = bf16[16,256,128]{2,1,0:T(8,128)(2,1)} async-done(((bf16[16,256,128]{2,1,0:T(8,128)(2,1)}), bf16[16,256,128]{2,1,0:T(8,128)(2,1)}, u32[]{:S(2)}, u32[]{:S(2)}) %all-to-all-start.4) | async-done | bytes 1048608 | tf_op jit(solution)/shard_map/all_to_all | solution.py:23
  223.0 5.5 %all-to-all-start.5 = ((f32[8,32,128]{2,1,0:T(8,128)}), f32[8,32,128]{2,1,0:T(8,128)S(1)}, u32[]{:S(2)}, u32[]{:S(2)}) async-start(f32[8,32,128]{2,1,0:T(8,128)} %bitcast.20), calls=%async_computation.5 | async-start | bytes 262144 | tf_op jit(solution)/shard_map/all_to_all | solution.py:23
  228.5 4.9 %shard_map.222.outs = bf16[64,80,128]{2,1,0:T(8,128)(2,1)} custom-call(s32[1]{0:T(128)} %bitcast.index, bf16[640,768]{1,0:T(8,128)(2,1)} %constant_dynamic-update-slice_fusion.7.hidden, s32[640,1]{1,0:T(8,128)S(1)} %copy-done, bf16[768,512]{1,0:T(8,128)(2,1)S(1)} %bitcast.70, bf16[768,512]{1,0:T(8,128)(2,1)} %collective-permute-done.2.refs_1_.second_other), custom_call_target="tpu_custom_call" | custom-call | tf_op jit(solution)/shard_map/pallas_call | solution.py:41
  236.0 7.5 %shard_map.223 = (bf16[64,160,128]{2,1,0:T(8,128)(2,1)}, f32[1,1024]{1,0:T(1,128)S(1)}) custom-call(s32[1]{0:T(128)} %bitcast.index, bf16[640,1536]{1,0:T(8,128)(2,1)} %all-gather.4.cloned.1.call-done.pre_grad, s32[640,1]{1,0:T(8,128)S(1)} %copy-done, bf16[512,1536]{1,0:T(8,128)(2,1)} %bitcast.75, bf16[640,1024]{1,0:T(8,128)(2,1)} %get-tuple-element.37.rows, ...), custom_call_target="tpu_custom_call" | custom-call | tf_op jit(solution)/shard_map/pallas_call | solution.py:41
  245.9 5.3 %all-to-all-start.6 = ((bf16[32,64,128]{2,1,0:T(8,128)(2,1)}), bf16[32,64,128]{2,1,0:T(8,128)(2,1)S(1)}, u32[]{:S(2)}, u32[]{:S(2)}) async-start(bf16[32,64,128]{2,1,0:T(8,128)(2,1)} %broadcast_in_dim.54), calls=%async_computation.6 | async-start | bytes 1048576 | tf_op jit(solution)/shard_map/all_to_all | solution.py:23
  251.1 4.3 %convolution_convert_fusion = bf16[512,1536]{1,0:T(8,128)(2,1)} fusion(bf16[640,1536]{1,0:T(8,128)(2,1)} %all-gather.4.cloned.1.call-done.pre_grad, bf16[640,1024]{1,0:T(8,128)(2,1)} %get-tuple-element.37.rows), kind=kOutput, calls=%fused_computation.3 | convolution fusion | flops 1007419392 | bytes 4194304 | tf_op jit(solution)/shard_map/dot_general | solution.py:27
  255.5 11.1 %all-to-all-done.6 = bf16[32,64,128]{2,1,0:T(8,128)(2,1)S(1)} async-done(((bf16[32,64,128]{2,1,0:T(8,128)(2,1)}), bf16[32,64,128]{2,1,0:T(8,128)(2,1)S(1)}, u32[]{:S(2)}, u32[]{:S(2)}) %all-to-all-start.6) | async-done | bytes 524320 | tf_op jit(solution)/shard_map/all_to_all | solution.py:23
  266.6 8.2 %all-to-all-start.7 = ((bf16[64,160,128]{2,1,0:T(8,128)(2,1)}), bf16[64,160,128]{2,1,0:T(8,128)(2,1)}, u32[]{:S(2)}, u32[]{:S(2)}) async-start(bf16[64,160,128]{2,1,0:T(8,128)(2,1)} %get-tuple-element.45), calls=%async_computation.7 | async-start | bytes 5242880 | tf_op jit(solution)/shard_map/all_to_all | solution.py:23
  277.9 3.2 add_convert_fusion
  281.1 55.0 %collective-permute-done.11 = bf16[512,1536]{1,0:T(8,128)(2,1)} collective-permute-done((bf16[512,1536]{1,0:T(8,128)(2,1)}, bf16[512,1536]{1,0:T(8,128)(2,1)}, u32[]{:S(2)}, u32[]{:S(2)}) %collective-permute-start.11) | collective-permute-done | bytes 1572896 | tf_op jit(solution)/shard_map/ppermute | solution.py:292
  336.1 4.0 %fusion.1 = bf16[512,1536]{1,0:T(8,128)(2,1)} fusion(bf16[512,1536]{1,0:T(8,128)(2,1)} %collective-permute-done.11, bf16[640,1536]{1,0:T(8,128)(2,1)S(1)} %copy-done.21, bf16[640,1024]{1,0:T(8,128)(2,1)S(1)} %copy-done.22), kind=kOutput, calls=%fused_computation.4 | convolution fusion | flops 1008992256 | bytes 5767168 | tf_op jit(solution)/shard_map/dot_general | solution.py:27
  342.5 5.3 %shard_map.224 = bf16[128,4096]{1,0:T(8,128)(2,1)S(1)} custom-call(bf16[64,160,128]{2,1,0:T(8,128)(2,1)} %all-to-all-done.7.returned, bf16[128,4096]{1,0:T(8,128)(2,1)} %bitcast.77, f32[128,128]{1,0:T(8,128)S(1)} %get-tuple-element.42.gates, f32[128,128]{1,0:T(8,128)S(1)} %get-tuple-element.28.place, s32[1,1280]{1,0:T(1,128)S(1)} %copy-done.14, ...), custom_call_target="tpu_custom_call" | custom-call | tf_op jit(solution)/shard_map/pallas_call | solution.py:41
  347.9 5.5 %shard_map.225 = bf16[128,4096]{1,0:T(8,128)(2,1)S(1)} custom-call(bf16[64,160,128]{2,1,0:T(8,128)(2,1)} %all-to-all-done.7.returned, bf16[128,4096]{1,0:T(8,128)(2,1)} %bitcast.78, bf16[128,4096]{1,0:T(8,128)(2,1)} %bitcast.82, f32[1,4096]{1,0:T(1,128)S(1)} %copy-done.10, bf16[4096,128]{1,0:T(8,128)(2,1)} %bitcast.80, ...), custom_call_target="tpu_custom_call" | custom-call | tf_op jit(solution)/shard_map/pallas_call | solution.py:41
  (141 shorter events, 60.0 us)
Async XLA Ops:
  8.2 12.4 %collective-permute-start = (bf16[128,1536]{1,0:T(8,128)(2,1)S(1)}, bf16[128,1536]{1,0:T(8,128)(2,1)S(1)}, u32[]{:S(2)}, u32[]{:S(2)}) collective-permute-start(bf16[128,1536]{1,0:T(8,128)(2,1)S(1)} %slice_bitcast_fusion.1), channel_id=1, source_target_pairs={{0,4},{4,0},{1,5},{5,1},{2,6},{6,2},{3,7},{7,3},{8,12},{12,8},{9,1... | collective-permute-start | bytes 1179656 | tf_op jit(solution)/shard_map/ppermute | solution.py:292
  20.6 73.5 %copy-start.5 = (bf16[128,1536]{1,0:T(8,128)(2,1)}, bf16[128,1536]{1,0:T(8,128)(2,1)S(1)}, u32[]{:S(2)}) copy-start(bf16[128,1536]{1,0:T(8,128)(2,1)S(1)} %collective-permute-done.refs_1_.refs_0_) | copy-start | bytes 1179652
  20.6 51.2 %all-to-all-start = ((bf16[64,80,128]{2,1,0:T(8,128)(2,1)}), bf16[64,80,128]{2,1,0:T(8,128)(2,1)}, u32[]{:S(2)}, u32[]{:S(2)}) async-start(bf16[64,80,128]{2,1,0:T(8,128)(2,1)} %get-tuple-element.31), calls=%async_computation | async-start | bytes 2621440 | tf_op jit(solution)/shard_map/all_to_all | solution.py:23
  35.2 36.6 %collective-permute-start.1 = (bf16[320,1536]{1,0:T(8,128)(2,1)S(1)}, bf16[320,1536]{1,0:T(8,128)(2,1)S(1)}, u32[]{:S(2)}, u32[]{:S(2)}) collective-permute-start(bf16[320,1536]{1,0:T(8,128)(2,1)S(1)} %slice_bitcast_fusion), channel_id=1, source_target_pairs={{0,4},{4,0},{1,5},{5,1},{2,6},{6,2},{3,7},{7,3},{8,12},{12,8},{9,1... | collective-permute-start | bytes 2949128 | tf_op jit(solution)/shard_map/ppermute | solution.py:292
  43.7 50.4 %copy-start = (s32[640,1]{1,0:T(8,128)S(1)}, s32[640,1]{1,0:T(8,128)}, u32[]{:S(2)}) copy-start(s32[640,1]{1,0:T(8,128)} %constant.109.clone.order) | copy-start | bytes 7684
  71.8 63.5 %all-to-all-start.1 = ((bf16[64,80,128]{2,1,0:T(8,128)(2,1)}), bf16[64,80,128]{2,1,0:T(8,128)(2,1)}, u32[]{:S(2)}, u32[]{:S(2)}) async-start(bf16[64,80,128]{2,1,0:T(8,128)(2,1)} %get-tuple-element.32), calls=%async_computation.1 | async-start | bytes 2621440 | tf_op jit(solution)/shard_map/all_to_all | solution.py:23
  83.0 11.1 %collective-permute-start.3 = (bf16[64,1536]{1,0:T(8,128)(2,1)S(1)}, bf16[64,1536]{1,0:T(8,128)(2,1)S(1)}, u32[]{:S(2)}, u32[]{:S(2)}) collective-permute-start(bf16[64,1536]{1,0:T(8,128)(2,1)S(1)} %slice_bitcast_fusion.2), channel_id=1, source_target_pairs={{0,4},{4,0},{1,5},{5,1},{2,6},{6,2},{3,7},{7,3},{8,12},{12,8},{9,1... | collective-permute-start | bytes 589832 | tf_op jit(solution)/shard_map/ppermute | solution.py:292
  105.2 16.2 %collective-permute-start.4 = (bf16[160,1536]{1,0:T(8,128)(2,1)}, bf16[160,1536]{1,0:T(8,128)(2,1)}, u32[]{:S(2)}, u32[]{:S(2)}) collective-permute-start(bf16[160,1536]{1,0:T(8,128)(2,1)} %get-tuple-element.52), channel_id=1, source_target_pairs={{0,1},{1,2},{2,3},{3,0},{4,5},{5,6},{6,7},{7,4},{8,9},{9,10},{10,1... | collective-permute-start | bytes 1474568 | tf_op jit(solution)/shard_map/ppermute | solution.py:384
  106.7 15.6 %collective-permute-start.6 = (bf16[160,1536]{1,0:T(8,128)(2,1)}, bf16[160,1536]{1,0:T(8,128)(2,1)}, u32[]{:S(2)}, u32[]{:S(2)}) collective-permute-start(bf16[160,1536]{1,0:T(8,128)(2,1)} %get-tuple-element.53), channel_id=1, source_target_pairs={{0,3},{1,0},{2,1},{3,2},{4,7},{5,4},{6,5},{7,6},{8,11},{9,8},{10,9... | collective-permute-start | bytes 1474568 | tf_op jit(solution)/shard_map/ppermute | solution.py:384
  107.2 25.4 %collective-permute-start.5 = (bf16[160,1536]{1,0:T(8,128)(2,1)}, bf16[160,1536]{1,0:T(8,128)(2,1)}, u32[]{:S(2)}, u32[]{:S(2)}) collective-permute-start(bf16[160,1536]{1,0:T(8,128)(2,1)} %get-tuple-element.54), channel_id=1, source_target_pairs={{0,2},{1,3},{2,0},{3,1},{4,6},{5,7},{6,4},{7,5},{8,10},{9,11},{10,... | collective-permute-start | bytes 1474568 | tf_op jit(solution)/shard_map/ppermute | solution.py:384
  109.5 25.8 %collective-permute-start.2 = (bf16[768,512]{1,0:T(8,128)(2,1)S(1)}, bf16[768,512]{1,0:T(8,128)(2,1)}, u32[]{:S(2)}, u32[]{:S(2)}) collective-permute-start(bf16[768,512]{1,0:T(8,128)(2,1)S(1)} %bitcast.68), channel_id=1, source_target_pairs={{0,4},{4,0},{1,5},{5,1},{2,6},{6,2},{3,7},{7,3},{8,12},{12,8},{9,1... | collective-permute-start | bytes 2359304 | tf_op jit(solution)/shard_map/ppermute | solution.py:292
  140.9 29.0 %all-to-all-start.2 = ((bf16[4,160,768]{2,1,0:T(8,128)(2,1)}), bf16[4,160,768]{2,1,0:T(8,128)(2,1)S(1)}, u32[]{:S(2)}, u32[]{:S(2)}) async-start(bf16[4,160,768]{2,1,0:T(8,128)(2,1)} %bitcast.92), calls=%async_computation.2 | async-start | bytes 1966080 | tf_op jit(solution)/shard_map/all_to_all | solution.py:23
  146.9 23.0 %copy-start.17 = (s32[1,160]{1,0:T(1,128)S(1)}, s32[1,160]{1,0:T(1,128)}, u32[]{:S(2)}) copy-start(s32[1,160]{1,0:T(1,128)} %constant.110.clone.sender_of) | copy-start | bytes 1924
  148.7 14.8 %collective-permute-start.7 = (bf16[160,768]{1,0:T(8,128)(2,1)}, bf16[160,768]{1,0:T(8,128)(2,1)}, u32[]{:S(2)}, u32[]{:S(2)}) collective-permute-start(bf16[160,768]{1,0:T(8,128)(2,1)} %get-tuple-element.51.hidden), channel_id=1, source_target_pairs={{0,1},{1,2},{2,3},{3,0},{4,5},{5,6},{6,7},{7,4},{8,9},{9,10},{10,1... | collective-permute-start | bytes 737288 | tf_op jit(solution)/shard_map/ppermute | solution.py:398
  150.2 15.4 %collective-permute-start.8 = (bf16[160,768]{1,0:T(8,128)(2,1)}, bf16[160,768]{1,0:T(8,128)(2,1)}, u32[]{:S(2)}, u32[]{:S(2)}) collective-permute-start(bf16[160,768]{1,0:T(8,128)(2,1)} %get-tuple-element.51.hidden), channel_id=1, source_target_pairs={{0,2},{1,3},{2,0},{3,1},{4,6},{5,7},{6,4},{7,5},{8,10},{9,11},{10,... | collective-permute-start | bytes 737288 | tf_op jit(solution)/shard_map/ppermute | solution.py:398
  150.8 17.4 %collective-permute-start.9 = (bf16[160,768]{1,0:T(8,128)(2,1)}, bf16[160,768]{1,0:T(8,128)(2,1)}, u32[]{:S(2)}, u32[]{:S(2)}) collective-permute-start(bf16[160,768]{1,0:T(8,128)(2,1)} %get-tuple-element.51.hidden), channel_id=1, source_target_pairs={{0,3},{1,0},{2,1},{3,2},{4,7},{5,4},{6,5},{7,6},{8,11},{9,8},{10,9... | collective-permute-start | bytes 737288 | tf_op jit(solution)/shard_map/ppermute | solution.py:398
  173.3 15.1 %all-to-all-start.3 = ((f32[16,1,128]{2,1,0:T(1,128)}), f32[16,1,128]{2,1,0:T(1,128)S(1)}, u32[]{:S(2)}, u32[]{:S(2)}) async-start(f32[16,1,128]{2,1,0:T(1,128)} %bitcast.17), calls=%async_computation.3 | async-start | bytes 16384 | tf_op jit(solution)/shard_map/all_to_all | solution.py:23
  180.0 56.0 %all-gather.4.cloned.1.call-start = ((), (), s32[]{:S(2)}) async-start(), calls=%async_computation.8 | async-start | bytes 2457600 | tf_op jit(solution)/shard_map/all_gather | solution.py:410
  190.7 37.8 %copy-start.2 = (bf16[1,1,768,512]{3,2,1,0:T(8,128)(2,1)S(1)}, bf16[1,1,768,512]{3,2,1,0:T(8,128)(2,1)}, u32[]{:S(2)}) copy-start(bf16[1,1,768,512]{3,2,1,0:T(8,128)(2,1)} %param.24) | copy-start | bytes 2359300
  190.7 30.2 %all-to-all-start.4 = ((bf16[16,256,128]{2,1,0:T(8,128)(2,1)}), bf16[16,256,128]{2,1,0:T(8,128)(2,1)}, u32[]{:S(2)}, u32[]{:S(2)}) async-start(bf16[16,256,128]{2,1,0:T(8,128)(2,1)} %bitcast.84), calls=%async_computation.4 | async-start | bytes 2097152 | tf_op jit(solution)/shard_map/all_to_all | solution.py:23
  195.2 38.2 %collective-permute-start.10 = (bf16[768,512]{1,0:T(8,128)(2,1)}, bf16[768,512]{1,0:T(8,128)(2,1)}, u32[]{:S(2)}, u32[]{:S(2)}) collective-permute-start(bf16[768,512]{1,0:T(8,128)(2,1)} %convolution_convert_fusion.1), channel_id=1, source_target_pairs={{0,4},{4,0},{1,5},{5,1},{2,6},{6,2},{3,7},{7,3},{8,12},{12,8},{9,1... | collective-permute-start | bytes 2359304 | tf_op jit(solution)/shard_map/ppermute | solution.py:292
  223.0 12.1 %all-to-all-start.5 = ((f32[8,32,128]{2,1,0:T(8,128)}), f32[8,32,128]{2,1,0:T(8,128)S(1)}, u32[]{:S(2)}, u32[]{:S(2)}) async-start(f32[8,32,128]{2,1,0:T(8,128)} %bitcast.20), calls=%async_computation.5 | async-start | bytes 262144 | tf_op jit(solution)/shard_map/all_to_all | solution.py:23
  228.5 7.5 %copy-start.6 = (bf16[128,1536]{1,0:T(8,128)(2,1)S(1)}, bf16[128,1536]{1,0:T(8,128)(2,1)}, u32[]{:S(2)}) copy-start(bf16[128,1536]{1,0:T(8,128)(2,1)} %copy-done.5) | copy-start | bytes 1179652
  228.5 7.5 %copy-start.8 = (bf16[64,1536]{1,0:T(8,128)(2,1)S(1)}, bf16[64,1536]{1,0:T(8,128)(2,1)}, u32[]{:S(2)}) copy-start(bf16[64,1536]{1,0:T(8,128)(2,1)} %copy-done.7) | copy-start | bytes 589828
  245.9 20.7 %all-to-all-start.6 = ((bf16[32,64,128]{2,1,0:T(8,128)(2,1)}), bf16[32,64,128]{2,1,0:T(8,128)(2,1)S(1)}, u32[]{:S(2)}, u32[]{:S(2)}) async-start(bf16[32,64,128]{2,1,0:T(8,128)(2,1)} %broadcast_in_dim.54), calls=%async_computation.6 | async-start | bytes 1048576 | tf_op jit(solution)/shard_map/all_to_all | solution.py:23
  266.6 75.9 %all-to-all-start.7 = ((bf16[64,160,128]{2,1,0:T(8,128)(2,1)}), bf16[64,160,128]{2,1,0:T(8,128)(2,1)}, u32[]{:S(2)}, u32[]{:S(2)}) async-start(bf16[64,160,128]{2,1,0:T(8,128)(2,1)} %get-tuple-element.45), calls=%async_computation.7 | async-start | bytes 5242880 | tf_op jit(solution)/shard_map/all_to_all | solution.py:23
  274.7 65.3 %all-gather.6.cloned.1.call-start = ((), (), s32[]{:S(2)}) async-start(), calls=%async_computation.9 | async-start | bytes 1372160 | tf_op jit(solution)/shard_map/all_gather | solution.py:487
  274.8 61.3 %collective-permute-start.11 = (bf16[512,1536]{1,0:T(8,128)(2,1)}, bf16[512,1536]{1,0:T(8,128)(2,1)}, u32[]{:S(2)}, u32[]{:S(2)}) collective-permute-start(bf16[512,1536]{1,0:T(8,128)(2,1)} %convolution_convert_fusion), channel_id=1, source_target_pairs={{0,4},{4,0},{1,5},{5,1},{2,6},{6,2},{3,7},{7,3},{8,12},{12,8},{9,1... | collective-permute-start | bytes 4718600 | tf_op jit(solution)/shard_map/ppermute | solution.py:292
  277.9 58.2 %copy-start.21 = (bf16[640,1536]{1,0:T(8,128)(2,1)S(1)}, bf16[640,1536]{1,0:T(8,128)(2,1)}, u32[]{:S(2)}) copy-start(bf16[640,1536]{1,0:T(8,128)(2,1)} %all-gather.4.cloned.1.call-done.pre_grad) | copy-start | bytes 5898244
  277.9 58.2 %copy-start.22 = (bf16[640,1024]{1,0:T(8,128)(2,1)S(1)}, bf16[640,1024]{1,0:T(8,128)(2,1)}, u32[]{:S(2)}) copy-start(bf16[640,1024]{1,0:T(8,128)(2,1)} %get-tuple-element.37.rows) | copy-start | bytes 3932164
  347.8 8.0 %collective-permute-start.12 = (bf16[128,4096]{1,0:T(8,128)(2,1)S(1)}, bf16[128,4096]{1,0:T(8,128)(2,1)}, u32[]{:S(2)}, u32[]{:S(2)}) collective-permute-start(bf16[128,4096]{1,0:T(8,128)(2,1)S(1)} %shard_map.224), channel_id=1, source_target_pairs={{0,128},{128,0},{1,129},{129,1},{2,130},{130,2},{3,131},{131,3},{4... | collective-permute-start | bytes 3145736 | tf_op jit(solution)/shard_map/ppermute | solution.py:292
  353.4 2.9 collective-permute-start.13
  (16 other events, 36.7 us)
Sparse Core Ops, SparseCore 0:
  183.3 34.0 all-gather.3
  278.0 31.6 all-gather.5

commit v7 on v6

--- a/solution.py
+++ b/solution.py
@@ -158,7 +158,12 @@
                     rows_out[rows, c * LANES : (c + 1) * LANES] = own[:, lanes]
                     rows_out[rows, part + c * LANES : part + (c + 1) * LANES] = other[:, lanes]
 
-    weight = jnp.concatenate([piece[...] for piece in weights], axis=side)
+    if side == 0:
+        weight = jnp.concatenate([piece[...] for piece in weights], axis=0)
+    else:
+        last = pl.program_id(0) == pl.num_programs(0) - 1
+        own, early, late = weights
+        weight = jnp.concatenate([own[...], jnp.where(last, late[...], early[...])], axis=1)
     partial[...] = mm(rows_out[...], weight, ((1,), (side,))).astype(BF)
 
 
@@ -209,9 +214,9 @@
             )
 
 
-def out_kernel(group, chunks, slots, index, hidden, order, second, second_other, message):
+def out_kernel(group, chunks, slots, index, hidden, order, second, early, late, message):
     own = mm(hidden[...], second[...])
-    other = mm(hidden[...], second_other[...])
+    other = mm(hidden[...], jnp.concatenate([early[...], late[...]], axis=0))
     return_rows(group, chunks, slots, index[0] == 0, order, own, other, message)
 
 
@@ -317,7 +322,10 @@
     index = side.astype(jnp.int32)[None]
     cuts = (0, part // 4, 7 * part // 8, part)
     first_other = tuple(swapped(first[a:b], "half") for a, b in zip(cuts, cuts[1:]))
-    second_other = swapped(second, "half")
+    step_width = hidden_width // HIDDEN_STEPS
+    cut = hidden_width - step_width
+    second_early = swapped(second[:cut], "half")
+    second_other = (second_early, swapped(after(second[cut:], second_early), "half"))
 
     at = np.arange(experts * half, dtype=np.int32)
     owner, chunk_of, slot_of = (at // half)[None], at % half // slots, (at % slots)[None]
@@ -348,7 +356,6 @@
     into_messages = (at % half // slots * group + at // half) * slots + at % slots
     into_rows = np.zeros_like(at)
     into_rows[into_messages] = at
-    step_width = hidden_width // HIDDEN_STEPS
     all_rows = peers * slots
     whole = lambda shape: pl.BlockSpec(shape, lambda i: (0,) * len(shape))
     scalar = pl.BlockSpec(memory_space=pltpu.SMEM)
@@ -377,27 +384,31 @@
     )
     partial = partial.reshape(replicas, rows, 2 * hidden_width)
     place_in_dp = lax.axis_index("dp")
-    pre_act = lax.dynamic_index_in_dim(partial, place_in_dp, 0, False).astype(F32)
+    terms = [lax.dynamic_index_in_dim(partial, place_in_dp, 0, False)]
     for step in range(1, replicas):
         shift = [(j, (j + step) % replicas) for j in range(replicas)]
         block = lax.dynamic_index_in_dim(partial, (place_in_dp + step) % replicas, 0, False)
-        pre_act = pre_act + lax.ppermute(block, "dp", shift).astype(F32)
+        terms.append(lax.ppermute(block, "dp", shift))
     partial, grad_rows = products(
         arrived_grad,
-        (second, second_other),
+        (second,) + second_other,
         1,
         HIDDEN_STEPS,
-        [pl.BlockSpec((step_width, part), lambda i: (i, 0))] * 2,
-    )
+        [
+            pl.BlockSpec((step_width, part), lambda i: (i, 0)),
+            pl.BlockSpec((step_width, part), lambda i: (jnp.minimum(i, HIDDEN_STEPS - 2), 0)),
+            whole((step_width, part)),
+        ],
+    )
+    terms = [after(term, partial) for term in terms]
     summands = exchange(partial.reshape(replicas, rows, hidden_width), "dp")
+    pre_act = sum(term.astype(F32) for term in terms)
     gate_pre, up = pre_act[:, :hidden_width], pre_act[:, hidden_width:]
     hidden = (gate_pre / (1.0 + jnp.exp(-gate_pre)) * up).astype(BF)
-    hidden_all = jnp.zeros((all_rows, hidden_width), BF)
-    for step in range(replicas):
+    hidden_blocks = [hidden]
+    for step in range(1, replicas):
         shift = [(j, (j + step) % replicas) for j in range(replicas)]
-        block = lax.ppermute(hidden, "dp", shift) if step else hidden
-        at_row = (place_in_dp + replicas - step) % replicas * rows
-        hidden_all = lax.dynamic_update_slice(hidden_all, block, (at_row, 0))
+        hidden_blocks.append(lax.ppermute(hidden, "dp", shift))
     at = np.arange(rows, dtype=np.int32)
     pre_grad, worth = kernel_call(
         functools.partial(act_kernel, slots),
@@ -408,6 +419,11 @@
         (summands, pre_act, hidden, at[None] // slots, at[:, None] % slots),
     )
     pre_grad_all = lax.all_gather(pre_grad, "dp", axis=0, tiled=True)
+    hidden_blocks = [after(block, worth) for block in hidden_blocks]
+    hidden_all = jnp.zeros((all_rows, hidden_width), BF)
+    for step, block in enumerate(hidden_blocks):
+        at_row = (place_in_dp + replicas - step) % replicas * rows
+        hidden_all = lax.dynamic_update_slice(hidden_all, block, (at_row, 0))
 
     worth = exchange(worth[:, None], "expert")[:, 0, :slots]
     slot_ids = jnp.arange(slots, dtype=F32)
@@ -422,14 +438,6 @@
     second_other_grad = mm(hidden_all, grad_rows[:, part:], ((0,), (0,))).astype(BF)
     second_sent = swapped(second_other_grad, "half")
     local_router = after(local_router, second_other_grad)
-    router_part = jnp.sum(exchange(local_router, "expert").astype(F32), axis=0)
-    piece = router_part.shape[0] // (2 * replicas)
-    router_part = router_part.reshape(2 * replicas, piece, router_width)
-    router_own = jnp.sum(exchange(router_part, ("half", "dp")), axis=0)
-    at = lax.axis_index("expert") * 2 * replicas + side * replicas + place_in_dp
-    table_own = lax.dynamic_slice_in_dim(table, at * piece, piece, axis=0).astype(F32)
-    gain_own = jnp.sum(router_own * table_own, axis=1)
-
     steps = 2 if all_rows // 2 % (2 * group * slots) == 0 else 1
 
     def by_rows(width):
@@ -440,11 +448,17 @@
     out_message = kernel_call(
         functools.partial(out_kernel, group, chunks, slots),
         message_shape,
-        (index, hidden_all, order, second, second_other),
+        (index, hidden_all, order, second) + second_other,
         grid=(steps,),
-        in_specs=[scalar, by_rows(hidden_width), whole(order.shape), whole(second.shape), whole(second.shape)],
+        in_specs=[scalar, by_rows(hidden_width), whole(order.shape), whole(second.shape)]
+        + [whole(piece.shape) for piece in second_other],
         out_specs=messages,
     )
+    summed = exchange(local_router, "expert")
+    router_part = jnp.sum(after(summed, out_message).astype(F32), axis=0)
+    piece = router_part.shape[0] // (2 * replicas)
+    router_part = exchange(router_part.reshape(2 * replicas, piece, router_width), ("half", "dp"))
+
     message, gain_part = kernel_call(
         functools.partial(back_kernel, group, chunks, slots),
         (jax.ShapeDtypeStruct((peers, 2 * half, LANES), BF), jax.ShapeDtypeStruct((1, 2 * part), F32)),
@@ -464,6 +478,10 @@
             whole((1, 2 * part)),
         ],
     )
+    router_own = jnp.sum(after(router_part, gain_part), axis=0)
+    at = lax.axis_index("expert") * 2 * replicas + side * replicas + place_in_dp
+    table_own = lax.dynamic_slice_in_dim(table, at * piece, piece, axis=0).astype(F32)
+    gain_own = jnp.sum(router_own * table_own, axis=1)
     gain_part = gain_part.reshape(2, part)
     gain_part = jnp.where(side == 0, gain_part, gain_part[::-1])
 
@@ -505,13 +523,13 @@
     layer_out = kernel_call(
         functools.partial(layer_kernel, experts, replicas, chunks),
         token_shape,
-        (returned, after(x, first_grad, second_grad), gates, place, owner, chunk_of[None], slot_of),
+        (returned, after(x, second_grad), gates, place, owner, chunk_of[None], slot_of),
         [joined_scratch],
     )
     in_grad = kernel_call(
         functools.partial(in_grad_kernel, experts, replicas, chunks),
         token_shape,
-        (returned, x, grad_top, gain, table, place, logit_grad, owner, chunk_of[None], slot_of),
+        (returned, after(x, first_sent), grad_top, gain, table, place, logit_grad, owner, chunk_of[None], slot_of),
         [joined_scratch, pltpu.VMEM((tokens, width), F32)],
     )
     handoff = swapped(layer_out, "section")

time: 370 us -> 336 us (0.908)
  waiting for transfers between devices: 168 us -> 132 us
  starting transfers between devices: 81.3 us -> 87.6 us
    ppermute x6, waiting for transfers between devices: 33.5 us -> 0.02 us  [the longest x3 0.01 us: shards(): terms.append(lax.ppermute(block, 'dp', shift))]
    all_to_all x8, waiting for transfers between devices: 41.8 us -> 33.7 us  [exchange(): return lax.all_to_all(blocks, axes, split_axis=0, concat_axis=0, tiled=True)]
    ppermute x8 -> x9, waiting for transfers between devices: 92.9 us -> 98.3 us  [swapped(): return lax.ppermute(block, axis, [(0, 1), (1, 0)])]
    all_to_all x8, starting transfers between devices: 58.4 us -> 62.7 us  [exchange(): return lax.all_to_all(blocks, axes, split_axis=0, concat_axis=0, tiled=True)]
    ppermute x8 -> x9, starting transfers between devices: 13.9 us -> 15.2 us  [swapped(): return lax.ppermute(block, axis, [(0, 1), (1, 0)])]
    unnamed x52 -> x72, local copies, waits for them, and re-layouts: 11.6 us -> 12.7 us
  transfers between devices with their start and end apart: 24 -> 25, of which waited for: 15 -> 11; matrix products, arithmetic and copies ran while one was open for 10% -> 10% of each run, Pallas kernels for 8% -> 13%
where the time goes in v7:
time: 336 us; the launch traced here: 332 us
  waiting for transfers between devices  132 us (39%)
  starting transfers between devices  87.6 us (26%)
  Pallas kernels  49.1 us (15%)
  local copies, waits for them, and re-layouts  28.1 us (8%)
  matrix products  14.9 us (4%)
  between operations  14.6 us (4%)
  other arithmetic  6.07 us (2%)
    ppermute x9, waiting for transfers between devices, swapped(): return lax.ppermute(block, axis, [(0, 1), (1, 0)])  98.3 us
    all_to_all x8, starting transfers between devices, exchange(): return lax.all_to_all(blocks, axes, split_axis=0, concat_axis=0, tiled=True)  62.7 us
    pallas_call x9, Pallas kernels, kernel_call(): pl.pallas_call(body, out_shape=outs, scratch_shapes=scratch, compiler_par...  49.1 us
    all_to_all x8, waiting for transfers between devices, exchange(): return lax.all_to_all(blocks, axes, split_axis=0, concat_axis=0, tiled=True)  33.7 us
    ppermute x9, starting transfers between devices, swapped(): return lax.ppermute(block, axis, [(0, 1), (1, 0)])  15.2 us
    dot_general x6, matrix products, mm(): lax.dot_general(left, right, (contract, ((), ())), preferred_element_type...  14.9 us
    unnamed x72, local copies, waits for them, and re-layouts  12.7 us
  transfers between devices with their start and end apart: 25, of which 11 were waited for; matrix products, arithmetic and copies ran while one was open for 10% of the time, Pallas kernels for 13%

profile of v7, /device:TPU:8, one launch (start us, length us, event | category | flops | bytes accessed | tf_op | source)
XLA Modules:
  0.0 332.3 jit_solution(2672942850954850862)
XLA Ops:
  8.2 3.1 collective-permute-start
  15.3 5.0 %shard_map.217 = (bf16[64,80,128]{2,1,0:T(8,128)(2,1)}, bf16[128,4096]{1,0:T(8,128)(2,1)S(1)}, f32[128,128]{1,0:T(8,128)S(1)}) custom-call(bf16[128,4096]{1,0:T(8,128)(2,1)} %bitcast.80, s32[128,8]{1,0:T(8,128)S(1)} %bitcast.75, f32[1,4096]{1,0:T(1,128)S(1)} %copy-done.15, s32[1,1280]{1,0:T(1,128)S(1)} %copy-done.19, s32[1280,1]{1,0:T(8,128)S(1)} %copy-done.4, ...), custom_call_target="tpu_custom_call" | custom-call | tf_op jit(solution)/shard_map/pallas_call | solution.py:41
  20.6 13.2 %all-to-all-start = ((bf16[64,80,128]{2,1,0:T(8,128)(2,1)}), bf16[64,80,128]{2,1,0:T(8,128)(2,1)}, u32[]{:S(2)}, u32[]{:S(2)}) async-start(bf16[64,80,128]{2,1,0:T(8,128)(2,1)} %get-tuple-element.43), calls=%async_computation | async-start | bytes 2621440 | tf_op jit(solution)/shard_map/all_to_all | solution.py:23
  34.0 2.8 collective-permute-start.1
  36.8 5.7 %shard_map.218 = (bf16[64,80,128]{2,1,0:T(8,128)(2,1)}, f32[128,128]{1,0:T(8,128)S(1)}) custom-call(bf16[128,4096]{1,0:T(8,128)(2,1)S(1)} %get-tuple-element.39.normed, s32[128,8]{1,0:T(8,128)S(1)} %bitcast.76, bf16[128,4096]{1,0:T(8,128)(2,1)} %bitcast.85, bf16[4096,128]{1,0:T(8,128)(2,1)} %bitcast.83, f32[128,128]{1,0:T(8,128)S(1)} %get-tuple-element.40.place, ...), custom_call_target="tpu_custom_call" | custom-call | tf_op jit(solution)/shard_map/pallas_call | solution.py:41
  43.2 27.5 %collective-permute-done.1.refs_2_.refs_1_ = bf16[320,1536]{1,0:T(8,128)(2,1)S(1)} collective-permute-done((bf16[320,1536]{1,0:T(8,128)(2,1)S(1)}, bf16[320,1536]{1,0:T(8,128)(2,1)S(1)}, u32[]{:S(2)}, u32[]{:S(2)}) %collective-permute-start.1) | collective-permute-done | bytes 983072 | tf_op jit(solution)/shard_map/ppermute | solution.py:297
  70.6 11.0 %all-to-all-start.1 = ((bf16[64,80,128]{2,1,0:T(8,128)(2,1)}), bf16[64,80,128]{2,1,0:T(8,128)(2,1)}, u32[]{:S(2)}, u32[]{:S(2)}) async-start(bf16[64,80,128]{2,1,0:T(8,128)(2,1)} %get-tuple-element.44), calls=%async_computation.1 | async-start | bytes 2621440 | tf_op jit(solution)/shard_map/all_to_all | solution.py:23
  83.3 2.5 collective-permute-start.4
  87.7 8.3 %collective-permute-done.4.refs_3_.refs_2_ = bf16[64,1536]{1,0:T(8,128)(2,1)} collective-permute-done((bf16[64,1536]{1,0:T(8,128)(2,1)}, bf16[64,1536]{1,0:T(8,128)(2,1)}, u32[]{:S(2)}, u32[]{:S(2)}) %collective-permute-start.4) | collective-permute-done | bytes 196640 | tf_op jit(solution)/shard_map/ppermute | solution.py:297
  96.0 7.9 %shard_map.220 = (bf16[640,1536]{1,0:T(8,128)(2,1)}, bf16[640,1024]{1,0:T(8,128)(2,1)}) custom-call(s32[1]{0:T(128)} %bitcast.index, bf16[64,80,128]{2,1,0:T(8,128)(2,1)} %all-to-all-done.arrived, s32[640,1]{1,0:T(8,128)S(1)} %copy-done.1, bf16[512,1536]{1,0:T(8,128)(2,1)} %bitcast.78, bf16[128,1536]{1,0:T(8,128)(2,1)S(1)} %collective-permute-done.refs_1_.refs_0_, ...), custom_call_target="tpu_custom_call" | custom-call | tf_op jit(solution)/shard_map/pallas_call | solution.py:41
  103.9 2.8 dynamic-slice_bitcast_fusion.3
  107.3 2.4 collective-permute-start.6
  115.3 7.2 %collective-permute-done.3.refs_2_.late = bf16[256,512]{1,0:T(8,128)(2,1)S(1)} collective-permute-done((bf16[256,512]{1,0:T(8,128)(2,1)S(1)}, bf16[256,512]{1,0:T(8,128)(2,1)S(1)}, u32[]{:S(2)}, u32[]{:S(2)}) %collective-permute-start.3) | collective-permute-done | bytes 262176 | tf_op jit(solution)/shard_map/ppermute | solution.py:297
  122.6 5.4 %shard_map.219 = (bf16[640,768]{1,0:T(8,128)(2,1)}, bf16[640,1024]{1,0:T(8,128)(2,1)}) custom-call(s32[1]{0:T(128)} %bitcast.index, bf16[64,80,128]{2,1,0:T(8,128)(2,1)} %all-to-all-done.1.arrived, s32[640,1]{1,0:T(8,128)S(1)} %copy-done.1, bf16[768,512]{1,0:T(8,128)(2,1)S(1)} %bitcast.72, bf16[512,512]{1,0:T(8,128)(2,1)} %collective-permute-done.2.refs_1_.early, ...), custom_call_target="tpu_custom_call" | custom-call | tf_op jit(solution)/shard_map/pallas_call | solution.py:41
  127.9 4.9 %all-to-all-start.2 = ((bf16[4,160,768]{2,1,0:T(8,128)(2,1)}), bf16[4,160,768]{2,1,0:T(8,128)(2,1)S(1)}, u32[]{:S(2)}, u32[]{:S(2)}) async-start(bf16[4,160,768]{2,1,0:T(8,128)(2,1)} %bitcast.95), calls=%async_computation.2 | async-start | bytes 1966080 | tf_op jit(solution)/shard_map/all_to_all | solution.py:23
  140.2 7.1 %all-to-all-done.2.arrived = bf16[4,160,768]{2,1,0:T(8,128)(2,1)S(1)} async-done(((bf16[4,160,768]{2,1,0:T(8,128)(2,1)}), bf16[4,160,768]{2,1,0:T(8,128)(2,1)S(1)}, u32[]{:S(2)}, u32[]{:S(2)}) %all-to-all-start.2) | async-done | bytes 983072 | tf_op jit(solution)/shard_map/all_to_all | solution.py:23
  151.2 7.0 %all-to-all-start.3 = ((f32[16,1,128]{2,1,0:T(1,128)}), f32[16,1,128]{2,1,0:T(1,128)S(1)}, u32[]{:S(2)}, u32[]{:S(2)}) async-start(f32[16,1,128]{2,1,0:T(1,128)} %bitcast.77), calls=%async_computation.3 | async-start | bytes 16384 | tf_op jit(solution)/shard_map/all_to_all | solution.py:23
  164.0 2.6 all-to-all-done.3
  169.0 5.6 %all-to-all-start.4 = ((bf16[16,256,128]{2,1,0:T(8,128)(2,1)}), bf16[16,256,128]{2,1,0:T(8,128)(2,1)S(1)}, u32[]{:S(2)}, u32[]{:S(2)}) async-start(bf16[16,256,128]{2,1,0:T(8,128)(2,1)} %bitcast.88), calls=%async_computation.4 | async-start | bytes 2097152 | tf_op jit(solution)/shard_map/all_to_all | solution.py:23
  176.2 4.8 %shard_map.222.outs = bf16[64,80,128]{2,1,0:T(8,128)(2,1)} custom-call(s32[1]{0:T(128)} %bitcast.index, bf16[640,768]{1,0:T(8,128)(2,1)} %copy-done.27, s32[640,1]{1,0:T(8,128)S(1)} %copy-done.1, bf16[768,512]{1,0:T(8,128)(2,1)S(1)} %bitcast.73, bf16[512,512]{1,0:T(8,128)(2,1)} %collective-permute-done.2.refs_1_.early, bf16[256,512]{1,0:T(8,128)(2,1)S(1)} %copy-done.11), custom_call_target="tpu_custom_call" | custom-call | tf_op jit(solution)/shard_map/pallas_call | solution.py:41
  181.0 14.0 %all-to-all-done.4 = bf16[16,256,128]{2,1,0:T(8,128)(2,1)S(1)} async-done(((bf16[16,256,128]{2,1,0:T(8,128)(2,1)}), bf16[16,256,128]{2,1,0:T(8,128)(2,1)S(1)}, u32[]{:S(2)}, u32[]{:S(2)}) %all-to-all-start.4) | async-done | bytes 1048608 | tf_op jit(solution)/shard_map/all_to_all | solution.py:23
  195.9 5.8 %all-to-all-start.5 = ((f32[8,32,128]{2,1,0:T(8,128)}), f32[8,32,128]{2,1,0:T(8,128)S(1)}, u32[]{:S(2)}, u32[]{:S(2)}) async-start(f32[8,32,128]{2,1,0:T(8,128)} %bitcast.22), calls=%async_computation.5 | async-start | bytes 262144 | tf_op jit(solution)/shard_map/all_to_all | solution.py:23
  201.7 7.8 %shard_map.223 = (bf16[64,160,128]{2,1,0:T(8,128)(2,1)}, f32[1,1024]{1,0:T(1,128)S(1)}) custom-call(s32[1]{0:T(128)} %bitcast.index, bf16[640,1536]{1,0:T(8,128)(2,1)} %all-gather.4.cloned.1.call-done.pre_grad, s32[640,1]{1,0:T(8,128)S(1)} %copy-done.1, bf16[512,1536]{1,0:T(8,128)(2,1)} %bitcast.79, bf16[640,1024]{1,0:T(8,128)(2,1)} %get-tuple-element.54.rows, ...), custom_call_target="tpu_custom_call" | custom-call | tf_op jit(solution)/shard_map/pallas_call | solution.py:41
  212.9 6.8 %all-to-all-start.6 = ((bf16[32,64,128]{2,1,0:T(8,128)(2,1)}), bf16[32,64,128]{2,1,0:T(8,128)(2,1)S(1)}, u32[]{:S(2)}, u32[]{:S(2)}) async-start(bf16[32,64,128]{2,1,0:T(8,128)(2,1)} %broadcast_in_dim.54), calls=%async_computation.6 | async-start | bytes 1048576 | tf_op jit(solution)/shard_map/all_to_all | solution.py:23
  219.7 4.1 %convolution_convert_fusion = bf16[512,1536]{1,0:T(8,128)(2,1)} fusion(bf16[640,1536]{1,0:T(8,128)(2,1)} %all-gather.4.cloned.1.call-done.pre_grad, bf16[640,1024]{1,0:T(8,128)(2,1)S(1)} %copy-done.30), kind=kOutput, calls=%fused_computation.3 | convolution fusion | flops 1007419392 | bytes 4194304 | tf_op jit(solution)/shard_map/dot_general | solution.py:27
  223.8 9.9 %all-to-all-done.6 = bf16[32,64,128]{2,1,0:T(8,128)(2,1)S(1)} async-done(((bf16[32,64,128]{2,1,0:T(8,128)(2,1)}), bf16[32,64,128]{2,1,0:T(8,128)(2,1)S(1)}, u32[]{:S(2)}, u32[]{:S(2)}) %all-to-all-start.6) | async-done | bytes 524320 | tf_op jit(solution)/shard_map/all_to_all | solution.py:23
  233.7 8.3 %all-to-all-start.7 = ((bf16[64,160,128]{2,1,0:T(8,128)(2,1)}), bf16[64,160,128]{2,1,0:T(8,128)(2,1)}, u32[]{:S(2)}, u32[]{:S(2)}) async-start(bf16[64,160,128]{2,1,0:T(8,128)(2,1)} %get-tuple-element.68), calls=%async_computation.7 | async-start | bytes 5242880 | tf_op jit(solution)/shard_map/all_to_all | solution.py:23
  246.9 3.2 add_convert_fusion
  250.0 52.0 %collective-permute-done.13 = bf16[512,1536]{1,0:T(8,128)(2,1)} collective-permute-done((bf16[512,1536]{1,0:T(8,128)(2,1)}, bf16[512,1536]{1,0:T(8,128)(2,1)}, u32[]{:S(2)}, u32[]{:S(2)}) %collective-permute-start.13) | collective-permute-done | bytes 1572896 | tf_op jit(solution)/shard_map/ppermute | solution.py:297
  302.0 4.0 %fusion.2 = bf16[1,1,512,1536]{3,2,1,0:T(8,128)(2,1)} fusion(bf16[512,1536]{1,0:T(8,128)(2,1)} %collective-permute-done.13, bf16[640,1536]{1,0:T(8,128)(2,1)S(1)} %copy-done.29, bf16[640,1024]{1,0:T(8,128)(2,1)S(1)} %copy-done.30), kind=kOutput, calls=%fused_computation.5 | convolution fusion | flops 1008992256 | bytes 5767168 | tf_op jit(solution)/shard_map/dot_general | solution.py:27
  308.4 5.3 %shard_map.224 = bf16[128,4096]{1,0:T(8,128)(2,1)S(1)} custom-call(bf16[64,160,128]{2,1,0:T(8,128)(2,1)} %all-to-all-done.7.returned, bf16[128,4096]{1,0:T(8,128)(2,1)} %bitcast.81, f32[128,128]{1,0:T(8,128)S(1)} %copy-done.14, f32[128,128]{1,0:T(8,128)S(1)} %copy-done.9, s32[1,1280]{1,0:T(1,128)S(1)} %copy-done.20, s32[1,1280]{1,0:T(1,128)S(1)} %copy-done.22, ...), custom_call_target="tpu_custom_call" | custom-call | tf_op jit(solution)/shard_map/pallas_call | solution.py:41
  313.8 5.5 %shard_map.225 = bf16[128,4096]{1,0:T(8,128)(2,1)S(1)} custom-call(bf16[64,160,128]{2,1,0:T(8,128)(2,1)} %all-to-all-done.7.returned, bf16[128,4096]{1,0:T(8,128)(2,1)} %bitcast.82, bf16[128,4096]{1,0:T(8,128)(2,1)} %bitcast.86, f32[1,4096]{1,0:T(1,128)S(1)} %copy-done.16, bf16[4096,128]{1,0:T(8,128)(2,1)} %bitcast.84, f32[128,128]{1,0:T(8,128)S(1)} %copy-done.9, ...), custom_call_target="tpu_custom_call" | custom-call | tf_op jit(solution)/shard_map/pallas_call | solution.py:41
  (166 shorter events, 54.3 us)
Async XLA Ops:
  8.2 12.4 %collective-permute-start = (bf16[128,1536]{1,0:T(8,128)(2,1)S(1)}, bf16[128,1536]{1,0:T(8,128)(2,1)S(1)}, u32[]{:S(2)}, u32[]{:S(2)}) collective-permute-start(bf16[128,1536]{1,0:T(8,128)(2,1)S(1)} %slice_bitcast_fusion.2), channel_id=1, source_target_pairs={{0,4},{4,0},{1,5},{5,1},{2,6},{6,2},{3,7},{7,3},{8,12},{12,8},{9,1... | collective-permute-start | bytes 1179656 | tf_op jit(solution)/shard_map/ppermute | solution.py:297
  20.6 75.4 %copy-start.6 = (bf16[128,1536]{1,0:T(8,128)(2,1)}, bf16[128,1536]{1,0:T(8,128)(2,1)S(1)}, u32[]{:S(2)}) copy-start(bf16[128,1536]{1,0:T(8,128)(2,1)S(1)} %collective-permute-done.refs_1_.refs_0_) | copy-start | bytes 1179652
  20.6 50.0 %all-to-all-start = ((bf16[64,80,128]{2,1,0:T(8,128)(2,1)}), bf16[64,80,128]{2,1,0:T(8,128)(2,1)}, u32[]{:S(2)}, u32[]{:S(2)}) async-start(bf16[64,80,128]{2,1,0:T(8,128)(2,1)} %get-tuple-element.43), calls=%async_computation | async-start | bytes 2621440 | tf_op jit(solution)/shard_map/all_to_all | solution.py:23
  34.0 36.7 %collective-permute-start.1 = (bf16[320,1536]{1,0:T(8,128)(2,1)S(1)}, bf16[320,1536]{1,0:T(8,128)(2,1)S(1)}, u32[]{:S(2)}, u32[]{:S(2)}) collective-permute-start(bf16[320,1536]{1,0:T(8,128)(2,1)S(1)} %slice_bitcast_fusion), channel_id=1, source_target_pairs={{0,4},{4,0},{1,5},{5,1},{2,6},{6,2},{3,7},{7,3},{8,12},{12,8},{9,1... | collective-permute-start | bytes 2949128 | tf_op jit(solution)/shard_map/ppermute | solution.py:297
  43.1 42.7 %copy-start = (bf16[1,1,768,512]{3,2,1,0:T(8,128)(2,1)S(1)}, bf16[1,1,768,512]{3,2,1,0:T(8,128)(2,1)}, u32[]{:S(2)}) copy-start(bf16[1,1,768,512]{3,2,1,0:T(8,128)(2,1)} %param.24) | copy-start | bytes 2359300
  70.6 25.4 %copy-start.2 = (bf16[320,1536]{1,0:T(8,128)(2,1)}, bf16[320,1536]{1,0:T(8,128)(2,1)S(1)}, u32[]{:S(2)}) copy-start(bf16[320,1536]{1,0:T(8,128)(2,1)S(1)} %collective-permute-done.1.refs_2_.refs_1_) | copy-start | bytes 2949124
  70.6 25.3 %copy-start.1 = (s32[640,1]{1,0:T(8,128)S(1)}, s32[640,1]{1,0:T(8,128)}, u32[]{:S(2)}) copy-start(s32[640,1]{1,0:T(8,128)} %constant.109.clone.order) | copy-start | bytes 7684
  70.6 51.9 %all-to-all-start.1 = ((bf16[64,80,128]{2,1,0:T(8,128)(2,1)}), bf16[64,80,128]{2,1,0:T(8,128)(2,1)}, u32[]{:S(2)}, u32[]{:S(2)}) async-start(bf16[64,80,128]{2,1,0:T(8,128)(2,1)} %get-tuple-element.44), calls=%async_computation.1 | async-start | bytes 2621440 | tf_op jit(solution)/shard_map/all_to_all | solution.py:23
  83.3 12.7 %collective-permute-start.4 = (bf16[64,1536]{1,0:T(8,128)(2,1)}, bf16[64,1536]{1,0:T(8,128)(2,1)}, u32[]{:S(2)}, u32[]{:S(2)}) collective-permute-start(bf16[64,1536]{1,0:T(8,128)(2,1)} %slice_bitcast_fusion.4), channel_id=1, source_target_pairs={{0,4},{4,0},{1,5},{5,1},{2,6},{6,2},{3,7},{7,3},{8,12},{12,8},{9,1... | collective-permute-start | bytes 589832 | tf_op jit(solution)/shard_map/ppermute | solution.py:297
  86.7 27.3 %collective-permute-start.2 = (bf16[512,512]{1,0:T(8,128)(2,1)}, bf16[512,512]{1,0:T(8,128)(2,1)}, u32[]{:S(2)}, u32[]{:S(2)}) collective-permute-start(bf16[512,512]{1,0:T(8,128)(2,1)} %slice_bitcast_fusion.1), channel_id=1, source_target_pairs={{0,4},{4,0},{1,5},{5,1},{2,6},{6,2},{3,7},{7,3},{8,12},{12,8},{9,1... | collective-permute-start | bytes 1572872 | tf_op jit(solution)/shard_map/ppermute | solution.py:297
  106.7 26.1 %collective-permute-start.7 = (bf16[160,1536]{1,0:T(8,128)(2,1)}, bf16[160,1536]{1,0:T(8,128)(2,1)}, u32[]{:S(2)}, u32[]{:S(2)}) collective-permute-start(bf16[160,1536]{1,0:T(8,128)(2,1)} %get-tuple-element.75), channel_id=1, source_target_pairs={{0,3},{1,0},{2,1},{3,2},{4,7},{5,4},{6,5},{7,6},{8,11},{9,8},{10,9... | collective-permute-start | bytes 1474568 | tf_op jit(solution)/shard_map/ppermute | solution.py:391
  107.3 25.5 %collective-permute-start.6 = (bf16[160,1536]{1,0:T(8,128)(2,1)}, bf16[160,1536]{1,0:T(8,128)(2,1)}, u32[]{:S(2)}, u32[]{:S(2)}) collective-permute-start(bf16[160,1536]{1,0:T(8,128)(2,1)} %get-tuple-element.76), channel_id=1, source_target_pairs={{0,2},{1,3},{2,0},{3,1},{4,6},{5,7},{6,4},{7,5},{8,10},{9,11},{10,... | collective-permute-start | bytes 1474568 | tf_op jit(solution)/shard_map/ppermute | solution.py:391
  109.7 23.2 %collective-permute-start.5 = (bf16[160,1536]{1,0:T(8,128)(2,1)}, bf16[160,1536]{1,0:T(8,128)(2,1)}, u32[]{:S(2)}, u32[]{:S(2)}) collective-permute-start(bf16[160,1536]{1,0:T(8,128)(2,1)} %get-tuple-element.77), channel_id=1, source_target_pairs={{0,1},{1,2},{2,3},{3,0},{4,5},{5,6},{6,7},{7,4},{8,9},{9,10},{10,1... | collective-permute-start | bytes 1474568 | tf_op jit(solution)/shard_map/ppermute | solution.py:391
  113.9 8.6 %collective-permute-start.3 = (bf16[256,512]{1,0:T(8,128)(2,1)S(1)}, bf16[256,512]{1,0:T(8,128)(2,1)S(1)}, u32[]{:S(2)}, u32[]{:S(2)}) collective-permute-start(bf16[256,512]{1,0:T(8,128)(2,1)S(1)} %slice_bitcast_fusion.3), channel_id=1, source_target_pairs={{0,4},{4,0},{1,5},{5,1},{2,6},{6,2},{3,7},{7,3},{8,12},{12,8},{9,1... | collective-permute-start | bytes 786440 | tf_op jit(solution)/shard_map/ppermute | solution.py:297
  127.9 19.4 %all-to-all-start.2 = ((bf16[4,160,768]{2,1,0:T(8,128)(2,1)}), bf16[4,160,768]{2,1,0:T(8,128)(2,1)S(1)}, u32[]{:S(2)}, u32[]{:S(2)}) async-start(bf16[4,160,768]{2,1,0:T(8,128)(2,1)} %bitcast.95), calls=%async_computation.2 | async-start | bytes 1966080 | tf_op jit(solution)/shard_map/all_to_all | solution.py:23
  132.8 68.9 %all-gather.4.cloned.1.call-start = ((), (), s32[]{:S(2)}) async-start(), calls=%async_computation.8 | async-start | bytes 2457600 | tf_op jit(solution)/shard_map/all_gather | solution.py:421
  134.8 23.5 %collective-permute-start.10 = (bf16[160,768]{1,0:T(8,128)(2,1)S(1)}, bf16[160,768]{1,0:T(8,128)(2,1)}, u32[]{:S(2)}, u32[]{:S(2)}) collective-permute-start(bf16[160,768]{1,0:T(8,128)(2,1)S(1)} %fusion.7.hidden), channel_id=1, source_target_pairs={{0,3},{1,0},{2,1},{3,2},{4,7},{5,4},{6,5},{7,6},{8,11},{9,8},{10,9... | collective-permute-start | bytes 737288 | tf_op jit(solution)/shard_map/ppermute | solution.py:411
  135.9 22.4 %collective-permute-start.9 = (bf16[160,768]{1,0:T(8,128)(2,1)S(1)}, bf16[160,768]{1,0:T(8,128)(2,1)}, u32[]{:S(2)}, u32[]{:S(2)}) collective-permute-start(bf16[160,768]{1,0:T(8,128)(2,1)S(1)} %fusion.7.hidden), channel_id=1, source_target_pairs={{0,2},{1,3},{2,0},{3,1},{4,6},{5,7},{6,4},{7,5},{8,10},{9,11},{10,... | collective-permute-start | bytes 737288 | tf_op jit(solution)/shard_map/ppermute | solution.py:411
  137.8 20.5 %collective-permute-start.8 = (bf16[160,768]{1,0:T(8,128)(2,1)S(1)}, bf16[160,768]{1,0:T(8,128)(2,1)}, u32[]{:S(2)}, u32[]{:S(2)}) collective-permute-start(bf16[160,768]{1,0:T(8,128)(2,1)S(1)} %fusion.7.hidden), channel_id=1, source_target_pairs={{0,1},{1,2},{2,3},{3,0},{4,5},{5,6},{6,7},{7,4},{8,9},{9,10},{10,1... | collective-permute-start | bytes 737288 | tf_op jit(solution)/shard_map/ppermute | solution.py:411
  151.2 15.4 %all-to-all-start.3 = ((f32[16,1,128]{2,1,0:T(1,128)}), f32[16,1,128]{2,1,0:T(1,128)S(1)}, u32[]{:S(2)}, u32[]{:S(2)}) async-start(f32[16,1,128]{2,1,0:T(1,128)} %bitcast.77), calls=%async_computation.3 | async-start | bytes 16384 | tf_op jit(solution)/shard_map/all_to_all | solution.py:23
  169.0 26.1 %all-to-all-start.4 = ((bf16[16,256,128]{2,1,0:T(8,128)(2,1)}), bf16[16,256,128]{2,1,0:T(8,128)(2,1)S(1)}, u32[]{:S(2)}, u32[]{:S(2)}) async-start(bf16[16,256,128]{2,1,0:T(8,128)(2,1)} %bitcast.88), calls=%async_computation.4 | async-start | bytes 2097152 | tf_op jit(solution)/shard_map/all_to_all | solution.py:23
  174.6 27.0 %collective-permute-start.11 = (bf16[768,512]{1,0:T(8,128)(2,1)}, bf16[768,512]{1,0:T(8,128)(2,1)}, u32[]{:S(2)}, u32[]{:S(2)}) collective-permute-start(bf16[768,512]{1,0:T(8,128)(2,1)} %convolution_convert_fusion.1), channel_id=1, source_target_pairs={{0,4},{4,0},{1,5},{5,1},{2,6},{6,2},{3,7},{7,3},{8,12},{12,8},{9,1... | collective-permute-start | bytes 2359304 | tf_op jit(solution)/shard_map/ppermute | solution.py:297
  181.0 20.7 %copy-start.3 = (bf16[320,1536]{1,0:T(8,128)(2,1)S(1)}, bf16[320,1536]{1,0:T(8,128)(2,1)}, u32[]{:S(2)}) copy-start(bf16[320,1536]{1,0:T(8,128)(2,1)} %copy-done.2) | copy-start | bytes 2949124
  181.0 20.7 %copy-start.7 = (bf16[128,1536]{1,0:T(8,128)(2,1)S(1)}, bf16[128,1536]{1,0:T(8,128)(2,1)}, u32[]{:S(2)}) copy-start(bf16[128,1536]{1,0:T(8,128)(2,1)} %copy-done.6) | copy-start | bytes 1179652
  195.9 13.6 %all-to-all-start.5 = ((f32[8,32,128]{2,1,0:T(8,128)}), f32[8,32,128]{2,1,0:T(8,128)S(1)}, u32[]{:S(2)}, u32[]{:S(2)}) async-start(f32[8,32,128]{2,1,0:T(8,128)} %bitcast.22), calls=%async_computation.5 | async-start | bytes 262144 | tf_op jit(solution)/shard_map/all_to_all | solution.py:23
  212.9 20.9 %all-to-all-start.6 = ((bf16[32,64,128]{2,1,0:T(8,128)(2,1)}), bf16[32,64,128]{2,1,0:T(8,128)(2,1)S(1)}, u32[]{:S(2)}, u32[]{:S(2)}) async-start(bf16[32,64,128]{2,1,0:T(8,128)(2,1)} %broadcast_in_dim.54), calls=%async_computation.6 | async-start | bytes 1048576 | tf_op jit(solution)/shard_map/all_to_all | solution.py:23
  233.7 74.6 %all-to-all-start.7 = ((bf16[64,160,128]{2,1,0:T(8,128)(2,1)}), bf16[64,160,128]{2,1,0:T(8,128)(2,1)}, u32[]{:S(2)}, u32[]{:S(2)}) async-start(bf16[64,160,128]{2,1,0:T(8,128)(2,1)} %get-tuple-element.68), calls=%async_computation.7 | async-start | bytes 5242880 | tf_op jit(solution)/shard_map/all_to_all | solution.py:23
  242.0 63.9 %all-gather.6.cloned.1.call-start = ((), (), s32[]{:S(2)}) async-start(), calls=%async_computation.9 | async-start | bytes 1372160 | tf_op jit(solution)/shard_map/all_gather | solution.py:505
  242.1 59.9 %collective-permute-start.13 = (bf16[512,1536]{1,0:T(8,128)(2,1)}, bf16[512,1536]{1,0:T(8,128)(2,1)}, u32[]{:S(2)}, u32[]{:S(2)}) collective-permute-start(bf16[512,1536]{1,0:T(8,128)(2,1)} %convolution_convert_fusion), channel_id=1, source_target_pairs={{0,4},{4,0},{1,5},{5,1},{2,6},{6,2},{3,7},{7,3},{8,12},{12,8},{9,1... | collective-permute-start | bytes 4718600 | tf_op jit(solution)/shard_map/ppermute | solution.py:297
  246.8 55.1 %copy-start.29 = (bf16[640,1536]{1,0:T(8,128)(2,1)S(1)}, bf16[640,1536]{1,0:T(8,128)(2,1)}, u32[]{:S(2)}) copy-start(bf16[640,1536]{1,0:T(8,128)(2,1)} %all-gather.4.cloned.1.call-done.pre_grad) | copy-start | bytes 5898244
  313.7 8.0 %collective-permute-start.12 = (bf16[128,4096]{1,0:T(8,128)(2,1)S(1)}, bf16[128,4096]{1,0:T(8,128)(2,1)S(1)}, u32[]{:S(2)}, u32[]{:S(2)}) collective-permute-start(bf16[128,4096]{1,0:T(8,128)(2,1)S(1)} %shard_map.224), channel_id=1, source_target_pairs={{0,128},{128,0},{1,129},{129,1},{2,130},{130,2},{3,131},{131,3},{4... | collective-permute-start | bytes 3145736 | tf_op jit(solution)/shard_map/ppermute | solution.py:297
  319.2 3.0 collective-permute-start.14
  (27 other events, 116.2 us)
Sparse Core Ops, SparseCore 0:
  151.4 30.3 all-gather.3
  247.0 30.8 all-gather.5

commit v8 on v7

--- a/solution.py
+++ b/solution.py
@@ -455,10 +455,6 @@
         out_specs=messages,
     )
     summed = exchange(local_router, "expert")
-    router_part = jnp.sum(after(summed, out_message).astype(F32), axis=0)
-    piece = router_part.shape[0] // (2 * replicas)
-    router_part = exchange(router_part.reshape(2 * replicas, piece, router_width), ("half", "dp"))
-
     message, gain_part = kernel_call(
         functools.partial(back_kernel, group, chunks, slots),
         (jax.ShapeDtypeStruct((peers, 2 * half, LANES), BF), jax.ShapeDtypeStruct((1, 2 * part), F32)),
@@ -478,45 +474,36 @@
             whole((1, 2 * part)),
         ],
     )
-    router_own = jnp.sum(after(router_part, gain_part), axis=0)
-    at = lax.axis_index("expert") * 2 * replicas + side * replicas + place_in_dp
-    table_own = lax.dynamic_slice_in_dim(table, at * piece, piece, axis=0).astype(F32)
-    gain_own = jnp.sum(router_own * table_own, axis=1)
     gain_part = gain_part.reshape(2, part)
     gain_part = jnp.where(side == 0, gain_part, gain_part[::-1])
 
     lines = 2 * part // LANES
-    terms = three_terms(gain_part.reshape(lines, LANES))
-    lone = [jnp.pad(term[None], ((0, 0), (0, LANES - piece))) for term in three_terms(gain_own)]
-    block = jnp.concatenate([router_own.astype(BF), *terms, *lone], axis=0)
-    block = jnp.pad(block, ((0, -block.shape[0] % 16), (0, 0)))
-    owners = 2 * experts
-    joined = exchange(jnp.broadcast_to(block[None], (owners,) + block.shape), OWNERS)
+    block_rows = summed.shape[1]
+    blocks = 2 * replicas
+    partly = jnp.sum(after(summed, out_message, gain_part).astype(F32), axis=0).astype(BF)
+    partly = jnp.concatenate([partly, *three_terms(gain_part.reshape(lines, LANES))], axis=0)
+    partly = jnp.pad(partly, ((0, -partly.shape[0] % 16), (0, 0)))
+    partly = exchange(jnp.broadcast_to(partly[None], (blocks,) + partly.shape), ("half", "dp"))
     first_other_grad = mm(expert_rows[:, part:], pre_grad_all, ((0,), (0,))).astype(BF)
     first_sent = swapped(first_other_grad, "half")
-    message, joined = lax.optimization_barrier((message, joined, first_other_grad))[:2]
-    returned = exchange(message, SHARE)
-    end = piece + 3 * lines
-    gain_rows = jnp.sum(joined[:, piece:end].astype(F32).reshape(owners, 3, lines, LANES), axis=(0, 1))
-    lone = jnp.sum(joined[:, end : end + 3, :piece].astype(F32), axis=1).reshape(-1, LANES)
-    sums = jnp.concatenate([*three_terms(gain_rows), *three_terms(lone)], axis=0)
-    sums = jnp.pad(sums, ((0, -sums.shape[0] % 16), (0, 0)))
-    packed = jnp.concatenate([joined[:, :piece].reshape(-1, LANES), sums], axis=0)
-    packed = lax.all_gather(packed, "dp", axis=0)
-    router_rows = owners * piece
-    router_total = packed[:, :router_rows].reshape(replicas, 2, experts, piece, router_width)
-    router_total = router_total.transpose(2, 1, 0, 3, 4).reshape(width, router_width)
-    gain_rows = packed[:, router_rows : router_rows + 3 * lines].astype(F32)
-    gain_rows = jnp.sum(gain_rows.reshape(replicas, 3, 2, part), axis=1)
-    lone = packed[:, router_rows + 3 * lines : router_rows + 6 * lines].astype(F32)
-    lone = jnp.sum(lone.reshape(replicas, 3, 2, experts, piece), axis=1)
-    gain_total = gain_rows.transpose(1, 0, 2).reshape(width) + lone.transpose(2, 1, 0, 3).reshape(width)
-    gain_total = gain_total / gain[0]
+    returned = exchange(after(message, partly, first_other_grad), SHARE)
+    router_block = jnp.sum(partly[:, :block_rows].astype(F32), axis=0)
+    gain_rows = partly[:, block_rows : block_rows + 3 * lines].astype(F32)
+    gain_rows = jnp.sum(gain_rows.reshape(2, replicas, 3, 2, part), axis=(0, 2))
+    gain_rows = gain_rows.transpose(1, 0, 2).reshape(width)
+    at = lax.axis_index("expert") * block_rows
+    table_own = lax.dynamic_slice_in_dim(table, at, block_rows, axis=0).astype(F32)
+    lone = jnp.sum(router_block * table_own, axis=1)
+    gain_rows = gain_rows + lax.dynamic_update_slice(jnp.zeros((width,), F32), lone, (at,))
+    terms = two_terms(gain_rows.reshape(-1, LANES))
+    payload = jnp.concatenate([router_block.astype(BF), *terms], axis=0)
+    payload = jnp.broadcast_to(payload[None], (experts,) + payload.shape)
+    joined = exchange(after(payload, returned), "expert")
+    router_total = joined[:, :block_rows].reshape(width, router_width)
+    gain_total = jnp.sum(joined[:, block_rows:].astype(F32).reshape(experts, 2, width), axis=(0, 1)) / gain[0]
 
     second_own_grad = mm(hidden_all, grad_rows[:, :part], ((0,), (0,)))
     second_grad = (second_own_grad + second_sent.astype(F32)).astype(BF)
-    first_own_grad = mm(expert_rows[:, :part], pre_grad_all, ((0,), (0,)))
-    first_grad = (first_own_grad + first_sent.astype(F32)).astype(BF)
 
     token_shape = jax.ShapeDtypeStruct((tokens, width), BF)
     joined_scratch = pltpu.VMEM((experts * half, replicas * LANES), BF)
@@ -534,6 +521,8 @@
     )
     handoff = swapped(layer_out, "section")
     handback = swapped(in_grad, "section")
+    first_own_grad = mm(expert_rows[:, :part], pre_grad_all, ((0,), (0,)))
+    first_grad = (first_own_grad + after(first_sent, in_grad).astype(F32)).astype(BF)
     return (
         handoff[None],
         handback[None],

time: 336 us -> 347 us (1.033)
  waiting for transfers between devices: 132 us -> 143 us
    all_to_all x8, waiting for transfers between devices: 33.7 us -> 74.1 us  [exchange(): return lax.all_to_all(blocks, axes, split_axis=0, concat_axis=0, tiled=True)]
    ppermute x9, waiting for transfers between devices: 98.3 us -> 64 us  [swapped(): return lax.ppermute(block, axis, [(0, 1), (1, 0)])]
    ppermute x3, waiting for transfers between devices: 0.01 us -> 4.3 us  [shards(): terms.append(lax.ppermute(block, 'dp', shift))]
    unnamed x72 -> x77, local copies, waits for them, and re-layouts: 12.7 us -> 11.3 us
  transfers between devices with their start and end apart: 25 -> 24, of which waited for: 11 -> 12; matrix products, arithmetic and copies ran while one was open for 10% -> 9% of each run, Pallas kernels for 13% -> 14%
where the time goes in v8:
time: 347 us; the launch traced here: 344 us
  waiting for transfers between devices  143 us (41%)
  starting transfers between devices  87.2 us (25%)
  Pallas kernels  49.2 us (14%)
  local copies, waits for them, and re-layouts  28 us (8%)
  matrix products  14.7 us (4%)
  between operations  14.5 us (4%)
  other arithmetic  7.16 us (2%)
    all_to_all x8, waiting for transfers between devices, exchange(): return lax.all_to_all(blocks, axes, split_axis=0, concat_axis=0, tiled=True)  74.1 us
    ppermute x9, waiting for transfers between devices, swapped(): return lax.ppermute(block, axis, [(0, 1), (1, 0)])  64 us
    all_to_all x8, starting transfers between devices, exchange(): return lax.all_to_all(blocks, axes, split_axis=0, concat_axis=0, tiled=True)  61.9 us
    pallas_call x9, Pallas kernels, kernel_call(): pl.pallas_call(body, out_shape=outs, scratch_shapes=scratch, compiler_par...  49.2 us
    ppermute x9, starting transfers between devices, swapped(): return lax.ppermute(block, axis, [(0, 1), (1, 0)])  16.2 us
    dot_general x6, matrix products, mm(): lax.dot_general(left, right, (contract, ((), ())), preferred_element_type...  14.7 us
    unnamed x77, local copies, waits for them, and re-layouts  11.3 us
  transfers between devices with their start and end apart: 24, of which 12 were waited for; matrix products, arithmetic and copies ran while one was open for 9% of the time, Pallas kernels for 14%

profile of v8, /device:TPU:8, one launch (start us, length us, event | category | flops | bytes accessed | tf_op | source)
XLA Modules:
  0.0 343.9 jit_solution(18219440024246834916)
XLA Ops:
  8.2 3.1 collective-permute-start
  15.3 4.9 %shard_map.217 = (bf16[64,80,128]{2,1,0:T(8,128)(2,1)}, bf16[128,4096]{1,0:T(8,128)(2,1)S(1)}, f32[128,128]{1,0:T(8,128)S(1)}) custom-call(bf16[128,4096]{1,0:T(8,128)(2,1)} %bitcast.69, s32[128,8]{1,0:T(8,128)S(1)} %bitcast.64, f32[1,4096]{1,0:T(1,128)S(1)} %copy-done.15, s32[1,1280]{1,0:T(1,128)S(1)} %copy-done.17, s32[1280,1]{1,0:T(8,128)S(1)} %copy-done.4, ...), custom_call_target="tpu_custom_call" | custom-call | tf_op jit(solution)/shard_map/pallas_call | solution.py:41
  20.6 13.2 %all-to-all-start = ((bf16[64,80,128]{2,1,0:T(8,128)(2,1)}), bf16[64,80,128]{2,1,0:T(8,128)(2,1)}, u32[]{:S(2)}, u32[]{:S(2)}) async-start(bf16[64,80,128]{2,1,0:T(8,128)(2,1)} %get-tuple-element.43), calls=%async_computation | async-start | bytes 2621440 | tf_op jit(solution)/shard_map/all_to_all | solution.py:23
  35.2 2.8 collective-permute-start.1
  38.1 5.7 %shard_map.218 = (bf16[64,80,128]{2,1,0:T(8,128)(2,1)}, f32[128,128]{1,0:T(8,128)S(1)}) custom-call(bf16[128,4096]{1,0:T(8,128)(2,1)S(1)} %get-tuple-element.39.normed, s32[128,8]{1,0:T(8,128)S(1)} %bitcast.65, bf16[128,4096]{1,0:T(8,128)(2,1)} %bitcast.74, bf16[4096,128]{1,0:T(8,128)(2,1)} %bitcast.72, f32[128,128]{1,0:T(8,128)S(1)} %get-tuple-element.40.place, ...), custom_call_target="tpu_custom_call" | custom-call | tf_op jit(solution)/shard_map/pallas_call | solution.py:41
  44.3 27.5 %collective-permute-done.1.refs_2_.refs_1_ = bf16[320,1536]{1,0:T(8,128)(2,1)S(1)} collective-permute-done((bf16[320,1536]{1,0:T(8,128)(2,1)S(1)}, bf16[320,1536]{1,0:T(8,128)(2,1)S(1)}, u32[]{:S(2)}, u32[]{:S(2)}) %collective-permute-start.1) | collective-permute-done | bytes 983072 | tf_op jit(solution)/shard_map/ppermute | solution.py:297
  71.8 10.4 %all-to-all-start.1 = ((bf16[64,80,128]{2,1,0:T(8,128)(2,1)}), bf16[64,80,128]{2,1,0:T(8,128)(2,1)}, u32[]{:S(2)}, u32[]{:S(2)}) async-start(bf16[64,80,128]{2,1,0:T(8,128)(2,1)} %get-tuple-element.44), calls=%async_computation.1 | async-start | bytes 2621440 | tf_op jit(solution)/shard_map/all_to_all | solution.py:23
  88.2 8.5 %collective-permute-done.4.refs_3_.refs_2_ = bf16[64,1536]{1,0:T(8,128)(2,1)} collective-permute-done((bf16[64,1536]{1,0:T(8,128)(2,1)}, bf16[64,1536]{1,0:T(8,128)(2,1)}, u32[]{:S(2)}, u32[]{:S(2)}) %collective-permute-start.4) | collective-permute-done | bytes 196640 | tf_op jit(solution)/shard_map/ppermute | solution.py:297
  96.7 7.9 %shard_map.220 = (bf16[640,1536]{1,0:T(8,128)(2,1)}, bf16[640,1024]{1,0:T(8,128)(2,1)}) custom-call(s32[1]{0:T(128)} %bitcast.index, bf16[64,80,128]{2,1,0:T(8,128)(2,1)} %all-to-all-done.arrived, s32[640,1]{1,0:T(8,128)S(1)} %copy-done.1, bf16[512,1536]{1,0:T(8,128)(2,1)} %bitcast.67, bf16[128,1536]{1,0:T(8,128)(2,1)S(1)} %collective-permute-done.refs_1_.refs_0_, ...), custom_call_target="tpu_custom_call" | custom-call | tf_op jit(solution)/shard_map/pallas_call | solution.py:41
  104.6 2.7 dynamic-slice_bitcast_fusion.3
  115.9 6.8 %collective-permute-done.3.refs_2_.late = bf16[256,512]{1,0:T(8,128)(2,1)S(1)} collective-permute-done((bf16[256,512]{1,0:T(8,128)(2,1)S(1)}, bf16[256,512]{1,0:T(8,128)(2,1)S(1)}, u32[]{:S(2)}, u32[]{:S(2)}) %collective-permute-start.3) | collective-permute-done | bytes 262176 | tf_op jit(solution)/shard_map/ppermute | solution.py:297
  122.7 5.4 %shard_map.219 = (bf16[640,768]{1,0:T(8,128)(2,1)}, bf16[640,1024]{1,0:T(8,128)(2,1)}) custom-call(s32[1]{0:T(128)} %bitcast.index, bf16[64,80,128]{2,1,0:T(8,128)(2,1)} %all-to-all-done.1.arrived, s32[640,1]{1,0:T(8,128)S(1)} %copy-done.1, bf16[768,512]{1,0:T(8,128)(2,1)S(1)} %bitcast.61, bf16[512,512]{1,0:T(8,128)(2,1)} %collective-permute-done.2.refs_1_.early, ...), custom_call_target="tpu_custom_call" | custom-call | tf_op jit(solution)/shard_map/pallas_call | solution.py:41
  128.1 4.3 %collective-permute-done.7 = bf16[160,1536]{1,0:T(8,128)(2,1)} collective-permute-done((bf16[160,1536]{1,0:T(8,128)(2,1)S(1)}, bf16[160,1536]{1,0:T(8,128)(2,1)}, u32[]{:S(2)}, u32[]{:S(2)}) %collective-permute-start.7) | collective-permute-done | bytes 491552 | tf_op jit(solution)/shard_map/ppermute | solution.py:391
  132.4 4.9 %all-to-all-start.2 = ((bf16[4,160,768]{2,1,0:T(8,128)(2,1)}), bf16[4,160,768]{2,1,0:T(8,128)(2,1)S(1)}, u32[]{:S(2)}, u32[]{:S(2)}) async-start(bf16[4,160,768]{2,1,0:T(8,128)(2,1)} %bitcast.80), calls=%async_computation.2 | async-start | bytes 1966080 | tf_op jit(solution)/shard_map/all_to_all | solution.py:23
  144.6 7.6 %all-to-all-done.2.arrived = bf16[4,160,768]{2,1,0:T(8,128)(2,1)S(1)} async-done(((bf16[4,160,768]{2,1,0:T(8,128)(2,1)}), bf16[4,160,768]{2,1,0:T(8,128)(2,1)S(1)}, u32[]{:S(2)}, u32[]{:S(2)}) %all-to-all-start.2) | async-done | bytes 983072 | tf_op jit(solution)/shard_map/all_to_all | solution.py:23
  156.1 6.2 %all-to-all-start.3 = ((f32[16,1,128]{2,1,0:T(1,128)}), f32[16,1,128]{2,1,0:T(1,128)S(1)}, u32[]{:S(2)}, u32[]{:S(2)}) async-start(f32[16,1,128]{2,1,0:T(1,128)} %bitcast.66), calls=%async_computation.3 | async-start | bytes 16384 | tf_op jit(solution)/shard_map/all_to_all | solution.py:23
  173.0 6.4 %all-to-all-start.4 = ((bf16[16,256,128]{2,1,0:T(8,128)(2,1)}), bf16[16,256,128]{2,1,0:T(8,128)(2,1)}, u32[]{:S(2)}, u32[]{:S(2)}) async-start(bf16[16,256,128]{2,1,0:T(8,128)(2,1)} %bitcast.21), calls=%async_computation.4 | async-start | bytes 2097152 | tf_op jit(solution)/shard_map/all_to_all | solution.py:23
  179.5 2.7 collective-permute-start.11
  182.1 4.8 %shard_map.222.outs = bf16[64,80,128]{2,1,0:T(8,128)(2,1)} custom-call(s32[1]{0:T(128)} %bitcast.index, bf16[640,768]{1,0:T(8,128)(2,1)} %copy-done.26, s32[640,1]{1,0:T(8,128)S(1)} %copy-done.1, bf16[768,512]{1,0:T(8,128)(2,1)S(1)} %bitcast.62, bf16[512,512]{1,0:T(8,128)(2,1)} %collective-permute-done.2.refs_1_.early, bf16[256,512]{1,0:T(8,128)(2,1)S(1)} %copy-done.11), custom_call_target="tpu_custom_call" | custom-call | tf_op jit(solution)/shard_map/pallas_call | solution.py:41
  186.9 18.9 %collective-permute-done.11 = bf16[768,512]{1,0:T(8,128)(2,1)} collective-permute-done((bf16[768,512]{1,0:T(8,128)(2,1)}, bf16[768,512]{1,0:T(8,128)(2,1)}, u32[]{:S(2)}, u32[]{:S(2)}) %collective-permute-start.11) | collective-permute-done | bytes 786464 | tf_op jit(solution)/shard_map/ppermute | solution.py:297
  205.9 7.8 %shard_map.223 = (bf16[64,160,128]{2,1,0:T(8,128)(2,1)}, f32[1,1024]{1,0:T(1,128)S(1)}) custom-call(s32[1]{0:T(128)} %bitcast.index, bf16[640,1536]{1,0:T(8,128)(2,1)} %all-gather.2.cloned.1.call-done.pre_grad, s32[640,1]{1,0:T(8,128)S(1)} %copy-done.1, bf16[512,1536]{1,0:T(8,128)(2,1)} %bitcast.68, bf16[640,1024]{1,0:T(8,128)(2,1)} %get-tuple-element.54.rows, ...), custom_call_target="tpu_custom_call" | custom-call | tf_op jit(solution)/shard_map/pallas_call | solution.py:41
  217.5 5.5 %all-to-all-start.5 = ((bf16[8,288,128]{2,1,0:T(8,128)(2,1)}), bf16[8,288,128]{2,1,0:T(8,128)(2,1)S(1)}, u32[]{:S(2)}, u32[]{:S(2)}) async-start(bf16[8,288,128]{2,1,0:T(8,128)(2,1)} %broadcast_in_dim.58), calls=%async_computation.5 | async-start | bytes 1179648 | tf_op jit(solution)/shard_map/all_to_all | solution.py:23
  223.1 4.1 %convolution_convert_fusion = bf16[512,1536]{1,0:T(8,128)(2,1)} fusion(bf16[640,1536]{1,0:T(8,128)(2,1)} %all-gather.2.cloned.1.call-done.pre_grad, bf16[640,1024]{1,0:T(8,128)(2,1)S(1)} %copy-done.29), kind=kOutput, calls=%fused_computation.3 | convolution fusion | flops 1007419392 | bytes 4194304 | tf_op jit(solution)/shard_map/dot_general | solution.py:27
  227.2 3.8 %all-to-all-done.5 = bf16[8,288,128]{2,1,0:T(8,128)(2,1)S(1)} async-done(((bf16[8,288,128]{2,1,0:T(8,128)(2,1)}), bf16[8,288,128]{2,1,0:T(8,128)(2,1)S(1)}, u32[]{:S(2)}, u32[]{:S(2)}) %all-to-all-start.5) | async-done | bytes 589856 | tf_op jit(solution)/shard_map/all_to_all | solution.py:23
  230.9 10.2 %all-to-all-start.6 = ((bf16[64,160,128]{2,1,0:T(8,128)(2,1)}), bf16[64,160,128]{2,1,0:T(8,128)(2,1)}, u32[]{:S(2)}, u32[]{:S(2)}) async-start(bf16[64,160,128]{2,1,0:T(8,128)(2,1)} %get-tuple-element.67), calls=%async_computation.6 | async-start | bytes 5242880 | tf_op jit(solution)/shard_map/all_to_all | solution.py:23
  244.4 53.4 %all-to-all-done.6.returned = bf16[64,160,128]{2,1,0:T(8,128)(2,1)} async-done(((bf16[64,160,128]{2,1,0:T(8,128)(2,1)}), bf16[64,160,128]{2,1,0:T(8,128)(2,1)}, u32[]{:S(2)}, u32[]{:S(2)}) %all-to-all-start.6) | async-done | bytes 2621472 | tf_op jit(solution)/shard_map/all_to_all | solution.py:23
  299.1 5.1 %all-to-all-start.7 = ((bf16[16,320,128]{2,1,0:T(8,128)(2,1)}), bf16[16,320,128]{2,1,0:T(8,128)(2,1)}, u32[]{:S(2)}, u32[]{:S(2)}) async-start(bf16[16,320,128]{2,1,0:T(8,128)(2,1)} %broadcast_in_dim.63), calls=%async_computation.7 | async-start | bytes 2621440 | tf_op jit(solution)/shard_map/all_to_all | solution.py:23
  304.2 3.0 add_convert_fusion
  307.2 5.5 %shard_map.225 = bf16[128,4096]{1,0:T(8,128)(2,1)S(1)} custom-call(bf16[64,160,128]{2,1,0:T(8,128)(2,1)} %all-to-all-done.6.returned, bf16[128,4096]{1,0:T(8,128)(2,1)} %bitcast.70, bf16[128,4096]{1,0:T(8,128)(2,1)} %bitcast.75, f32[1,4096]{1,0:T(1,128)S(1)} %copy-done.16, bf16[4096,128]{1,0:T(8,128)(2,1)} %bitcast.73, f32[128,128]{1,0:T(8,128)S(1)} %copy-done.9, ...), custom_call_target="tpu_custom_call" | custom-call | tf_op jit(solution)/shard_map/pallas_call | solution.py:41
  312.8 5.4 %shard_map.224 = bf16[128,4096]{1,0:T(8,128)(2,1)S(1)} custom-call(bf16[64,160,128]{2,1,0:T(8,128)(2,1)} %all-to-all-done.6.returned, bf16[128,4096]{1,0:T(8,128)(2,1)} %bitcast.71, f32[128,128]{1,0:T(8,128)S(1)} %copy-done.14, f32[128,128]{1,0:T(8,128)S(1)} %copy-done.9, s32[1,1280]{1,0:T(1,128)S(1)} %copy-done.18, s32[1,1280]{1,0:T(1,128)S(1)} %copy-done.22, ...), custom_call_target="tpu_custom_call" | custom-call | tf_op jit(solution)/shard_map/pallas_call | solution.py:41
  318.7 4.0 %fusion.2 = bf16[1,1,512,1536]{3,2,1,0:T(8,128)(2,1)} fusion(bf16[512,1536]{1,0:T(8,128)(2,1)} %collective-permute-done.13, bf16[640,1536]{1,0:T(8,128)(2,1)S(1)} %copy-done.28, bf16[640,1024]{1,0:T(8,128)(2,1)S(1)} %copy-done.30), kind=kOutput, calls=%fused_computation.5 | convolution fusion | flops 1008992256 | bytes 5767168 | tf_op jit(solution)/shard_map/dot_general | solution.py:27
  323.6 7.5 %all-to-all-done.7 = bf16[16,320,128]{2,1,0:T(8,128)(2,1)} async-done(((bf16[16,320,128]{2,1,0:T(8,128)(2,1)}), bf16[16,320,128]{2,1,0:T(8,128)(2,1)}, u32[]{:S(2)}, u32[]{:S(2)}) %all-to-all-start.7) | async-done | bytes 1310752 | tf_op jit(solution)/shard_map/all_to_all | solution.py:23
  (151 shorter events, 59.5 us)
Async XLA Ops:
  8.2 12.4 %collective-permute-start = (bf16[128,1536]{1,0:T(8,128)(2,1)S(1)}, bf16[128,1536]{1,0:T(8,128)(2,1)S(1)}, u32[]{:S(2)}, u32[]{:S(2)}) collective-permute-start(bf16[128,1536]{1,0:T(8,128)(2,1)S(1)} %slice_bitcast_fusion.2), channel_id=1, source_target_pairs={{0,4},{4,0},{1,5},{5,1},{2,6},{6,2},{3,7},{7,3},{8,12},{12,8},{9,1... | collective-permute-start | bytes 1179656 | tf_op jit(solution)/shard_map/ppermute | solution.py:297
  20.2 17.8 %copy-start.8 = (f32[128,128]{1,0:T(8,128)}, f32[128,128]{1,0:T(8,128)S(1)}, u32[]{:S(2)}) copy-start(f32[128,128]{1,0:T(8,128)S(1)} %get-tuple-element.40.place) | copy-start | bytes 196612
  20.6 76.0 %copy-start.6 = (bf16[128,1536]{1,0:T(8,128)(2,1)}, bf16[128,1536]{1,0:T(8,128)(2,1)S(1)}, u32[]{:S(2)}) copy-start(bf16[128,1536]{1,0:T(8,128)(2,1)S(1)} %collective-permute-done.refs_1_.refs_0_) | copy-start | bytes 1179652
  20.6 51.2 %all-to-all-start = ((bf16[64,80,128]{2,1,0:T(8,128)(2,1)}), bf16[64,80,128]{2,1,0:T(8,128)(2,1)}, u32[]{:S(2)}, u32[]{:S(2)}) async-start(bf16[64,80,128]{2,1,0:T(8,128)(2,1)} %get-tuple-element.43), calls=%async_computation | async-start | bytes 2621440 | tf_op jit(solution)/shard_map/all_to_all | solution.py:23
  35.2 36.6 %collective-permute-start.1 = (bf16[320,1536]{1,0:T(8,128)(2,1)S(1)}, bf16[320,1536]{1,0:T(8,128)(2,1)S(1)}, u32[]{:S(2)}, u32[]{:S(2)}) collective-permute-start(bf16[320,1536]{1,0:T(8,128)(2,1)S(1)} %slice_bitcast_fusion), channel_id=1, source_target_pairs={{0,4},{4,0},{1,5},{5,1},{2,6},{6,2},{3,7},{7,3},{8,12},{12,8},{9,1... | collective-permute-start | bytes 2949128 | tf_op jit(solution)/shard_map/ppermute | solution.py:297
  44.3 41.5 %copy-start = (bf16[1,1,768,512]{3,2,1,0:T(8,128)(2,1)S(1)}, bf16[1,1,768,512]{3,2,1,0:T(8,128)(2,1)}, u32[]{:S(2)}) copy-start(bf16[1,1,768,512]{3,2,1,0:T(8,128)(2,1)} %param.24) | copy-start | bytes 2359300
  71.8 24.8 %copy-start.2 = (bf16[320,1536]{1,0:T(8,128)(2,1)}, bf16[320,1536]{1,0:T(8,128)(2,1)S(1)}, u32[]{:S(2)}) copy-start(bf16[320,1536]{1,0:T(8,128)(2,1)S(1)} %collective-permute-done.1.refs_2_.refs_1_) | copy-start | bytes 2949124
  71.8 24.8 %copy-start.1 = (s32[640,1]{1,0:T(8,128)S(1)}, s32[640,1]{1,0:T(8,128)}, u32[]{:S(2)}) copy-start(s32[640,1]{1,0:T(8,128)} %constant.109.clone.order) | copy-start | bytes 7684
  71.8 50.9 %all-to-all-start.1 = ((bf16[64,80,128]{2,1,0:T(8,128)(2,1)}), bf16[64,80,128]{2,1,0:T(8,128)(2,1)}, u32[]{:S(2)}, u32[]{:S(2)}) async-start(bf16[64,80,128]{2,1,0:T(8,128)(2,1)} %get-tuple-element.44), calls=%async_computation.1 | async-start | bytes 2621440 | tf_op jit(solution)/shard_map/all_to_all | solution.py:23
  83.8 12.8 %collective-permute-start.4 = (bf16[64,1536]{1,0:T(8,128)(2,1)}, bf16[64,1536]{1,0:T(8,128)(2,1)}, u32[]{:S(2)}, u32[]{:S(2)}) collective-permute-start(bf16[64,1536]{1,0:T(8,128)(2,1)} %slice_bitcast_fusion.4), channel_id=1, source_target_pairs={{0,4},{4,0},{1,5},{5,1},{2,6},{6,2},{3,7},{7,3},{8,12},{12,8},{9,1... | collective-permute-start | bytes 589832 | tf_op jit(solution)/shard_map/ppermute | solution.py:297
  86.7 27.4 %collective-permute-start.2 = (bf16[512,512]{1,0:T(8,128)(2,1)}, bf16[512,512]{1,0:T(8,128)(2,1)}, u32[]{:S(2)}, u32[]{:S(2)}) collective-permute-start(bf16[512,512]{1,0:T(8,128)(2,1)} %slice_bitcast_fusion.1), channel_id=1, source_target_pairs={{0,4},{4,0},{1,5},{5,1},{2,6},{6,2},{3,7},{7,3},{8,12},{12,8},{9,1... | collective-permute-start | bytes 1572872 | tf_op jit(solution)/shard_map/ppermute | solution.py:297
  107.3 20.8 %collective-permute-start.5 = (bf16[160,1536]{1,0:T(8,128)(2,1)}, bf16[160,1536]{1,0:T(8,128)(2,1)S(1)}, u32[]{:S(2)}, u32[]{:S(2)}) collective-permute-start(bf16[160,1536]{1,0:T(8,128)(2,1)} %get-tuple-element.79), channel_id=1, source_target_pairs={{0,1},{1,2},{2,3},{3,0},{4,5},{5,6},{6,7},{7,4},{8,9},{9,10},{10,1... | collective-permute-start | bytes 1474568 | tf_op jit(solution)/shard_map/ppermute | solution.py:391
  108.8 19.2 %collective-permute-start.6 = (bf16[160,1536]{1,0:T(8,128)(2,1)}, bf16[160,1536]{1,0:T(8,128)(2,1)}, u32[]{:S(2)}, u32[]{:S(2)}) collective-permute-start(bf16[160,1536]{1,0:T(8,128)(2,1)} %get-tuple-element.78), channel_id=1, source_target_pairs={{0,2},{1,3},{2,0},{3,1},{4,6},{5,7},{6,4},{7,5},{8,10},{9,11},{10,... | collective-permute-start | bytes 1474568 | tf_op jit(solution)/shard_map/ppermute | solution.py:391
  109.9 22.5 %collective-permute-start.7 = (bf16[160,1536]{1,0:T(8,128)(2,1)S(1)}, bf16[160,1536]{1,0:T(8,128)(2,1)}, u32[]{:S(2)}, u32[]{:S(2)}) collective-permute-start(bf16[160,1536]{1,0:T(8,128)(2,1)S(1)} %get-tuple-element.77), channel_id=1, source_target_pairs={{0,3},{1,0},{2,1},{3,2},{4,7},{5,4},{6,5},{7,6},{8,11},{9,8},{10,9... | collective-permute-start | bytes 1474568 | tf_op jit(solution)/shard_map/ppermute | solution.py:391
  114.1 8.6 %collective-permute-start.3 = (bf16[256,512]{1,0:T(8,128)(2,1)S(1)}, bf16[256,512]{1,0:T(8,128)(2,1)S(1)}, u32[]{:S(2)}, u32[]{:S(2)}) collective-permute-start(bf16[256,512]{1,0:T(8,128)(2,1)S(1)} %slice_bitcast_fusion.3), channel_id=1, source_target_pairs={{0,4},{4,0},{1,5},{5,1},{2,6},{6,2},{3,7},{7,3},{8,12},{12,8},{9,1... | collective-permute-start | bytes 786440 | tf_op jit(solution)/shard_map/ppermute | solution.py:297
  132.4 19.8 %all-to-all-start.2 = ((bf16[4,160,768]{2,1,0:T(8,128)(2,1)}), bf16[4,160,768]{2,1,0:T(8,128)(2,1)S(1)}, u32[]{:S(2)}, u32[]{:S(2)}) async-start(bf16[4,160,768]{2,1,0:T(8,128)(2,1)} %bitcast.80), calls=%async_computation.2 | async-start | bytes 1966080 | tf_op jit(solution)/shard_map/all_to_all | solution.py:23
  137.2 14.9 %copy-start.21 = (s32[160,1]{1,0:T(8,128)S(1)}, s32[160,1]{1,0:T(8,128)}, u32[]{:S(2)}) copy-start(s32[160,1]{1,0:T(8,128)} %constant.111.clone.slot_of) | copy-start | bytes 1924
  139.2 23.2 %collective-permute-start.10 = (bf16[160,768]{1,0:T(8,128)(2,1)S(1)}, bf16[160,768]{1,0:T(8,128)(2,1)}, u32[]{:S(2)}, u32[]{:S(2)}) collective-permute-start(bf16[160,768]{1,0:T(8,128)(2,1)S(1)} %fusion.7.hidden), channel_id=1, source_target_pairs={{0,3},{1,0},{2,1},{3,2},{4,7},{5,4},{6,5},{7,6},{8,11},{9,8},{10,9... | collective-permute-start | bytes 737288 | tf_op jit(solution)/shard_map/ppermute | solution.py:411
  139.9 22.4 %collective-permute-start.9 = (bf16[160,768]{1,0:T(8,128)(2,1)S(1)}, bf16[160,768]{1,0:T(8,128)(2,1)}, u32[]{:S(2)}, u32[]{:S(2)}) collective-permute-start(bf16[160,768]{1,0:T(8,128)(2,1)S(1)} %fusion.7.hidden), channel_id=1, source_target_pairs={{0,2},{1,3},{2,0},{3,1},{4,6},{5,7},{6,4},{7,5},{8,10},{9,11},{10,... | collective-permute-start | bytes 737288 | tf_op jit(solution)/shard_map/ppermute | solution.py:411
  142.2 20.2 %collective-permute-start.8 = (bf16[160,768]{1,0:T(8,128)(2,1)S(1)}, bf16[160,768]{1,0:T(8,128)(2,1)}, u32[]{:S(2)}, u32[]{:S(2)}) collective-permute-start(bf16[160,768]{1,0:T(8,128)(2,1)S(1)} %fusion.7.hidden), channel_id=1, source_target_pairs={{0,1},{1,2},{2,3},{3,0},{4,5},{5,6},{6,7},{7,4},{8,9},{9,10},{10,1... | collective-permute-start | bytes 737288 | tf_op jit(solution)/shard_map/ppermute | solution.py:411
  156.1 14.6 %all-to-all-start.3 = ((f32[16,1,128]{2,1,0:T(1,128)}), f32[16,1,128]{2,1,0:T(1,128)S(1)}, u32[]{:S(2)}, u32[]{:S(2)}) async-start(f32[16,1,128]{2,1,0:T(1,128)} %bitcast.66), calls=%async_computation.3 | async-start | bytes 16384 | tf_op jit(solution)/shard_map/all_to_all | solution.py:23
  162.3 43.6 %all-gather.2.cloned.1.call-start = ((), (), s32[]{:S(2)}) async-start(), calls=%async_computation.8 | async-start | bytes 2457600 | tf_op jit(solution)/shard_map/all_gather | solution.py:421
  173.0 42.1 %all-to-all-start.4 = ((bf16[16,256,128]{2,1,0:T(8,128)(2,1)}), bf16[16,256,128]{2,1,0:T(8,128)(2,1)}, u32[]{:S(2)}, u32[]{:S(2)}) async-start(bf16[16,256,128]{2,1,0:T(8,128)(2,1)} %bitcast.21), calls=%async_computation.4 | async-start | bytes 2097152 | tf_op jit(solution)/shard_map/all_to_all | solution.py:23
  179.5 26.4 %collective-permute-start.11 = (bf16[768,512]{1,0:T(8,128)(2,1)}, bf16[768,512]{1,0:T(8,128)(2,1)}, u32[]{:S(2)}, u32[]{:S(2)}) collective-permute-start(bf16[768,512]{1,0:T(8,128)(2,1)} %convolution_convert_fusion.1), channel_id=1, source_target_pairs={{0,4},{4,0},{1,5},{5,1},{2,6},{6,2},{3,7},{7,3},{8,12},{12,8},{9,1... | collective-permute-start | bytes 2359304 | tf_op jit(solution)/shard_map/ppermute | solution.py:297
  182.1 23.8 %copy-start.3 = (bf16[320,1536]{1,0:T(8,128)(2,1)S(1)}, bf16[320,1536]{1,0:T(8,128)(2,1)}, u32[]{:S(2)}) copy-start(bf16[320,1536]{1,0:T(8,128)(2,1)} %copy-done.2) | copy-start | bytes 2949124
  182.1 23.8 %copy-start.7 = (bf16[128,1536]{1,0:T(8,128)(2,1)S(1)}, bf16[128,1536]{1,0:T(8,128)(2,1)}, u32[]{:S(2)}) copy-start(bf16[128,1536]{1,0:T(8,128)(2,1)} %copy-done.6) | copy-start | bytes 1179652
  217.5 13.4 %all-to-all-start.5 = ((bf16[8,288,128]{2,1,0:T(8,128)(2,1)}), bf16[8,288,128]{2,1,0:T(8,128)(2,1)S(1)}, u32[]{:S(2)}, u32[]{:S(2)}) async-start(bf16[8,288,128]{2,1,0:T(8,128)(2,1)} %broadcast_in_dim.58), calls=%async_computation.5 | async-start | bytes 1179648 | tf_op jit(solution)/shard_map/all_to_all | solution.py:23
  230.9 66.8 %all-to-all-start.6 = ((bf16[64,160,128]{2,1,0:T(8,128)(2,1)}), bf16[64,160,128]{2,1,0:T(8,128)(2,1)}, u32[]{:S(2)}, u32[]{:S(2)}) async-start(bf16[64,160,128]{2,1,0:T(8,128)(2,1)} %get-tuple-element.67), calls=%async_computation.6 | async-start | bytes 5242880 | tf_op jit(solution)/shard_map/all_to_all | solution.py:23
  241.1 66.1 %collective-permute-start.13 = (bf16[512,1536]{1,0:T(8,128)(2,1)}, bf16[512,1536]{1,0:T(8,128)(2,1)}, u32[]{:S(2)}, u32[]{:S(2)}) collective-permute-start(bf16[512,1536]{1,0:T(8,128)(2,1)} %convolution_convert_fusion), channel_id=1, source_target_pairs={{0,4},{4,0},{1,5},{5,1},{2,6},{6,2},{3,7},{7,3},{8,12},{12,8},{9,1... | collective-permute-start | bytes 4718600 | tf_op jit(solution)/shard_map/ppermute | solution.py:297
  299.1 32.1 %all-to-all-start.7 = ((bf16[16,320,128]{2,1,0:T(8,128)(2,1)}), bf16[16,320,128]{2,1,0:T(8,128)(2,1)}, u32[]{:S(2)}, u32[]{:S(2)}) async-start(bf16[16,320,128]{2,1,0:T(8,128)(2,1)} %broadcast_in_dim.63), calls=%async_computation.7 | async-start | bytes 2621440 | tf_op jit(solution)/shard_map/all_to_all | solution.py:23
  312.7 9.9 %collective-permute-start.14 = (bf16[128,4096]{1,0:T(8,128)(2,1)S(1)}, bf16[128,4096]{1,0:T(8,128)(2,1)S(1)}, u32[]{:S(2)}, u32[]{:S(2)}) collective-permute-start(bf16[128,4096]{1,0:T(8,128)(2,1)S(1)} %shard_map.225), channel_id=1, source_target_pairs={{0,128},{128,0},{1,129},{129,1},{2,130},{130,2},{3,131},{131,3},{4... | collective-permute-start | bytes 3145736 | tf_op jit(solution)/shard_map/ppermute | solution.py:297
  318.3 4.4 %collective-permute-start.12 = (bf16[128,4096]{1,0:T(8,128)(2,1)S(1)}, bf16[128,4096]{1,0:T(8,128)(2,1)S(1)}, u32[]{:S(2)}, u32[]{:S(2)}) collective-permute-start(bf16[128,4096]{1,0:T(8,128)(2,1)S(1)} %shard_map.224), channel_id=1, source_target_pairs={{0,128},{128,0},{1,129},{129,1},{2,130},{130,2},{3,131},{131,3},{4... | collective-permute-start | bytes 3145736 | tf_op jit(solution)/shard_map/ppermute | solution.py:297
  (28 other events, 101.2 us)
Sparse Core Ops, SparseCore 0:
  165.0 33.4 all-gather.1

commit v9 on v8

--- a/solution.py
+++ b/solution.py
@@ -419,11 +419,6 @@
         (summands, pre_act, hidden, at[None] // slots, at[:, None] % slots),
     )
     pre_grad_all = lax.all_gather(pre_grad, "dp", axis=0, tiled=True)
-    hidden_blocks = [after(block, worth) for block in hidden_blocks]
-    hidden_all = jnp.zeros((all_rows, hidden_width), BF)
-    for step, block in enumerate(hidden_blocks):
-        at_row = (place_in_dp + replicas - step) % replicas * rows
-        hidden_all = lax.dynamic_update_slice(hidden_all, block, (at_row, 0))
 
     worth = exchange(worth[:, None], "expert")[:, 0, :slots]
     slot_ids = jnp.arange(slots, dtype=F32)
@@ -435,9 +430,13 @@
     logit_high, logit_low = two_terms(logit_grad)
     local_router = mm(normed, logit_high, ((0,), (0,))) + mm(normed, logit_low, ((0,), (0,)))
     local_router = local_router.astype(BF).reshape(experts, -1, router_width)
+    hidden_blocks = [after(block, local_router) for block in hidden_blocks]
+    hidden_all = jnp.zeros((all_rows, hidden_width), BF)
+    for step, block in enumerate(hidden_blocks):
+        at_row = (place_in_dp + replicas - step) % replicas * rows
+        hidden_all = lax.dynamic_update_slice(hidden_all, block, (at_row, 0))
     second_other_grad = mm(hidden_all, grad_rows[:, part:], ((0,), (0,))).astype(BF)
     second_sent = swapped(second_other_grad, "half")
-    local_router = after(local_router, second_other_grad)
     steps = 2 if all_rows // 2 % (2 * group * slots) == 0 else 1
 
     def by_rows(width):
@@ -458,7 +457,7 @@
     message, gain_part = kernel_call(
         functools.partial(back_kernel, group, chunks, slots),
         (jax.ShapeDtypeStruct((peers, 2 * half, LANES), BF), jax.ShapeDtypeStruct((1, 2 * part), F32)),
-        (index, pre_grad_all, order, first, expert_rows, after(out_message, second_sent)) + first_other,
+        (index, pre_grad_all, order, first, expert_rows, out_message) + first_other,
         grid=(steps,),
         in_specs=[
             scalar,
@@ -486,7 +485,7 @@
     partly = exchange(jnp.broadcast_to(partly[None], (blocks,) + partly.shape), ("half", "dp"))
     first_other_grad = mm(expert_rows[:, part:], pre_grad_all, ((0,), (0,))).astype(BF)
     first_sent = swapped(first_other_grad, "half")
-    returned = exchange(after(message, partly, first_other_grad), SHARE)
+    returned = exchange(after(message, partly, first_other_grad, second_sent), SHARE)
     router_block = jnp.sum(partly[:, :block_rows].astype(F32), axis=0)
     gain_rows = partly[:, block_rows : block_rows + 3 * lines].astype(F32)
     gain_rows = jnp.sum(gain_rows.reshape(2, replicas, 3, 2, part), axis=(0, 2))
@@ -497,8 +496,7 @@
     gain_rows = gain_rows + lax.dynamic_update_slice(jnp.zeros((width,), F32), lone, (at,))
     terms = two_terms(gain_rows.reshape(-1, LANES))
     payload = jnp.concatenate([router_block.astype(BF), *terms], axis=0)
-    payload = jnp.broadcast_to(payload[None], (experts,) + payload.shape)
-    joined = exchange(after(payload, returned), "expert")
+    joined = lax.all_gather(payload, "expert")
     router_total = joined[:, :block_rows].reshape(width, router_width)
     gain_total = jnp.sum(joined[:, block_rows:].astype(F32).reshape(experts, 2, width), axis=(0, 1)) / gain[0]
 

time: 347 us -> 341 us (0.983)
  local copies, waits for them, and re-layouts: 28 us -> 22.5 us
  starting transfers between devices: 87.2 us -> 82.3 us
    all_to_all x8 -> x7, waiting for transfers between devices: 74.1 us -> 21.1 us  [exchange(): return lax.all_to_all(blocks, axes, split_axis=0, concat_axis=0, tiled=True)]
    ppermute x9, waiting for transfers between devices: 64 us -> 112 us  [swapped(): return lax.ppermute(block, axis, [(0, 1), (1, 0)])]
    ppermute x3, waiting for transfers between devices: 0.01 us -> 13.2 us  [shards(): hidden_blocks.append(lax.ppermute(hidden, 'dp', shift))]
    all_to_all x8 -> x7, starting transfers between devices: 61.9 us -> 57.2 us  [exchange(): return lax.all_to_all(blocks, axes, split_axis=0, concat_axis=0, tiled=True)]
    ppermute x3, waiting for transfers between devices: 4.3 us -> 0.01 us  [shards(): terms.append(lax.ppermute(block, 'dp', shift))]
    unnamed x77 -> x69, local copies, waits for them, and re-layouts: 11.3 us -> 11.9 us
  transfers between devices with their start and end apart: 24 -> 24, of which waited for: 12 -> 12; matrix products, arithmetic and copies ran while one was open for 9% -> 10% of each run, Pallas kernels for 14% -> 14%
where the time goes in v9:
time: 341 us; the launch traced here: 338 us
  waiting for transfers between devices  146 us (43%)
  starting transfers between devices  82.3 us (24%)
  Pallas kernels  49.6 us (15%)
  local copies, waits for them, and re-layouts  22.5 us (7%)
  matrix products  14.7 us (4%)
  between operations  14.5 us (4%)
  other arithmetic  7.78 us (2%)
    ppermute x9, waiting for transfers between devices, swapped(): return lax.ppermute(block, axis, [(0, 1), (1, 0)])  112 us
    all_to_all x7, starting transfers between devices, exchange(): return lax.all_to_all(blocks, axes, split_axis=0, concat_axis=0, tiled=True)  57.2 us
    pallas_call x9, Pallas kernels, kernel_call(): pl.pallas_call(body, out_shape=outs, scratch_shapes=scratch, compiler_par...  49.6 us
    all_to_all x7, waiting for transfers between devices, exchange(): return lax.all_to_all(blocks, axes, split_axis=0, concat_axis=0, tiled=True)  21.1 us
    ppermute x9, starting transfers between devices, swapped(): return lax.ppermute(block, axis, [(0, 1), (1, 0)])  16 us
    dot_general x6, matrix products, mm(): lax.dot_general(left, right, (contract, ((), ())), preferred_element_type...  14.7 us
    ppermute x3, waiting for transfers between devices, shards(): hidden_blocks.append(lax.ppermute(hidden, 'dp', shift))  13.2 us
    unnamed x69, local copies, waits for them, and re-layouts  11.9 us
  transfers between devices with their start and end apart: 24, of which 12 were waited for; matrix products, arithmetic and copies ran while one was open for 10% of the time, Pallas kernels for 14%

profile of v9, /device:TPU:8, one launch (start us, length us, event | category | flops | bytes accessed | tf_op | source)
XLA Modules:
  0.0 337.8 jit_solution(17348251343150966118)
XLA Ops:
  8.2 3.1 collective-permute-start
  15.3 5.0 %shard_map.217 = (bf16[64,80,128]{2,1,0:T(8,128)(2,1)}, bf16[128,4096]{1,0:T(8,128)(2,1)S(1)}, f32[128,128]{1,0:T(8,128)S(1)}) custom-call(bf16[128,4096]{1,0:T(8,128)(2,1)} %bitcast.69, s32[128,8]{1,0:T(8,128)S(1)} %bitcast.65, f32[1,4096]{1,0:T(1,128)S(1)} %copy-done.15, s32[1,1280]{1,0:T(1,128)S(1)} %copy-done.17, s32[1280,1]{1,0:T(8,128)S(1)} %copy-done.4, ...), custom_call_target="tpu_custom_call" | custom-call | tf_op jit(solution)/shard_map/pallas_call | solution.py:41
  20.6 13.2 %all-to-all-start = ((bf16[64,80,128]{2,1,0:T(8,128)(2,1)}), bf16[64,80,128]{2,1,0:T(8,128)(2,1)}, u32[]{:S(2)}, u32[]{:S(2)}) async-start(bf16[64,80,128]{2,1,0:T(8,128)(2,1)} %get-tuple-element.40), calls=%async_computation | async-start | bytes 2621440 | tf_op jit(solution)/shard_map/all_to_all | solution.py:23
  34.0 2.8 collective-permute-start.1
  36.8 5.7 %shard_map.218 = (bf16[64,80,128]{2,1,0:T(8,128)(2,1)}, f32[128,128]{1,0:T(8,128)S(1)}) custom-call(bf16[128,4096]{1,0:T(8,128)(2,1)S(1)} %get-tuple-element.36.normed, s32[128,8]{1,0:T(8,128)S(1)} %bitcast.66, bf16[128,4096]{1,0:T(8,128)(2,1)} %bitcast.74, bf16[4096,128]{1,0:T(8,128)(2,1)} %bitcast.72, f32[128,128]{1,0:T(8,128)S(1)} %get-tuple-element.37.place, ...), custom_call_target="tpu_custom_call" | custom-call | tf_op jit(solution)/shard_map/pallas_call | solution.py:41
  43.1 27.5 %collective-permute-done.1.refs_2_.refs_1_ = bf16[320,1536]{1,0:T(8,128)(2,1)S(1)} collective-permute-done((bf16[320,1536]{1,0:T(8,128)(2,1)S(1)}, bf16[320,1536]{1,0:T(8,128)(2,1)S(1)}, u32[]{:S(2)}, u32[]{:S(2)}) %collective-permute-start.1) | collective-permute-done | bytes 983072 | tf_op jit(solution)/shard_map/ppermute | solution.py:297
  70.6 11.0 %all-to-all-start.1 = ((bf16[64,80,128]{2,1,0:T(8,128)(2,1)}), bf16[64,80,128]{2,1,0:T(8,128)(2,1)}, u32[]{:S(2)}, u32[]{:S(2)}) async-start(bf16[64,80,128]{2,1,0:T(8,128)(2,1)} %get-tuple-element.41), calls=%async_computation.1 | async-start | bytes 2621440 | tf_op jit(solution)/shard_map/all_to_all | solution.py:23
  87.7 8.3 %collective-permute-done.4.refs_3_.refs_2_ = bf16[64,1536]{1,0:T(8,128)(2,1)} collective-permute-done((bf16[64,1536]{1,0:T(8,128)(2,1)}, bf16[64,1536]{1,0:T(8,128)(2,1)}, u32[]{:S(2)}, u32[]{:S(2)}) %collective-permute-start.4) | collective-permute-done | bytes 196640 | tf_op jit(solution)/shard_map/ppermute | solution.py:297
  96.0 7.9 %shard_map.220 = (bf16[640,1536]{1,0:T(8,128)(2,1)}, bf16[640,1024]{1,0:T(8,128)(2,1)}) custom-call(s32[1]{0:T(128)} %bitcast.index, bf16[64,80,128]{2,1,0:T(8,128)(2,1)} %all-to-all-done.arrived, s32[640,1]{1,0:T(8,128)S(1)} %copy-done.1, bf16[512,1536]{1,0:T(8,128)(2,1)} %bitcast.67, bf16[128,1536]{1,0:T(8,128)(2,1)S(1)} %collective-permute-done.refs_1_.refs_0_, ...), custom_call_target="tpu_custom_call" | custom-call | tf_op jit(solution)/shard_map/pallas_call | solution.py:41
  103.9 2.8 dynamic-slice_bitcast_fusion.3
  115.3 7.2 %collective-permute-done.3.refs_2_.late = bf16[256,512]{1,0:T(8,128)(2,1)S(1)} collective-permute-done((bf16[256,512]{1,0:T(8,128)(2,1)S(1)}, bf16[256,512]{1,0:T(8,128)(2,1)S(1)}, u32[]{:S(2)}, u32[]{:S(2)}) %collective-permute-start.3) | collective-permute-done | bytes 262176 | tf_op jit(solution)/shard_map/ppermute | solution.py:297
  122.6 5.4 %shard_map.219 = (bf16[640,768]{1,0:T(8,128)(2,1)}, bf16[640,1024]{1,0:T(8,128)(2,1)}) custom-call(s32[1]{0:T(128)} %bitcast.index, bf16[64,80,128]{2,1,0:T(8,128)(2,1)} %all-to-all-done.1.arrived, s32[640,1]{1,0:T(8,128)S(1)} %copy-done.1, bf16[768,512]{1,0:T(8,128)(2,1)S(1)} %bitcast.62, bf16[512,512]{1,0:T(8,128)(2,1)} %collective-permute-done.2.refs_1_.early, ...), custom_call_target="tpu_custom_call" | custom-call | tf_op jit(solution)/shard_map/pallas_call | solution.py:41
  127.9 4.9 %all-to-all-start.2 = ((bf16[4,160,768]{2,1,0:T(8,128)(2,1)}), bf16[4,160,768]{2,1,0:T(8,128)(2,1)S(1)}, u32[]{:S(2)}, u32[]{:S(2)}) async-start(bf16[4,160,768]{2,1,0:T(8,128)(2,1)} %bitcast.81), calls=%async_computation.2 | async-start | bytes 1966080 | tf_op jit(solution)/shard_map/all_to_all | solution.py:23
  135.7 8.2 %all-to-all-done.2.arrived = bf16[4,160,768]{2,1,0:T(8,128)(2,1)S(1)} async-done(((bf16[4,160,768]{2,1,0:T(8,128)(2,1)}), bf16[4,160,768]{2,1,0:T(8,128)(2,1)S(1)}, u32[]{:S(2)}, u32[]{:S(2)}) %all-to-all-start.2) | async-done | bytes 983072 | tf_op jit(solution)/shard_map/all_to_all | solution.py:23
  148.0 7.4 %all-to-all-start.3 = ((f32[16,1,128]{2,1,0:T(1,128)}), f32[16,1,128]{2,1,0:T(1,128)S(1)}, u32[]{:S(2)}, u32[]{:S(2)}) async-start(f32[16,1,128]{2,1,0:T(1,128)} %bitcast.19), calls=%async_computation.3 | async-start | bytes 16384 | tf_op jit(solution)/shard_map/all_to_all | solution.py:23
  155.5 8.3 %all-to-all-done.3 = f32[16,1,128]{2,1,0:T(1,128)S(1)} async-done(((f32[16,1,128]{2,1,0:T(1,128)}), f32[16,1,128]{2,1,0:T(1,128)S(1)}, u32[]{:S(2)}, u32[]{:S(2)}) %all-to-all-start.3) | async-done | bytes 8224 | tf_op jit(solution)/shard_map/all_to_all | solution.py:23
  166.2 4.3 %all-to-all-start.4 = ((bf16[16,256,128]{2,1,0:T(8,128)(2,1)}), bf16[16,256,128]{2,1,0:T(8,128)(2,1)}, u32[]{:S(2)}, u32[]{:S(2)}) async-start(bf16[16,256,128]{2,1,0:T(8,128)(2,1)} %bitcast.76), calls=%async_computation.4 | async-start | bytes 2097152 | tf_op jit(solution)/shard_map/all_to_all | solution.py:23
  170.6 3.5 %collective-permute-start.9 = (bf16[160,768]{1,0:T(8,128)(2,1)S(1)}, bf16[160,768]{1,0:T(8,128)(2,1)S(1)}, u32[]{:S(2)}, u32[]{:S(2)}) collective-permute-start(bf16[160,768]{1,0:T(8,128)(2,1)S(1)} %fusion.7.hidden), channel_id=1, source_target_pairs={{0,2},{1,3},{2,0},{3,1},{4,6},{5,7},{6,4},{7,5},{8,10},{9,11},{10,... | collective-permute-start | bytes 737288 | tf_op jit(solution)/shard_map/ppermute | solution.py:411
  174.7 8.9 %collective-permute-done.8 = bf16[160,768]{1,0:T(8,128)(2,1)S(1)} collective-permute-done((bf16[160,768]{1,0:T(8,128)(2,1)S(1)}, bf16[160,768]{1,0:T(8,128)(2,1)S(1)}, u32[]{:S(2)}, u32[]{:S(2)}) %collective-permute-start.8) | collective-permute-done | bytes 245792 | tf_op jit(solution)/shard_map/ppermute | solution.py:411
  185.1 2.8 collective-permute-done.10
  189.8 2.7 collective-permute-start.11
  192.6 4.7 %shard_map.222.outs = bf16[64,80,128]{2,1,0:T(8,128)(2,1)} custom-call(s32[1]{0:T(128)} %bitcast.index, bf16[640,768]{1,0:T(8,128)(2,1)} %copy-done.26, s32[640,1]{1,0:T(8,128)S(1)} %copy-done.1, bf16[768,512]{1,0:T(8,128)(2,1)S(1)} %bitcast.63, bf16[512,512]{1,0:T(8,128)(2,1)} %collective-permute-done.2.refs_1_.early, bf16[256,512]{1,0:T(8,128)(2,1)S(1)} %copy-done.11), custom_call_target="tpu_custom_call" | custom-call | tf_op jit(solution)/shard_map/pallas_call | solution.py:41
  197.3 7.8 %shard_map.223 = (bf16[64,160,128]{2,1,0:T(8,128)(2,1)}, f32[1,1024]{1,0:T(1,128)S(1)}) custom-call(s32[1]{0:T(128)} %bitcast.index, bf16[640,1536]{1,0:T(8,128)(2,1)} %all-gather.4.cloned.1.call-done.pre_grad, s32[640,1]{1,0:T(8,128)S(1)} %copy-done.1, bf16[512,1536]{1,0:T(8,128)(2,1)} %bitcast.68, bf16[640,1024]{1,0:T(8,128)(2,1)} %get-tuple-element.51.rows, ...), custom_call_target="tpu_custom_call" | custom-call | tf_op jit(solution)/shard_map/pallas_call | solution.py:41
  208.9 5.5 %all-to-all-start.5 = ((bf16[8,288,128]{2,1,0:T(8,128)(2,1)}), bf16[8,288,128]{2,1,0:T(8,128)(2,1)S(1)}, u32[]{:S(2)}, u32[]{:S(2)}) async-start(bf16[8,288,128]{2,1,0:T(8,128)(2,1)} %broadcast_in_dim.52), calls=%async_computation.5 | async-start | bytes 1179648 | tf_op jit(solution)/shard_map/all_to_all | solution.py:23
  214.3 3.6 %convolution_convert_fusion = bf16[512,1536]{1,0:T(8,128)(2,1)} fusion(bf16[640,1536]{1,0:T(8,128)(2,1)S(1)} %copy-done.28, bf16[640,1024]{1,0:T(8,128)(2,1)} %get-tuple-element.51.rows), kind=kOutput, calls=%fused_computation.3 | convolution fusion | flops 1007419392 | bytes 4194304 | tf_op jit(solution)/shard_map/dot_general | solution.py:27
  218.0 4.5 %all-to-all-done.5 = bf16[8,288,128]{2,1,0:T(8,128)(2,1)S(1)} async-done(((bf16[8,288,128]{2,1,0:T(8,128)(2,1)}), bf16[8,288,128]{2,1,0:T(8,128)(2,1)S(1)}, u32[]{:S(2)}, u32[]{:S(2)}) %all-to-all-start.5) | async-done | bytes 589856 | tf_op jit(solution)/shard_map/all_to_all | solution.py:23
  222.5 10.8 %all-to-all-start.6 = ((bf16[64,160,128]{2,1,0:T(8,128)(2,1)}), bf16[64,160,128]{2,1,0:T(8,128)(2,1)}, u32[]{:S(2)}, u32[]{:S(2)}) async-start(bf16[64,160,128]{2,1,0:T(8,128)(2,1)} %get-tuple-element.62), calls=%async_computation.6 | async-start | bytes 5242880 | tf_op jit(solution)/shard_map/all_to_all | solution.py:23
  237.3 2.8 add_convert_fusion
  240.1 66.2 %collective-permute-done.13 = bf16[512,1536]{1,0:T(8,128)(2,1)} collective-permute-done((bf16[512,1536]{1,0:T(8,128)(2,1)}, bf16[512,1536]{1,0:T(8,128)(2,1)}, u32[]{:S(2)}, u32[]{:S(2)}) %collective-permute-start.13) | collective-permute-done | bytes 1572896 | tf_op jit(solution)/shard_map/ppermute | solution.py:297
  306.3 5.3 %shard_map.224 = bf16[128,4096]{1,0:T(8,128)(2,1)S(1)} custom-call(bf16[64,160,128]{2,1,0:T(8,128)(2,1)} %all-to-all-done.6.returned, bf16[128,4096]{1,0:T(8,128)(2,1)} %bitcast.70, f32[128,128]{1,0:T(8,128)S(1)} %copy-done.14, f32[128,128]{1,0:T(8,128)S(1)} %copy-done.9, s32[1,1280]{1,0:T(1,128)S(1)} %copy-done.18, s32[1,1280]{1,0:T(1,128)S(1)} %copy-done.22, ...), custom_call_target="tpu_custom_call" | custom-call | tf_op jit(solution)/shard_map/pallas_call | solution.py:41
  311.7 5.5 %shard_map.225 = bf16[128,4096]{1,0:T(8,128)(2,1)S(1)} custom-call(bf16[64,160,128]{2,1,0:T(8,128)(2,1)} %all-to-all-done.6.returned, bf16[128,4096]{1,0:T(8,128)(2,1)} %bitcast.71, bf16[128,4096]{1,0:T(8,128)(2,1)} %bitcast.75, f32[1,4096]{1,0:T(1,128)S(1)} %copy-done.16, bf16[4096,128]{1,0:T(8,128)(2,1)} %bitcast.73, f32[128,128]{1,0:T(8,128)S(1)} %copy-done.9, ...), custom_call_target="tpu_custom_call" | custom-call | tf_op jit(solution)/shard_map/pallas_call | solution.py:41
  321.8 4.6 %fusion.2 = bf16[1,1,512,1536]{3,2,1,0:T(8,128)(2,1)} fusion(bf16[512,1536]{1,0:T(8,128)(2,1)} %collective-permute-done.13, bf16[640,1536]{1,0:T(8,128)(2,1)} %all-gather.4.cloned.1.call-done.pre_grad, bf16[640,1024]{1,0:T(8,128)(2,1)S(1)} %copy-done.29), kind=kOutput, calls=%fused_computation.5 | convolution fusion | flops 1008992256 | bytes 5767168 | tf_op jit(solution)/shard_map/dot_general | solution.py:27
  (143 shorter events, 50.8 us)
Async XLA Ops:
  8.2 12.4 %collective-permute-start = (bf16[128,1536]{1,0:T(8,128)(2,1)S(1)}, bf16[128,1536]{1,0:T(8,128)(2,1)S(1)}, u32[]{:S(2)}, u32[]{:S(2)}) collective-permute-start(bf16[128,1536]{1,0:T(8,128)(2,1)S(1)} %slice_bitcast_fusion.2), channel_id=1, source_target_pairs={{0,4},{4,0},{1,5},{5,1},{2,6},{6,2},{3,7},{7,3},{8,12},{12,8},{9,1... | collective-permute-start | bytes 1179656 | tf_op jit(solution)/shard_map/ppermute | solution.py:297
  20.6 75.4 %copy-start.6 = (bf16[128,1536]{1,0:T(8,128)(2,1)}, bf16[128,1536]{1,0:T(8,128)(2,1)S(1)}, u32[]{:S(2)}) copy-start(bf16[128,1536]{1,0:T(8,128)(2,1)S(1)} %collective-permute-done.refs_1_.refs_0_) | copy-start | bytes 1179652
  20.6 50.0 %all-to-all-start = ((bf16[64,80,128]{2,1,0:T(8,128)(2,1)}), bf16[64,80,128]{2,1,0:T(8,128)(2,1)}, u32[]{:S(2)}, u32[]{:S(2)}) async-start(bf16[64,80,128]{2,1,0:T(8,128)(2,1)} %get-tuple-element.40), calls=%async_computation | async-start | bytes 2621440 | tf_op jit(solution)/shard_map/all_to_all | solution.py:23
  34.0 36.7 %collective-permute-start.1 = (bf16[320,1536]{1,0:T(8,128)(2,1)S(1)}, bf16[320,1536]{1,0:T(8,128)(2,1)S(1)}, u32[]{:S(2)}, u32[]{:S(2)}) collective-permute-start(bf16[320,1536]{1,0:T(8,128)(2,1)S(1)} %slice_bitcast_fusion), channel_id=1, source_target_pairs={{0,4},{4,0},{1,5},{5,1},{2,6},{6,2},{3,7},{7,3},{8,12},{12,8},{9,1... | collective-permute-start | bytes 2949128 | tf_op jit(solution)/shard_map/ppermute | solution.py:297
  43.1 42.7 %copy-start = (bf16[1,1,768,512]{3,2,1,0:T(8,128)(2,1)S(1)}, bf16[1,1,768,512]{3,2,1,0:T(8,128)(2,1)}, u32[]{:S(2)}) copy-start(bf16[1,1,768,512]{3,2,1,0:T(8,128)(2,1)} %param.24) | copy-start | bytes 2359300
  70.6 25.4 %copy-start.2 = (bf16[320,1536]{1,0:T(8,128)(2,1)}, bf16[320,1536]{1,0:T(8,128)(2,1)S(1)}, u32[]{:S(2)}) copy-start(bf16[320,1536]{1,0:T(8,128)(2,1)S(1)} %collective-permute-done.1.refs_2_.refs_1_) | copy-start | bytes 2949124
  70.6 25.3 %copy-start.1 = (s32[640,1]{1,0:T(8,128)S(1)}, s32[640,1]{1,0:T(8,128)}, u32[]{:S(2)}) copy-start(s32[640,1]{1,0:T(8,128)} %constant.109.clone.order) | copy-start | bytes 7684
  70.6 51.9 %all-to-all-start.1 = ((bf16[64,80,128]{2,1,0:T(8,128)(2,1)}), bf16[64,80,128]{2,1,0:T(8,128)(2,1)}, u32[]{:S(2)}, u32[]{:S(2)}) async-start(bf16[64,80,128]{2,1,0:T(8,128)(2,1)} %get-tuple-element.41), calls=%async_computation.1 | async-start | bytes 2621440 | tf_op jit(solution)/shard_map/all_to_all | solution.py:23
  83.3 12.7 %collective-permute-start.4 = (bf16[64,1536]{1,0:T(8,128)(2,1)}, bf16[64,1536]{1,0:T(8,128)(2,1)}, u32[]{:S(2)}, u32[]{:S(2)}) collective-permute-start(bf16[64,1536]{1,0:T(8,128)(2,1)} %slice_bitcast_fusion.4), channel_id=1, source_target_pairs={{0,4},{4,0},{1,5},{5,1},{2,6},{6,2},{3,7},{7,3},{8,12},{12,8},{9,1... | collective-permute-start | bytes 589832 | tf_op jit(solution)/shard_map/ppermute | solution.py:297
  86.7 27.3 %collective-permute-start.2 = (bf16[512,512]{1,0:T(8,128)(2,1)}, bf16[512,512]{1,0:T(8,128)(2,1)}, u32[]{:S(2)}, u32[]{:S(2)}) collective-permute-start(bf16[512,512]{1,0:T(8,128)(2,1)} %slice_bitcast_fusion.1), channel_id=1, source_target_pairs={{0,4},{4,0},{1,5},{5,1},{2,6},{6,2},{3,7},{7,3},{8,12},{12,8},{9,1... | collective-permute-start | bytes 1572872 | tf_op jit(solution)/shard_map/ppermute | solution.py:297
  106.7 26.1 %collective-permute-start.7 = (bf16[160,1536]{1,0:T(8,128)(2,1)}, bf16[160,1536]{1,0:T(8,128)(2,1)}, u32[]{:S(2)}, u32[]{:S(2)}) collective-permute-start(bf16[160,1536]{1,0:T(8,128)(2,1)} %get-tuple-element.71), channel_id=1, source_target_pairs={{0,3},{1,0},{2,1},{3,2},{4,7},{5,4},{6,5},{7,6},{8,11},{9,8},{10,9... | collective-permute-start | bytes 1474568 | tf_op jit(solution)/shard_map/ppermute | solution.py:391
  107.4 25.5 %collective-permute-start.6 = (bf16[160,1536]{1,0:T(8,128)(2,1)}, bf16[160,1536]{1,0:T(8,128)(2,1)}, u32[]{:S(2)}, u32[]{:S(2)}) collective-permute-start(bf16[160,1536]{1,0:T(8,128)(2,1)} %get-tuple-element.72), channel_id=1, source_target_pairs={{0,2},{1,3},{2,0},{3,1},{4,6},{5,7},{6,4},{7,5},{8,10},{9,11},{10,... | collective-permute-start | bytes 1474568 | tf_op jit(solution)/shard_map/ppermute | solution.py:391
  109.7 23.1 %collective-permute-start.5 = (bf16[160,1536]{1,0:T(8,128)(2,1)}, bf16[160,1536]{1,0:T(8,128)(2,1)}, u32[]{:S(2)}, u32[]{:S(2)}) collective-permute-start(bf16[160,1536]{1,0:T(8,128)(2,1)} %get-tuple-element.73), channel_id=1, source_target_pairs={{0,1},{1,2},{2,3},{3,0},{4,5},{5,6},{6,7},{7,4},{8,9},{9,10},{10,1... | collective-permute-start | bytes 1474568 | tf_op jit(solution)/shard_map/ppermute | solution.py:391
  113.9 8.6 %collective-permute-start.3 = (bf16[256,512]{1,0:T(8,128)(2,1)S(1)}, bf16[256,512]{1,0:T(8,128)(2,1)S(1)}, u32[]{:S(2)}, u32[]{:S(2)}) collective-permute-start(bf16[256,512]{1,0:T(8,128)(2,1)S(1)} %slice_bitcast_fusion.3), channel_id=1, source_target_pairs={{0,4},{4,0},{1,5},{5,1},{2,6},{6,2},{3,7},{7,3},{8,12},{12,8},{9,1... | collective-permute-start | bytes 786440 | tf_op jit(solution)/shard_map/ppermute | solution.py:297
  127.9 15.9 %all-to-all-start.2 = ((bf16[4,160,768]{2,1,0:T(8,128)(2,1)}), bf16[4,160,768]{2,1,0:T(8,128)(2,1)S(1)}, u32[]{:S(2)}, u32[]{:S(2)}) async-start(bf16[4,160,768]{2,1,0:T(8,128)(2,1)} %bitcast.81), calls=%async_computation.2 | async-start | bytes 1966080 | tf_op jit(solution)/shard_map/all_to_all | solution.py:23
  132.8 64.5 %all-gather.4.cloned.1.call-start = ((), (), s32[]{:S(2)}) async-start(), calls=%async_computation.7 | async-start | bytes 2457600 | tf_op jit(solution)/shard_map/all_gather | solution.py:421
  135.7 19.8 %copy-start.9 = (f32[128,128]{1,0:T(8,128)S(1)}, f32[128,128]{1,0:T(8,128)}, u32[]{:S(2)}) copy-start(f32[128,128]{1,0:T(8,128)} %copy-done.8) | copy-start | bytes 196612
  135.7 28.5 %copy-start.14 = (f32[128,128]{1,0:T(8,128)S(1)}, f32[128,128]{1,0:T(8,128)}, u32[]{:S(2)}) copy-start(f32[128,128]{1,0:T(8,128)} %copy-done.13) | copy-start | bytes 196612
  148.0 15.8 %all-to-all-start.3 = ((f32[16,1,128]{2,1,0:T(1,128)}), f32[16,1,128]{2,1,0:T(1,128)S(1)}, u32[]{:S(2)}, u32[]{:S(2)}) async-start(f32[16,1,128]{2,1,0:T(1,128)} %bitcast.19), calls=%async_computation.3 | async-start | bytes 16384 | tf_op jit(solution)/shard_map/all_to_all | solution.py:23
  166.2 40.3 %all-to-all-start.4 = ((bf16[16,256,128]{2,1,0:T(8,128)(2,1)}), bf16[16,256,128]{2,1,0:T(8,128)(2,1)}, u32[]{:S(2)}, u32[]{:S(2)}) async-start(bf16[16,256,128]{2,1,0:T(8,128)(2,1)} %bitcast.76), calls=%async_computation.4 | async-start | bytes 2097152 | tf_op jit(solution)/shard_map/all_to_all | solution.py:23
  170.5 13.0 %collective-permute-start.8 = (bf16[160,768]{1,0:T(8,128)(2,1)S(1)}, bf16[160,768]{1,0:T(8,128)(2,1)S(1)}, u32[]{:S(2)}, u32[]{:S(2)}) collective-permute-start(bf16[160,768]{1,0:T(8,128)(2,1)S(1)} %fusion.7.hidden), channel_id=1, source_target_pairs={{0,1},{1,2},{2,3},{3,0},{4,5},{5,6},{6,7},{7,4},{8,9},{9,10},{10,1... | collective-permute-start | bytes 737288 | tf_op jit(solution)/shard_map/ppermute | solution.py:411
  170.6 14.5 %collective-permute-start.9 = (bf16[160,768]{1,0:T(8,128)(2,1)S(1)}, bf16[160,768]{1,0:T(8,128)(2,1)S(1)}, u32[]{:S(2)}, u32[]{:S(2)}) collective-permute-start(bf16[160,768]{1,0:T(8,128)(2,1)S(1)} %fusion.7.hidden), channel_id=1, source_target_pairs={{0,2},{1,3},{2,0},{3,1},{4,6},{5,7},{6,4},{7,5},{8,10},{9,11},{10,... | collective-permute-start | bytes 737288 | tf_op jit(solution)/shard_map/ppermute | solution.py:411
  174.1 13.8 %collective-permute-start.10 = (bf16[160,768]{1,0:T(8,128)(2,1)S(1)}, bf16[160,768]{1,0:T(8,128)(2,1)S(1)}, u32[]{:S(2)}, u32[]{:S(2)}) collective-permute-start(bf16[160,768]{1,0:T(8,128)(2,1)S(1)} %fusion.7.hidden), channel_id=1, source_target_pairs={{0,3},{1,0},{2,1},{3,2},{4,7},{5,4},{6,5},{7,6},{8,11},{9,8},{10,9... | collective-permute-start | bytes 737288 | tf_op jit(solution)/shard_map/ppermute | solution.py:411
  189.8 28.2 %collective-permute-start.11 = (bf16[768,512]{1,0:T(8,128)(2,1)}, bf16[768,512]{1,0:T(8,128)(2,1)}, u32[]{:S(2)}, u32[]{:S(2)}) collective-permute-start(bf16[768,512]{1,0:T(8,128)(2,1)} %convolution_convert_fusion.1), channel_id=1, source_target_pairs={{0,4},{4,0},{1,5},{5,1},{2,6},{6,2},{3,7},{7,3},{8,12},{12,8},{9,1... | collective-permute-start | bytes 2359304 | tf_op jit(solution)/shard_map/ppermute | solution.py:297
  208.9 13.7 %all-to-all-start.5 = ((bf16[8,288,128]{2,1,0:T(8,128)(2,1)}), bf16[8,288,128]{2,1,0:T(8,128)(2,1)S(1)}, u32[]{:S(2)}, u32[]{:S(2)}) async-start(bf16[8,288,128]{2,1,0:T(8,128)(2,1)} %broadcast_in_dim.52), calls=%async_computation.5 | async-start | bytes 1179648 | tf_op jit(solution)/shard_map/all_to_all | solution.py:23
  222.5 83.8 %all-to-all-start.6 = ((bf16[64,160,128]{2,1,0:T(8,128)(2,1)}), bf16[64,160,128]{2,1,0:T(8,128)(2,1)}, u32[]{:S(2)}, u32[]{:S(2)}) async-start(bf16[64,160,128]{2,1,0:T(8,128)(2,1)} %get-tuple-element.62), calls=%async_computation.6 | async-start | bytes 5242880 | tf_op jit(solution)/shard_map/all_to_all | solution.py:23
  233.3 84.4 %all-gather.6.cloned.1.call-start = ((), (), s32[]{:S(2)}) async-start(), calls=%async_computation.8 | async-start | bytes 1392640 | tf_op jit(solution)/shard_map/all_gather | solution.py:499
  235.4 70.9 %copy-start.22 = (s32[1,1280]{1,0:T(1,128)S(1)}, s32[1,1280]{1,0:T(1,128)}, u32[]{:S(2)}) copy-start(s32[1,1280]{1,0:T(1,128)} %constant.112.clone.chunk_of) | copy-start | bytes 15364
  235.5 70.8 %collective-permute-start.13 = (bf16[512,1536]{1,0:T(8,128)(2,1)}, bf16[512,1536]{1,0:T(8,128)(2,1)}, u32[]{:S(2)}, u32[]{:S(2)}) collective-permute-start(bf16[512,1536]{1,0:T(8,128)(2,1)} %convolution_convert_fusion), channel_id=1, source_target_pairs={{0,4},{4,0},{1,5},{5,1},{2,6},{6,2},{3,7},{7,3},{8,12},{12,8},{9,1... | collective-permute-start | bytes 4718600 | tf_op jit(solution)/shard_map/ppermute | solution.py:297
  240.1 71.6 %copy-start.16 = (f32[1,4096]{1,0:T(1,128)S(1)}, f32[1,4096]{1,0:T(1,128)}, u32[]{:S(2)}) copy-start(f32[1,4096]{1,0:T(1,128)} %gain.3) | copy-start | bytes 49156
  311.6 14.7 %collective-permute-start.12 = (bf16[128,4096]{1,0:T(8,128)(2,1)S(1)}, bf16[128,4096]{1,0:T(8,128)(2,1)}, u32[]{:S(2)}, u32[]{:S(2)}) collective-permute-start(bf16[128,4096]{1,0:T(8,128)(2,1)S(1)} %shard_map.224), channel_id=1, source_target_pairs={{0,128},{128,0},{1,129},{129,1},{2,130},{130,2},{3,131},{131,3},{4... | collective-permute-start | bytes 3145736 | tf_op jit(solution)/shard_map/ppermute | solution.py:297
  317.2 9.1 %collective-permute-start.14 = (bf16[128,4096]{1,0:T(8,128)(2,1)S(1)}, bf16[128,4096]{1,0:T(8,128)(2,1)}, u32[]{:S(2)}, u32[]{:S(2)}) collective-permute-start(bf16[128,4096]{1,0:T(8,128)(2,1)S(1)} %shard_map.225), channel_id=1, source_target_pairs={{0,128},{128,0},{1,129},{129,1},{2,130},{130,2},{3,131},{131,3},{4... | collective-permute-start | bytes 3145736 | tf_op jit(solution)/shard_map/ppermute | solution.py:297
  (24 other events, 127.6 us)
Sparse Core Ops, SparseCore 0:
  148.1 39.4 all-gather.3
  236.5 78.7 all-gather.5

commit v10 on v7

--- a/solution.py
+++ b/solution.py
@@ -419,13 +419,17 @@
         (summands, pre_act, hidden, at[None] // slots, at[:, None] % slots),
     )
     pre_grad_all = lax.all_gather(pre_grad, "dp", axis=0, tiled=True)
+
     hidden_blocks = [after(block, worth) for block in hidden_blocks]
     hidden_all = jnp.zeros((all_rows, hidden_width), BF)
     for step, block in enumerate(hidden_blocks):
         at_row = (place_in_dp + replicas - step) % replicas * rows
         hidden_all = lax.dynamic_update_slice(hidden_all, block, (at_row, 0))
-
-    worth = exchange(worth[:, None], "expert")[:, 0, :slots]
+    second_other_grad = mm(hidden_all, grad_rows[:, part:], ((0,), (0,))).astype(BF)
+    second_sent = swapped(second_other_grad, "half")
+
+    worth = exchange(worth[:, None], "expert")
+    worth = after(worth, second_other_grad)[:, 0, :slots]
     slot_ids = jnp.arange(slots, dtype=F32)
     gate_worth = jnp.sum(
         jnp.where(place[:, :experts, None] == slot_ids, worth[None], 0.0), axis=2
@@ -435,9 +439,6 @@
     logit_high, logit_low = two_terms(logit_grad)
     local_router = mm(normed, logit_high, ((0,), (0,))) + mm(normed, logit_low, ((0,), (0,)))
     local_router = local_router.astype(BF).reshape(experts, -1, router_width)
-    second_other_grad = mm(hidden_all, grad_rows[:, part:], ((0,), (0,))).astype(BF)
-    second_sent = swapped(second_other_grad, "half")
-    local_router = after(local_router, second_other_grad)
     steps = 2 if all_rows // 2 % (2 * group * slots) == 0 else 1
 
     def by_rows(width):
@@ -455,14 +456,11 @@
         out_specs=messages,
     )
     summed = exchange(local_router, "expert")
-    router_part = jnp.sum(after(summed, out_message).astype(F32), axis=0)
-    piece = router_part.shape[0] // (2 * replicas)
-    router_part = exchange(router_part.reshape(2 * replicas, piece, router_width), ("half", "dp"))
 
     message, gain_part = kernel_call(
         functools.partial(back_kernel, group, chunks, slots),
         (jax.ShapeDtypeStruct((peers, 2 * half, LANES), BF), jax.ShapeDtypeStruct((1, 2 * part), F32)),
-        (index, pre_grad_all, order, first, expert_rows, after(out_message, second_sent)) + first_other,
+        (index, pre_grad_all, order, first, expert_rows, out_message) + first_other,
         grid=(steps,),
         in_specs=[
             scalar,
@@ -478,7 +476,10 @@
             whole((1, 2 * part)),
         ],
     )
-    router_own = jnp.sum(after(router_part, gain_part), axis=0)
+    router_part = jnp.sum(after(summed, out_message, gain_part).astype(F32), axis=0)
+    piece = router_part.shape[0] // (2 * replicas)
+    router_part = exchange(router_part.reshape(2 * replicas, piece, router_width), ("half", "dp"))
+    router_own = jnp.sum(after(router_part, second_sent), axis=0)
     at = lax.axis_index("expert") * 2 * replicas + side * replicas + place_in_dp
     table_own = lax.dynamic_slice_in_dim(table, at * piece, piece, axis=0).astype(F32)
     gain_own = jnp.sum(router_own * table_own, axis=1)
@@ -494,8 +495,7 @@
     joined = exchange(jnp.broadcast_to(block[None], (owners,) + block.shape), OWNERS)
     first_other_grad = mm(expert_rows[:, part:], pre_grad_all, ((0,), (0,))).astype(BF)
     first_sent = swapped(first_other_grad, "half")
-    message, joined = lax.optimization_barrier((message, joined, first_other_grad))[:2]
-    returned = exchange(message, SHARE)
+    returned = exchange(after(message, joined, first_other_grad), SHARE)
     end = piece + 3 * lines
     gain_rows = jnp.sum(joined[:, piece:end].astype(F32).reshape(owners, 3, lines, LANES), axis=(0, 1))
     lone = jnp.sum(joined[:, end : end + 3, :piece].astype(F32), axis=1).reshape(-1, LANES)
@@ -503,6 +503,28 @@
     sums = jnp.pad(sums, ((0, -sums.shape[0] % 16), (0, 0)))
     packed = jnp.concatenate([joined[:, :piece].reshape(-1, LANES), sums], axis=0)
     packed = lax.all_gather(packed, "dp", axis=0)
+
+    second_own_grad = mm(hidden_all, grad_rows[:, :part], ((0,), (0,)))
+    second_grad = (second_own_grad + second_sent.astype(F32)).astype(BF)
+    first_own_grad = lax.optimization_barrier(mm(expert_rows[:, :part], pre_grad_all, ((0,), (0,))))
+
+    token_shape = jax.ShapeDtypeStruct((tokens, width), BF)
+    joined_scratch = pltpu.VMEM((experts * half, replicas * LANES), BF)
+    layer_out = kernel_call(
+        functools.partial(layer_kernel, experts, replicas, chunks),
+        token_shape,
+        (returned, after(x, second_grad, first_own_grad), gates, place, owner, chunk_of[None], slot_of),
+        [joined_scratch],
+    )
+    in_grad = kernel_call(
+        functools.partial(in_grad_kernel, experts, replicas, chunks),
+        token_shape,
+        (returned, after(x, first_sent), grad_top, gain, table, place, logit_grad, owner, chunk_of[None], slot_of),
+        [joined_scratch, pltpu.VMEM((tokens, width), F32)],
+    )
+    handoff = swapped(layer_out, "section")
+    handback = swapped(in_grad, "section")
+    packed = after(packed, in_grad)
     router_rows = owners * piece
     router_total = packed[:, :router_rows].reshape(replicas, 2, experts, piece, router_width)
     router_total = router_total.transpose(2, 1, 0, 3, 4).reshape(width, router_width)
@@ -512,28 +534,7 @@
     lone = jnp.sum(lone.reshape(replicas, 3, 2, experts, piece), axis=1)
     gain_total = gain_rows.transpose(1, 0, 2).reshape(width) + lone.transpose(2, 1, 0, 3).reshape(width)
     gain_total = gain_total / gain[0]
-
-    second_own_grad = mm(hidden_all, grad_rows[:, :part], ((0,), (0,)))
-    second_grad = (second_own_grad + second_sent.astype(F32)).astype(BF)
-    first_own_grad = mm(expert_rows[:, :part], pre_grad_all, ((0,), (0,)))
-    first_grad = (first_own_grad + first_sent.astype(F32)).astype(BF)
-
-    token_shape = jax.ShapeDtypeStruct((tokens, width), BF)
-    joined_scratch = pltpu.VMEM((experts * half, replicas * LANES), BF)
-    layer_out = kernel_call(
-        functools.partial(layer_kernel, experts, replicas, chunks),
-        token_shape,
-        (returned, after(x, second_grad), gates, place, owner, chunk_of[None], slot_of),
-        [joined_scratch],
-    )
-    in_grad = kernel_call(
-        functools.partial(in_grad_kernel, experts, replicas, chunks),
-        token_shape,
-        (returned, after(x, first_sent), grad_top, gain, table, place, logit_grad, owner, chunk_of[None], slot_of),
-        [joined_scratch, pltpu.VMEM((tokens, width), F32)],
-    )
-    handoff = swapped(layer_out, "section")
-    handback = swapped(in_grad, "section")
+    first_grad = (first_own_grad + after(first_sent, in_grad).astype(F32)).astype(BF)
     return (
         handoff[None],
         handback[None],

time: 336 us -> 342 us (1.018)
  waiting for transfers between devices: 132 us -> 137 us
  other arithmetic: 6.07 us -> 10.2 us
    all_to_all x8, starting transfers between devices: 62.7 us -> 58.6 us  [exchange(): return lax.all_to_all(blocks, axes, split_axis=0, concat_axis=0, tiled=True)]
  transfers between devices with their start and end apart: 25 -> 25, of which waited for: 11 -> 13; matrix products, arithmetic and copies ran while one was open for 10% -> 11% of each run, Pallas kernels for 13% -> 15%
where the time goes in v10:
time: 342 us; the launch traced here: 339 us
  waiting for transfers between devices  137 us (40%)
  starting transfers between devices  85.9 us (25%)
  Pallas kernels  49.3 us (14%)
  local copies, waits for them, and re-layouts  27.8 us (8%)
  between operations  14.5 us (4%)
  matrix products  14.2 us (4%)
  other arithmetic  10.2 us (3%)
    ppermute x9, waiting for transfers between devices, swapped(): return lax.ppermute(block, axis, [(0, 1), (1, 0)])  97.6 us
    all_to_all x8, starting transfers between devices, exchange(): return lax.all_to_all(blocks, axes, split_axis=0, concat_axis=0, tiled=True)  58.6 us
    pallas_call x9, Pallas kernels, kernel_call(): pl.pallas_call(body, out_shape=outs, scratch_shapes=scratch, compiler_par...  49.3 us
    all_to_all x8, waiting for transfers between devices, exchange(): return lax.all_to_all(blocks, axes, split_axis=0, concat_axis=0, tiled=True)  36 us
    ppermute x9, starting transfers between devices, swapped(): return lax.ppermute(block, axis, [(0, 1), (1, 0)])  17.5 us
    dot_general x6, matrix products, mm(): lax.dot_general(left, right, (contract, ((), ())), preferred_element_type...  14.2 us
    unnamed x72, local copies, waits for them, and re-layouts  11.7 us
  transfers between devices with their start and end apart: 25, of which 13 were waited for; matrix products, arithmetic and copies ran while one was open for 11% of the time, Pallas kernels for 15%

profile of v10, /device:TPU:8, one launch (start us, length us, event | category | flops | bytes accessed | tf_op | source)
XLA Modules:
  0.0 338.9 jit_solution(5333117233591977361)
XLA Ops:
  8.2 3.1 collective-permute-start
  15.3 4.9 %shard_map.217 = (bf16[64,80,128]{2,1,0:T(8,128)(2,1)}, bf16[128,4096]{1,0:T(8,128)(2,1)S(1)}, f32[128,128]{1,0:T(8,128)S(1)}) custom-call(bf16[128,4096]{1,0:T(8,128)(2,1)} %bitcast.80, s32[128,8]{1,0:T(8,128)S(1)} %bitcast.75, f32[1,4096]{1,0:T(1,128)S(1)} %copy-done.15, s32[1,1280]{1,0:T(1,128)S(1)} %copy-done.17, s32[1280,1]{1,0:T(8,128)S(1)} %copy-done.4, ...), custom_call_target="tpu_custom_call" | custom-call | tf_op jit(solution)/shard_map/pallas_call | solution.py:41
  20.6 13.2 %all-to-all-start = ((bf16[64,80,128]{2,1,0:T(8,128)(2,1)}), bf16[64,80,128]{2,1,0:T(8,128)(2,1)}, u32[]{:S(2)}, u32[]{:S(2)}) async-start(bf16[64,80,128]{2,1,0:T(8,128)(2,1)} %get-tuple-element.43), calls=%async_computation | async-start | bytes 2621440 | tf_op jit(solution)/shard_map/all_to_all | solution.py:23
  35.2 2.8 collective-permute-start.1
  38.1 5.7 %shard_map.218 = (bf16[64,80,128]{2,1,0:T(8,128)(2,1)}, f32[128,128]{1,0:T(8,128)S(1)}) custom-call(bf16[128,4096]{1,0:T(8,128)(2,1)S(1)} %get-tuple-element.39.normed, s32[128,8]{1,0:T(8,128)S(1)} %bitcast.76, bf16[128,4096]{1,0:T(8,128)(2,1)} %bitcast.85, bf16[4096,128]{1,0:T(8,128)(2,1)} %bitcast.83, f32[128,128]{1,0:T(8,128)S(1)} %get-tuple-element.40.place, ...), custom_call_target="tpu_custom_call" | custom-call | tf_op jit(solution)/shard_map/pallas_call | solution.py:41
  44.3 27.5 %collective-permute-done.1.refs_2_.refs_1_ = bf16[320,1536]{1,0:T(8,128)(2,1)S(1)} collective-permute-done((bf16[320,1536]{1,0:T(8,128)(2,1)S(1)}, bf16[320,1536]{1,0:T(8,128)(2,1)S(1)}, u32[]{:S(2)}, u32[]{:S(2)}) %collective-permute-start.1) | collective-permute-done | bytes 983072 | tf_op jit(solution)/shard_map/ppermute | solution.py:297
  71.8 10.4 %all-to-all-start.1 = ((bf16[64,80,128]{2,1,0:T(8,128)(2,1)}), bf16[64,80,128]{2,1,0:T(8,128)(2,1)}, u32[]{:S(2)}, u32[]{:S(2)}) async-start(bf16[64,80,128]{2,1,0:T(8,128)(2,1)} %get-tuple-element.44), calls=%async_computation.1 | async-start | bytes 2621440 | tf_op jit(solution)/shard_map/all_to_all | solution.py:23
  88.2 8.5 %collective-permute-done.4.refs_3_.refs_2_ = bf16[64,1536]{1,0:T(8,128)(2,1)} collective-permute-done((bf16[64,1536]{1,0:T(8,128)(2,1)}, bf16[64,1536]{1,0:T(8,128)(2,1)}, u32[]{:S(2)}, u32[]{:S(2)}) %collective-permute-start.4) | collective-permute-done | bytes 196640 | tf_op jit(solution)/shard_map/ppermute | solution.py:297
  96.7 8.0 %shard_map.220 = (bf16[640,1536]{1,0:T(8,128)(2,1)}, bf16[640,1024]{1,0:T(8,128)(2,1)}) custom-call(s32[1]{0:T(128)} %bitcast.index, bf16[64,80,128]{2,1,0:T(8,128)(2,1)} %all-to-all-done.arrived, s32[640,1]{1,0:T(8,128)S(1)} %copy-done.1, bf16[512,1536]{1,0:T(8,128)(2,1)} %bitcast.78, bf16[128,1536]{1,0:T(8,128)(2,1)S(1)} %collective-permute-done.refs_1_.refs_0_, ...), custom_call_target="tpu_custom_call" | custom-call | tf_op jit(solution)/shard_map/pallas_call | solution.py:41
  104.7 2.8 dynamic-slice_bitcast_fusion.3
  115.9 6.8 %collective-permute-done.3.refs_2_.late = bf16[256,512]{1,0:T(8,128)(2,1)S(1)} collective-permute-done((bf16[256,512]{1,0:T(8,128)(2,1)S(1)}, bf16[256,512]{1,0:T(8,128)(2,1)S(1)}, u32[]{:S(2)}, u32[]{:S(2)}) %collective-permute-start.3) | collective-permute-done | bytes 262176 | tf_op jit(solution)/shard_map/ppermute | solution.py:297
  122.7 5.4 %shard_map.219 = (bf16[640,768]{1,0:T(8,128)(2,1)}, bf16[640,1024]{1,0:T(8,128)(2,1)}) custom-call(s32[1]{0:T(128)} %bitcast.index, bf16[64,80,128]{2,1,0:T(8,128)(2,1)} %all-to-all-done.1.arrived, s32[640,1]{1,0:T(8,128)S(1)} %copy-done.1, bf16[768,512]{1,0:T(8,128)(2,1)S(1)} %bitcast.72, bf16[512,512]{1,0:T(8,128)(2,1)} %collective-permute-done.2.refs_1_.early, ...), custom_call_target="tpu_custom_call" | custom-call | tf_op jit(solution)/shard_map/pallas_call | solution.py:41
  128.1 4.9 %all-to-all-start.2 = ((bf16[4,160,768]{2,1,0:T(8,128)(2,1)}), bf16[4,160,768]{2,1,0:T(8,128)(2,1)S(1)}, u32[]{:S(2)}, u32[]{:S(2)}) async-start(bf16[4,160,768]{2,1,0:T(8,128)(2,1)} %bitcast.94), calls=%async_computation.2 | async-start | bytes 1966080 | tf_op jit(solution)/shard_map/all_to_all | solution.py:23
  140.4 7.0 %all-to-all-done.2.arrived = bf16[4,160,768]{2,1,0:T(8,128)(2,1)S(1)} async-done(((bf16[4,160,768]{2,1,0:T(8,128)(2,1)}), bf16[4,160,768]{2,1,0:T(8,128)(2,1)S(1)}, u32[]{:S(2)}, u32[]{:S(2)}) %all-to-all-start.2) | async-done | bytes 983072 | tf_op jit(solution)/shard_map/all_to_all | solution.py:23
  154.6 6.8 %all-to-all-start.3 = ((f32[16,1,128]{2,1,0:T(1,128)}), f32[16,1,128]{2,1,0:T(1,128)S(1)}, u32[]{:S(2)}, u32[]{:S(2)}) async-start(f32[16,1,128]{2,1,0:T(1,128)} %bitcast.77), calls=%async_computation.3 | async-start | bytes 16384 | tf_op jit(solution)/shard_map/all_to_all | solution.py:23
  172.1 5.8 %all-to-all-start.4 = ((bf16[16,256,128]{2,1,0:T(8,128)(2,1)}), bf16[16,256,128]{2,1,0:T(8,128)(2,1)}, u32[]{:S(2)}, u32[]{:S(2)}) async-start(bf16[16,256,128]{2,1,0:T(8,128)(2,1)} %bitcast.21), calls=%async_computation.4 | async-start | bytes 2097152 | tf_op jit(solution)/shard_map/all_to_all | solution.py:23
  177.9 3.3 collective-permute-start.11
  181.2 4.8 %shard_map.222.outs = bf16[64,80,128]{2,1,0:T(8,128)(2,1)} custom-call(s32[1]{0:T(128)} %bitcast.index, bf16[640,768]{1,0:T(8,128)(2,1)} %copy-done.26, s32[640,1]{1,0:T(8,128)S(1)} %copy-done.1, bf16[768,512]{1,0:T(8,128)(2,1)S(1)} %bitcast.73, bf16[512,512]{1,0:T(8,128)(2,1)} %collective-permute-done.2.refs_1_.early, bf16[256,512]{1,0:T(8,128)(2,1)S(1)} %copy-done.11), custom_call_target="tpu_custom_call" | custom-call | tf_op jit(solution)/shard_map/pallas_call | solution.py:41
  186.0 7.8 %shard_map.223 = (bf16[64,160,128]{2,1,0:T(8,128)(2,1)}, f32[1,1024]{1,0:T(1,128)S(1)}) custom-call(s32[1]{0:T(128)} %bitcast.index, bf16[640,1536]{1,0:T(8,128)(2,1)} %all-gather.4.cloned.1.call-done.pre_grad, s32[640,1]{1,0:T(8,128)S(1)} %copy-done.1, bf16[512,1536]{1,0:T(8,128)(2,1)} %bitcast.79, bf16[640,1024]{1,0:T(8,128)(2,1)} %get-tuple-element.54.rows, ...), custom_call_target="tpu_custom_call" | custom-call | tf_op jit(solution)/shard_map/pallas_call | solution.py:41
  193.8 9.4 %all-to-all-done.4 = bf16[16,256,128]{2,1,0:T(8,128)(2,1)} async-done(((bf16[16,256,128]{2,1,0:T(8,128)(2,1)}), bf16[16,256,128]{2,1,0:T(8,128)(2,1)}, u32[]{:S(2)}, u32[]{:S(2)}) %all-to-all-start.4) | async-done | bytes 1048608 | tf_op jit(solution)/shard_map/all_to_all | solution.py:23
  205.2 6.2 %all-to-all-start.5 = ((f32[8,32,128]{2,1,0:T(8,128)}), f32[8,32,128]{2,1,0:T(8,128)S(1)}, u32[]{:S(2)}, u32[]{:S(2)}) async-start(f32[8,32,128]{2,1,0:T(8,128)} %bitcast.22), calls=%async_computation.5 | async-start | bytes 262144 | tf_op jit(solution)/shard_map/all_to_all | solution.py:23
  212.8 5.2 %all-to-all-done.5 = f32[8,32,128]{2,1,0:T(8,128)S(1)} async-done(((f32[8,32,128]{2,1,0:T(8,128)}), f32[8,32,128]{2,1,0:T(8,128)S(1)}, u32[]{:S(2)}, u32[]{:S(2)}) %all-to-all-start.5) | async-done | bytes 131104 | tf_op jit(solution)/shard_map/all_to_all | solution.py:23
  219.8 4.6 %all-to-all-start.6 = ((bf16[32,64,128]{2,1,0:T(8,128)(2,1)}), bf16[32,64,128]{2,1,0:T(8,128)(2,1)S(1)}, u32[]{:S(2)}, u32[]{:S(2)}) async-start(bf16[32,64,128]{2,1,0:T(8,128)(2,1)} %broadcast_in_dim.54), calls=%async_computation.6 | async-start | bytes 1048576 | tf_op jit(solution)/shard_map/all_to_all | solution.py:23
  224.4 4.3 %convolution_convert_fusion = bf16[512,1536]{1,0:T(8,128)(2,1)} fusion(bf16[640,1536]{1,0:T(8,128)(2,1)} %all-gather.4.cloned.1.call-done.pre_grad, bf16[640,1024]{1,0:T(8,128)(2,1)} %get-tuple-element.54.rows), kind=kOutput, calls=%fused_computation.3 | convolution fusion | flops 1007419392 | bytes 4194304 | tf_op jit(solution)/shard_map/dot_general | solution.py:27
  228.7 11.8 %all-to-all-done.6 = bf16[32,64,128]{2,1,0:T(8,128)(2,1)S(1)} async-done(((bf16[32,64,128]{2,1,0:T(8,128)(2,1)}), bf16[32,64,128]{2,1,0:T(8,128)(2,1)S(1)}, u32[]{:S(2)}, u32[]{:S(2)}) %all-to-all-start.6) | async-done | bytes 524320 | tf_op jit(solution)/shard_map/all_to_all | solution.py:23
  240.6 6.9 %all-to-all-start.7 = ((bf16[64,160,128]{2,1,0:T(8,128)(2,1)}), bf16[64,160,128]{2,1,0:T(8,128)(2,1)}, u32[]{:S(2)}, u32[]{:S(2)}) async-start(bf16[64,160,128]{2,1,0:T(8,128)(2,1)} %get-tuple-element.67), calls=%async_computation.7 | async-start | bytes 5242880 | tf_op jit(solution)/shard_map/all_to_all | solution.py:23
  250.7 3.2 add_convert_fusion.1
  253.9 3.1 fusion.2
  257.0 52.7 %collective-permute-done.13 = bf16[512,1536]{1,0:T(8,128)(2,1)} collective-permute-done((bf16[512,1536]{1,0:T(8,128)(2,1)}, bf16[512,1536]{1,0:T(8,128)(2,1)}, u32[]{:S(2)}, u32[]{:S(2)}) %collective-permute-start.13) | collective-permute-done | bytes 1572896 | tf_op jit(solution)/shard_map/ppermute | solution.py:297
  309.7 5.3 %shard_map.224 = bf16[128,4096]{1,0:T(8,128)(2,1)S(1)} custom-call(bf16[64,160,128]{2,1,0:T(8,128)(2,1)} %all-to-all-done.7.returned, bf16[128,4096]{1,0:T(8,128)(2,1)} %bitcast.81, f32[128,128]{1,0:T(8,128)S(1)} %copy-done.14, f32[128,128]{1,0:T(8,128)S(1)} %copy-done.9, s32[1,1280]{1,0:T(1,128)S(1)} %copy-done.18, s32[1,1280]{1,0:T(1,128)S(1)} %copy-done.22, ...), custom_call_target="tpu_custom_call" | custom-call | tf_op jit(solution)/shard_map/pallas_call | solution.py:41
  315.4 5.6 %shard_map.225 = bf16[128,4096]{1,0:T(8,128)(2,1)S(1)} custom-call(bf16[64,160,128]{2,1,0:T(8,128)(2,1)} %all-to-all-done.7.returned, bf16[128,4096]{1,0:T(8,128)(2,1)} %bitcast.82, bf16[128,4096]{1,0:T(8,128)(2,1)} %bitcast.86, f32[1,4096]{1,0:T(1,128)S(1)} %copy-done.16, bf16[4096,128]{1,0:T(8,128)(2,1)} %bitcast.84, f32[128,128]{1,0:T(8,128)S(1)} %copy-done.9, ...), custom_call_target="tpu_custom_call" | custom-call | tf_op jit(solution)/shard_map/pallas_call | solution.py:41
  321.6 3.0 fusion.1
  (167 shorter events, 63.7 us)
Async XLA Ops:
  8.2 12.4 %collective-permute-start = (bf16[128,1536]{1,0:T(8,128)(2,1)S(1)}, bf16[128,1536]{1,0:T(8,128)(2,1)S(1)}, u32[]{:S(2)}, u32[]{:S(2)}) collective-permute-start(bf16[128,1536]{1,0:T(8,128)(2,1)S(1)} %slice_bitcast_fusion.2), channel_id=1, source_target_pairs={{0,4},{4,0},{1,5},{5,1},{2,6},{6,2},{3,7},{7,3},{8,12},{12,8},{9,1... | collective-permute-start | bytes 1179656 | tf_op jit(solution)/shard_map/ppermute | solution.py:297
  20.2 17.8 %copy-start.8 = (f32[128,128]{1,0:T(8,128)}, f32[128,128]{1,0:T(8,128)S(1)}, u32[]{:S(2)}) copy-start(f32[128,128]{1,0:T(8,128)S(1)} %get-tuple-element.40.place) | copy-start | bytes 196612
  20.6 76.0 %copy-start.6 = (bf16[128,1536]{1,0:T(8,128)(2,1)}, bf16[128,1536]{1,0:T(8,128)(2,1)S(1)}, u32[]{:S(2)}) copy-start(bf16[128,1536]{1,0:T(8,128)(2,1)S(1)} %collective-permute-done.refs_1_.refs_0_) | copy-start | bytes 1179652
  20.6 51.2 %all-to-all-start = ((bf16[64,80,128]{2,1,0:T(8,128)(2,1)}), bf16[64,80,128]{2,1,0:T(8,128)(2,1)}, u32[]{:S(2)}, u32[]{:S(2)}) async-start(bf16[64,80,128]{2,1,0:T(8,128)(2,1)} %get-tuple-element.43), calls=%async_computation | async-start | bytes 2621440 | tf_op jit(solution)/shard_map/all_to_all | solution.py:23
  35.2 36.6 %collective-permute-start.1 = (bf16[320,1536]{1,0:T(8,128)(2,1)S(1)}, bf16[320,1536]{1,0:T(8,128)(2,1)S(1)}, u32[]{:S(2)}, u32[]{:S(2)}) collective-permute-start(bf16[320,1536]{1,0:T(8,128)(2,1)S(1)} %slice_bitcast_fusion), channel_id=1, source_target_pairs={{0,4},{4,0},{1,5},{5,1},{2,6},{6,2},{3,7},{7,3},{8,12},{12,8},{9,1... | collective-permute-start | bytes 2949128 | tf_op jit(solution)/shard_map/ppermute | solution.py:297
  44.3 41.5 %copy-start = (bf16[1,1,768,512]{3,2,1,0:T(8,128)(2,1)S(1)}, bf16[1,1,768,512]{3,2,1,0:T(8,128)(2,1)}, u32[]{:S(2)}) copy-start(bf16[1,1,768,512]{3,2,1,0:T(8,128)(2,1)} %param.24) | copy-start | bytes 2359300
  71.8 24.8 %copy-start.2 = (bf16[320,1536]{1,0:T(8,128)(2,1)}, bf16[320,1536]{1,0:T(8,128)(2,1)S(1)}, u32[]{:S(2)}) copy-start(bf16[320,1536]{1,0:T(8,128)(2,1)S(1)} %collective-permute-done.1.refs_2_.refs_1_) | copy-start | bytes 2949124
  71.8 24.8 %copy-start.1 = (s32[640,1]{1,0:T(8,128)S(1)}, s32[640,1]{1,0:T(8,128)}, u32[]{:S(2)}) copy-start(s32[640,1]{1,0:T(8,128)} %constant.109.clone.order) | copy-start | bytes 7684
  71.8 50.9 %all-to-all-start.1 = ((bf16[64,80,128]{2,1,0:T(8,128)(2,1)}), bf16[64,80,128]{2,1,0:T(8,128)(2,1)}, u32[]{:S(2)}, u32[]{:S(2)}) async-start(bf16[64,80,128]{2,1,0:T(8,128)(2,1)} %get-tuple-element.44), calls=%async_computation.1 | async-start | bytes 2621440 | tf_op jit(solution)/shard_map/all_to_all | solution.py:23
  83.8 12.8 %collective-permute-start.4 = (bf16[64,1536]{1,0:T(8,128)(2,1)}, bf16[64,1536]{1,0:T(8,128)(2,1)}, u32[]{:S(2)}, u32[]{:S(2)}) collective-permute-start(bf16[64,1536]{1,0:T(8,128)(2,1)} %slice_bitcast_fusion.4), channel_id=1, source_target_pairs={{0,4},{4,0},{1,5},{5,1},{2,6},{6,2},{3,7},{7,3},{8,12},{12,8},{9,1... | collective-permute-start | bytes 589832 | tf_op jit(solution)/shard_map/ppermute | solution.py:297
  86.7 27.4 %collective-permute-start.2 = (bf16[512,512]{1,0:T(8,128)(2,1)}, bf16[512,512]{1,0:T(8,128)(2,1)}, u32[]{:S(2)}, u32[]{:S(2)}) collective-permute-start(bf16[512,512]{1,0:T(8,128)(2,1)} %slice_bitcast_fusion.1), channel_id=1, source_target_pairs={{0,4},{4,0},{1,5},{5,1},{2,6},{6,2},{3,7},{7,3},{8,12},{12,8},{9,1... | collective-permute-start | bytes 1572872 | tf_op jit(solution)/shard_map/ppermute | solution.py:297
  107.5 25.5 %collective-permute-start.7 = (bf16[160,1536]{1,0:T(8,128)(2,1)}, bf16[160,1536]{1,0:T(8,128)(2,1)}, u32[]{:S(2)}, u32[]{:S(2)}) collective-permute-start(bf16[160,1536]{1,0:T(8,128)(2,1)} %get-tuple-element.75), channel_id=1, source_target_pairs={{0,3},{1,0},{2,1},{3,2},{4,7},{5,4},{6,5},{7,6},{8,11},{9,8},{10,9... | collective-permute-start | bytes 1474568 | tf_op jit(solution)/shard_map/ppermute | solution.py:391
  108.0 24.9 %collective-permute-start.6 = (bf16[160,1536]{1,0:T(8,128)(2,1)}, bf16[160,1536]{1,0:T(8,128)(2,1)}, u32[]{:S(2)}, u32[]{:S(2)}) collective-permute-start(bf16[160,1536]{1,0:T(8,128)(2,1)} %get-tuple-element.76), channel_id=1, source_target_pairs={{0,2},{1,3},{2,0},{3,1},{4,6},{5,7},{6,4},{7,5},{8,10},{9,11},{10,... | collective-permute-start | bytes 1474568 | tf_op jit(solution)/shard_map/ppermute | solution.py:391
  110.5 22.5 %collective-permute-start.5 = (bf16[160,1536]{1,0:T(8,128)(2,1)}, bf16[160,1536]{1,0:T(8,128)(2,1)}, u32[]{:S(2)}, u32[]{:S(2)}) collective-permute-start(bf16[160,1536]{1,0:T(8,128)(2,1)} %get-tuple-element.77), channel_id=1, source_target_pairs={{0,1},{1,2},{2,3},{3,0},{4,5},{5,6},{6,7},{7,4},{8,9},{9,10},{10,1... | collective-permute-start | bytes 1474568 | tf_op jit(solution)/shard_map/ppermute | solution.py:391
  114.1 8.6 %collective-permute-start.3 = (bf16[256,512]{1,0:T(8,128)(2,1)S(1)}, bf16[256,512]{1,0:T(8,128)(2,1)S(1)}, u32[]{:S(2)}, u32[]{:S(2)}) collective-permute-start(bf16[256,512]{1,0:T(8,128)(2,1)S(1)} %slice_bitcast_fusion.3), channel_id=1, source_target_pairs={{0,4},{4,0},{1,5},{5,1},{2,6},{6,2},{3,7},{7,3},{8,12},{12,8},{9,1... | collective-permute-start | bytes 786440 | tf_op jit(solution)/shard_map/ppermute | solution.py:297
  128.1 19.3 %all-to-all-start.2 = ((bf16[4,160,768]{2,1,0:T(8,128)(2,1)}), bf16[4,160,768]{2,1,0:T(8,128)(2,1)S(1)}, u32[]{:S(2)}, u32[]{:S(2)}) async-start(bf16[4,160,768]{2,1,0:T(8,128)(2,1)} %bitcast.94), calls=%async_computation.2 | async-start | bytes 1966080 | tf_op jit(solution)/shard_map/all_to_all | solution.py:23
  133.0 53.0 %all-gather.4.cloned.1.call-start = ((), (), s32[]{:S(2)}) async-start(), calls=%async_computation.8 | async-start | bytes 2457600 | tf_op jit(solution)/shard_map/all_gather | solution.py:421
  134.9 16.4 %collective-permute-start.8 = (bf16[160,768]{1,0:T(8,128)(2,1)S(1)}, bf16[160,768]{1,0:T(8,128)(2,1)}, u32[]{:S(2)}, u32[]{:S(2)}) collective-permute-start(bf16[160,768]{1,0:T(8,128)(2,1)S(1)} %fusion.7.hidden), channel_id=1, source_target_pairs={{0,1},{1,2},{2,3},{3,0},{4,5},{5,6},{6,7},{7,4},{8,9},{9,10},{10,1... | collective-permute-start | bytes 737288 | tf_op jit(solution)/shard_map/ppermute | solution.py:411
  136.4 15.6 %collective-permute-start.9 = (bf16[160,768]{1,0:T(8,128)(2,1)S(1)}, bf16[160,768]{1,0:T(8,128)(2,1)}, u32[]{:S(2)}, u32[]{:S(2)}) collective-permute-start(bf16[160,768]{1,0:T(8,128)(2,1)S(1)} %fusion.7.hidden), channel_id=1, source_target_pairs={{0,2},{1,3},{2,0},{3,1},{4,6},{5,7},{6,4},{7,5},{8,10},{9,11},{10,... | collective-permute-start | bytes 737288 | tf_op jit(solution)/shard_map/ppermute | solution.py:411
  138.7 15.9 %collective-permute-start.10 = (bf16[160,768]{1,0:T(8,128)(2,1)S(1)}, bf16[160,768]{1,0:T(8,128)(2,1)}, u32[]{:S(2)}, u32[]{:S(2)}) collective-permute-start(bf16[160,768]{1,0:T(8,128)(2,1)S(1)} %fusion.7.hidden), channel_id=1, source_target_pairs={{0,3},{1,0},{2,1},{3,2},{4,7},{5,4},{6,5},{7,6},{8,11},{9,8},{10,9... | collective-permute-start | bytes 737288 | tf_op jit(solution)/shard_map/ppermute | solution.py:411
  154.6 15.1 %all-to-all-start.3 = ((f32[16,1,128]{2,1,0:T(1,128)}), f32[16,1,128]{2,1,0:T(1,128)S(1)}, u32[]{:S(2)}, u32[]{:S(2)}) async-start(f32[16,1,128]{2,1,0:T(1,128)} %bitcast.77), calls=%async_computation.3 | async-start | bytes 16384 | tf_op jit(solution)/shard_map/all_to_all | solution.py:23
  172.1 31.1 %all-to-all-start.4 = ((bf16[16,256,128]{2,1,0:T(8,128)(2,1)}), bf16[16,256,128]{2,1,0:T(8,128)(2,1)}, u32[]{:S(2)}, u32[]{:S(2)}) async-start(bf16[16,256,128]{2,1,0:T(8,128)(2,1)} %bitcast.21), calls=%async_computation.4 | async-start | bytes 2097152 | tf_op jit(solution)/shard_map/all_to_all | solution.py:23
  177.9 34.9 %collective-permute-start.11 = (bf16[768,512]{1,0:T(8,128)(2,1)}, bf16[768,512]{1,0:T(8,128)(2,1)}, u32[]{:S(2)}, u32[]{:S(2)}) collective-permute-start(bf16[768,512]{1,0:T(8,128)(2,1)} %convolution_convert_fusion.1), channel_id=1, source_target_pairs={{0,4},{4,0},{1,5},{5,1},{2,6},{6,2},{3,7},{7,3},{8,12},{12,8},{9,1... | collective-permute-start | bytes 2359304 | tf_op jit(solution)/shard_map/ppermute | solution.py:297
  205.2 12.7 %all-to-all-start.5 = ((f32[8,32,128]{2,1,0:T(8,128)}), f32[8,32,128]{2,1,0:T(8,128)S(1)}, u32[]{:S(2)}, u32[]{:S(2)}) async-start(f32[8,32,128]{2,1,0:T(8,128)} %bitcast.22), calls=%async_computation.5 | async-start | bytes 262144 | tf_op jit(solution)/shard_map/all_to_all | solution.py:23
  219.8 20.7 %all-to-all-start.6 = ((bf16[32,64,128]{2,1,0:T(8,128)(2,1)}), bf16[32,64,128]{2,1,0:T(8,128)(2,1)S(1)}, u32[]{:S(2)}, u32[]{:S(2)}) async-start(bf16[32,64,128]{2,1,0:T(8,128)(2,1)} %broadcast_in_dim.54), calls=%async_computation.6 | async-start | bytes 1048576 | tf_op jit(solution)/shard_map/all_to_all | solution.py:23
  240.6 69.2 %all-to-all-start.7 = ((bf16[64,160,128]{2,1,0:T(8,128)(2,1)}), bf16[64,160,128]{2,1,0:T(8,128)(2,1)}, u32[]{:S(2)}, u32[]{:S(2)}) async-start(bf16[64,160,128]{2,1,0:T(8,128)(2,1)} %get-tuple-element.67), calls=%async_computation.7 | async-start | bytes 5242880 | tf_op jit(solution)/shard_map/all_to_all | solution.py:23
  247.5 77.1 %all-gather.6.cloned.1.call-start = ((), (), s32[]{:S(2)}) async-start(), calls=%async_computation.9 | async-start | bytes 1372160 | tf_op jit(solution)/shard_map/all_gather | solution.py:505
  247.6 62.2 %collective-permute-start.13 = (bf16[512,1536]{1,0:T(8,128)(2,1)}, bf16[512,1536]{1,0:T(8,128)(2,1)}, u32[]{:S(2)}, u32[]{:S(2)}) collective-permute-start(bf16[512,1536]{1,0:T(8,128)(2,1)} %convolution_convert_fusion), channel_id=1, source_target_pairs={{0,4},{4,0},{1,5},{5,1},{2,6},{6,2},{3,7},{7,3},{8,12},{12,8},{9,1... | collective-permute-start | bytes 4718600 | tf_op jit(solution)/shard_map/ppermute | solution.py:297
  253.9 55.9 %copy-start.22 = (s32[1,1280]{1,0:T(1,128)S(1)}, s32[1,1280]{1,0:T(1,128)}, u32[]{:S(2)}) copy-start(s32[1,1280]{1,0:T(1,128)} %constant.112.clone.chunk_of) | copy-start | bytes 15364
  257.0 58.4 %copy-start.16 = (f32[1,4096]{1,0:T(1,128)S(1)}, f32[1,4096]{1,0:T(1,128)}, u32[]{:S(2)}) copy-start(f32[1,4096]{1,0:T(1,128)} %gain.3) | copy-start | bytes 49156
  315.0 13.8 %collective-permute-start.12 = (bf16[128,4096]{1,0:T(8,128)(2,1)S(1)}, bf16[128,4096]{1,0:T(8,128)(2,1)S(1)}, u32[]{:S(2)}, u32[]{:S(2)}) collective-permute-start(bf16[128,4096]{1,0:T(8,128)(2,1)S(1)} %shard_map.224), channel_id=1, source_target_pairs={{0,128},{128,0},{1,129},{129,1},{2,130},{130,2},{3,131},{131,3},{4... | collective-permute-start | bytes 3145736 | tf_op jit(solution)/shard_map/ppermute | solution.py:297
  321.0 7.8 %collective-permute-start.14 = (bf16[128,4096]{1,0:T(8,128)(2,1)S(1)}, bf16[128,4096]{1,0:T(8,128)(2,1)}, u32[]{:S(2)}, u32[]{:S(2)}) collective-permute-start(bf16[128,4096]{1,0:T(8,128)(2,1)S(1)} %shard_map.225), channel_id=1, source_target_pairs={{0,128},{128,0},{1,129},{129,1},{2,130},{130,2},{3,131},{131,3},{4... | collective-permute-start | bytes 3145736 | tf_op jit(solution)/shard_map/ppermute | solution.py:297
  (27 other events, 95.7 us)
Sparse Core Ops, SparseCore 0:
  151.4 30.3 all-gather.3
  250.8 30.4 all-gather.5

commit v11 on v10

--- a/solution.py
+++ b/solution.py
@@ -419,17 +419,13 @@
         (summands, pre_act, hidden, at[None] // slots, at[:, None] % slots),
     )
     pre_grad_all = lax.all_gather(pre_grad, "dp", axis=0, tiled=True)
-
     hidden_blocks = [after(block, worth) for block in hidden_blocks]
     hidden_all = jnp.zeros((all_rows, hidden_width), BF)
     for step, block in enumerate(hidden_blocks):
         at_row = (place_in_dp + replicas - step) % replicas * rows
         hidden_all = lax.dynamic_update_slice(hidden_all, block, (at_row, 0))
-    second_other_grad = mm(hidden_all, grad_rows[:, part:], ((0,), (0,))).astype(BF)
-    second_sent = swapped(second_other_grad, "half")
-
-    worth = exchange(worth[:, None], "expert")
-    worth = after(worth, second_other_grad)[:, 0, :slots]
+
+    worth = exchange(worth[:, None], "expert")[:, 0, :slots]
     slot_ids = jnp.arange(slots, dtype=F32)
     gate_worth = jnp.sum(
         jnp.where(place[:, :experts, None] == slot_ids, worth[None], 0.0), axis=2
@@ -439,6 +435,9 @@
     logit_high, logit_low = two_terms(logit_grad)
     local_router = mm(normed, logit_high, ((0,), (0,))) + mm(normed, logit_low, ((0,), (0,)))
     local_router = local_router.astype(BF).reshape(experts, -1, router_width)
+    second_other_grad = mm(hidden_all, grad_rows[:, part:], ((0,), (0,))).astype(BF)
+    second_sent = swapped(second_other_grad, "half")
+    local_router = after(local_router, second_other_grad)
     steps = 2 if all_rows // 2 % (2 * group * slots) == 0 else 1
 
     def by_rows(width):
@@ -456,11 +455,14 @@
         out_specs=messages,
     )
     summed = exchange(local_router, "expert")
+    router_part = jnp.sum(after(summed, out_message).astype(F32), axis=0)
+    piece = router_part.shape[0] // (2 * replicas)
+    router_part = exchange(router_part.reshape(2 * replicas, piece, router_width), ("half", "dp"))
 
     message, gain_part = kernel_call(
         functools.partial(back_kernel, group, chunks, slots),
         (jax.ShapeDtypeStruct((peers, 2 * half, LANES), BF), jax.ShapeDtypeStruct((1, 2 * part), F32)),
-        (index, pre_grad_all, order, first, expert_rows, out_message) + first_other,
+        (index, pre_grad_all, order, first, expert_rows, after(out_message, second_sent)) + first_other,
         grid=(steps,),
         in_specs=[
             scalar,
@@ -476,10 +478,7 @@
             whole((1, 2 * part)),
         ],
     )
-    router_part = jnp.sum(after(summed, out_message, gain_part).astype(F32), axis=0)
-    piece = router_part.shape[0] // (2 * replicas)
-    router_part = exchange(router_part.reshape(2 * replicas, piece, router_width), ("half", "dp"))
-    router_own = jnp.sum(after(router_part, second_sent), axis=0)
+    router_own = jnp.sum(after(router_part, gain_part), axis=0)
     at = lax.axis_index("expert") * 2 * replicas + side * replicas + place_in_dp
     table_own = lax.dynamic_slice_in_dim(table, at * piece, piece, axis=0).astype(F32)
     gain_own = jnp.sum(router_own * table_own, axis=1)
@@ -495,7 +494,8 @@
     joined = exchange(jnp.broadcast_to(block[None], (owners,) + block.shape), OWNERS)
     first_other_grad = mm(expert_rows[:, part:], pre_grad_all, ((0,), (0,))).astype(BF)
     first_sent = swapped(first_other_grad, "half")
-    returned = exchange(after(message, joined, first_other_grad), SHARE)
+    message, joined = lax.optimization_barrier((message, joined, first_other_grad))[:2]
+    returned = exchange(message, SHARE)
     end = piece + 3 * lines
     gain_rows = jnp.sum(joined[:, piece:end].astype(F32).reshape(owners, 3, lines, LANES), axis=(0, 1))
     lone = jnp.sum(joined[:, end : end + 3, :piece].astype(F32), axis=1).reshape(-1, LANES)

time: 342 us -> 347 us (1.015)
  waiting for transfers between devices: 137 us -> 141 us
  transfers between devices with their start and end apart: 25 -> 25, of which waited for: 13 -> 12; matrix products, arithmetic and copies ran while one was open for 11% -> 10% of each run, Pallas kernels for 15% -> 14%
where the time goes in v11:
time: 347 us; the launch traced here: 344 us
  waiting for transfers between devices  141 us (41%)
  starting transfers between devices  88.6 us (26%)
  Pallas kernels  49.1 us (14%)
  local copies, waits for them, and re-layouts  27.8 us (8%)
  between operations  14.6 us (4%)
  matrix products  14.2 us (4%)
  other arithmetic  8.98 us (3%)
    ppermute x9, waiting for transfers between devices, swapped(): return lax.ppermute(block, axis, [(0, 1), (1, 0)])  98.4 us
    all_to_all x8, starting transfers between devices, exchange(): return lax.all_to_all(blocks, axes, split_axis=0, concat_axis=0, tiled=True)  61.8 us
    pallas_call x9, Pallas kernels, kernel_call(): pl.pallas_call(body, out_shape=outs, scratch_shapes=scratch, compiler_par...  49.1 us
    all_to_all x8, waiting for transfers between devices, exchange(): return lax.all_to_all(blocks, axes, split_axis=0, concat_axis=0, tiled=True)  39.1 us
    ppermute x9, starting transfers between devices, swapped(): return lax.ppermute(block, axis, [(0, 1), (1, 0)])  17 us
    dot_general x6, matrix products, mm(): lax.dot_general(left, right, (contract, ((), ())), preferred_element_type...  14.2 us
    unnamed x72, local copies, waits for them, and re-layouts  11.7 us
  transfers between devices with their start and end apart: 25, of which 12 were waited for; matrix products, arithmetic and copies ran while one was open for 10% of the time, Pallas kernels for 14%

profile of v11, /device:TPU:8, one launch (start us, length us, event | category | flops | bytes accessed | tf_op | source)
XLA Modules:
  0.0 344.2 jit_solution(2815237500659994444)
XLA Ops:
  8.2 3.1 collective-permute-start
  15.3 4.9 %shard_map.217 = (bf16[64,80,128]{2,1,0:T(8,128)(2,1)}, bf16[128,4096]{1,0:T(8,128)(2,1)S(1)}, f32[128,128]{1,0:T(8,128)S(1)}) custom-call(bf16[128,4096]{1,0:T(8,128)(2,1)} %bitcast.80, s32[128,8]{1,0:T(8,128)S(1)} %bitcast.75, f32[1,4096]{1,0:T(1,128)S(1)} %copy-done.15, s32[1,1280]{1,0:T(1,128)S(1)} %copy-done.17, s32[1280,1]{1,0:T(8,128)S(1)} %copy-done.4, ...), custom_call_target="tpu_custom_call" | custom-call | tf_op jit(solution)/shard_map/pallas_call | solution.py:41
  20.6 13.2 %all-to-all-start = ((bf16[64,80,128]{2,1,0:T(8,128)(2,1)}), bf16[64,80,128]{2,1,0:T(8,128)(2,1)}, u32[]{:S(2)}, u32[]{:S(2)}) async-start(bf16[64,80,128]{2,1,0:T(8,128)(2,1)} %get-tuple-element.45), calls=%async_computation | async-start | bytes 2621440 | tf_op jit(solution)/shard_map/all_to_all | solution.py:23
  35.2 2.8 collective-permute-start.1
  38.1 5.7 %shard_map.218 = (bf16[64,80,128]{2,1,0:T(8,128)(2,1)}, f32[128,128]{1,0:T(8,128)S(1)}) custom-call(bf16[128,4096]{1,0:T(8,128)(2,1)S(1)} %get-tuple-element.41.normed, s32[128,8]{1,0:T(8,128)S(1)} %bitcast.76, bf16[128,4096]{1,0:T(8,128)(2,1)} %bitcast.85, bf16[4096,128]{1,0:T(8,128)(2,1)} %bitcast.83, f32[128,128]{1,0:T(8,128)S(1)} %get-tuple-element.42.place, ...), custom_call_target="tpu_custom_call" | custom-call | tf_op jit(solution)/shard_map/pallas_call | solution.py:41
  44.3 27.5 %collective-permute-done.1.refs_2_.refs_1_ = bf16[320,1536]{1,0:T(8,128)(2,1)S(1)} collective-permute-done((bf16[320,1536]{1,0:T(8,128)(2,1)S(1)}, bf16[320,1536]{1,0:T(8,128)(2,1)S(1)}, u32[]{:S(2)}, u32[]{:S(2)}) %collective-permute-start.1) | collective-permute-done | bytes 983072 | tf_op jit(solution)/shard_map/ppermute | solution.py:297
  71.8 10.4 %all-to-all-start.1 = ((bf16[64,80,128]{2,1,0:T(8,128)(2,1)}), bf16[64,80,128]{2,1,0:T(8,128)(2,1)}, u32[]{:S(2)}, u32[]{:S(2)}) async-start(bf16[64,80,128]{2,1,0:T(8,128)(2,1)} %get-tuple-element.46), calls=%async_computation.1 | async-start | bytes 2621440 | tf_op jit(solution)/shard_map/all_to_all | solution.py:23
  88.2 8.5 %collective-permute-done.4.refs_3_.refs_2_ = bf16[64,1536]{1,0:T(8,128)(2,1)} collective-permute-done((bf16[64,1536]{1,0:T(8,128)(2,1)}, bf16[64,1536]{1,0:T(8,128)(2,1)}, u32[]{:S(2)}, u32[]{:S(2)}) %collective-permute-start.4) | collective-permute-done | bytes 196640 | tf_op jit(solution)/shard_map/ppermute | solution.py:297
  96.7 7.9 %shard_map.220 = (bf16[640,1536]{1,0:T(8,128)(2,1)}, bf16[640,1024]{1,0:T(8,128)(2,1)}) custom-call(s32[1]{0:T(128)} %bitcast.index, bf16[64,80,128]{2,1,0:T(8,128)(2,1)} %all-to-all-done.arrived, s32[640,1]{1,0:T(8,128)S(1)} %copy-done.1, bf16[512,1536]{1,0:T(8,128)(2,1)} %bitcast.78, bf16[128,1536]{1,0:T(8,128)(2,1)S(1)} %collective-permute-done.refs_1_.refs_0_, ...), custom_call_target="tpu_custom_call" | custom-call | tf_op jit(solution)/shard_map/pallas_call | solution.py:41
  104.6 2.8 dynamic-slice_bitcast_fusion.3
  115.9 6.8 %collective-permute-done.3.refs_2_.late = bf16[256,512]{1,0:T(8,128)(2,1)S(1)} collective-permute-done((bf16[256,512]{1,0:T(8,128)(2,1)S(1)}, bf16[256,512]{1,0:T(8,128)(2,1)S(1)}, u32[]{:S(2)}, u32[]{:S(2)}) %collective-permute-start.3) | collective-permute-done | bytes 262176 | tf_op jit(solution)/shard_map/ppermute | solution.py:297
  122.7 5.4 %shard_map.219 = (bf16[640,768]{1,0:T(8,128)(2,1)}, bf16[640,1024]{1,0:T(8,128)(2,1)}) custom-call(s32[1]{0:T(128)} %bitcast.index, bf16[64,80,128]{2,1,0:T(8,128)(2,1)} %all-to-all-done.1.arrived, s32[640,1]{1,0:T(8,128)S(1)} %copy-done.1, bf16[768,512]{1,0:T(8,128)(2,1)S(1)} %bitcast.72, bf16[512,512]{1,0:T(8,128)(2,1)} %collective-permute-done.2.refs_1_.early, ...), custom_call_target="tpu_custom_call" | custom-call | tf_op jit(solution)/shard_map/pallas_call | solution.py:41
  128.1 4.9 %all-to-all-start.2 = ((bf16[4,160,768]{2,1,0:T(8,128)(2,1)}), bf16[4,160,768]{2,1,0:T(8,128)(2,1)S(1)}, u32[]{:S(2)}, u32[]{:S(2)}) async-start(bf16[4,160,768]{2,1,0:T(8,128)(2,1)} %bitcast.95), calls=%async_computation.2 | async-start | bytes 1966080 | tf_op jit(solution)/shard_map/all_to_all | solution.py:23
  140.4 7.0 %all-to-all-done.2.arrived = bf16[4,160,768]{2,1,0:T(8,128)(2,1)S(1)} async-done(((bf16[4,160,768]{2,1,0:T(8,128)(2,1)}), bf16[4,160,768]{2,1,0:T(8,128)(2,1)S(1)}, u32[]{:S(2)}, u32[]{:S(2)}) %all-to-all-start.2) | async-done | bytes 983072 | tf_op jit(solution)/shard_map/all_to_all | solution.py:23
  152.0 2.6 collective-permute-done.10
  154.6 6.8 %all-to-all-start.3 = ((f32[16,1,128]{2,1,0:T(1,128)}), f32[16,1,128]{2,1,0:T(1,128)S(1)}, u32[]{:S(2)}, u32[]{:S(2)}) async-start(f32[16,1,128]{2,1,0:T(1,128)} %bitcast.77), calls=%async_computation.3 | async-start | bytes 16384 | tf_op jit(solution)/shard_map/all_to_all | solution.py:23
  172.1 5.7 %all-to-all-start.4 = ((bf16[16,256,128]{2,1,0:T(8,128)(2,1)}), bf16[16,256,128]{2,1,0:T(8,128)(2,1)S(1)}, u32[]{:S(2)}, u32[]{:S(2)}) async-start(bf16[16,256,128]{2,1,0:T(8,128)(2,1)} %bitcast.88), calls=%async_computation.4 | async-start | bytes 2097152 | tf_op jit(solution)/shard_map/all_to_all | solution.py:23
  177.8 3.1 collective-permute-start.11
  180.9 4.7 %shard_map.222.outs = bf16[64,80,128]{2,1,0:T(8,128)(2,1)} custom-call(s32[1]{0:T(128)} %bitcast.index, bf16[640,768]{1,0:T(8,128)(2,1)} %copy-done.26, s32[640,1]{1,0:T(8,128)S(1)} %copy-done.1, bf16[768,512]{1,0:T(8,128)(2,1)S(1)} %bitcast.73, bf16[512,512]{1,0:T(8,128)(2,1)} %collective-permute-done.2.refs_1_.early, bf16[256,512]{1,0:T(8,128)(2,1)S(1)} %copy-done.11), custom_call_target="tpu_custom_call" | custom-call | tf_op jit(solution)/shard_map/pallas_call | solution.py:41
  185.6 17.4 %all-to-all-done.4 = bf16[16,256,128]{2,1,0:T(8,128)(2,1)S(1)} async-done(((bf16[16,256,128]{2,1,0:T(8,128)(2,1)}), bf16[16,256,128]{2,1,0:T(8,128)(2,1)S(1)}, u32[]{:S(2)}, u32[]{:S(2)}) %all-to-all-start.4) | async-done | bytes 1048608 | tf_op jit(solution)/shard_map/all_to_all | solution.py:23
  203.8 6.1 %all-to-all-start.5 = ((f32[8,32,128]{2,1,0:T(8,128)}), f32[8,32,128]{2,1,0:T(8,128)S(1)}, u32[]{:S(2)}, u32[]{:S(2)}) async-start(f32[8,32,128]{2,1,0:T(8,128)} %bitcast.22), calls=%async_computation.5 | async-start | bytes 262144 | tf_op jit(solution)/shard_map/all_to_all | solution.py:23
  209.9 7.9 %shard_map.223 = (bf16[64,160,128]{2,1,0:T(8,128)(2,1)}, f32[1,1024]{1,0:T(1,128)S(1)}) custom-call(s32[1]{0:T(128)} %bitcast.index, bf16[640,1536]{1,0:T(8,128)(2,1)} %all-gather.4.cloned.1.call-done.pre_grad, s32[640,1]{1,0:T(8,128)S(1)} %copy-done.1, bf16[512,1536]{1,0:T(8,128)(2,1)} %bitcast.79, bf16[640,1024]{1,0:T(8,128)(2,1)} %get-tuple-element.56.rows, ...), custom_call_target="tpu_custom_call" | custom-call | tf_op jit(solution)/shard_map/pallas_call | solution.py:41
  221.1 7.0 %all-to-all-start.6 = ((bf16[32,64,128]{2,1,0:T(8,128)(2,1)}), bf16[32,64,128]{2,1,0:T(8,128)(2,1)S(1)}, u32[]{:S(2)}, u32[]{:S(2)}) async-start(bf16[32,64,128]{2,1,0:T(8,128)(2,1)} %broadcast_in_dim.54), calls=%async_computation.6 | async-start | bytes 1048576 | tf_op jit(solution)/shard_map/all_to_all | solution.py:23
  228.1 4.3 %convolution_convert_fusion = bf16[512,1536]{1,0:T(8,128)(2,1)} fusion(bf16[640,1536]{1,0:T(8,128)(2,1)} %all-gather.4.cloned.1.call-done.pre_grad, bf16[640,1024]{1,0:T(8,128)(2,1)} %get-tuple-element.56.rows), kind=kOutput, calls=%fused_computation.3 | convolution fusion | flops 1007419392 | bytes 4194304 | tf_op jit(solution)/shard_map/dot_general | solution.py:27
  232.4 12.2 %all-to-all-done.6 = bf16[32,64,128]{2,1,0:T(8,128)(2,1)S(1)} async-done(((bf16[32,64,128]{2,1,0:T(8,128)(2,1)}), bf16[32,64,128]{2,1,0:T(8,128)(2,1)S(1)}, u32[]{:S(2)}, u32[]{:S(2)}) %all-to-all-start.6) | async-done | bytes 524320 | tf_op jit(solution)/shard_map/all_to_all | solution.py:23
  244.6 7.7 %all-to-all-start.7 = ((bf16[64,160,128]{2,1,0:T(8,128)(2,1)}), bf16[64,160,128]{2,1,0:T(8,128)(2,1)}, u32[]{:S(2)}, u32[]{:S(2)}) async-start(bf16[64,160,128]{2,1,0:T(8,128)(2,1)} %get-tuple-element.70), calls=%async_computation.7 | async-start | bytes 5242880 | tf_op jit(solution)/shard_map/all_to_all | solution.py:23
  255.6 3.2 add_convert_fusion.1
  258.7 3.1 fusion.2
  261.8 53.5 %collective-permute-done.13 = bf16[512,1536]{1,0:T(8,128)(2,1)} collective-permute-done((bf16[512,1536]{1,0:T(8,128)(2,1)}, bf16[512,1536]{1,0:T(8,128)(2,1)}, u32[]{:S(2)}, u32[]{:S(2)}) %collective-permute-start.13) | collective-permute-done | bytes 1572896 | tf_op jit(solution)/shard_map/ppermute | solution.py:297
  315.3 5.3 %shard_map.224 = bf16[128,4096]{1,0:T(8,128)(2,1)S(1)} custom-call(bf16[64,160,128]{2,1,0:T(8,128)(2,1)} %all-to-all-done.7.returned, bf16[128,4096]{1,0:T(8,128)(2,1)} %bitcast.81, f32[128,128]{1,0:T(8,128)S(1)} %copy-done.14, f32[128,128]{1,0:T(8,128)S(1)} %copy-done.9, s32[1,1280]{1,0:T(1,128)S(1)} %copy-done.18, s32[1,1280]{1,0:T(1,128)S(1)} %copy-done.22, ...), custom_call_target="tpu_custom_call" | custom-call | tf_op jit(solution)/shard_map/pallas_call | solution.py:41
  320.7 5.6 %shard_map.225 = bf16[128,4096]{1,0:T(8,128)(2,1)S(1)} custom-call(bf16[64,160,128]{2,1,0:T(8,128)(2,1)} %all-to-all-done.7.returned, bf16[128,4096]{1,0:T(8,128)(2,1)} %bitcast.82, bf16[128,4096]{1,0:T(8,128)(2,1)} %bitcast.86, f32[1,4096]{1,0:T(1,128)S(1)} %copy-done.16, bf16[4096,128]{1,0:T(8,128)(2,1)} %bitcast.84, f32[128,128]{1,0:T(8,128)S(1)} %copy-done.9, ...), custom_call_target="tpu_custom_call" | custom-call | tf_op jit(solution)/shard_map/pallas_call | solution.py:41
  326.9 3.0 fusion.1
  (167 shorter events, 59.8 us)
Async XLA Ops:
  8.2 12.4 %collective-permute-start = (bf16[128,1536]{1,0:T(8,128)(2,1)S(1)}, bf16[128,1536]{1,0:T(8,128)(2,1)S(1)}, u32[]{:S(2)}, u32[]{:S(2)}) collective-permute-start(bf16[128,1536]{1,0:T(8,128)(2,1)S(1)} %slice_bitcast_fusion.2), channel_id=1, source_target_pairs={{0,4},{4,0},{1,5},{5,1},{2,6},{6,2},{3,7},{7,3},{8,12},{12,8},{9,1... | collective-permute-start | bytes 1179656 | tf_op jit(solution)/shard_map/ppermute | solution.py:297
  20.6 76.0 %copy-start.6 = (bf16[128,1536]{1,0:T(8,128)(2,1)}, bf16[128,1536]{1,0:T(8,128)(2,1)S(1)}, u32[]{:S(2)}) copy-start(bf16[128,1536]{1,0:T(8,128)(2,1)S(1)} %collective-permute-done.refs_1_.refs_0_) | copy-start | bytes 1179652
  20.6 51.2 %all-to-all-start = ((bf16[64,80,128]{2,1,0:T(8,128)(2,1)}), bf16[64,80,128]{2,1,0:T(8,128)(2,1)}, u32[]{:S(2)}, u32[]{:S(2)}) async-start(bf16[64,80,128]{2,1,0:T(8,128)(2,1)} %get-tuple-element.45), calls=%async_computation | async-start | bytes 2621440 | tf_op jit(solution)/shard_map/all_to_all | solution.py:23
  35.2 36.6 %collective-permute-start.1 = (bf16[320,1536]{1,0:T(8,128)(2,1)S(1)}, bf16[320,1536]{1,0:T(8,128)(2,1)S(1)}, u32[]{:S(2)}, u32[]{:S(2)}) collective-permute-start(bf16[320,1536]{1,0:T(8,128)(2,1)S(1)} %slice_bitcast_fusion), channel_id=1, source_target_pairs={{0,4},{4,0},{1,5},{5,1},{2,6},{6,2},{3,7},{7,3},{8,12},{12,8},{9,1... | collective-permute-start | bytes 2949128 | tf_op jit(solution)/shard_map/ppermute | solution.py:297
  44.3 41.5 %copy-start = (bf16[1,1,768,512]{3,2,1,0:T(8,128)(2,1)S(1)}, bf16[1,1,768,512]{3,2,1,0:T(8,128)(2,1)}, u32[]{:S(2)}) copy-start(bf16[1,1,768,512]{3,2,1,0:T(8,128)(2,1)} %param.24) | copy-start | bytes 2359300
  71.8 24.8 %copy-start.2 = (bf16[320,1536]{1,0:T(8,128)(2,1)}, bf16[320,1536]{1,0:T(8,128)(2,1)S(1)}, u32[]{:S(2)}) copy-start(bf16[320,1536]{1,0:T(8,128)(2,1)S(1)} %collective-permute-done.1.refs_2_.refs_1_) | copy-start | bytes 2949124
  71.8 24.8 %copy-start.1 = (s32[640,1]{1,0:T(8,128)S(1)}, s32[640,1]{1,0:T(8,128)}, u32[]{:S(2)}) copy-start(s32[640,1]{1,0:T(8,128)} %constant.109.clone.order) | copy-start | bytes 7684
  71.8 50.9 %all-to-all-start.1 = ((bf16[64,80,128]{2,1,0:T(8,128)(2,1)}), bf16[64,80,128]{2,1,0:T(8,128)(2,1)}, u32[]{:S(2)}, u32[]{:S(2)}) async-start(bf16[64,80,128]{2,1,0:T(8,128)(2,1)} %get-tuple-element.46), calls=%async_computation.1 | async-start | bytes 2621440 | tf_op jit(solution)/shard_map/all_to_all | solution.py:23
  83.8 12.8 %collective-permute-start.4 = (bf16[64,1536]{1,0:T(8,128)(2,1)}, bf16[64,1536]{1,0:T(8,128)(2,1)}, u32[]{:S(2)}, u32[]{:S(2)}) collective-permute-start(bf16[64,1536]{1,0:T(8,128)(2,1)} %slice_bitcast_fusion.4), channel_id=1, source_target_pairs={{0,4},{4,0},{1,5},{5,1},{2,6},{6,2},{3,7},{7,3},{8,12},{12,8},{9,1... | collective-permute-start | bytes 589832 | tf_op jit(solution)/shard_map/ppermute | solution.py:297
  86.7 27.4 %collective-permute-start.2 = (bf16[512,512]{1,0:T(8,128)(2,1)}, bf16[512,512]{1,0:T(8,128)(2,1)}, u32[]{:S(2)}, u32[]{:S(2)}) collective-permute-start(bf16[512,512]{1,0:T(8,128)(2,1)} %slice_bitcast_fusion.1), channel_id=1, source_target_pairs={{0,4},{4,0},{1,5},{5,1},{2,6},{6,2},{3,7},{7,3},{8,12},{12,8},{9,1... | collective-permute-start | bytes 1572872 | tf_op jit(solution)/shard_map/ppermute | solution.py:297
  107.4 25.6 %collective-permute-start.7 = (bf16[160,1536]{1,0:T(8,128)(2,1)}, bf16[160,1536]{1,0:T(8,128)(2,1)}, u32[]{:S(2)}, u32[]{:S(2)}) collective-permute-start(bf16[160,1536]{1,0:T(8,128)(2,1)} %get-tuple-element.79), channel_id=1, source_target_pairs={{0,3},{1,0},{2,1},{3,2},{4,7},{5,4},{6,5},{7,6},{8,11},{9,8},{10,9... | collective-permute-start | bytes 1474568 | tf_op jit(solution)/shard_map/ppermute | solution.py:391
  107.9 25.0 %collective-permute-start.6 = (bf16[160,1536]{1,0:T(8,128)(2,1)}, bf16[160,1536]{1,0:T(8,128)(2,1)}, u32[]{:S(2)}, u32[]{:S(2)}) collective-permute-start(bf16[160,1536]{1,0:T(8,128)(2,1)} %get-tuple-element.80), channel_id=1, source_target_pairs={{0,2},{1,3},{2,0},{3,1},{4,6},{5,7},{6,4},{7,5},{8,10},{9,11},{10,... | collective-permute-start | bytes 1474568 | tf_op jit(solution)/shard_map/ppermute | solution.py:391
  110.4 22.5 %collective-permute-start.5 = (bf16[160,1536]{1,0:T(8,128)(2,1)}, bf16[160,1536]{1,0:T(8,128)(2,1)}, u32[]{:S(2)}, u32[]{:S(2)}) collective-permute-start(bf16[160,1536]{1,0:T(8,128)(2,1)} %get-tuple-element.81), channel_id=1, source_target_pairs={{0,1},{1,2},{2,3},{3,0},{4,5},{5,6},{6,7},{7,4},{8,9},{9,10},{10,1... | collective-permute-start | bytes 1474568 | tf_op jit(solution)/shard_map/ppermute | solution.py:391
  114.1 8.6 %collective-permute-start.3 = (bf16[256,512]{1,0:T(8,128)(2,1)S(1)}, bf16[256,512]{1,0:T(8,128)(2,1)S(1)}, u32[]{:S(2)}, u32[]{:S(2)}) collective-permute-start(bf16[256,512]{1,0:T(8,128)(2,1)S(1)} %slice_bitcast_fusion.3), channel_id=1, source_target_pairs={{0,4},{4,0},{1,5},{5,1},{2,6},{6,2},{3,7},{7,3},{8,12},{12,8},{9,1... | collective-permute-start | bytes 786440 | tf_op jit(solution)/shard_map/ppermute | solution.py:297
  128.1 19.3 %all-to-all-start.2 = ((bf16[4,160,768]{2,1,0:T(8,128)(2,1)}), bf16[4,160,768]{2,1,0:T(8,128)(2,1)S(1)}, u32[]{:S(2)}, u32[]{:S(2)}) async-start(bf16[4,160,768]{2,1,0:T(8,128)(2,1)} %bitcast.95), calls=%async_computation.2 | async-start | bytes 1966080 | tf_op jit(solution)/shard_map/all_to_all | solution.py:23
  133.0 77.0 %all-gather.4.cloned.1.call-start = ((), (), s32[]{:S(2)}) async-start(), calls=%async_computation.8 | async-start | bytes 2457600 | tf_op jit(solution)/shard_map/all_gather | solution.py:421
  134.9 16.4 %collective-permute-start.8 = (bf16[160,768]{1,0:T(8,128)(2,1)S(1)}, bf16[160,768]{1,0:T(8,128)(2,1)}, u32[]{:S(2)}, u32[]{:S(2)}) collective-permute-start(bf16[160,768]{1,0:T(8,128)(2,1)S(1)} %fusion.7.hidden), channel_id=1, source_target_pairs={{0,1},{1,2},{2,3},{3,0},{4,5},{5,6},{6,7},{7,4},{8,9},{9,10},{10,1... | collective-permute-start | bytes 737288 | tf_op jit(solution)/shard_map/ppermute | solution.py:411
  136.4 15.6 %collective-permute-start.9 = (bf16[160,768]{1,0:T(8,128)(2,1)S(1)}, bf16[160,768]{1,0:T(8,128)(2,1)}, u32[]{:S(2)}, u32[]{:S(2)}) collective-permute-start(bf16[160,768]{1,0:T(8,128)(2,1)S(1)} %fusion.7.hidden), channel_id=1, source_target_pairs={{0,2},{1,3},{2,0},{3,1},{4,6},{5,7},{6,4},{7,5},{8,10},{9,11},{10,... | collective-permute-start | bytes 737288 | tf_op jit(solution)/shard_map/ppermute | solution.py:411
  138.7 15.9 %collective-permute-start.10 = (bf16[160,768]{1,0:T(8,128)(2,1)S(1)}, bf16[160,768]{1,0:T(8,128)(2,1)}, u32[]{:S(2)}, u32[]{:S(2)}) collective-permute-start(bf16[160,768]{1,0:T(8,128)(2,1)S(1)} %fusion.7.hidden), channel_id=1, source_target_pairs={{0,3},{1,0},{2,1},{3,2},{4,7},{5,4},{6,5},{7,6},{8,11},{9,8},{10,9... | collective-permute-start | bytes 737288 | tf_op jit(solution)/shard_map/ppermute | solution.py:411
  154.6 15.1 %all-to-all-start.3 = ((f32[16,1,128]{2,1,0:T(1,128)}), f32[16,1,128]{2,1,0:T(1,128)S(1)}, u32[]{:S(2)}, u32[]{:S(2)}) async-start(f32[16,1,128]{2,1,0:T(1,128)} %bitcast.77), calls=%async_computation.3 | async-start | bytes 16384 | tf_op jit(solution)/shard_map/all_to_all | solution.py:23
  172.1 30.9 %all-to-all-start.4 = ((bf16[16,256,128]{2,1,0:T(8,128)(2,1)}), bf16[16,256,128]{2,1,0:T(8,128)(2,1)S(1)}, u32[]{:S(2)}, u32[]{:S(2)}) async-start(bf16[16,256,128]{2,1,0:T(8,128)(2,1)} %bitcast.88), calls=%async_computation.4 | async-start | bytes 2097152 | tf_op jit(solution)/shard_map/all_to_all | solution.py:23
  177.8 32.1 %collective-permute-start.11 = (bf16[768,512]{1,0:T(8,128)(2,1)}, bf16[768,512]{1,0:T(8,128)(2,1)}, u32[]{:S(2)}, u32[]{:S(2)}) collective-permute-start(bf16[768,512]{1,0:T(8,128)(2,1)} %convolution_convert_fusion.1), channel_id=1, source_target_pairs={{0,4},{4,0},{1,5},{5,1},{2,6},{6,2},{3,7},{7,3},{8,12},{12,8},{9,1... | collective-permute-start | bytes 2359304 | tf_op jit(solution)/shard_map/ppermute | solution.py:297
  185.6 24.3 %copy-start.7 = (bf16[128,1536]{1,0:T(8,128)(2,1)S(1)}, bf16[128,1536]{1,0:T(8,128)(2,1)}, u32[]{:S(2)}) copy-start(bf16[128,1536]{1,0:T(8,128)(2,1)} %copy-done.6) | copy-start | bytes 1179652
  203.8 14.0 %all-to-all-start.5 = ((f32[8,32,128]{2,1,0:T(8,128)}), f32[8,32,128]{2,1,0:T(8,128)S(1)}, u32[]{:S(2)}, u32[]{:S(2)}) async-start(f32[8,32,128]{2,1,0:T(8,128)} %bitcast.22), calls=%async_computation.5 | async-start | bytes 262144 | tf_op jit(solution)/shard_map/all_to_all | solution.py:23
  221.1 23.5 %all-to-all-start.6 = ((bf16[32,64,128]{2,1,0:T(8,128)(2,1)}), bf16[32,64,128]{2,1,0:T(8,128)(2,1)S(1)}, u32[]{:S(2)}, u32[]{:S(2)}) async-start(bf16[32,64,128]{2,1,0:T(8,128)(2,1)} %broadcast_in_dim.54), calls=%async_computation.6 | async-start | bytes 1048576 | tf_op jit(solution)/shard_map/all_to_all | solution.py:23
  244.6 70.7 %all-to-all-start.7 = ((bf16[64,160,128]{2,1,0:T(8,128)(2,1)}), bf16[64,160,128]{2,1,0:T(8,128)(2,1)}, u32[]{:S(2)}, u32[]{:S(2)}) async-start(bf16[64,160,128]{2,1,0:T(8,128)(2,1)} %get-tuple-element.70), calls=%async_computation.7 | async-start | bytes 5242880 | tf_op jit(solution)/shard_map/all_to_all | solution.py:23
  252.4 77.5 %all-gather.6.cloned.1.call-start = ((), (), s32[]{:S(2)}) async-start(), calls=%async_computation.9 | async-start | bytes 1372160 | tf_op jit(solution)/shard_map/all_gather | solution.py:505
  252.4 62.9 %collective-permute-start.13 = (bf16[512,1536]{1,0:T(8,128)(2,1)}, bf16[512,1536]{1,0:T(8,128)(2,1)}, u32[]{:S(2)}, u32[]{:S(2)}) collective-permute-start(bf16[512,1536]{1,0:T(8,128)(2,1)} %convolution_convert_fusion), channel_id=1, source_target_pairs={{0,4},{4,0},{1,5},{5,1},{2,6},{6,2},{3,7},{7,3},{8,12},{12,8},{9,1... | collective-permute-start | bytes 4718600 | tf_op jit(solution)/shard_map/ppermute | solution.py:297
  258.7 56.5 %copy-start.22 = (s32[1,1280]{1,0:T(1,128)S(1)}, s32[1,1280]{1,0:T(1,128)}, u32[]{:S(2)}) copy-start(s32[1,1280]{1,0:T(1,128)} %constant.112.clone.chunk_of) | copy-start | bytes 15364
  261.8 58.9 %copy-start.16 = (f32[1,4096]{1,0:T(1,128)S(1)}, f32[1,4096]{1,0:T(1,128)}, u32[]{:S(2)}) copy-start(f32[1,4096]{1,0:T(1,128)} %gain.3) | copy-start | bytes 49156
  320.6 13.5 %collective-permute-start.12 = (bf16[128,4096]{1,0:T(8,128)(2,1)S(1)}, bf16[128,4096]{1,0:T(8,128)(2,1)S(1)}, u32[]{:S(2)}, u32[]{:S(2)}) collective-permute-start(bf16[128,4096]{1,0:T(8,128)(2,1)S(1)} %shard_map.224), channel_id=1, source_target_pairs={{0,128},{128,0},{1,129},{129,1},{2,130},{130,2},{3,131},{131,3},{4... | collective-permute-start | bytes 3145736 | tf_op jit(solution)/shard_map/ppermute | solution.py:297
  326.3 7.8 %collective-permute-start.14 = (bf16[128,4096]{1,0:T(8,128)(2,1)S(1)}, bf16[128,4096]{1,0:T(8,128)(2,1)}, u32[]{:S(2)}, u32[]{:S(2)}) collective-permute-start(bf16[128,4096]{1,0:T(8,128)(2,1)S(1)} %shard_map.225), channel_id=1, source_target_pairs={{0,128},{128,0},{1,129},{129,1},{2,130},{130,2},{3,131},{131,3},{4... | collective-permute-start | bytes 3145736 | tf_op jit(solution)/shard_map/ppermute | solution.py:297
  (27 other events, 128.0 us)
Sparse Core Ops, SparseCore 0:
  151.4 30.3 all-gather.3
  255.7 30.2 all-gather.5
